TPU v7x, 32 devices: a whole 2x2x4 slice. The times are simulated.
32 devices in a mesh: seq: 8 (over z, y), grp: 4 (over x, core).
Axes of the slice: x: 2, y: 2, z: 4, core: 2. Of those that a mesh axis runs over, the one named last changes fastest.
Arguments:
- tokens: bfloat16 [2, 8192, 2048], P(None, 'seq'), may hold values from -6 to 6
- cotangent: bfloat16 [2, 8192, 2048], P(None, 'seq'), may hold values from -6 to 6
- lengths: int32 [2, 6], replicated, may hold values from 1 to 7872, as said below
- attention_norm_gain: bfloat16 [2048], replicated, may hold values from 0.099609375 to 1.8984375
- feedforward_norm_gain: bfloat16 [2048], replicated, may hold values from 0.099609375 to 1.8984375
- query_weight: bfloat16 [2048, 2048], P('seq', 'grp'), may hold values from -0.125 to 0.125
- keyvalue_weight: bfloat16 [2048, 2, 512], P('seq', None, 'grp'), may hold values from -0.125 to 0.125
- output_weight: bfloat16 [2048, 2048], P('grp', 'seq'), may hold values from -1 to 1
- gate_up_weight: bfloat16 [2048, 2, 8192], P('seq', None, 'grp'), may hold values from -0.125 to 0.125
- down_weight: bfloat16 [8192, 2048], P('grp', 'seq'), may hold values from -0.0625 to 0.0625
- adapter_width_factor: bfloat16 [4, 2048, 8], P(None, 'seq'), may hold values from -0.125 to 0.125
- query_up_factor: bfloat16 [8, 2048], P(None, 'grp'), may hold values from -1 to 1
- keyvalue_up_factor: bfloat16 [2, 8, 512], P(None, None, 'grp'), may hold values from -1 to 1
- output_input_factor: bfloat16 [2048, 8], P('grp'), may hold values from -1 to 1
- query_feature_weight: bfloat16 [32, 64, 64], P('grp'), may hold values from -0.75 to 0.75
- key_feature_weight: bfloat16 [8, 64, 64], P('grp'), may hold values from -0.75 to 0.75
Outputs:
- block_out: bfloat16 [2, 8192, 2048], P(None, ('seq', 'grp'))
- grad_tokens: float32 [2, 8192, 2048], P(None, ('seq', 'grp'))
- grad_lora_in: float32 [4, 2048, 8], P(None, ('seq', 'grp'))
- grad_lora_q_up: float32 [8, 2048], P(None, 'grp')
- grad_lora_kv_up: float32 [2, 8, 512], P(None, None, 'grp')
- grad_lora_o_in: float32 [2048, 8], P('grp')
- grad_feat_query: float32 [32, 64, 64], P('grp')
- grad_feat_key: float32 [8, 64, 64], P('grp')
Inputs may be any that keep to these rules, and one draw needn't show every extreme that they name: `lengths`: each micro-batch packs its 6 sequences in order, each starting at a multiple of 64 slots, and their whole blocks of 64 slots fill exactly 8192 slots; in one micro-batch, which one varies, one sequence starts within the first 1024 slots and ends within the last 1024.
All inputs are finite; a program needn't handle non-finite values.
Results may differ from a plain program's by a relative error of at most 0.02.
Values may be sent and summed in bfloat16 or wider, within the bound.
No kernel may reach another device: no remote copies, remote signals or barrier semaphores. Data moves between devices by JAX's collectives and lax.ppermute only.
A program may use at most 264 MiB of HBM per device.

v0:
```python
import jax
import jax.numpy as jnp
from jax import lax
from jax.sharding import PartitionSpec as P

STRETCH = 64


EPS = 1e-05
ADAPTER_SCALE = 2.0
PRECISE_MODE = lax.Precision.HIGHEST


def shifted(value, axis, steps):
    count = lax.axis_size(axis)
    initial, last = (max(0, -steps), min(count, count - steps))
    return lax.ppermute(value, axis, [(source, source + steps) for source in range(initial, last)])


def prefix(shard, axis, join, neutral):
    place = lax.axis_index(axis)
    gathered = jax.tree.map(
        lambda a, kind: lax.all_gather(a.astype(kind), axis),
        shard,
        (
            jnp.bfloat16,
            jnp.bfloat16,
            jnp.bfloat16,
            jnp.bfloat16,
            jnp.bfloat16,
            jnp.bfloat16,
            jnp.bfloat16,
        ),
    )
    state = jax.tree.map(lambda a, e: jnp.zeros_like(a) + jnp.asarray(e, a.dtype), shard, neutral)

    def one(hop, state):
        return join(
            state,
            jax.tree.map(
                lambda a, own: lax.dynamic_index_in_dim(a, hop, 0, False).astype(own.dtype),
                gathered,
                shard,
            ),
        )

    return lax.fori_loop(0, place, one, state)


def prefix_2(shard, axis, join, neutral):
    count = lax.axis_size(axis)
    place = lax.axis_index(axis)
    ahead = count - 1 - place
    gathered = jax.tree.map(
        lambda a, kind: lax.all_gather(a.astype(kind), axis),
        shard,
        jax.tree.map(lambda a: jnp.bfloat16 if a.dtype == jnp.float32 else a.dtype, shard),
    )
    state = jax.tree.map(lambda a, e: jnp.zeros_like(a) + jnp.asarray(e, a.dtype), shard, neutral)

    def one(hop, state):
        source = count - 1 - hop
        return join(
            state,
            jax.tree.map(
                lambda a, own: lax.dynamic_index_in_dim(a, source, 0, False).astype(own.dtype),
                gathered,
                shard,
            ),
        )

    return lax.fori_loop(0, ahead, one, state)


def reduced_product(left, right):
    return jnp.dot(left, right, preferred_element_type=jnp.float32)


def precise_product(left, right):
    return jnp.dot(left.astype(jnp.float32), right.astype(jnp.float32), precision=PRECISE_MODE)


def pick(weights, stacked):
    return jnp.tensordot(weights, stacked, axes=1, precision=PRECISE_MODE)


def rms_norm(rows_in, gain):
    factor = lax.rsqrt(jnp.mean(rows_in * rows_in, axis=-1, keepdims=True) + EPS)
    return rows_in * factor * gain


def hedgehog(vectors, maps):
    mixed = jnp.einsum("cthd,hde->cthe", vectors, maps, precision=PRECISE_MODE)
    return jnp.concatenate(
        [jax.nn.softmax(mixed, axis=-1), jax.nn.softmax(-mixed, axis=-1)], axis=-1
    )


def swiglu(gate_up):
    return jax.nn.silu(gate_up[:, 0]) * gate_up[:, 1]


def seq_owner(stretch_ids, starts):
    return jnp.sum((starts[None, :] <= stretch_ids[:, None]).astype(jnp.int32), axis=1) - 1


def slot_valid(first_slot, count, starts, lengths_row):
    slots = first_slot + jnp.arange(count, dtype=jnp.int32)
    sequence_owner = seq_owner(jnp.floor_divide(slots, STRETCH), starts)
    ends = starts * STRETCH + lengths_row
    member = (
        sequence_owner[:, None] == jnp.arange(starts.shape[0], dtype=jnp.int32)[None, :]
    ).astype(jnp.int32)
    return (slots < jnp.sum(member * ends[None, :], axis=1)).astype(jnp.float32)


def guarded(earlier, later, joined):
    return tuple(
        (
            jnp.where(later[-1] > 0.5, first, jnp.where(earlier[-1] > 0.5, second, third))
            for first, second, third in zip(earlier, later, joined)
        )
    )


def forward_join(earlier, later):
    keep_tail = 1.0 - later[4]
    keep_mid = 1.0 - later[5]
    joined = (
        later[0] + keep_tail * earlier[0],
        later[1] + keep_tail * earlier[1],
        later[2] + keep_mid * earlier[0],
        later[3] + keep_mid * earlier[1],
        jnp.maximum(earlier[4], later[4]),
        jnp.maximum(earlier[4], later[5]),
        earlier[6] * later[6],
    )
    return guarded(earlier, later, joined)


def backward_join(earlier, later):
    keep = 1.0 - later[4]
    joined = (
        later[0] + keep * earlier[0],
        later[1] + keep * earlier[1],
        later[2] + keep * earlier[0],
        later[3] + keep * earlier[1],
        jnp.maximum(earlier[4], later[4]),
        earlier[5] * later[5],
    )
    return guarded(earlier, later, joined)


def gather_weight_list(
    query_weight, keyvalue_weight, output_weight, gate_up_weight, down_weight, adapter_width_factor
):
    return (
        lax.all_gather(query_weight, "seq", axis=0, tiled=True),
        lax.all_gather(keyvalue_weight, "seq", axis=0, tiled=True),
        lax.all_gather(output_weight, "seq", axis=1, tiled=True),
        lax.all_gather(gate_up_weight, "seq", axis=0, tiled=True),
        lax.all_gather(down_weight, "seq", axis=1, tiled=True),
        lax.all_gather(adapter_width_factor, "seq", axis=1, tiled=True),
    )


def local(
    tokens,
    cotangent,
    lengths,
    attention_norm_gain,
    feedforward_norm_gain,
    query_weight,
    keyvalue_weight,
    output_weight,
    gate_up_weight,
    down_weight,
    adapter_width_factor,
    query_up_factor,
    keyvalue_up_factor,
    output_input_factor,
    query_feature_weight,
    key_feature_weight,
):
    batches, rows, model_width = tokens.shape
    shard_rows = rows // lax.axis_size("grp")
    group_index = lax.axis_index("grp")
    seq_index = lax.axis_index("seq")
    local_heads = query_feature_weight.shape[0]
    head_dim = query_feature_weight.shape[1]
    local_kv = key_feature_weight.shape[0]
    per_group = local_heads // local_kv
    features = 2 * head_dim
    blocks = rows // STRETCH
    scale = head_dim ** (-0.5)
    gain_attn = attention_norm_gain.astype(jnp.float32)
    gain_mlp = feedforward_norm_gain.astype(jnp.float32)
    query_maps = query_feature_weight.astype(jnp.float32)
    key_maps = key_feature_weight.astype(jnp.float32)
    order = jnp.arange(blocks, dtype=jnp.int32)
    inner = jnp.arange(STRETCH, dtype=jnp.int32)
    causal = (inner[None, :] <= inner[:, None]).astype(jnp.float32)
    lag_base = order[None, :] <= order[:, None] - 2
    width_gradient = jnp.zeros((4, model_width, adapter_width_factor.shape[2]), jnp.float32)
    query_up_gradient = jnp.zeros(query_up_factor.shape, jnp.float32)
    keyvalue_up_gradient = jnp.zeros(keyvalue_up_factor.shape, jnp.float32)
    output_in_gradient = jnp.zeros(output_input_factor.shape, jnp.float32)
    grad_fquery = jnp.zeros(query_feature_weight.shape, jnp.float32)
    grad_fkey = jnp.zeros(key_feature_weight.shape, jnp.float32)
    block_rows = []
    input_grads = []
    for batch in range(batches):
        gathered_weight = gather_weight_list(
            query_weight,
            keyvalue_weight,
            output_weight,
            gate_up_weight,
            down_weight,
            adapter_width_factor,
        )
        (
            query_merged,
            keyvalue_merged,
            output_merged,
            gate_up_merged,
            down_weight_merged,
            adapter_merged,
        ) = gathered_weight
        x_full = tokens[batch].astype(jnp.float32)
        x_share = lax.dynamic_slice_in_dim(x_full, group_index * shard_rows, shard_rows, 0)
        normalized_input = rms_norm(x_full, gain_attn).astype(jnp.bfloat16)
        adapter_middle = jnp.einsum(
            "kv,mvs->kms", normalized_input, adapter_merged[:3], preferred_element_type=jnp.float32
        )
        query_vectors = reduced_product(
            normalized_input, query_merged
        ) + ADAPTER_SCALE * precise_product(adapter_middle[:, 0], query_up_factor)
        keyvalue_rows = jnp.einsum(
            "fc,cyq->fyq", normalized_input, keyvalue_merged, preferred_element_type=jnp.float32
        ) + ADAPTER_SCALE * jnp.einsum(
            "fxw,xwg->fxg",
            adapter_middle[:, 1:3],
            keyvalue_up_factor.astype(jnp.float32),
            precision=PRECISE_MODE,
        )
        query_low = query_vectors.astype(jnp.bfloat16)
        keyval_low = keyvalue_rows.astype(jnp.bfloat16)
        lengths_row = lengths[batch]
        seq_blocks = (lengths_row + STRETCH - 1) // STRETCH
        starts = jnp.cumsum(seq_blocks) - seq_blocks
        base = seq_index * blocks
        sequence_owner = seq_owner(base + order, starts)
        edges = seq_owner(jnp.stack([base - 2, base - 1]), starts)
        valid_mask = slot_valid(base * STRETCH, rows, starts, lengths_row).reshape(blocks, STRETCH)
        halo_valid = slot_valid(base * STRETCH - STRETCH, STRETCH, starts, lengths_row)
        before = jnp.concatenate([edges[1:2], sequence_owner[:-1]])
        begins = (sequence_owner != before).astype(jnp.float32)
        prev_valid = (
            jnp.concatenate([halo_valid[None], valid_mask[:-1]])
            * (before == sequence_owner).astype(jnp.float32)[:, None]
        )
        mask = jnp.concatenate(
            [
                jnp.broadcast_to(prev_valid[:, None, :], (blocks, STRETCH, STRETCH)),
                causal[None] * valid_mask[:, None, :],
            ],
            axis=2,
        )
        lag = (lag_base & (sequence_owner[None, :] == sequence_owner[:, None])).astype(jnp.float32)
        halo = shifted(keyval_low[rows - STRETCH :], "seq", 1)
        stretches_kv = keyval_low.reshape(blocks, STRETCH, 2, local_kv, head_dim)
        prev_kv = jnp.concatenate(
            [halo.reshape(1, STRETCH, 2, local_kv, head_dim), stretches_kv[:-1]]
        )
        window = jnp.concatenate([prev_kv, stretches_kv], axis=1)
        win_keys = window[:, :, 0]
        win_vals = window[:, :, 1]
        keys = stretches_kv[:, :, 0]
        values = stretches_kv[:, :, 1]
        query_heads = query_low.reshape(blocks, STRETCH, local_heads, head_dim)
        phi_query, query_map_back = jax.vjp(hedgehog, query_heads.astype(jnp.float32), query_maps)
        phi_key, key_map_back = jax.vjp(hedgehog, keys.astype(jnp.float32), key_maps)
        key_mask = valid_mask[:, :, None, None]
        masked = phi_key * key_mask
        values_wide = values.astype(jnp.float32)
        stretch_states = jnp.einsum("ctkf,ctkd->ckfd", masked, values_wide, precision=PRECISE_MODE)
        stretch_norms = jnp.sum(masked, axis=1)
        tail_pick = (sequence_owner == sequence_owner[blocks - 1]).astype(jnp.float32)
        mid_pick = ((order <= blocks - 2) & (sequence_owner == sequence_owner[blocks - 2])).astype(
            jnp.float32
        )
        tail_states = pick(tail_pick, stretch_states)
        tail_norms = pick(tail_pick, stretch_norms)
        mid_states = pick(mid_pick, stretch_states)
        mid_norms = pick(mid_pick, stretch_norms)
        nothing = jnp.zeros((), jnp.float32)
        entering = prefix(
            (
                tail_states,
                tail_norms,
                mid_states,
                mid_norms,
                jnp.max(begins),
                jnp.max(begins[:-1]),
                nothing,
            ),
            "seq",
            forward_join,
            (
                jnp.zeros_like(tail_states),
                jnp.zeros_like(tail_norms),
                jnp.zeros_like(mid_states),
                jnp.zeros_like(mid_norms),
                nothing,
                nothing,
                jnp.ones((), jnp.float32),
            ),
        )
        use_tail = ((order >= 1) & (sequence_owner == edges[1])).astype(jnp.float32)
        use_mid = ((order == 0) & (sequence_owner == edges[0])).astype(jnp.float32)
        states = (
            jnp.einsum("cj,jkfd->ckfd", lag, stretch_states, precision=PRECISE_MODE)
            + use_tail[:, None, None, None] * entering[0]
            + use_mid[:, None, None, None] * entering[2]
        )
        norms = (
            jnp.einsum("cj,jkf->ckf", lag, stretch_norms, precision=PRECISE_MODE)
            + use_tail[:, None, None] * entering[1]
            + use_mid[:, None, None] * entering[3]
        )
        group_query = query_low.reshape(blocks, STRETCH, local_kv, per_group, head_dim)
        group_phi = phi_query.reshape(blocks, STRETCH, local_kv, per_group, features)
        lin_num = jnp.einsum("ctkgf,ckfd->ckgtd", group_phi, states, precision=PRECISE_MODE)
        lin_den = jnp.einsum("ctkgf,ckf->ckgt", group_phi, norms, precision=PRECISE_MODE)
        scores = (
            jnp.einsum(
                "ctkgd,cskd->ckgts", group_query, win_keys, preferred_element_type=jnp.float32
            )
            * scale
        )
        weights = jnp.exp(scores) * mask[:, None, None]
        weights_low = weights.astype(jnp.bfloat16)
        win_den = jnp.sum(weights, axis=-1)
        win_num = jnp.einsum(
            "ckgts,cskd->ckgtd", weights_low, win_vals, preferred_element_type=jnp.float32
        )
        denom = win_den + lin_den
        attended = (win_num + lin_num) / denom[..., None]
        attention_reduced = (
            jnp.transpose(attended, (0, 3, 1, 2, 4))
            .reshape(rows, local_heads * head_dim)
            .astype(jnp.bfloat16)
        )
        output_middle = precise_product(attention_reduced, output_input_factor)
        side_branch = lax.psum_scatter(
            (
                reduced_product(attention_reduced, output_merged)
                + ADAPTER_SCALE * precise_product(output_middle, adapter_merged[3].T)
            ).astype(jnp.bfloat16),
            "grp",
            scatter_dimension=0,
            tiled=True,
        ).astype(jnp.float32)
        resid = x_share + side_branch
        mlp_norm, mlp_norm_back = jax.vjp(lambda rows_in: rms_norm(rows_in, gain_mlp), resid)
        mlp_in = lax.all_gather(mlp_norm.astype(jnp.bfloat16), "grp", axis=0, tiled=True)
        gate_up = jnp.einsum(
            "td,dgf->tgf", mlp_in, gate_up_merged, preferred_element_type=jnp.float32
        )
        hidden_wide, silu_back = jax.vjp(swiglu, gate_up)
        hidden = hidden_wide.astype(jnp.bfloat16)
        mlp_out = lax.psum_scatter(
            reduced_product(hidden, down_weight_merged).astype(jnp.bfloat16),
            "grp",
            scatter_dimension=0,
            tiled=True,
        ).astype(jnp.float32)
        block_rows.append((resid + mlp_out).astype(jnp.bfloat16))
        upstream = cotangent[batch]
        upstream_share = lax.dynamic_slice_in_dim(
            upstream, group_index * shard_rows, shard_rows, 0
        ).astype(jnp.float32)
        d_hidden = jnp.einsum(
            "td,fd->tf", upstream, down_weight_merged, preferred_element_type=jnp.float32
        )
        d_gate_up = silu_back(d_hidden)[0].astype(jnp.bfloat16)
        d_mlp_in = lax.psum_scatter(
            jnp.einsum(
                "tgf,dgf->td", d_gate_up, gate_up_merged, preferred_element_type=jnp.float32
            ).astype(jnp.bfloat16),
            "grp",
            scatter_dimension=0,
            tiled=True,
        ).astype(jnp.float32)
        d_resid = upstream_share + mlp_norm_back(d_mlp_in)[0]
        branch_gradient = lax.all_gather(d_resid.astype(jnp.bfloat16), "grp", axis=0, tiled=True)
        output_backward = ADAPTER_SCALE * precise_product(branch_gradient, adapter_merged[3])
        d_att = jnp.einsum(
            "td,hd->th", branch_gradient, output_merged, preferred_element_type=jnp.float32
        ) + precise_product(output_backward, output_input_factor.T)
        output_in_gradient = output_in_gradient + jnp.einsum(
            "th,te->he",
            attention_reduced.astype(jnp.float32),
            output_backward,
            precision=PRECISE_MODE,
        )
        output_factor_gradient = ADAPTER_SCALE * jnp.einsum(
            "td,te->de", branch_gradient.astype(jnp.float32), output_middle, precision=PRECISE_MODE
        )
        d_heads = jnp.transpose(
            d_att.reshape(blocks, STRETCH, local_kv, per_group, head_dim), (0, 2, 3, 1, 4)
        )
        ratio = d_heads / denom[..., None]
        ratio_low = ratio.astype(jnp.bfloat16)
        d_den = -jnp.sum(d_heads * attended, axis=-1) / denom
        d_states = jnp.einsum("ctkgf,ckgtd->ckfd", group_phi, ratio, precision=PRECISE_MODE)
        d_norms = jnp.einsum("ctkgf,ckgt->ckf", group_phi, d_den, precision=PRECISE_MODE)
        d_phi = jnp.einsum("ckgtd,ckfd->ctkgf", ratio, states, precision=PRECISE_MODE) + jnp.einsum(
            "ckgt,ckf->ctkgf", d_den, norms, precision=PRECISE_MODE
        )
        d_weights = (
            jnp.einsum("ckgtd,cskd->ckgts", ratio_low, win_vals, preferred_element_type=jnp.float32)
            + d_den[..., None]
        )
        d_scores = (d_weights * weights).astype(jnp.bfloat16)
        d_query = (
            jnp.einsum("ckgts,cskd->ctkgd", d_scores, win_keys, preferred_element_type=jnp.float32)
            * scale
        )
        d_win_keys = (
            jnp.einsum(
                "ckgts,ctkgd->cskd", d_scores, group_query, preferred_element_type=jnp.float32
            )
            * scale
        )
        d_win_vals = jnp.einsum(
            "ckgts,ckgtd->cskd", weights_low, ratio_low, preferred_element_type=jnp.float32
        )
        query_map_grads = query_map_back(d_phi.reshape(blocks, STRETCH, local_heads, features))
        d_query = d_query.reshape(blocks, STRETCH, local_heads, head_dim) + query_map_grads[0]
        grad_fquery = grad_fquery + query_map_grads[1]
        head_pick = (sequence_owner == edges[1]).astype(jnp.float32)
        rest_pick = head_pick * (order >= 1).astype(jnp.float32)
        nothing = jnp.zeros((), jnp.float32)
        leaving = prefix_2(
            (
                pick(head_pick, d_states),
                pick(head_pick, d_norms),
                pick(rest_pick, d_states),
                pick(rest_pick, d_norms),
                jnp.max(begins),
                nothing,
            ),
            "seq",
            backward_join,
            (
                jnp.zeros_like(tail_states),
                jnp.zeros_like(tail_norms),
                jnp.zeros_like(tail_states),
                jnp.zeros_like(tail_norms),
                nothing,
                jnp.ones((), jnp.float32),
            ),
        )
        from_tail = ((order <= blocks - 2) & (sequence_owner == sequence_owner[blocks - 1])).astype(
            jnp.float32
        )
        from_mid = (order == blocks - 1).astype(jnp.float32)
        key_grads = (
            jnp.einsum("cj,ckfd->jkfd", lag, d_states, precision=PRECISE_MODE)
            + from_tail[:, None, None, None] * leaving[0]
            + from_mid[:, None, None, None] * leaving[2]
        )
        key_norm_grads = (
            jnp.einsum("cj,ckf->jkf", lag, d_norms, precision=PRECISE_MODE)
            + from_tail[:, None, None] * leaving[1]
            + from_mid[:, None, None] * leaving[3]
        )
        d_masked = (
            jnp.einsum("jkfd,jtkd->jtkf", key_grads, values_wide, precision=PRECISE_MODE)
            + key_norm_grads[:, None]
        )
        d_values_state = jnp.einsum("jtkf,jkfd->jtkd", masked, key_grads, precision=PRECISE_MODE)
        key_map_grads = key_map_back(d_masked * key_mask)
        grad_fkey = grad_fkey + key_map_grads[1]
        prev_dk = d_win_keys[:, :STRETCH]
        prev_dv = d_win_vals[:, :STRETCH]
        returned = shifted(
            jnp.stack([prev_dk[0], prev_dv[0]]).astype(jnp.bfloat16), "seq", -1
        ).astype(jnp.float32)
        d_keys = (
            d_win_keys[:, STRETCH:]
            + jnp.concatenate([prev_dk[1:], returned[0][None]])
            + key_map_grads[0]
        )
        d_values = (
            d_win_vals[:, STRETCH:]
            + jnp.concatenate([prev_dv[1:], returned[1][None]])
            + d_values_state
        )
        keyvalue_reduced_gradient = (
            jnp.stack([d_keys, d_values], axis=2)
            .reshape(rows, 2, local_kv * head_dim)
            .astype(jnp.bfloat16)
        )
        query_reduced_gradient = d_query.reshape(rows, local_heads * head_dim).astype(jnp.bfloat16)
        query_backward = ADAPTER_SCALE * precise_product(query_reduced_gradient, query_up_factor.T)
        keyvalue_backward = ADAPTER_SCALE * jnp.einsum(
            "tsk,sek->tse",
            keyvalue_reduced_gradient.astype(jnp.float32),
            keyvalue_up_factor.astype(jnp.float32),
            precision=PRECISE_MODE,
        )
        input_backward = jnp.concatenate([query_backward[:, None], keyvalue_backward], axis=1)
        query_up_gradient = query_up_gradient + ADAPTER_SCALE * jnp.einsum(
            "yg,ym->gm",
            adapter_middle[:, 0],
            query_reduced_gradient.astype(jnp.float32),
            precision=PRECISE_MODE,
        )
        keyvalue_up_gradient = keyvalue_up_gradient + ADAPTER_SCALE * jnp.einsum(
            "pov,pom->ovm",
            adapter_middle[:, 1:3],
            keyvalue_reduced_gradient.astype(jnp.float32),
            precision=PRECISE_MODE,
        )
        wide_in = jnp.einsum(
            "td,tae->ade",
            normalized_input.astype(jnp.float32),
            input_backward,
            precision=PRECISE_MODE,
        )
        width_gradient = width_gradient + jnp.concatenate(
            [wide_in, output_factor_gradient[None]], axis=0
        )
        d_normed = lax.psum_scatter(
            (
                jnp.einsum(
                    "th,dh->td",
                    query_reduced_gradient,
                    query_merged,
                    preferred_element_type=jnp.float32,
                )
                + jnp.einsum(
                    "tsk,dsk->td",
                    keyvalue_reduced_gradient,
                    keyvalue_merged,
                    preferred_element_type=jnp.float32,
                )
                + jnp.einsum(
                    "hri,rji->hj",
                    input_backward,
                    adapter_merged[:3].astype(jnp.float32),
                    precision=PRECISE_MODE,
                )
            ).astype(jnp.bfloat16),
            "grp",
            scatter_dimension=0,
            tiled=True,
        ).astype(jnp.float32)
        unused_norm, attn_norm_back = jax.vjp(lambda rows_in: rms_norm(rows_in, gain_attn), x_share)
        input_grads.append(d_resid + attn_norm_back(d_normed)[0])
    wide_share = lax.psum_scatter(width_gradient, ("seq", "grp"), scatter_dimension=1, tiled=True)
    summed = (
        lax.psum(query_up_gradient.astype(jnp.bfloat16), "seq").astype(jnp.float32),
        lax.psum(keyvalue_up_gradient.astype(jnp.bfloat16), "seq").astype(jnp.float32),
        lax.psum(output_in_gradient.astype(jnp.bfloat16), "seq").astype(jnp.float32),
        lax.psum(grad_fquery.astype(jnp.bfloat16), "seq").astype(jnp.float32),
        lax.psum(grad_fkey.astype(jnp.bfloat16), "seq").astype(jnp.float32),
    )
    return (
        jnp.stack(block_rows),
        jnp.stack(input_grads),
        wide_share,
        summed[0],
        summed[1],
        summed[2],
        summed[3],
        summed[4],
    )


def solution(mesh):
    return jax.shard_map(
        local,
        mesh=mesh,
        in_specs=(
            P(None, "seq", None),
            P(None, "seq", None),
            P(),
            P(),
            P(),
            P("seq", "grp"),
            P("seq", None, "grp"),
            P("grp", "seq"),
            P("seq", None, "grp"),
            P("grp", "seq"),
            P(None, "seq", None),
            P(None, "grp"),
            P(None, None, "grp"),
            P("grp", None),
            P("grp", None, None),
            P("grp", None, None),
        ),
        out_specs=(
            P(None, ("seq", "grp"), None),
            P(None, ("seq", "grp"), None),
            P(None, ("seq", "grp"), None),
            P(None, "grp"),
            P(None, None, "grp"),
            P("grp", None),
            P("grp", None, None),
            P("grp", None, None),
        ),
        check_vma=False,
    )
```

profile of v0, /device:TPU:0, one launch (start us, length us, event | category | flops | bytes accessed | tf_op | source)
XLA Modules:
  0.0 2357.4 jit_solution(16732438979269180479)
XLA Ops:
  24.8 32.6 %all_gather.167 = bf16[4,2048,8]{1,2,0:T(8,128)(2,1)S(1)} all-gather(bf16[4,256,8]{1,2,0:T(8,128)(2,1)S(1)} %copy-done.202), channel_id=1, replica_groups=mesh['seq'=8,'grp'=4] {'seq'}, dimensions={1}, use_global_device_ids=true | all-gather | bytes 147456 | tf_op jit(solution)/shard_map/all_gather | solution.py:163
  77.8 22.8 all-reduce.10
  143.5 6.1 fusion.403
  163.8 32.7 %all-gather.6 = bf16[16,128,64]{1,2,0:T(8,128)(2,1)} all-gather(bf16[2,128,64]{1,2,0:T(8,128)(2,1)S(1)} %convert_element_type.791), channel_id=8, replica_groups=mesh['seq'=8,'grp'=4] {'seq'}, dimensions={0}, use_global_device_ids=true | all-gather | bytes 294912 | tf_op jit(solution)/shard_map/all_gather | solution.py:23
  196.5 16.9 all-gather.16
  213.4 18.9 all-gather.17
  232.4 32.9 %all-gather.2 = bf16[16,128,64]{1,2,0:T(8,128)(2,1)} all-gather(bf16[2,128,64]{1,2,0:T(8,128)(2,1)S(1)} %convert_element_type.759), channel_id=4, replica_groups=mesh['seq'=8,'grp'=4] {'seq'}, dimensions={0}, use_global_device_ids=true | all-gather | bytes 294912 | tf_op jit(solution)/shard_map/all_gather | solution.py:23
  265.2 32.7 %all-gather = bf16[16,128,64]{1,2,0:T(8,128)(2,1)} all-gather(bf16[2,128,64]{1,2,0:T(8,128)(2,1)S(1)} %convert_element_type.755), channel_id=2, replica_groups=mesh['seq'=8,'grp'=4] {'seq'}, dimensions={0}, use_global_device_ids=true | all-gather | bytes 294912 | tf_op jit(solution)/shard_map/all_gather | solution.py:23
  305.0 111.3 %all-gather.4 = bf16[16,128,64]{1,2,0:T(8,128)(2,1)} all-gather(bf16[2,128,64]{1,2,0:T(8,128)(2,1)} %convert_element_type.787), channel_id=6, replica_groups=mesh['seq'=8,'grp'=4] {'seq'}, dimensions={0}, use_global_device_ids=true | all-gather | bytes 294912 | tf_op jit(solution)/shard_map/all_gather | solution.py:23
  421.7 20.9 all-gather.18
  442.6 16.1 all-gather.19
  481.4 22.3 fusion.402
  505.7 22.3 fusion.401
  531.4 9.8 fusion.108
  546.1 13.8 fusion.83
  583.9 5.8 fusion.412
  604.8 22.4 fusion.397
  627.2 22.3 fusion.398
  654.1 9.8 fusion.100
  670.1 14.1 fusion.73
  697.8 11.4 slice_convert_fusion.1
  712.1 80.7 %reduce-scatter.16.cloned.1.call-done = bf16[256,2048]{1,0:T(8,128)(2,1)} async-done(((bf16[1024,2048]{1,0:T(8,128)(2,1)}), bf16[256,2048]{1,0:T(8,128)(2,1)}) %reduce-scatter.16.cloned.1.call-update) | async-done | bytes 1048592 | tf_op jit(solution)/shard_map/reduce_scatter | solution.py:355
  803.9 29.1 %all-gather.46.cloned.1.call-done = bf16[1024,2048]{1,0:T(8,128)(2,1)} async-done(((bf16[256,2048]{1,0:T(8,128)(2,1)}), bf16[1024,2048]{1,0:T(8,128)(2,1)}) %all-gather.46.cloned.1.call-update) | async-done | bytes 4194320 | tf_op jit(solution)/shard_map/all_gather | solution.py:366
  833.0 229.8 %all-gather.42.cloned.1.call-done = bf16[2048,2,2048]{2,0,1:T(8,128)(2,1)} async-done(((bf16[256,2,2048]{2,0,1:T(8,128)(2,1)}), bf16[2048,2,2048]{2,0,1:T(8,128)(2,1)}) %all-gather.42.cloned.1.call-update) | async-done | bytes 16777232 | tf_op jit(solution)/shard_map/all_gather | solution.py:161
  1062.8 23.5 fusion.70
  1086.2 102.2 %all-gather.44.cloned.1.call-done = bf16[2048,2048]{1,0:T(8,128)(2,1)} async-done(((bf16[2048,256]{1,0:T(8,128)(2,1)}), bf16[2048,2048]{1,0:T(8,128)(2,1)}) %all-gather.44.cloned.1.call-update) | async-done | bytes 8388624 | tf_op jit(solution)/shard_map/all_gather | solution.py:162
  1188.4 22.4 multiply_bitcast_fusion
  1210.8 26.4 %bitcast_convert_fusion = bf16[1024,2048]{1,0:T(8,128)(2,1)} fusion(bf16[2048,2,2048]{2,0,1:T(8,128)(2,1)} %all-gather.42.cloned.1.call-done, f32[1024,1,2048]{2,0,1:T(8,128)} %get-tuple-element.1008, f32[1024,1,2048]{2,0,1:T(8,128)} %get-tuple-element.1007), kind=kOutput, calls=%fused_computation.83 | convolution fusion | flops 17190354944 | bytes 37748736 | tf_op jit(solution)/shard_map/tgf,dgf->td/dot_general | solution.py:388
  1237.5 23.9 %fusion.80 = f32[1024,2,2048]{2,0,1:T(8,128)} fusion(bf16[2048,2,2048]{2,0,1:T(8,128)(2,1)} %all-gather.42.cloned.1.call-done, bf16[1024,2048]{1,0:T(8,128)(2,1)} %all-gather.40.cloned.1.call-done), kind=kOutput, calls=%fused_computation.152 | convolution fusion | flops 17179869184 | bytes 37748736 | tf_op jit(solution)/shard_map/td,dgf->tgf/dot_general | solution.py:367
  1261.3 21.9 multiply_bitcast_fusion.1
  1283.2 26.2 %bitcast_convert_fusion.1 = bf16[1024,2048]{1,0:T(8,128)(2,1)} fusion(bf16[2048,2,2048]{2,0,1:T(8,128)(2,1)} %all-gather.42.cloned.1.call-done, f32[1024,1,2048]{2,0,1:T(8,128)} %get-tuple-element.1010, f32[1024,1,2048]{2,0,1:T(8,128)} %get-tuple-element.1009), kind=kOutput, calls=%fused_computation.87 | convolution fusion | flops 17190354944 | bytes 37748736 | tf_op jit(solution)/shard_map/tgf,dgf->td/dot_general | solution.py:388
  1309.9 7.4 fusion.390
  1317.4 34.5 %reduce-scatter.20.cloned.1.call-done = bf16[256,2048]{1,0:T(8,128)(2,1)} async-done(((bf16[1024,2048]{1,0:T(8,128)(2,1)}), bf16[256,2048]{1,0:T(8,128)(2,1)}) %reduce-scatter.20.cloned.1.call-update) | async-done | bytes 1048592 | tf_op jit(solution)/shard_map/reduce_scatter | solution.py:387
  1372.9 20.9 all-gather.48.cloned.1.call-done
  1411.2 6.8 fusion.90
  1455.8 7.8 fusion.153
  1483.7 20.7 all-gather.20
  1504.4 16.9 all-gather.21
  1521.3 32.8 %all-gather.10 = bf16[16,128,64]{1,2,0:T(8,128)(2,1)} all-gather(bf16[2,128,64]{1,2,0:T(8,128)(2,1)S(1)} %convert_element_type.819), channel_id=12, replica_groups=mesh['seq'=8,'grp'=4] {'seq'}, dimensions={0}, use_global_device_ids=true | all-gather | bytes 294912 | tf_op jit(solution)/shard_map/all_gather | solution.py:55
  1554.1 32.9 %all-gather.8 = bf16[16,128,64]{1,2,0:T(8,128)(2,1)} all-gather(bf16[2,128,64]{1,2,0:T(8,128)(2,1)S(1)} %convert_element_type.816), channel_id=10, replica_groups=mesh['seq'=8,'grp'=4] {'seq'}, dimensions={0}, use_global_device_ids=true | all-gather | bytes 294912 | tf_op jit(solution)/shard_map/all_gather | solution.py:55
  1588.3 64.2 %while.90 = (s32[]{:T(128)}, f32[2,128,64]{2,1,0:T(8,128)S(1)}, f32[2,128]{1,0:T(2,128)S(1)}, f32[2,128,64]{2,1,0:T(8,128)}, f32[2,128]{1,0:T(2,128)}, /*index=5...) while((s32[]{:T(128)}, f32[2,128,64]{2,1,0:T(8,128)S(1)}, ...), condition=%wide.region_56.57_spmd, body=%wide.region_55.56_spmd.sunk | while | flops 149772 | bytes 595267 | solution.py:72
  1662.7 7.7 add_bitcast_fusion.1
  1673.9 5.8 multiply_reduce_fusion.3
  1681.4 6.5 multiply_add_fusion.1
  1700.2 5.9 fusion.61
  1713.5 19.1 all-gather.22
  1732.6 16.4 all-gather.23
  1749.1 32.8 %all-gather.14 = bf16[16,128,64]{1,2,0:T(8,128)(2,1)} all-gather(bf16[2,128,64]{1,2,0:T(8,128)(2,1)S(1)} %convert_element_type.839), channel_id=16, replica_groups=mesh['seq'=8,'grp'=4] {'seq'}, dimensions={0}, use_global_device_ids=true | all-gather | bytes 294912 | tf_op jit(solution)/shard_map/all_gather | solution.py:55
  1781.8 32.7 %all-gather.12 = bf16[16,128,64]{1,2,0:T(8,128)(2,1)} all-gather(bf16[2,128,64]{1,2,0:T(8,128)(2,1)S(1)} %convert_element_type.836), channel_id=14, replica_groups=mesh['seq'=8,'grp'=4] {'seq'}, dimensions={0}, use_global_device_ids=true | all-gather | bytes 294912 | tf_op jit(solution)/shard_map/all_gather | solution.py:55
  1816.4 74.6 %while.91 = (s32[]{:T(128)}, f32[2,128,64]{2,1,0:T(8,128)}, f32[2,128]{1,0:T(2,128)}, f32[2,128,64]{2,1,0:T(8,128)S(1)}, f32[2,128]{1,0:T(2,128)}, /*index=5*/f3...) while((s32[]{:T(128)}, f32[2,128,64]{2,1,0:T(8,128)}, ...), condition=%wide.region_68.69_spmd, body=%wide.region_67.68_spmd.sunk | while | flops 149772 | bytes 595267 | solution.py:72
  1901.9 7.7 add_bitcast_fusion
  1913.1 5.8 multiply_reduce_fusion.1
  1920.7 6.3 multiply_add_fusion
  1939.5 5.9 fusion.52
  2026.8 7.7 fusion.41
  2034.5 16.6 fusion.93
  2062.0 16.6 fusion.92
  2085.4 36.0 %all-reduce.9 = (bf16[8,512]{1,0:T(8,128)(2,1)S(1)}, bf16[2,8,128]{2,1,0:T(8,128)(2,1)S(1)}, bf16[512,8]{0,1:T(8,128)(2,1)S(1)}, bf16[2,64,64]{2,1,0:T(8,128)(2,1)S(1)}) all-reduce(bf16[8,512]{1,0:T(8,128)(2,1)S(1)} %fusion.199, bf16[2,8,128]{2,1,0:T(8,128)(2,1)S(1)} %fusion.202, ...), channel_id=1, replica_groups=mesh['seq'=8,'grp'=4] {'seq'}, use_global_device_ids=true, to_apply=%region_75.76 | all-reduce | flops 18432 | bytes 73728 | tf_op jit(solution)/shard_map/psum | solution.py:565
  2125.5 32.2 %reduce-scatter.28.cloned.1.call-done = f32[64,32]{1,0:T(8,128)} async-done(((f32[2048,32]{1,0:T(8,128)}), f32[64,32]{1,0:T(8,128)}) %reduce-scatter.28.cloned.1.call-update) | async-done | bytes 8208
  2159.3 41.3 %reduce-scatter.22.cloned.1.call-done = bf16[256,2048]{1,0:T(8,128)(2,1)} async-done(((bf16[1024,2048]{1,0:T(8,128)(2,1)}), bf16[256,2048]{1,0:T(8,128)(2,1)}) %reduce-scatter.22.cloned.1.call-update) | async-done | bytes 1048592 | tf_op jit(solution)/shard_map/reduce_scatter | solution.py:536
  2203.0 44.7 %reduce-scatter.14.cloned.1.call-done = bf16[256,2048]{1,0:T(8,128)(2,1)} async-done(((bf16[1024,2048]{1,0:T(8,128)(2,1)}), bf16[256,2048]{1,0:T(8,128)(2,1)}) %reduce-scatter.14.cloned.1.call-update) | async-done | bytes 1048592 | tf_op jit(solution)/shard_map/reduce_scatter | solution.py:372
  2247.7 47.5 %reduce-scatter.26.cloned.1.call-done = bf16[256,2048]{1,0:T(8,128)(2,1)} async-done(((bf16[1024,2048]{1,0:T(8,128)(2,1)}), bf16[256,2048]{1,0:T(8,128)(2,1)}) %reduce-scatter.26.cloned.1.call-update) | async-done | bytes 1048592 | tf_op jit(solution)/shard_map/reduce_scatter | solution.py:536
  2295.2 6.1 fusion.130
  2301.3 41.1 %reduce-scatter.18.cloned.1.call-done = bf16[256,2048]{1,0:T(8,128)(2,1)} async-done(((bf16[1024,2048]{1,0:T(8,128)(2,1)}), bf16[256,2048]{1,0:T(8,128)(2,1)}) %reduce-scatter.18.cloned.1.call-update) | async-done | bytes 1048592 | tf_op jit(solution)/shard_map/reduce_scatter | solution.py:372
  (947 shorter events, 596.9 us)
Async XLA Ops:
  7.2 473.4 %copy-start = (bf16[8,64,64]{2,1,0:T(8,128)(2,1)S(1)}, bf16[8,64,64]{2,1,0:T(8,128)(2,1)}, u32[]{:S(2)}) copy-start(bf16[8,64,64]{2,1,0:T(8,128)(2,1)} %param.38) | copy-start | bytes 196612
  7.2 93.5 %all-gather.34.cloned.1.call-start = ((), (), s32[]{:S(2)}) async-start(), calls=%async_computation.9 | async-start | bytes 1179648 | tf_op jit(solution)/shard_map/all_gather | solution.py:159
  8.9 452.4 %all-gather.36.cloned.1.call-start = ((), (), s32[]{:S(2)}) async-start(), calls=%async_computation.10 | async-start | bytes 2359296 | tf_op jit(solution)/shard_map/all_gather | solution.py:158
  9.6 556.6 %all-gather.38.cloned.1.call-start = ((), (), s32[]{:S(2)}) async-start(), calls=%async_computation.11 | async-start | bytes 2359296 | tf_op jit(solution)/shard_map/all_gather | solution.py:160
  10.3 698.9 %reduce-scatter.12.cloned.1.call-start = ((), (), s32[]{:S(2)}) async-start(), calls=%async_computation.12 | async-start | bytes 5242880 | tf_op jit(solution)/shard_map/reduce_scatter | solution.py:355
  13.0 56.9 %copy-start.197 = (s32[16]{0:T(128)}, s32[16]{0:T(128)S(1)}, u32[]{:S(2)}) copy-start(s32[16]{0:T(128)S(1)} %broadcast_add_fusion.3) | copy-start | bytes 196
  13.0 56.9 %copy-start.195 = (s32[16]{0:T(128)}, s32[16]{0:T(128)S(1)}, u32[]{:S(2)}) copy-start(s32[16]{0:T(128)S(1)} %broadcast_add_fusion.2) | copy-start | bytes 196
  19.3 112.0 %copy-start.174 = (f32[16,64]{1,0:T(8,128)}, f32[16,64]{1,0:T(8,128)S(1)}, u32[]{:S(2)}) copy-start(f32[16,64]{1,0:T(8,128)S(1)} %fusion.316) | copy-start | bytes 12292
  20.1 131.3 %copy-start.176 = (f32[16,64]{1,0:T(8,128)}, f32[16,64]{1,0:T(8,128)S(1)}, u32[]{:S(2)}) copy-start(f32[16,64]{1,0:T(8,128)S(1)} %fusion.315) | copy-start | bytes 12292
  60.8 43.6 %copy-start.109 = (f32[1024,3,8]{0,2,1:T(8,128)}, f32[1024,3,8]{0,2,1:T(8,128)S(1)}, u32[]{:S(2)}) copy-start(f32[1024,3,8]{0,2,1:T(8,128)S(1)} %convolution_bitcast_fusion.11) | copy-start | bytes 294916
  63.1 49.3 %copy-start.107 = (f32[1024,3,8]{0,2,1:T(8,128)}, f32[1024,3,8]{0,2,1:T(8,128)S(1)}, u32[]{:S(2)}) copy-start(f32[1024,3,8]{0,2,1:T(8,128)S(1)} %convolution_bitcast_fusion.10) | copy-start | bytes 294916
  108.6 351.0 %copy-start.57 = (bf16[16,64,2,2,64]{1,4,3,0,2:T(8,128)(2,1)}, bf16[16,64,2,2,64]{1,4,3,0,2:T(8,128)(2,1)S(1)}, u32[]{:S(2)}) copy-start(bf16[16,64,2,2,64]{1,4,3,0,2:T(8,128)(2,1)S(1)} %copy.291) | copy-start | bytes 1572868
  152.0 147.8 %copy-start.180 = (f32[16,2,128]{2,0,1:T(8,128)}, f32[16,2,128]{2,0,1:T(8,128)S(1)}, u32[]{:S(2)}) copy-start(f32[16,2,128]{2,0,1:T(8,128)S(1)} %get-tuple-element.971) | copy-start | bytes 49156
  157.5 301.2 %collective-permute-start = (bf16[64,2,128]{2,0,1:T(8,128)(2,1)}, bf16[64,2,128]{2,0,1:T(8,128)(2,1)}, u32[]{:S(2)}, u32[]{:S(2)}) collective-permute-start(bf16[64,2,128]{2,0,1:T(8,128)(2,1)} %slice.277), channel_id=1, source_target_pairs={{0,4},{4,8},{8,12},{12,16},{16,20},{20,24},{24,28},{1,5},{5,9},{9,... | collective-permute-start | bytes 98312 | tf_op jit(solution)/shard_map/ppermute | solution.py:17
  159.4 423.0 %collective-permute-start.1 = (bf16[64,2,128]{2,0,1:T(8,128)(2,1)}, bf16[64,2,128]{2,0,1:T(8,128)(2,1)}, u32[]{:S(2)}, u32[]{:S(2)}) collective-permute-start(bf16[64,2,128]{2,0,1:T(8,128)(2,1)} %slice.288), channel_id=1, source_target_pairs={{0,4},{4,8},{8,12},{12,16},{16,20},{20,24},{24,28},{1,5},{5,9},{9,... | collective-permute-start | bytes 98312 | tf_op jit(solution)/shard_map/ppermute | solution.py:17
  300.9 120.8 %copy-start.225 = (bf16[1,2,128]{2,1,0:T(2,128)(2,1)S(1)}, bf16[1,2,128]{2,1,0:T(2,128)(2,1)}, u32[]{:S(2)}) copy-start(bf16[1,2,128]{2,1,0:T(2,128)(2,1)} %convert_bitcast_fusion.5) | copy-start | bytes 1540
  300.9 141.7 %copy-start.224 = (bf16[1,2,128]{2,1,0:T(2,128)(2,1)S(1)}, bf16[1,2,128]{2,1,0:T(2,128)(2,1)}, u32[]{:S(2)}) copy-start(bf16[1,2,128]{2,1,0:T(2,128)(2,1)} %convert_bitcast_fusion.4) | copy-start | bytes 1540
  301.9 229.5 %copy-start.187 = (f32[16,2,128]{2,0,1:T(8,128)}, f32[16,2,128]{2,0,1:T(8,128)S(1)}, u32[]{:S(2)}) copy-start(f32[16,2,128]{2,0,1:T(8,128)S(1)} %fusion.198) | copy-start | bytes 49156
  576.1 216.7 %reduce-scatter.16.cloned.1.call-start = ((), (), s32[]{:S(2)}) async-start(), calls=%async_computation.17 | async-start | bytes 5242880 | tf_op jit(solution)/shard_map/reduce_scatter | solution.py:355
  577.6 76.5 %copy-start.190 = (f32[16,2,128]{2,0,1:T(8,128)}, f32[16,2,128]{2,0,1:T(8,128)S(1)}, u32[]{:S(2)}) copy-start(f32[16,2,128]{2,0,1:T(8,128)S(1)} %fusion.197) | copy-start | bytes 49156
  583.9 82.7 %copy-start.87 = (bf16[16,128,2,2,64]{1,4,3,0,2:T(8,128)(2,1)}, bf16[16,128,2,2,64]{1,4,3,0,2:T(8,128)(2,1)S(1)}, u32[]{:S(2)}) copy-start(bf16[16,128,2,2,64]{1,4,3,0,2:T(8,128)(2,1)S(1)} %pad_maximum_fusion.5) | copy-start | bytes 3145732
  697.2 135.8 %all-gather.46.cloned.1.call-start = ((), (), s32[]{:S(2)}) async-start(), calls=%async_computation.18 | async-start | bytes 5242880 | tf_op jit(solution)/shard_map/all_gather | solution.py:366
  697.8 97.8 %copy-start.149 = (f32[2048]{0:T(1024)}, f32[2048]{0:T(1024)S(1)}, u32[]{:S(2)}) copy-start(f32[2048]{0:T(1024)S(1)} %convert_element_type.767) | copy-start | bytes 24580
  711.5 86.7 %copy-start.13 = (f32[256,2048]{1,0:T(8,128)}, f32[256,2048]{1,0:T(8,128)S(1)}, u32[]{:S(2)}) copy-start(f32[256,2048]{1,0:T(8,128)S(1)} %get-tuple-element.968) | copy-start | bytes 6291460
  712.1 86.2 %copy-start.199 = (f32[256]{0:T(256)}, f32[256]{0:T(256)S(1)}, u32[]{:S(2)}) copy-start(f32[256]{0:T(256)S(1)} %fusion.350) | copy-start | bytes 3076
  798.3 264.5 %all-gather.42.cloned.1.call-start = ((), (), s32[]{:S(2)}) async-start(), calls=%async_computation.14 | async-start | bytes 18874368 | tf_op jit(solution)/shard_map/all_gather | solution.py:161
  802.2 386.3 %all-gather.44.cloned.1.call-start = ((), (), s32[]{:S(2)}) async-start(), calls=%async_computation.15 | async-start | bytes 9437184 | tf_op jit(solution)/shard_map/all_gather | solution.py:162
  802.9 434.6 %all-gather.40.cloned.1.call-start = ((), (), s32[]{:S(2)}) async-start(), calls=%async_computation.13 | async-start | bytes 5242880 | tf_op jit(solution)/shard_map/all_gather | solution.py:366
  803.7 513.7 %reduce-scatter.24.cloned.1.call-start = ((), (), s32[]{:S(2)}) async-start(), calls=%async_computation.23 | async-start | bytes 5242880 | tf_op jit(solution)/shard_map/reduce_scatter | solution.py:387
  1237.2 114.7 %reduce-scatter.20.cloned.1.call-start = ((), (), s32[]{:S(2)}) async-start(), calls=%async_computation.20 | async-start | bytes 5242880 | tf_op jit(solution)/shard_map/reduce_scatter | solution.py:387
  1309.4 42.4 %copy-start.11 = (f32[256,2048]{1,0:T(8,128)S(1)}, f32[256,2048]{1,0:T(8,128)}, u32[]{:S(2)}) copy-start(f32[256,2048]{1,0:T(8,128)} %copy-done.10) | copy-start | bytes 6291460
  1309.4 42.4 %copy-start.150 = (f32[2048]{0:T(1024)S(1)}, f32[2048]{0:T(1024)}, u32[]{:S(2)}) copy-start(f32[2048]{0:T(1024)} %copy-done.149) | copy-start | bytes 24580
  1309.5 84.4 %all-gather.48.cloned.1.call-start = ((), (), s32[]{:S(2)}) async-start(), calls=%async_computation.21 | async-start | bytes 5242880 | tf_op jit(solution)/shard_map/all_gather | solution.py:396
  1317.3 37.5 %copy-start.215 = (f32[256]{0:T(256)S(1)}, f32[256]{0:T(256)}, u32[]{:S(2)}) copy-start(f32[256]{0:T(256)} %copy-done.214) | copy-start | bytes 3076
  1317.3 37.6 %copy-start.200 = (f32[256]{0:T(256)S(1)}, f32[256]{0:T(256)}, u32[]{:S(2)}) copy-start(f32[256]{0:T(256)} %copy-done.199) | copy-start | bytes 3076
  1317.3 37.6 %copy-start.206 = (f32[256]{0:T(256)S(1)}, f32[256]{0:T(256)}, u32[]{:S(2)}) copy-start(f32[256]{0:T(256)} %copy-done.205) | copy-start | bytes 3076
  1317.4 37.5 %copy-start.77 = (bf16[256,2048]{1,0:T(8,128)(2,1)S(1)}, bf16[256,2048]{1,0:T(8,128)(2,1)}, u32[]{:S(2)}) copy-start(bf16[256,2048]{1,0:T(8,128)(2,1)} %reduce-scatter.24.cloned.1.call-done) | copy-start | bytes 3145732
  1359.2 78.5 %all-gather.50.cloned.1.call-start = ((), (), s32[]{:S(2)}) async-start(), calls=%async_computation.24 | async-start | bytes 5242880 | tf_op jit(solution)/shard_map/all_gather | solution.py:396
  1370.3 65.3 %copy-start.133 = (f32[16,2,4,64]{3,2,1,0:T(4,128)}, f32[16,2,4,64]{3,2,1,0:T(4,128)S(1)}, u32[]{:S(2)}) copy-start(f32[16,2,4,64]{3,2,1,0:T(4,128)S(1)} %add.808) | copy-start | bytes 98308
  1372.9 751.0 %all-reduce.13.cloned.1.call-start = ((), (), s32[]{:S(2)}) async-start(), calls=%async_computation.26 | async-start | bytes 262144 | tf_op jit(solution)/shard_map/psum | solution.py:568
  1483.7 169.9 %copy-start.198 = (s32[16]{0:T(128)S(1)}, s32[16]{0:T(128)}, u32[]{:S(2)}) copy-start(s32[16]{0:T(128)} %copy-done.197) | copy-start | bytes 196
  1587.6 70.1 %copy-start.177 = (f32[16,64]{1,0:T(8,128)S(1)}, f32[16,64]{1,0:T(8,128)}, u32[]{:S(2)}) copy-start(f32[16,64]{1,0:T(8,128)} %copy-done.176) | copy-start | bytes 12292
  1588.3 71.6 %copy-start.52 = (f32[16,64,2,64]{3,1,0,2:T(8,128)S(1)}, f32[16,64,2,64]{3,1,0,2:T(8,128)}, u32[]{:S(2)}) copy-start(f32[16,64,2,64]{3,1,0,2:T(8,128)} %copy-done.51) | copy-start | bytes 1572868
  1588.3 71.6 %copy-start.54 = (f32[16,64,2,64]{3,1,0,2:T(8,128)S(1)}, f32[16,64,2,64]{3,1,0,2:T(8,128)}, u32[]{:S(2)}) copy-start(f32[16,64,2,64]{3,1,0,2:T(8,128)} %copy-done.53) | copy-start | bytes 1572868
  1693.6 279.7 %collective-permute-start.2 = (bf16[2,64,2,64]{1,3,2,0:T(8,128)(2,1)}, bf16[2,64,2,64]{1,3,2,0:T(8,128)(2,1)}, u32[]{:S(2)}, u32[]{:S(2)}) collective-permute-start(bf16[2,64,2,64]{1,3,2,0:T(8,128)(2,1)} %pad_maximum_fusion.14), channel_id=1, source_target_pairs={{4,0},{8,4},{12,8},{16,12},{20,16},{24,20},{28,24},{5,1},{9,5},{13... | collective-permute-start | bytes 98312 | tf_op jit(solution)/shard_map/ppermute | solution.py:17
  1706.1 42.9 %copy-start.163 = (f32[1,2,128,64]{2,0,3,1:T(1,128)S(1)}, f32[1,2,128,64]{2,0,3,1:T(1,128)}, u32[]{:S(2)}) copy-start(f32[1,2,128,64]{2,0,3,1:T(1,128)} %fusion.247) | copy-start | bytes 196612
  1706.2 42.9 %copy-start.162 = (f32[1,2,128,64]{2,0,3,1:T(1,128)S(1)}, f32[1,2,128,64]{2,0,3,1:T(1,128)}, u32[]{:S(2)}) copy-start(f32[1,2,128,64]{2,0,3,1:T(1,128)} %fusion.245) | copy-start | bytes 196612
  1712.5 180.6 %copy-start.62 = (bf16[1024,512]{1,0:T(8,128)(2,1)}, bf16[1024,512]{1,0:T(8,128)(2,1)S(1)}, u32[]{:S(2)}) copy-start(bf16[1024,512]{1,0:T(8,128)(2,1)S(1)} %convert_element_type.813) | copy-start | bytes 3145732
  1815.7 81.2 %copy-start.175 = (f32[16,64]{1,0:T(8,128)S(1)}, f32[16,64]{1,0:T(8,128)}, u32[]{:S(2)}) copy-start(f32[16,64]{1,0:T(8,128)} %copy-done.174) | copy-start | bytes 12292
  1816.4 82.6 %copy-start.48 = (f32[16,64,2,64]{3,1,0,2:T(8,128)S(1)}, f32[16,64,2,64]{3,1,0,2:T(8,128)}, u32[]{:S(2)}) copy-start(f32[16,64,2,64]{3,1,0,2:T(8,128)} %copy-done.47) | copy-start | bytes 1572868
  1932.2 225.5 %reduce-scatter.28.cloned.1.call-start = ((), (), s32[]{:S(2)}) async-start(), calls=%async_computation.27 | async-start | bytes 1081344
  1932.9 59.1 %collective-permute-start.3 = (bf16[2,64,2,64]{1,3,2,0:T(8,128)(2,1)}, bf16[2,64,2,64]{1,3,2,0:T(8,128)(2,1)}, u32[]{:S(2)}, u32[]{:S(2)}) collective-permute-start(bf16[2,64,2,64]{1,3,2,0:T(8,128)(2,1)} %pad_maximum_fusion.15), channel_id=1, source_target_pairs={{4,0},{8,4},{12,8},{16,12},{20,16},{24,20},{28,24},{5,1},{9,5},{13... | collective-permute-start | bytes 98312 | tf_op jit(solution)/shard_map/ppermute | solution.py:17
  2024.2 176.4 %reduce-scatter.22.cloned.1.call-start = ((), (), s32[]{:S(2)}) async-start(), calls=%async_computation.22 | async-start | bytes 5242880 | tf_op jit(solution)/shard_map/reduce_scatter | solution.py:536
  2034.5 213.2 %reduce-scatter.14.cloned.1.call-start = ((), (), s32[]{:S(2)}) async-start(), calls=%async_computation.16 | async-start | bytes 5242880 | tf_op jit(solution)/shard_map/reduce_scatter | solution.py:372
  2051.1 244.1 %reduce-scatter.26.cloned.1.call-start = ((), (), s32[]{:S(2)}) async-start(), calls=%async_computation.25 | async-start | bytes 5242880 | tf_op jit(solution)/shard_map/reduce_scatter | solution.py:536
  2062.0 280.4 %reduce-scatter.18.cloned.1.call-start = ((), (), s32[]{:S(2)}) async-start(), calls=%async_computation.19 | async-start | bytes 5242880 | tf_op jit(solution)/shard_map/reduce_scatter | solution.py:372
  2081.0 119.6 %copy-start.173 = (f32[2048]{0:T(1024)S(1)}, f32[2048]{0:T(1024)}, u32[]{:S(2)}) copy-start(f32[2048]{0:T(1024)} %copy-done.172) | copy-start | bytes 24580
  2083.4 211.8 %copy-start.76 = (bf16[256,2048]{1,0:T(8,128)(2,1)S(1)}, bf16[256,2048]{1,0:T(8,128)(2,1)}, u32[]{:S(2)}) copy-start(bf16[256,2048]{1,0:T(8,128)(2,1)} %reduce-scatter.20.cloned.1.call-done) | copy-start | bytes 3145732
  2083.4 211.8 %copy-start.151 = (f32[2048]{0:T(1024)S(1)}, f32[2048]{0:T(1024)}, u32[]{:S(2)}) copy-start(f32[2048]{0:T(1024)} %copy-done.149) | copy-start | bytes 24580
  2083.4 211.8 %copy-start.201 = (f32[256]{0:T(256)S(1)}, f32[256]{0:T(256)}, u32[]{:S(2)}) copy-start(f32[256]{0:T(256)} %copy-done.199) | copy-start | bytes 3076
  2083.4 211.7 %copy-start.211 = (f32[256]{0:T(256)S(1)}, f32[256]{0:T(256)}, u32[]{:S(2)}) copy-start(f32[256]{0:T(256)} %copy-done.210) | copy-start | bytes 3076
  2295.2 47.2 %copy-start.12 = (f32[256,2048]{1,0:T(8,128)S(1)}, f32[256,2048]{1,0:T(8,128)}, u32[]{:S(2)}) copy-start(f32[256,2048]{1,0:T(8,128)} %copy-done.10) | copy-start | bytes 6291460
  2295.2 47.2 %copy-start.207 = (f32[256]{0:T(256)S(1)}, f32[256]{0:T(256)}, u32[]{:S(2)}) copy-start(f32[256]{0:T(256)} %copy-done.205) | copy-start | bytes 3076
  2295.2 47.2 %copy-start.217 = (f32[256]{0:T(256)S(1)}, f32[256]{0:T(256)}, u32[]{:S(2)}) copy-start(f32[256]{0:T(256)} %copy-done.216) | copy-start | bytes 3076
  (189 other events, 1247.9 us)
Sparse Core Ops, SparseCore 0:
  10.8 43.2 all-gather.33
  56.2 48.5 all-gather.35
  106.8 50.0 all-gather.37
  576.2 43.1 reduce-scatter.11
  697.3 95.5 reduce-scatter.15
  798.4 34.4 all-gather.45
  835.1 227.5 all-gather.41
  1064.8 123.5 all-gather.43
  1190.0 32.6 all-gather.39
  1237.3 42.4 reduce-scatter.23
  1309.6 42.2 reduce-scatter.19
  1359.4 34.4 all-gather.47
  1395.4 34.4 all-gather.49
  1932.3 66.0 all-reduce.12
  2024.3 133.3 reduce-scatter.27
  2160.1 40.4 reduce-scatter.21
  2203.1 44.5 reduce-scatter.13
  2250.6 44.5 reduce-scatter.25
  2297.9 44.5 reduce-scatter.17
where the time goes:
time: 2370 us; the launch traced here: 2360 us
  waiting for transfers between devices  707 us (30%)
  blocking collectives  578 us (24%)
  matrix products  472 us (20%)
  other arithmetic  285 us (12%)
  local copies, waits for them, and re-layouts  253 us (11%)
  loops' own time  35.8 us (2%)
    all_gather x8, blocking collectives, prefix(): lax.all_gather(a.astype(kind), axis)  282 us
    all_gather x1, waiting for transfers between devices, gather_weight_list(): lax.all_gather(gate_up_weight, 'seq', axis=0, tiled=True)  230 us
    all_gather x8, blocking collectives, prefix_2(): lax.all_gather(a.astype(kind), axis)  204 us
    all_gather x1, waiting for transfers between devices, gather_weight_list(): lax.all_gather(down_weight, 'seq', axis=1, tiled=True)  102 us
    reduce_scatter x2, waiting for transfers between devices, local(): lax.psum_scatter((jnp.einsum('th,dh->td', query_reduced_gradient, query_m...  88.8 us
    reduce_scatter x2, waiting for transfers between devices, local(): lax.psum_scatter(reduced_product(hidden, down_weight_merged).astype(jnp.b...  85.8 us
    reduce_scatter x2, waiting for transfers between devices, local(): lax.psum_scatter((reduced_product(attention_reduced, output_merged) + ADA...  80.7 us
    dynamic_slice x70, local copies, waits for them, and re-layouts, one(): lax.dynamic_index_in_dim(a, source, 0, False).astype(own.dtype)  68.8 us
  transfers between devices with their start and end apart: 23, of which 11 were waited for; matrix products, arithmetic and copies ran while one was open for 35% of the time, Pallas kernels for 0%

commit v1 on v0

v1 whole, which is shorter than its diff:
```python
import functools
import math

import jax
import jax.numpy as jnp
from jax import lax
from jax.experimental import pallas as pl
from jax.experimental.pallas import tpu as pltpu
from jax.sharding import PartitionSpec as P

STRETCH = 64
PAIR = 2 * STRETCH
WIN = 3 * STRETCH
EXT = 80
EPS = 1e-05
ADAPTER_SCALE = 2.0
BF = jnp.bfloat16
F32 = jnp.float32
VMEM_LIMIT = 48 * 1024 * 1024


def dotg(left, right, lc, rc):
    return lax.dot_general(left, right, (((lc,), (rc,)), ((), ())), preferred_element_type=F32)


def ring_order(count):
    if count % 8:
        return list(range(count))
    deep, wide = 4, count // 4
    path = [z * wide for z in range(deep)]
    for step, z in enumerate(reversed(range(deep))):
        ys = list(range(1, wide))
        path += [z * wide + y for y in (ys if step % 2 == 0 else ys[::-1])]
    return path


def ring_parts(shard):
    count = lax.axis_size("seq")
    order = ring_order(count)

    def hop(value, step):
        pairs = [(order[i], order[(i + step) % count]) for i in range(count)]
        return lax.ppermute(value, "seq", pairs)

    parts = [(0, 0, shard)]
    ahead = back = shard
    for distance in range(1, (count + 1) // 2):
        ahead, back = hop(ahead, 1), hop(back, -1)
        parts += [(-distance, 0, ahead), (distance, 0, back)]
    half = shard.shape[0] // 2
    parts.append((count // 2, 0, hop(ahead[:half], 1)))
    parts.append((count // 2, half, hop(back[half:], -1)))
    return parts


def ring_gather(shard):
    count = lax.axis_size("seq")
    order = ring_order(count)
    inverse = [0] * count
    for place, index in enumerate(order):
        inverse[index] = place
    me = jnp.asarray(inverse, jnp.int32)[lax.axis_index("seq")]
    table = jnp.asarray(order, jnp.int32)
    rows = shard.shape[0]
    out = jnp.zeros((count * rows,) + shard.shape[1:], shard.dtype)
    for offset, first, part in ring_parts(shard):
        source = table[(me + offset) % count]
        out = lax.dynamic_update_slice_in_dim(out, part, source * rows + first, 0)
    return out


def flip(value, axis, bit):
    count = lax.axis_size(axis)
    return lax.ppermute(value, axis, [(i, i ^ bit) for i in range(count)])


def group_gather(share):
    count = lax.axis_size("grp")
    out = []
    for far in range(0, count, 2):
        mine = share if far == 0 else flip(share, "grp", far)
        out += [mine, flip(mine, "grp", 1)]
    return out


def group_scatter(block):
    count = lax.axis_size("grp")
    total = None
    for far in list(range(2, count, 2)) + [0]:
        there = flip(block(far + 1).astype(BF), "grp", 1)
        both = block(far).astype(F32) + there.astype(F32)
        if far:
            both = flip(both.astype(BF), "grp", far).astype(F32)
        total = both if total is None else total + both
    return total


def shifted(value, axis, steps):
    count = lax.axis_size(axis)
    first, last = max(0, -steps), min(count, count - steps)
    return lax.ppermute(value, axis, [(i, i + steps) for i in range(first, last)])


def small_sums(wide, rest):
    n_seq, n_grp = lax.axis_size("seq"), lax.axis_size("grp")
    seq_index, group_index = lax.axis_index("seq"), lax.axis_index("grp")
    planes = wide.shape[0]
    blocks = wide.reshape(planes, n_seq, n_grp, -1).transpose(2, 1, 0, 3)
    blocks = jnp.take(blocks, jnp.arange(n_grp) ^ group_index, axis=0)
    blocks = jnp.take(blocks, jnp.arange(n_seq) ^ seq_index, axis=1)
    bit = n_grp // 2
    while bit:
        sent = flip(blocks[bit:].astype(BF), "grp", bit)
        blocks = blocks[:bit] + sent.astype(F32)
        bit //= 2
    blocks = blocks[0]
    rest = rest.astype(BF)
    bit = n_seq // 2
    while bit:
        cut = blocks[bit:].astype(BF)
        packed = jnp.concatenate([rest, cut.reshape(-1)])
        sent = flip(packed, "seq", bit)
        rest = (rest.astype(F32) + sent[: rest.shape[0]].astype(F32)).astype(BF)
        blocks = blocks[:bit] + sent[rest.shape[0] :].reshape(cut.shape).astype(F32)
        bit //= 2
    return blocks[0], rest.astype(F32)


def owners(stretch_ids, starts):
    return jnp.sum((starts[None, :] <= stretch_ids[:, None]).astype(jnp.int32), axis=1) - 1


def layout(lengths_row, base, blocks):
    counts = (lengths_row + STRETCH - 1) // STRETCH
    starts = jnp.cumsum(counts) - counts
    ids = base + jnp.arange(-3, blocks + 2, dtype=jnp.int32)
    owner = owners(ids, starts)
    ends = starts * STRETCH + lengths_row
    member = owner[:, None] == jnp.arange(starts.shape[0], dtype=jnp.int32)[None, :]
    end = jnp.sum(jnp.where(member, ends[None, :], 0), axis=1)
    valid = jnp.clip(end - ids * STRETCH, 0, STRETCH)[2:]
    one = (owner[2:] == owner[1:-1]).astype(jnp.int32)
    two = (owner[2:] == owner[:-2]).astype(jnp.int32)
    return jnp.stack([valid, one, two]), starts


def half_mask(shape):
    return (lax.broadcasted_iota(jnp.int32, shape, 1) & (PAIR - 1)) < STRETCH


def states_kernel(tab, kv_ref, wk_ref, phi_ref, ve_ref, st_ref, tail_ref, carry):
    step = pl.program_id(0)
    heads = kv_ref.shape[1] // PAIR

    @pl.when(step == 0)
    def _():
        carry[...] = jnp.zeros_like(carry)

    one_a, one_b = (tab[1, 2 * step + 1 + i].astype(F32) for i in range(2))
    lane = lax.broadcasted_iota(jnp.int32, (1, PAIR), 1)
    low = lane < STRETCH
    inside = lane & (STRETCH - 1)
    valid = inside < jnp.where(low, tab[0, 2 * step + 1], tab[0, 2 * step + 2])
    valid = jnp.where(valid, 1.0, 0.0)
    valid_low = jnp.where(low, valid, 0.0)
    valid_high = valid - valid_low
    wide = lax.broadcasted_iota(jnp.int32, (PAIR, PAIR), 1)
    for k in range(heads):
        kv = kv_ref[:, k * PAIR : (k + 1) * PAIR]
        moved = pltpu.roll(kv.astype(F32), STRETCH, 1)
        ve = jnp.where(
            wide < STRETCH, moved, jnp.where(wide < STRETCH + 2, 1.0, 0.0)
        ).astype(BF)
        ve_ref[:, k * PAIR : (k + 1) * PAIR] = ve
        mixed = dotg(wk_ref[k], kv, 1, 1)
        top = jnp.exp(mixed - jnp.max(mixed, axis=0, keepdims=True))
        bottom = jnp.exp(jnp.min(mixed, axis=0, keepdims=True) - mixed)
        top = top * (1.0 / jnp.sum(top, axis=0, keepdims=True))
        bottom = bottom * (1.0 / jnp.sum(bottom, axis=0, keepdims=True))
        phi = jnp.concatenate([top, bottom], axis=0)
        phi_ref[k * PAIR : (k + 1) * PAIR, :] = (phi * valid).astype(BF)
        first = dotg(ve, (phi * valid_low).astype(BF), 0, 1)[:EXT]
        second = dotg(ve, (phi * valid_high).astype(BF), 0, 1)[:EXT]
        st_ref[0, k, :EXT] = first
        st_ref[0, k, EXT:] = second
        mid = carry[k] * one_a + first
        tail = mid * one_b + second
        carry[k] = tail
        tail_ref[k, 0] = mid.astype(BF)
        tail_ref[k, 1] = tail.astype(BF)


def window_mask(tab, pair):
    lane = lax.broadcasted_iota(jnp.int32, (1, PAIR), 1)
    low = lane < STRETCH
    before = tab[0, 2 * pair] * tab[1, 2 * pair + 1]
    limits = [
        jnp.where(low, before, 0),
        jnp.where(
            low,
            jnp.minimum(lane + 1, tab[0, 2 * pair + 1]),
            tab[0, 2 * pair + 1] * tab[1, 2 * pair + 2],
        ),
        jnp.where(low, 0, jnp.minimum(lane - STRETCH + 1, tab[0, 2 * pair + 2])),
    ]
    row = lax.broadcasted_iota(jnp.int32, (STRETCH, PAIR), 0)
    return jnp.concatenate([jnp.where(row < limit, 1.0, 0.0) for limit in limits], axis=0)


def forward_kernel(
    per, scale, tab, q_ref, kv_ref, ve_ref, wq_ref, st_ref, ent_ref,
    att_ref, w_ref, phi_ref, s_ref, r_ref, carry,
):
    step = pl.program_id(0)
    heads = kv_ref.shape[1] // PAIR

    @pl.when(step == 0)
    def _():
        carry[...] = ent_ref[...]

    one_a, one_b = (tab[1, 2 * step + 1 + i].astype(F32) for i in range(2))
    two_a, two_b = (tab[2, 2 * step + 1 + i].astype(F32) for i in range(2))
    mask = window_mask(tab, step)
    mask = jnp.concatenate([mask] * per, axis=1)
    lanes = per * PAIR
    low = half_mask((EXT, lanes))
    rows = pl.ds(pl.multiple_of(step * PAIR, PAIR), WIN)
    for k in range(heads):
        kv = kv_ref[rows, k * PAIR : (k + 1) * PAIR]
        ve = ve_ref[rows, k * PAIR : (k + 1) * PAIR]
        base = k * per * STRETCH
        stacked = q_ref[base : base + per * STRETCH, :]
        q = jnp.concatenate(
            [stacked[g * STRETCH : (g + 1) * STRETCH] for g in range(per)], axis=1
        )
        q = jnp.concatenate([q, jnp.zeros_like(q)], axis=0)
        scores = dotg(kv, q, 1, 0)
        weights = (jnp.exp2(scores * scale) * mask).astype(BF)
        w_ref[0, k] = weights
        mixed = dotg(wq_ref[k], stacked, 1, 0)
        parts = []
        for g in range(per):
            u = mixed[g * STRETCH : (g + 1) * STRETCH]
            top = jnp.exp(u - jnp.max(u, axis=0, keepdims=True))
            bottom = jnp.exp(jnp.min(u, axis=0, keepdims=True) - u)
            top = top * (1.0 / jnp.sum(top, axis=0, keepdims=True))
            bottom = bottom * (1.0 / jnp.sum(bottom, axis=0, keepdims=True))
            parts.append(jnp.concatenate([top, bottom], axis=0).astype(BF))
        phi = jnp.concatenate(parts, axis=1)
        phi_ref[0, k] = phi
        older, old = carry[k, 0], carry[k, 1]
        states = jnp.concatenate([older * two_a, old * two_b], axis=0).astype(BF)
        s_ref[0, k] = states
        linear = dotg(states, phi, 1, 0)
        total = dotg(ve, weights, 0, 0)[:EXT] + jnp.where(low, linear[:EXT], linear[EXT:])
        inverse = 1.0 / total[STRETCH : STRETCH + 1]
        att = (total[:STRETCH] * inverse).astype(BF)
        for g in range(per):
            att_ref[base + g * STRETCH : base + (g + 1) * STRETCH, :] = att[
                :, g * PAIR : (g + 1) * PAIR
            ]
            r_ref[0, k * per + g : k * per + g + 1, :] = inverse[:, g * PAIR : (g + 1) * PAIR]
        current = old * one_a + st_ref[0, k, :EXT]
        carry[k, 0] = current
        carry[k, 1] = current * one_b + st_ref[0, k, EXT:]


def backward_kernel(
    per, pairs, scale, tab, order, q_ref, kv_ref, ve_ref, wq_ref, d_ref, att_ref, w_ref, phi_ref,
    s_ref, r_ref, dq_ref, dkv_ref, ds_ref, head_ref, map_ref, carry,
):
    step = pl.program_id(0)
    pair = pairs - 1 - step
    heads = kv_ref.shape[1] // PAIR

    @pl.when(step == 0)
    def _():
        carry[...] = jnp.zeros_like(carry)
        dkv_ref[...] = jnp.zeros_like(dkv_ref)
        map_ref[...] = jnp.zeros_like(map_ref)

    one_b = tab[1, 2 * pair + 2].astype(F32)
    one_c = tab[1, 2 * pair + 3].astype(F32)
    lanes = per * PAIR
    low = half_mask((EXT, lanes))
    rows = pl.ds(pl.multiple_of(pair * PAIR, PAIR), WIN)
    for k in range(heads):
        kv = kv_ref[rows, k * PAIR : (k + 1) * PAIR]
        ve = ve_ref[rows, k * PAIR : (k + 1) * PAIR]
        base = k * per * STRETCH

        def side(ref):
            return jnp.concatenate(
                [ref[base + g * STRETCH : base + (g + 1) * STRETCH, :] for g in range(per)], axis=1
            )

        stacked = q_ref[base : base + per * STRETCH, :]
        q = side(q_ref)
        d_att = side(d_ref)
        att = side(att_ref).astype(F32)
        inverse = jnp.concatenate(
            [r_ref[0, k * per + g : k * per + g + 1, :] for g in range(per)], axis=1
        )
        ratio = d_att * inverse
        d_den = -jnp.sum(ratio * att, axis=0, keepdims=True)
        d_high = d_den.astype(BF).astype(F32)
        row = lax.broadcasted_iota(jnp.int32, (EXT - STRETCH, lanes), 0)
        extra = jnp.where(row == 0, d_high, jnp.where(row == 1, d_den - d_high, 0.0))
        ratio_ext = jnp.concatenate([ratio, extra], axis=0)
        ratio_low = ratio_ext.astype(BF)
        weights = w_ref[0, k]
        padded = jnp.concatenate(
            [ratio_low, jnp.zeros((PAIR - EXT, lanes), BF)], axis=0
        )
        d_weights = dotg(ve, padded, 1, 0)
        d_scores = (d_weights * weights.astype(F32)).astype(BF)
        d_query = dotg(kv, d_scores, 0, 0)[:STRETCH] * scale
        zeros = jnp.zeros((STRETCH, lanes), BF)
        q_scaled = (q.astype(F32) * scale).astype(BF)
        d_kv = dotg(d_scores, jnp.concatenate([q_scaled, zeros], axis=0), 1, 1) + dotg(
            weights, jnp.concatenate([zeros, ratio_low[:STRETCH]], axis=0), 1, 1
        )
        dkv_ref[rows, k * PAIR : (k + 1) * PAIR] += d_kv
        phi = phi_ref[0, k]
        both = jnp.concatenate(
            [jnp.where(low, ratio_ext, 0.0), jnp.where(low, 0.0, ratio_ext)], axis=0
        ).astype(BF)
        d_phi = dotg(s_ref[0, k], both, 0, 0)
        d_state = dotg(both, phi, 1, 1)
        ds_ref[0, k] = d_state
        top, bottom = phi[:STRETCH].astype(F32), phi[STRETCH:].astype(F32)
        a, b = d_phi[:STRETCH], d_phi[STRETCH:]
        d_mixed = top * (a - jnp.sum(top * a, axis=0, keepdims=True)) - bottom * (
            b - jnp.sum(bottom * b, axis=0, keepdims=True)
        )
        d_mixed = d_mixed.astype(BF)
        d_mixed = jnp.concatenate(
            [d_mixed[:, g * PAIR : (g + 1) * PAIR] for g in range(per)], axis=0
        )
        d_stacked = jnp.concatenate(
            [d_query[:, g * PAIR : (g + 1) * PAIR] for g in range(per)], axis=0
        ) + dotg(wq_ref[k], d_mixed, 0, 0)
        dq_ref[base : base + per * STRETCH, :] = d_stacked.astype(BF)
        map_ref[k] += dotg(stacked, d_mixed, 1, 1)
        rest = d_state[EXT:] + one_c * carry[k]
        head = d_state[:EXT] + one_b * rest
        carry[k] = head
        head_ref[k, 0] = rest.astype(BF)
        head_ref[k, 1] = head.astype(BF)


def keys_kernel(
    pairs, tab, kv_ref, ve_ref, wk_ref, phi_ref, dkv_ref, back_ref, ds_ref, ent_ref,
    out_ref, map_ref, carry,
):
    step = pl.program_id(0)
    pair = pairs - 1 - step
    heads = kv_ref.shape[1] // PAIR

    @pl.when(step == 0)
    def _():
        carry[...] = ent_ref[...]
        map_ref[...] = jnp.zeros_like(map_ref)

    one_b = tab[1, 2 * pair + 2].astype(F32)
    one_c = tab[1, 2 * pair + 3].astype(F32)
    two_c = tab[2, 2 * pair + 3].astype(F32)
    two_d = tab[2, 2 * pair + 4].astype(F32)
    row = lax.broadcasted_iota(jnp.int32, (PAIR, PAIR), 0)
    lane = lax.broadcasted_iota(jnp.int32, (PAIR, PAIR), 1)
    last = jnp.where(step == 0, 1.0, 0.0)
    rows = pl.ds(pl.multiple_of(pair * PAIR + STRETCH, STRETCH), PAIR)
    for k in range(heads):
        kv = kv_ref[rows, k * PAIR : (k + 1) * PAIR]
        ve = ve_ref[rows, k * PAIR : (k + 1) * PAIR].astype(F32)
        next_one, next_two = carry[k, 0], carry[k, 1]
        pad = jnp.zeros((PAIR - EXT, PAIR), F32)
        grads = jnp.concatenate(
            [next_one * two_c, pad, next_two * two_d, pad], axis=0
        ).astype(BF)
        both = jnp.concatenate(
            [jnp.where(row < STRETCH, ve, 0.0), jnp.where(row < STRETCH, 0.0, ve)], axis=1
        ).astype(BF)
        d_phi = dotg(grads, both, 0, 1)
        phi = phi_ref[k * PAIR : (k + 1) * PAIR, :]
        d_both = dotg(phi, grads, 0, 1)
        d_value = jnp.where(row < STRETCH, d_both[:, :PAIR], d_both[:, PAIR:])
        d_value = jnp.where(lane < STRETCH, 0.0, pltpu.roll(d_value, STRETCH, 1))
        top, bottom = phi[:STRETCH].astype(F32), phi[STRETCH:].astype(F32)
        a, b = d_phi[:STRETCH], d_phi[STRETCH:]
        d_mixed = top * (a - jnp.sum(top * a, axis=0, keepdims=True)) - bottom * (
            b - jnp.sum(bottom * b, axis=0, keepdims=True)
        )
        d_mixed = d_mixed.astype(BF)
        d_key = dotg(d_mixed, wk_ref[k], 0, 0)
        map_ref[k] += dotg(kv, d_mixed, 0, 1)
        total = dkv_ref[rows, k * PAIR : (k + 1) * PAIR] + d_value + d_key
        returned = back_ref[:, k * PAIR : (k + 1) * PAIR].astype(F32) * last
        total = total + jnp.concatenate([jnp.zeros_like(returned), returned], axis=0)
        out_ref[k * PAIR : (k + 1) * PAIR, :] = jnp.transpose(total).astype(BF)
        state = ds_ref[0, k]
        rest = state[EXT:] + one_c * next_one
        carry[k, 1] = rest
        carry[k, 0] = state[:EXT] + one_b * rest


def whole(shape):
    return pl.BlockSpec(shape, lambda i, *_: (0,) * len(shape))


def sds(shape, kind):
    return jax.ShapeDtypeStruct(shape, kind)


def params():
    return pltpu.CompilerParams(
        dimension_semantics=("arbitrary",), vmem_limit_bytes=VMEM_LIMIT
    )


def run_states(table, kv, maps):
    rows, width = kv.shape
    heads, pairs = width // PAIR, rows // PAIR
    return pl.pallas_call(
        states_kernel,
        grid_spec=pltpu.PrefetchScalarGridSpec(
            num_scalar_prefetch=1,
            grid=(pairs,),
            in_specs=[pl.BlockSpec((PAIR, width), lambda i, *_: (i, 0)), whole(maps.shape)],
            out_specs=[
                pl.BlockSpec((width, PAIR), lambda i, *_: (0, i)),
                pl.BlockSpec((PAIR, width), lambda i, *_: (i, 0)),
                pl.BlockSpec((1, heads, 2 * EXT, PAIR), lambda i, *_: (i, 0, 0, 0)),
                whole((heads, 2, EXT, PAIR)),
            ],
            scratch_shapes=[pltpu.VMEM((heads, EXT, PAIR), F32)],
        ),
        out_shape=[
            sds((width, rows), BF),
            sds((rows, width), BF),
            sds((pairs, heads, 2 * EXT, PAIR), F32),
            sds((heads, 2, EXT, PAIR), BF),
        ],
        compiler_params=params(),
        name="states",
    )(table, kv, maps)


def run_forward(table, q, kv, ve, maps, states, entering):
    q_width, rows = q.shape
    width = kv.shape[1]
    heads, pairs = width // PAIR, rows // PAIR
    per = q_width // STRETCH // heads
    scale = STRETCH ** (-0.5) * math.log2(math.e)
    step = lambda *shape: pl.BlockSpec((1,) + shape, lambda i, *_: (i,) + (0,) * len(shape))
    return pl.pallas_call(
        functools.partial(forward_kernel, per, scale),
        grid_spec=pltpu.PrefetchScalarGridSpec(
            num_scalar_prefetch=1,
            grid=(pairs,),
            in_specs=[
                pl.BlockSpec((q_width, PAIR), lambda i, *_: (0, i)),
                whole(kv.shape),
                whole(ve.shape),
                whole(maps.shape),
                step(heads, 2 * EXT, PAIR),
                whole(entering.shape),
            ],
            out_specs=[
                pl.BlockSpec((q_width, PAIR), lambda i, *_: (0, i)),
                step(heads, WIN, per * PAIR),
                step(heads, PAIR, per * PAIR),
                step(heads, 2 * EXT, PAIR),
                step(heads * per, PAIR),
            ],
            scratch_shapes=[pltpu.VMEM((heads, 2, EXT, PAIR), F32)],
        ),
        out_shape=[
            sds((q_width, rows), BF),
            sds((pairs, heads, WIN, per * PAIR), BF),
            sds((pairs, heads, PAIR, per * PAIR), BF),
            sds((pairs, heads, 2 * EXT, PAIR), BF),
            sds((pairs, heads * per, PAIR), F32),
        ],
        compiler_params=params(),
        name="attention_forward",
    )(table, q, kv, ve, maps, states, entering)


def run_backward(table, order, q, kv, ve, maps, d_att, att, weights, phi, states, inverse):
    q_width, rows = q.shape
    width = kv.shape[1]
    heads, pairs = width // PAIR, rows // PAIR
    per = q_width // STRETCH // heads
    rev = lambda i: pairs - 1 - i
    step = lambda *shape: pl.BlockSpec((1,) + shape, lambda i, *_: (rev(i),) + (0,) * len(shape))
    column = pl.BlockSpec((q_width, PAIR), lambda i, *_: (0, rev(i)))
    return pl.pallas_call(
        functools.partial(backward_kernel, per, pairs, STRETCH ** (-0.5)),
        grid_spec=pltpu.PrefetchScalarGridSpec(
            num_scalar_prefetch=2,
            grid=(pairs,),
            in_specs=[
                column,
                whole(kv.shape),
                whole(ve.shape),
                whole(maps.shape),
                pl.BlockSpec((q_width, PAIR), lambda i, tab, order: (0, order[rev(i)])),
                column,
                step(heads, WIN, per * PAIR),
                step(heads, PAIR, per * PAIR),
                step(heads, 2 * EXT, PAIR),
                step(heads * per, PAIR),
            ],
            out_specs=[
                column,
                whole(kv.shape),
                step(heads, 2 * EXT, PAIR),
                whole((heads, 2, EXT, PAIR)),
                whole(maps.shape),
            ],
            scratch_shapes=[pltpu.VMEM((heads, EXT, PAIR), F32)],
        ),
        out_shape=[
            sds((q_width, rows), BF),
            sds(kv.shape, F32),
            sds((pairs, heads, 2 * EXT, PAIR), F32),
            sds((heads, 2, EXT, PAIR), BF),
            sds(maps.shape, F32),
        ],
        compiler_params=params(),
        name="attention_backward",
    )(table, order, q, kv, ve, maps, d_att, att, weights, phi, states, inverse)


def run_keys(table, kv, ve, maps, phi, d_kv, returned, d_states, entering):
    width, rows = phi.shape
    heads, pairs = width // PAIR, rows // PAIR
    rev = lambda i: pairs - 1 - i
    return pl.pallas_call(
        functools.partial(keys_kernel, pairs),
        grid_spec=pltpu.PrefetchScalarGridSpec(
            num_scalar_prefetch=1,
            grid=(pairs,),
            in_specs=[
                whole(kv.shape),
                whole(ve.shape),
                whole(maps.shape),
                pl.BlockSpec((width, PAIR), lambda i, *_: (0, rev(i))),
                whole(d_kv.shape),
                whole(returned.shape),
                pl.BlockSpec((1, heads, 2 * EXT, PAIR), lambda i, *_: (rev(i), 0, 0, 0)),
                whole(entering.shape),
            ],
            out_specs=[
                pl.BlockSpec((width, PAIR), lambda i, *_: (0, rev(i))),
                whole((heads, PAIR, STRETCH)),
            ],
            scratch_shapes=[pltpu.VMEM((heads, 2, EXT, PAIR), F32)],
        ),
        out_shape=[sds((width, rows), BF), sds((heads, PAIR, STRETCH), F32)],
        compiler_params=params(),
        name="attention_keys",
    )(table, kv, ve, maps, phi, d_kv, returned, d_states, entering)


def exchange(ends, starts, base, blocks, sign):
    count = lax.axis_size("seq")
    edge = base - 1 if sign > 0 else base + blocks
    near = shifted(ends, "seq", sign)
    outer = near[:, 1].astype(F32)
    inner = near[:, 0].astype(F32)
    full = ends[:, 1]
    ids = jnp.stack(
        [edge, edge - sign] + [edge - sign * (r - 1) * blocks for r in range(2, count)]
    )
    owner = owners(ids, starts)
    for r in range(2, count):
        far = shifted(full, "seq", sign * r).astype(F32)
        outer = outer + jnp.where(owner[r] == owner[0], far, 0.0)
        inner = inner + jnp.where(owner[r] == owner[1], far, 0.0)
    return inner, outer


def local(
    tokens,
    cotangent,
    lengths,
    attention_norm_gain,
    feedforward_norm_gain,
    query_weight,
    keyvalue_weight,
    output_weight,
    gate_up_weight,
    down_weight,
    adapter_width_factor,
    query_up_factor,
    keyvalue_up_factor,
    output_input_factor,
    query_feature_weight,
    key_feature_weight,
):
    batches, rows, model = tokens.shape
    n_seq, n_grp = lax.axis_size("seq"), lax.axis_size("grp")
    group_index, seq_index = lax.axis_index("grp"), lax.axis_index("seq")
    share = rows // n_grp
    blocks, pairs = rows // STRETCH, rows // PAIR
    rank = adapter_width_factor.shape[2]
    depth = query_weight.shape[0]
    q_width = query_weight.shape[1]
    kv_heads = key_feature_weight.shape[0]
    kv_width = kv_heads * PAIR
    per = query_feature_weight.shape[0] // kv_heads
    hidden_width = down_weight.shape[0]
    gain_attn = attention_norm_gain.astype(F32)
    gain_mlp = feedforward_norm_gain.astype(F32)
    base = seq_index * blocks
    width = q_width + kv_width

    kv_shard = (
        keyvalue_weight.reshape(depth, 2, kv_heads, STRETCH)
        .transpose(0, 2, 1, 3)
        .reshape(depth, kv_width)
    )
    adapter_shard = adapter_width_factor.transpose(1, 0, 2).reshape(depth, 4 * rank)
    in_weight = ring_gather(jnp.concatenate([query_weight, kv_shard, adapter_shard], axis=1))
    out_shard, gate_shard, down_shard, in_weight = lax.optimization_barrier(
        (output_weight.T, gate_up_weight.reshape(depth, -1), down_weight.T, in_weight)
    )
    out_weight = ring_gather(out_shard)
    out_weight, gate_shard, down_shard = lax.optimization_barrier(
        (out_weight, gate_shard, down_shard)
    )
    gate_weight = ring_gather(gate_shard)
    down_merged = ring_gather(down_shard)
    adapter_merged = in_weight[:, width:]
    out_factor = adapter_merged[:, 3 * rank :]

    key_up = keyvalue_up_factor.reshape(2, rank, kv_heads, 1, STRETCH)
    kv_up = (
        jnp.zeros((2, rank, kv_heads, 2, STRETCH), BF)
        .at[0, :, :, 0].set(key_up[0, :, :, 0])
        .at[1, :, :, 1].set(key_up[1, :, :, 0])
        .reshape(2 * rank, kv_width)
    )
    maps_t = query_feature_weight.transpose(0, 2, 1).reshape(kv_heads, per, STRETCH, STRETCH)
    query_maps = jnp.zeros((kv_heads, per, STRETCH, per, STRETCH), BF)
    for g in range(per):
        query_maps = query_maps.at[:, g, :, g, :].set(maps_t[:, g])
    query_maps = query_maps.reshape(kv_heads, per * STRETCH, per * STRETCH)
    key_maps = jnp.concatenate(
        [key_feature_weight.transpose(0, 2, 1), jnp.zeros((kv_heads, STRETCH, STRETCH), BF)], axis=2
    )

    def rel_rows(array, r):
        return lax.dynamic_slice_in_dim(array, (group_index ^ r) * share, share, 0)

    def rel_lanes(array, r):
        return lax.dynamic_slice_in_dim(array, (group_index ^ r) * share, share, 1)

    saved = []
    for batch in range(batches):
        x = tokens[batch].astype(F32)
        factor = lax.rsqrt(jnp.mean(x * x, axis=-1, keepdims=True) + EPS)
        normed = (x * factor * gain_attn).astype(BF)
        side = dotg(normed, in_weight[:, q_width:], 1, 0)
        mids = side[:, kv_width:].astype(BF)
        query = dotg(in_weight[:, :q_width], normed, 0, 1) + ADAPTER_SCALE * dotg(
            query_up_factor, mids[:, :rank], 0, 1
        )
        query = query.astype(BF)
        kv = side[:, :kv_width] + ADAPTER_SCALE * dotg(mids[:, rank : 3 * rank], kv_up, 1, 0)
        kv = kv.astype(BF)
        table, starts = layout(lengths[batch], base, blocks)
        phi_key, ve, states, ends = run_states(table, kv, key_maps)
        halo = shifted(
            jnp.concatenate([kv[rows - STRETCH :], ve[rows - STRETCH :]], axis=1), "seq", 1
        )
        kv = jnp.concatenate([halo[:, :kv_width], kv])
        ve = jnp.concatenate([halo[:, kv_width:], ve])
        entering = jnp.stack(exchange(ends, starts, base, blocks, 1), axis=1)
        saved.append([normed, mids, query, kv, ve, table, starts, phi_key, states, entering])

    attended = []
    for batch in range(batches):
        normed, mids, query, kv, ve, table, starts, phi_key, states, entering = saved[batch]
        att, weights, phi, sums, inverse = run_forward(
            table, query, kv, ve, query_maps, states, entering
        )
        out_mid = dotg(output_input_factor, att, 0, 0)
        att_ext = jnp.concatenate([att, (ADAPTER_SCALE * out_mid).astype(BF)], axis=0)
        out_ext = jnp.concatenate([out_weight, out_factor], axis=1)
        branch = group_scatter(
            lambda r: dotg(rel_lanes(att_ext, r), out_ext, 0, 1).astype(BF)
        )
        resid = rel_rows(tokens[batch], 0).astype(F32) + branch
        mlp_factor = lax.rsqrt(jnp.mean(resid * resid, axis=-1, keepdims=True) + EPS)
        mlp_in = group_gather((resid * mlp_factor * gain_mlp).astype(BF))
        attended.append([att, weights, phi, sums, inverse, out_mid, resid, mlp_factor, mlp_in])

    block_rows, d_resids, d_branches = [], [], []
    for batch in range(batches):
        resid, mlp_factor, mlp_in = attended[batch][6:]
        mlp_in = jnp.concatenate(mlp_in)
        upstream = jnp.concatenate([rel_rows(cotangent[batch], r) for r in range(n_grp)])
        gate_up = dotg(mlp_in, gate_weight, 1, 0)
        gate, up = gate_up[:, :hidden_width], gate_up[:, hidden_width:]
        sig = 1.0 / (1.0 + jnp.exp(-gate))
        hidden = (gate * sig * up).astype(BF)
        d_hidden = dotg(upstream, down_merged, 1, 0)
        d_gate = d_hidden * up * sig * (1.0 + gate * (1.0 - sig))
        d_up = d_hidden * gate * sig
        d_gate_up = jnp.concatenate([d_gate.astype(BF), d_up.astype(BF)], axis=1)
        d_in = dotg(d_gate_up, gate_weight, 1, 1).astype(BF)
        d_in = group_scatter(lambda r: d_in[r * share : (r + 1) * share])
        mlp_out = dotg(hidden, down_merged, 1, 1).astype(BF)
        mlp_out = group_scatter(lambda r: mlp_out[r * share : (r + 1) * share])
        block_rows.append((resid + mlp_out).astype(BF))
        e = gain_mlp * d_in
        d_resid = (
            upstream[:share].astype(F32)
            + mlp_factor * e
            - resid * mlp_factor**3 * jnp.mean(resid * e, axis=-1, keepdims=True)
        )
        d_resids.append(d_resid)
        d_branches.append(group_gather(d_resid.astype(BF)))

    order_index = jnp.arange(pairs, dtype=jnp.int32)
    per_share = share // PAIR
    order = ((order_index // per_share) ^ group_index) * per_share + order_index % per_share
    gone = []
    for batch in range(batches):
        normed, mids, query, kv, ve, table, starts, phi_key, states, entering = saved[batch]
        att, weights, phi, sums, inverse, out_mid = attended[batch][:6]
        d_branch = jnp.concatenate(d_branches[batch])
        back_out = ADAPTER_SCALE * dotg(out_factor, d_branch, 0, 1)
        d_att = dotg(out_weight, d_branch, 0, 1) + dotg(
            output_input_factor, back_out.astype(BF), 1, 0
        )
        dq, d_kv, d_states, heads_sum, map_grad = run_backward(
            table, order, query, kv, ve, query_maps, d_att, att, weights, phi, sums, inverse
        )
        returned = shifted(d_kv[:STRETCH].astype(BF), "seq", -1)
        leaving = exchange(heads_sum, starts, base, blocks, -1)
        leaving = jnp.stack([leaving[1], leaving[0]], axis=1)
        gone.append([dq, d_kv, d_states, map_grad, returned, leaving, d_branch, back_out])

    input_grads = []
    wide = jnp.zeros((4 * rank, model), F32)
    up_grad = jnp.zeros((3 * rank, width), F32)
    out_in_grad = jnp.zeros((q_width, rank), F32)
    query_map_grad = jnp.zeros(query_maps.shape, F32)
    key_map_grad = jnp.zeros((kv_heads, STRETCH, STRETCH), F32)
    for batch in range(batches):
        normed, mids, query, kv, ve, table, starts, phi_key, states, entering = saved[batch]
        att, _, _, _, _, out_mid, resid, mlp_factor, _ = attended[batch]
        dq, d_kv, d_states, map_grad, returned, leaving, d_branch, back_out = gone[batch]
        d_kv_low, key_grad = run_keys(
            table, kv, ve, key_maps, phi_key, d_kv, returned, d_states, leaving
        )
        back_in = jnp.concatenate(
            [dotg(query_up_factor, dq, 1, 0), dotg(kv_up, d_kv_low, 1, 0)], axis=0
        )
        back_in = (ADAPTER_SCALE * back_in).astype(BF)
        stacked = jnp.concatenate([dq, d_kv_low, back_in], axis=0)
        d_normed = group_scatter(
            lambda r: dotg(
                rel_lanes(stacked, r), in_weight[:, : width + 3 * rank], 0, 1
            ).astype(BF)
        )
        x = rel_rows(tokens[batch], 0).astype(F32)
        factor = lax.rsqrt(jnp.mean(x * x, axis=-1, keepdims=True) + EPS)
        e = gain_attn * d_normed
        input_grads.append(
            d_resids[batch]
            + factor * e
            - x * factor**3 * jnp.mean(x * e, axis=-1, keepdims=True)
        )
        order_rel = [rel_lanes(out_mid, r) for r in range(n_grp)]
        out_mid_rel = jnp.concatenate(order_rel, axis=1).astype(BF)
        att_rel = jnp.concatenate([rel_lanes(att, r) for r in range(n_grp)], axis=1)
        wide = wide + jnp.concatenate(
            [dotg(back_in, normed, 1, 0), ADAPTER_SCALE * dotg(out_mid_rel, d_branch, 1, 0)]
        )
        up_grad = up_grad + ADAPTER_SCALE * dotg(
            mids[:, : 3 * rank], jnp.concatenate([dq, d_kv_low]), 0, 1
        )
        out_in_grad = out_in_grad + dotg(att_rel, back_out.astype(BF), 1, 1)
        query_map_grad = query_map_grad + map_grad
        key_map_grad = key_map_grad + key_grad[:, :STRETCH]

    kv_grad = up_grad[rank:, q_width:].reshape(2, rank, kv_heads, 2, STRETCH)
    kv_grad = jnp.stack([kv_grad[0, :, :, 0], kv_grad[1, :, :, 1]])
    map_blocks = query_map_grad.reshape(kv_heads, per, STRETCH, per, STRETCH)
    query_map_grad = jnp.stack([map_blocks[:, g, :, g] for g in range(per)], axis=1)
    pieces = [
        (up_grad[:rank, :q_width], query_up_factor.shape),
        (kv_grad, keyvalue_up_factor.shape),
        (out_in_grad, output_input_factor.shape),
        (query_map_grad, query_feature_weight.shape),
        (key_map_grad, key_feature_weight.shape),
    ]
    wide_share, rest = small_sums(
        wide, jnp.concatenate([piece.reshape(-1) for piece, _ in pieces])
    )
    wide_share = wide_share.reshape(4, rank, -1).transpose(0, 2, 1)
    outs, first = [], 0
    for piece, shape in pieces:
        outs.append(rest[first : first + piece.size].reshape(shape))
        first += piece.size
    return (jnp.stack(block_rows), jnp.stack(input_grads), wide_share, *outs)


def solution(mesh):
    return jax.shard_map(
        local,
        mesh=mesh,
        in_specs=(
            P(None, "seq", None),
            P(None, "seq", None),
            P(),
            P(),
            P(),
            P("seq", "grp"),
            P("seq", None, "grp"),
            P("grp", "seq"),
            P("seq", None, "grp"),
            P("grp", "seq"),
            P(None, "seq", None),
            P(None, "grp"),
            P(None, None, "grp"),
            P("grp", None),
            P("grp", None, None),
            P("grp", None, None),
        ),
        out_specs=(
            P(None, ("seq", "grp"), None),
            P(None, ("seq", "grp"), None),
            P(None, ("seq", "grp"), None),
            P(None, "grp"),
            P(None, None, "grp"),
            P("grp", None),
            P("grp", None, None),
            P("grp", None, None),
        ),
        check_vma=False,
    )
```

time: 2370 us -> 1100 us (0.46)
  blocking collectives: 578 us -> 0 us
  waiting for transfers between devices: 707 us -> 366 us
  other arithmetic: 285 us -> 55.7 us
  matrix products: 472 us -> 271 us
  local copies, waits for them, and re-layouts: 253 us -> 134 us
  starting transfers between devices: 8.58 us -> 113 us
  Pallas kernels: 0 us -> 68.4 us
  between operations: 18.1 us -> 77.5 us
  loops' own time: 35.8 us -> 0 us
    all_gather x17 -> x0, blocking collectives: 519 us -> none  [the longest x8 282 us: prefix(): lax.all_gather(a.astype(kind), axis)]
    all_gather x9 -> x0, waiting for transfers between devices: 382 us -> none  [the longest x1 230 us: gather_weight_list(): lax.all_gather(gate_up_weight, 'seq', axis=0, tiled=True)]
    ppermute x4 -> x105, waiting for transfers between devices: 0.01 us -> 366 us  [the longest x32 210 us: hop(): return lax.ppermute(value, 'seq', pairs)]
    reduce_scatter x8 -> x0, waiting for transfers between devices: 290 us -> none  [the longest x2 88.8 us: local(): lax.psum_scatter((jnp.einsum('th,dh->td', query_reduced_gradient, query_m...]
    dot_general x112 -> x52, matrix products: 470 us -> 271 us  [dotg(): lax.dot_general(left, right, (((lc,), (rc,)), ((), ())), preferred_elemen...]
    sub x17 -> x4, other arithmetic: 113 us -> 0.02 us  [owners(): jnp.sum((starts[None, :] <= stretch_ids[:, None]).astype(jnp.int32), axis=1)]
    ppermute x4 -> x105, starting transfers between devices: 7.02 us -> 113 us  [the longest x32 55.3 us: shifted(): lax.ppermute(value, axis, [(i, i + steps) for i in range(first, last)])]
    pallas_call x0 -> x8, Pallas kernels: none -> 68.4 us  [the longest x2 28.3 us: run_backward(): pl.pallas_call(functools.partial(backward_kernel, per, pairs, STRETCH **...]
  transfers between devices with their start and end apart: 23 -> 105, of which waited for: 11 -> 36; matrix products, arithmetic and copies ran while one was open for 35% -> 37% of each run, Pallas kernels for 0% -> 5%
where the time goes in v1:
time: 1100 us; the launch traced here: 1090 us
  waiting for transfers between devices  366 us (33%)
  matrix products  271 us (25%)
  local copies, waits for them, and re-layouts  134 us (12%)
  starting transfers between devices  113 us (10%)
  between operations  77.5 us (7%)
  Pallas kernels  68.4 us (6%)
  other arithmetic  55.7 us (5%)
    dot_general x52, matrix products, dotg(): lax.dot_general(left, right, (((lc,), (rc,)), ((), ())), preferred_elemen...  271 us
    ppermute x32, waiting for transfers between devices, hop(): return lax.ppermute(value, 'seq', pairs)  210 us
    ppermute x41, waiting for transfers between devices, flip(): return lax.ppermute(value, axis, [(i, i ^ bit) for i in range(count)])  146 us
    ppermute x32, starting transfers between devices, shifted(): lax.ppermute(value, axis, [(i, i + steps) for i in range(first, last)])  55.3 us
    ppermute x32, starting transfers between devices, hop(): return lax.ppermute(value, 'seq', pairs)  34 us
    pallas_call x2, Pallas kernels, run_backward(): pl.pallas_call(functools.partial(backward_kernel, per, pairs, STRETCH **...  28.3 us
    dynamic_update_slice x36, local copies, waits for them, and re-layouts, ring_gather(): out = lax.dynamic_update_slice_in_dim(out, part, source * rows + first, 0)  26.8 us
    unnamed x325, local copies, waits for them, and re-layouts  26.1 us
  transfers between devices with their start and end apart: 105, of which 36 were waited for; matrix products, arithmetic and copies ran while one was open for 37% of the time, Pallas kernels for 5%

profile of v1, /device:TPU:0, one launch (start us, length us, event | category | flops | bytes accessed | tf_op | source)
XLA Modules:
  0.0 1085.5 jit_solution(16182751146723012262)
XLA Ops:
  40.1 4.5 fusion
  45.9 3.8 fusion.330
  70.1 6.1 fusion.329
  79.9 6.6 fusion.321
  94.8 6.2 collective-permute-done.2
  108.0 4.1 collective-permute-done.4
  120.8 4.0 fusion.346
  127.9 5.5 states.3
  144.7 6.8 fusion.76
  152.3 3.7 fusion.345
  161.2 5.5 states.2
  166.8 5.4 fusion.78
  178.0 3.7 collective-permute-start.8
  203.6 8.1 attention_forward.3
  214.1 4.7 collective-permute-done.18
  221.7 4.2 collective-permute-done.20
  237.6 8.1 attention_forward.2
  252.6 6.1 broadcast_in_dim.148
  265.9 52.1 %collective-permute-done.38 = bf16[256,2048]{0,1:T(8,128)(2,1)} collective-permute-done((bf16[256,2048]{0,1:T(8,128)(2,1)S(1)}, bf16[256,2048]{0,1:T(8,128)(2,1)}, u32[]{:S(2)}, u32[]{:S(2)}) %collective-permute-start.38) | collective-permute-done | bytes 1048608 | tf_op jit(solution)/shard_map/ppermute | solution.py:43
  321.8 4.3 broadcast_in_dim.149
  339.2 5.1 collective-permute-done.25
  352.7 5.5 collective-permute-done.40
  358.5 4.1 collective-permute-done.41
  365.8 37.4 %collective-permute-done.32 = bf16[256,4096]{1,0:T(8,128)(2,1)S(1)} collective-permute-done((bf16[256,4096]{1,0:T(8,128)(2,1)S(1)}, bf16[256,4096]{1,0:T(8,128)(2,1)S(1)}, u32[]{:S(2)}, u32[]{:S(2)}) %collective-permute-start.32) | collective-permute-done | bytes 2097184 | tf_op jit(solution)/shard_map/ppermute | solution.py:43
  405.1 20.5 %collective-permute-done.42 = bf16[256,2048]{0,1:T(8,128)(2,1)S(1)} collective-permute-done((bf16[256,2048]{0,1:T(8,128)(2,1)S(1)}, bf16[256,2048]{0,1:T(8,128)(2,1)S(1)}, u32[]{:S(2)}, u32[]{:S(2)}) %collective-permute-start.42) | collective-permute-done | bytes 1048608 | tf_op jit(solution)/shard_map/ppermute | solution.py:43
  432.1 47.2 %collective-permute-done.44 = bf16[128,2048]{0,1:T(8,128)(2,1)S(1)} collective-permute-done((bf16[128,2048]{0,1:T(8,128)(2,1)S(1)}, bf16[128,2048]{0,1:T(8,128)(2,1)S(1)}, u32[]{:S(2)}, u32[]{:S(2)}) %collective-permute-start.44) | collective-permute-done | bytes 524320 | tf_op jit(solution)/shard_map/ppermute | solution.py:43
  480.2 4.3 collective-permute-done.45
  493.1 12.4 %collective-permute-done.28 = bf16[256,2048]{1,0:T(8,128)(2,1)} collective-permute-done((bf16[256,2048]{1,0:T(8,128)(2,1)}, bf16[256,2048]{1,0:T(8,128)(2,1)}, u32[]{:S(2)}, u32[]{:S(2)}) %collective-permute-start.28) | collective-permute-done | bytes 1048608 | tf_op jit(solution)/shard_map/ppermute | solution.py:74
  505.5 6.5 collective-permute-done.36
  515.5 22.4 %fusion.22 = f32[1024,4096]{1,0:T(8,128)} fusion(bf16[2048,4096]{1,0:T(8,128)(2,1)} %constant_dynamic-update-slice_fusion.10, bf16[256,2048]{1,0:T(8,128)(2,1)S(1)} %collective-permute-done.62, bf16[256,2048]{1,0:T(8,128)(2,1)S(1)} %collective-permute-done.61, bf16[256,2048]{1,0:T(8,128)(2,1)S(1)} %collective-permute-done.60, ...), kind=kOutput, calls=%fused_computation.36 | convolution fusion | flops 17196646400 | bytes 37748736 | tf_op jit(solution)/shard_map/dot_general | solution.py:23
  537.9 12.9 %fusion.48 = bf16[1024,2048]{1,0:T(8,128)(2,1)S(1)} fusion(bf16[2048,2048]{0,1:T(8,128)(2,1)S(1)} %constant_dynamic-update-slice_fusion.16, f32[1024,4096]{1,0:T(8,128)} %fusion.22), kind=kOutput, calls=%fused_computation.65 | convolution fusion | flops 8604614656 | bytes 29360128 | tf_op jit(solution)/shard_map/dot_general | solution.py:23
  555.3 21.6 %multiply_convert_fusion.1 = (bf16[1024,2048]{1,0:T(8,128)(2,1)}, bf16[1024,2048]{1,0:T(8,128)(2,1)}) fusion(f32[1024,4096]{1,0:T(8,128)} %fusion.22, bf16[2048,2048]{0,1:T(8,128)(2,1)} %copy-done.58, bf16[256,2048]{1,0:T(8,128)(2,1)S(1)} %copy-done.81, bf16[256,2048]{1,0:T(8,128)(2,1)S(1)} %copy-done.82, bf16[256,2048]{1,0:T(8,128)(2,1)} %get-tuple-element.215, ...), kind=kOutput, calls=%fused_computation.21 | convolution fusion | flops 8633974784 | bytes 37748736 | tf_op jit(solution)/shard_map/dot_general | solution.py:23
  576.9 22.8 %fusion.50 = bf16[1024,2048]{1,0:T(8,128)(2,1)S(1)} fusion(bf16[2048,4096]{1,0:T(8,128)(2,1)} %constant_dynamic-update-slice_fusion.10, bf16[1024,2048]{1,0:T(8,128)(2,1)} %get-tuple-element.201, bf16[1024,2048]{1,0:T(8,128)(2,1)} %get-tuple-element.200), kind=kOutput, calls=%fused_computation.67 | convolution fusion | flops 17198743552 | bytes 29360128 | tf_op jit(solution)/shard_map/dot_general | solution.py:23
  602.8 24.3 %fusion.14 = f32[1024,4096]{1,0:T(8,128)} fusion(bf16[2048,4096]{1,0:T(8,128)(2,1)} %constant_dynamic-update-slice_fusion.10, bf16[256,2048]{1,0:T(8,128)(2,1)} %collective-permute-done.29, bf16[256,2048]{1,0:T(8,128)(2,1)} %collective-permute-done.28, bf16[256,2048]{1,0:T(8,128)(2,1)} %collective-permute-done.27, bf16[256,2048]{1,0:T(8,128)(2,1)} %get-tuple-element.260), kind=kOutput, calls=%fused_computation.28 | convolution fusion | flops 17196646400 | bytes 37748736 | tf_op jit(solution)/shard_map/dot_general | solution.py:23
  627.2 14.4 %fusion.49 = bf16[1024,2048]{1,0:T(8,128)(2,1)} fusion(bf16[2048,2048]{0,1:T(8,128)(2,1)S(1)} %bitcast.383, f32[1024,4096]{1,0:T(8,128)} %fusion.14), kind=kOutput, calls=%fused_computation.66 | convolution fusion | flops 8604614656 | bytes 29360128 | tf_op jit(solution)/shard_map/dot_general | solution.py:23
  641.6 21.4 %multiply_convert_fusion.3 = (bf16[1024,2048]{1,0:T(8,128)(2,1)}, bf16[1024,2048]{1,0:T(8,128)(2,1)}) fusion(f32[1024,4096]{1,0:T(8,128)} %fusion.14, bf16[2048,2048]{0,1:T(8,128)(2,1)} %copy-done.58, bf16[256,2048]{1,0:T(8,128)(2,1)S(1)} %copy-done.79, bf16[256,2048]{1,0:T(8,128)(2,1)S(1)} %copy-done.80, bf16[256,2048]{1,0:T(8,128)(2,1)} %get-tuple-element.221, ...), kind=kOutput, calls=%fused_computation.23 | convolution fusion | flops 8633974784 | bytes 37748736 | tf_op jit(solution)/shard_map/dot_general | solution.py:23
  663.0 23.1 %fusion.53 = bf16[1024,2048]{1,0:T(8,128)(2,1)S(1)} fusion(bf16[2048,4096]{1,0:T(8,128)(2,1)} %constant_dynamic-update-slice_fusion.10, bf16[1024,2048]{1,0:T(8,128)(2,1)} %get-tuple-element.203, bf16[1024,2048]{1,0:T(8,128)(2,1)} %get-tuple-element.202), kind=kOutput, calls=%fused_computation.68 | convolution fusion | flops 17198743552 | bytes 29360128 | tf_op jit(solution)/shard_map/dot_general | solution.py:23
  696.7 20.1 %collective-permute-done.84 = bf16[256,2048]{1,0:T(8,128)(2,1)S(1)} collective-permute-done((bf16[256,2048]{1,0:T(8,128)(2,1)S(1)}, bf16[256,2048]{1,0:T(8,128)(2,1)S(1)}, u32[]{:S(2)}, u32[]{:S(2)}) %collective-permute-start.84) | collective-permute-done | bytes 1048608 | tf_op jit(solution)/shard_map/ppermute | solution.py:74
  717.5 21.9 %collective-permute-done.67 = bf16[256,2048]{1,0:T(8,128)(2,1)S(1)} collective-permute-done((bf16[256,2048]{1,0:T(8,128)(2,1)S(1)}, bf16[256,2048]{1,0:T(8,128)(2,1)S(1)}, u32[]{:S(2)}, u32[]{:S(2)}) %collective-permute-start.67) | collective-permute-done | bytes 1048608 | tf_op jit(solution)/shard_map/ppermute | solution.py:74
  741.9 20.0 %collective-permute-done.64 = bf16[256,2048]{1,0:T(8,128)(2,1)} collective-permute-done((bf16[256,2048]{1,0:T(8,128)(2,1)S(1)}, bf16[256,2048]{1,0:T(8,128)(2,1)}, u32[]{:S(2)}, u32[]{:S(2)}) %collective-permute-start.64) | collective-permute-done | bytes 1048608 | tf_op jit(solution)/shard_map/ppermute | solution.py:74
  762.0 5.1 fusion.328
  767.7 16.7 %collective-permute-done.47 = bf16[256,2048]{1,0:T(8,128)(2,1)} collective-permute-done((bf16[256,2048]{1,0:T(8,128)(2,1)S(1)}, bf16[256,2048]{1,0:T(8,128)(2,1)}, u32[]{:S(2)}, u32[]{:S(2)}) %collective-permute-start.47) | collective-permute-done | bytes 1048608 | tf_op jit(solution)/shard_map/ppermute | solution.py:74
  784.4 4.8 fusion.327
  789.8 17.1 %collective-permute-done.87 = bf16[256,2048]{1,0:T(8,128)(2,1)} collective-permute-done((bf16[256,2048]{1,0:T(8,128)(2,1)}, bf16[256,2048]{1,0:T(8,128)(2,1)}, u32[]{:S(2)}, u32[]{:S(2)}) %collective-permute-start.87) | collective-permute-done | bytes 1048608 | tf_op jit(solution)/shard_map/ppermute | solution.py:74
  838.3 6.7 copy.203
  845.0 6.6 copy.201
  861.9 5.7 bitcast_add_fusion.d_ref
  867.7 14.1 %attention_backward.3 = (bf16[512,1024]{1,0:T(8,128)(2,1)S(1)}, f32[1088,256]{1,0:T(8,128)}, f32[8,2,160,128]{3,2,1,0:T(8,128)}, bf16[2,2,80,128]{3,2,1,0:T(8,128)(2,1)S(1)}, f32[2,256,256]{2,1,0:T(8,128)S(1)}) custom-call(s32[3,19]{1,0:T(4,128)S(1)} %copy-done.46, s32[8]{0:T(128)S(1)} %fusion.288.order, bf16[512,1024]{1,0:T(8,128)(2,1)S(1)} %copy-done.4, ...), custom_call_target="tpu_custom_call" | custom-call | tf_op jit(solution)/shard_map/attention_backward/pallas_call | solution.py:498
  892.3 5.4 bitcast_add_fusion.1.d_ref
  897.8 14.2 %attention_backward.2 = (bf16[512,1024]{1,0:T(8,128)(2,1)S(1)}, f32[1088,256]{1,0:T(8,128)}, f32[8,2,160,128]{3,2,1,0:T(8,128)}, bf16[2,2,80,128]{3,2,1,0:T(8,128)(2,1)S(1)}, f32[2,256,256]{2,1,0:T(8,128)S(1)}) custom-call(s32[3,19]{1,0:T(4,128)S(1)} %copy-done.44, s32[8]{0:T(128)S(1)} %fusion.288.order, bf16[512,1024]{1,0:T(8,128)(2,1)S(1)} %copy-done.2, ...), custom_call_target="tpu_custom_call" | custom-call | tf_op jit(solution)/shard_map/attention_backward/pallas_call | solution.py:498
  951.8 6.3 attention_keys.3
  964.0 4.2 collective-permute-done.79
  969.1 6.5 attention_keys.2
  982.8 4.1 fusion.227
  992.6 4.4 convolution_convert_fusion.14
  998.6 5.4 collective-permute-start.102
  1004.0 4.3 convolution_convert_fusion.12
  1014.9 3.7 fusion.60
  1021.8 3.8 add_convert_fusion
  1027.1 4.0 add_convert_fusion.2
  1043.7 8.3 collective-permute-done.98
  1052.0 21.4 %collective-permute-done.81 = bf16[256,2048]{1,0:T(8,128)(2,1)} collective-permute-done((bf16[256,2048]{1,0:T(8,128)(2,1)}, bf16[256,2048]{1,0:T(8,128)(2,1)}, u32[]{:S(2)}, u32[]{:S(2)}) %collective-permute-start.81) | collective-permute-done | bytes 1048608 | tf_op jit(solution)/shard_map/ppermute | solution.py:74
  1073.3 5.7 fusion.64
  1079.1 3.9 fusion.67
  (787 shorter events, 304.3 us)
Async XLA Ops:
  3.6 85.2 %collective-permute-start = (bf16[256,800]{1,0:T(8,128)(2,1)S(1)}, bf16[256,800]{1,0:T(8,128)(2,1)}, u32[]{:S(2)}, u32[]{:S(2)}) collective-permute-start(bf16[256,800]{1,0:T(8,128)(2,1)S(1)} %pad_maximum_fusion.11), channel_id=1, source_target_pairs={{0,8},{8,16},{16,24},{24,28},{28,20},{20,12},{12,4},{4,0},{1,9},{9... | collective-permute-start | bytes 1228808 | tf_op jit(solution)/shard_map/ppermute | solution.py:43
  6.7 84.1 %collective-permute-start.1 = (bf16[256,800]{1,0:T(8,128)(2,1)S(1)}, bf16[256,800]{1,0:T(8,128)(2,1)}, u32[]{:S(2)}, u32[]{:S(2)}) collective-permute-start(bf16[256,800]{1,0:T(8,128)(2,1)S(1)} %pad_maximum_fusion.11), channel_id=1, source_target_pairs={{0,4},{8,0},{16,8},{24,16},{28,24},{20,28},{12,20},{4,12},{1,5},{9... | collective-permute-start | bytes 1228808 | tf_op jit(solution)/shard_map/ppermute | solution.py:43
  133.5 52.4 %collective-permute-start.51 = (bf16[2,80,128]{2,1,0:T(8,128)(2,1)S(1)}, bf16[2,80,128]{2,1,0:T(8,128)(2,1)S(1)}, u32[]{:S(2)}, u32[]{:S(2)}) collective-permute-start(bf16[2,80,128]{2,1,0:T(8,128)(2,1)S(1)} %slice_bitcast_fusion.8), channel_id=1, source_target_pairs={{0,8},{4,12},{8,16},{12,20},{16,24},{20,28},{1,9},{5,13},{9,17},{1... | collective-permute-start | bytes 122888 | tf_op jit(solution)/shard_map/ppermute | solution.py:101
  137.0 50.3 %collective-permute-start.52 = (bf16[2,80,128]{2,1,0:T(8,128)(2,1)S(1)}, bf16[2,80,128]{2,1,0:T(8,128)(2,1)S(1)}, u32[]{:S(2)}, u32[]{:S(2)}) collective-permute-start(bf16[2,80,128]{2,1,0:T(8,128)(2,1)S(1)} %slice_bitcast_fusion.8), channel_id=1, source_target_pairs={{0,12},{4,16},{8,20},{12,24},{16,28},{1,13},{5,17},{9,21},{13,25},... | collective-permute-start | bytes 122888 | tf_op jit(solution)/shard_map/ppermute | solution.py:101
  140.5 49.5 %collective-permute-start.53 = (bf16[2,80,128]{2,1,0:T(8,128)(2,1)S(1)}, bf16[2,80,128]{2,1,0:T(8,128)(2,1)S(1)}, u32[]{:S(2)}, u32[]{:S(2)}) collective-permute-start(bf16[2,80,128]{2,1,0:T(8,128)(2,1)S(1)} %slice_bitcast_fusion.8), channel_id=1, source_target_pairs={{0,16},{4,20},{8,24},{12,28},{1,17},{5,21},{9,25},{13,29},{2,18},{... | collective-permute-start | bytes 122888 | tf_op jit(solution)/shard_map/ppermute | solution.py:101
  143.4 48.4 %collective-permute-start.54 = (bf16[2,80,128]{2,1,0:T(8,128)(2,1)S(1)}, bf16[2,80,128]{2,1,0:T(8,128)(2,1)S(1)}, u32[]{:S(2)}, u32[]{:S(2)}) collective-permute-start(bf16[2,80,128]{2,1,0:T(8,128)(2,1)S(1)} %slice_bitcast_fusion.8), channel_id=1, source_target_pairs={{0,20},{4,24},{8,28},{1,21},{5,25},{9,29},{2,22},{6,26},{10,30},{3... | collective-permute-start | bytes 122888 | tf_op jit(solution)/shard_map/ppermute | solution.py:101
  237.0 13.6 %collective-permute-start.57 = (bf16[256,2048]{1,0:T(8,128)(2,1)}, bf16[256,2048]{1,0:T(8,128)(2,1)S(1)}, u32[]{:S(2)}, u32[]{:S(2)}) collective-permute-start(bf16[256,2048]{1,0:T(8,128)(2,1)} %convolution_convert_fusion.2), channel_id=1, source_target_pairs={{0,1},{1,0},{2,3},{3,2},{4,5},{5,4},{6,7},{7,6},{8,9},{9,8},{10,11... | collective-permute-start | bytes 3145736 | tf_op jit(solution)/shard_map/ppermute | solution.py:74
  237.0 15.6 %collective-permute-start.59 = (bf16[256,2048]{1,0:T(8,128)(2,1)}, bf16[256,2048]{1,0:T(8,128)(2,1)S(1)}, u32[]{:S(2)}, u32[]{:S(2)}) collective-permute-start(bf16[256,2048]{1,0:T(8,128)(2,1)} %convolution_convert_fusion), channel_id=1, source_target_pairs={{0,1},{1,0},{2,3},{3,2},{4,5},{5,4},{6,7},{7,6},{8,9},{9,8},{10,11... | collective-permute-start | bytes 3145736 | tf_op jit(solution)/shard_map/ppermute | solution.py:74
  247.1 16.3 %collective-permute-start.24 = (bf16[256,2048]{1,0:T(8,128)(2,1)S(1)}, bf16[256,2048]{1,0:T(8,128)(2,1)S(1)}, u32[]{:S(2)}, u32[]{:S(2)}) collective-permute-start(bf16[256,2048]{1,0:T(8,128)(2,1)S(1)} %convolution_convert_fusion.6), channel_id=1, source_target_pairs={{0,1},{1,0},{2,3},{3,2},{4,5},{5,4},{6,7},{7,6},{8,9},{9,8},{10,11... | collective-permute-start | bytes 3145736 | tf_op jit(solution)/shard_map/ppermute | solution.py:74
  247.9 85.0 %collective-permute-start.30 = (bf16[256,4096]{1,0:T(8,128)(2,1)S(1)}, bf16[256,4096]{1,0:T(8,128)(2,1)S(1)}, u32[]{:S(2)}, u32[]{:S(2)}) collective-permute-start(bf16[256,4096]{1,0:T(8,128)(2,1)S(1)} %bitcast.384), channel_id=1, source_target_pairs={{0,8},{8,16},{16,24},{24,28},{28,20},{20,12},{12,4},{4,0},{1,9},{9... | collective-permute-start | bytes 6291464 | tf_op jit(solution)/shard_map/ppermute | solution.py:43
  250.5 87.4 %collective-permute-start.31 = (bf16[256,4096]{1,0:T(8,128)(2,1)S(1)}, bf16[256,4096]{1,0:T(8,128)(2,1)S(1)}, u32[]{:S(2)}, u32[]{:S(2)}) collective-permute-start(bf16[256,4096]{1,0:T(8,128)(2,1)S(1)} %bitcast.385), channel_id=1, source_target_pairs={{0,4},{8,0},{16,8},{24,16},{28,24},{20,28},{12,20},{4,12},{1,5},{9... | collective-permute-start | bytes 6291464 | tf_op jit(solution)/shard_map/ppermute | solution.py:43
  250.6 67.4 %collective-permute-start.38 = (bf16[256,2048]{0,1:T(8,128)(2,1)S(1)}, bf16[256,2048]{0,1:T(8,128)(2,1)}, u32[]{:S(2)}, u32[]{:S(2)}) collective-permute-start(bf16[256,2048]{0,1:T(8,128)(2,1)S(1)} %bitcast.388), channel_id=1, source_target_pairs={{0,8},{8,16},{16,24},{24,28},{28,20},{20,12},{12,4},{4,0},{1,9},{9... | collective-permute-start | bytes 3145736 | tf_op jit(solution)/shard_map/ppermute | solution.py:43
  252.6 67.8 %collective-permute-start.39 = (bf16[256,2048]{0,1:T(8,128)(2,1)S(1)}, bf16[256,2048]{0,1:T(8,128)(2,1)}, u32[]{:S(2)}, u32[]{:S(2)}) collective-permute-start(bf16[256,2048]{0,1:T(8,128)(2,1)S(1)} %bitcast.389), channel_id=1, source_target_pairs={{0,4},{8,0},{16,8},{24,16},{28,24},{20,28},{12,20},{4,12},{1,5},{9... | collective-permute-start | bytes 3145736 | tf_op jit(solution)/shard_map/ppermute | solution.py:43
  263.4 68.5 %collective-permute-start.58 = (bf16[256,2048]{1,0:T(8,128)(2,1)S(1)}, bf16[256,2048]{1,0:T(8,128)(2,1)S(1)}, u32[]{:S(2)}, u32[]{:S(2)}) collective-permute-start(bf16[256,2048]{1,0:T(8,128)(2,1)S(1)} %add_convert_fusion.6), channel_id=1, source_target_pairs={{0,2},{1,3},{2,0},{3,1},{4,6},{5,7},{6,4},{7,5},{8,10},{9,11},{10,... | collective-permute-start | bytes 3145736 | tf_op jit(solution)/shard_map/ppermute | solution.py:74
  318.0 18.2 %collective-permute-start.26 = (bf16[256,2048]{1,0:T(8,128)(2,1)}, bf16[256,2048]{1,0:T(8,128)(2,1)S(1)}, u32[]{:S(2)}, u32[]{:S(2)}) collective-permute-start(bf16[256,2048]{1,0:T(8,128)(2,1)} %convolution_convert_fusion.4), channel_id=1, source_target_pairs={{0,1},{1,0},{2,3},{3,2},{4,5},{5,4},{6,7},{7,6},{8,9},{9,8},{10,11... | collective-permute-start | bytes 3145736 | tf_op jit(solution)/shard_map/ppermute | solution.py:74
  320.4 23.9 %collective-permute-start.25 = (bf16[256,2048]{1,0:T(8,128)(2,1)S(1)}, bf16[256,2048]{1,0:T(8,128)(2,1)S(1)}, u32[]{:S(2)}, u32[]{:S(2)}) collective-permute-start(bf16[256,2048]{1,0:T(8,128)(2,1)S(1)} %add_convert_fusion.9), channel_id=1, source_target_pairs={{0,2},{1,3},{2,0},{3,1},{4,6},{5,7},{6,4},{7,5},{8,10},{9,11},{10,... | collective-permute-start | bytes 3145736 | tf_op jit(solution)/shard_map/ppermute | solution.py:74
  331.9 26.3 %collective-permute-start.40 = (bf16[256,2048]{0,1:T(8,128)(2,1)}, bf16[256,2048]{0,1:T(8,128)(2,1)S(1)}, u32[]{:S(2)}, u32[]{:S(2)}) collective-permute-start(bf16[256,2048]{0,1:T(8,128)(2,1)} %collective-permute-done.38), channel_id=1, source_target_pairs={{0,8},{8,16},{16,24},{24,28},{28,20},{20,12},{12,4},{4,0},{1,9},{9... | collective-permute-start | bytes 3145736 | tf_op jit(solution)/shard_map/ppermute | solution.py:43
  332.9 70.3 %collective-permute-start.32 = (bf16[256,4096]{1,0:T(8,128)(2,1)S(1)}, bf16[256,4096]{1,0:T(8,128)(2,1)S(1)}, u32[]{:S(2)}, u32[]{:S(2)}) collective-permute-start(bf16[256,4096]{1,0:T(8,128)(2,1)S(1)} %collective-permute-done.30), channel_id=1, source_target_pairs={{0,8},{8,16},{16,24},{24,28},{28,20},{20,12},{12,4},{4,0},{1,9},{9... | collective-permute-start | bytes 6291464 | tf_op jit(solution)/shard_map/ppermute | solution.py:43
  336.3 26.4 %collective-permute-start.41 = (bf16[256,2048]{0,1:T(8,128)(2,1)}, bf16[256,2048]{0,1:T(8,128)(2,1)S(1)}, u32[]{:S(2)}, u32[]{:S(2)}) collective-permute-start(bf16[256,2048]{0,1:T(8,128)(2,1)} %collective-permute-done.39), channel_id=1, source_target_pairs={{0,4},{8,0},{16,8},{24,16},{28,24},{20,28},{12,20},{4,12},{1,5},{9... | collective-permute-start | bytes 3145736 | tf_op jit(solution)/shard_map/ppermute | solution.py:43
  338.0 88.1 %collective-permute-start.33 = (bf16[256,4096]{1,0:T(8,128)(2,1)S(1)}, bf16[256,4096]{1,0:T(8,128)(2,1)S(1)}, u32[]{:S(2)}, u32[]{:S(2)}) collective-permute-start(bf16[256,4096]{1,0:T(8,128)(2,1)S(1)} %collective-permute-done.31), channel_id=1, source_target_pairs={{0,4},{8,0},{16,8},{24,16},{28,24},{20,28},{12,20},{4,12},{1,5},{9... | collective-permute-start | bytes 6291464 | tf_op jit(solution)/shard_map/ppermute | solution.py:43
  351.3 128.2 %collective-permute-start.61 = (bf16[256,2048]{1,0:T(8,128)(2,1)S(1)}, bf16[256,2048]{1,0:T(8,128)(2,1)S(1)}, u32[]{:S(2)}, u32[]{:S(2)}) collective-permute-start(bf16[256,2048]{1,0:T(8,128)(2,1)S(1)} %get-tuple-element.261), channel_id=1, source_target_pairs={{0,2},{1,3},{2,0},{3,1},{4,6},{5,7},{6,4},{7,5},{8,10},{9,11},{10,... | collective-permute-start | bytes 3145736 | tf_op jit(solution)/shard_map/ppermute | solution.py:74
  358.2 67.4 %collective-permute-start.42 = (bf16[256,2048]{0,1:T(8,128)(2,1)S(1)}, bf16[256,2048]{0,1:T(8,128)(2,1)S(1)}, u32[]{:S(2)}, u32[]{:S(2)}) collective-permute-start(bf16[256,2048]{0,1:T(8,128)(2,1)S(1)} %collective-permute-done.40), channel_id=1, source_target_pairs={{0,8},{8,16},{16,24},{24,28},{28,20},{20,12},{12,4},{4,0},{1,9},{9... | collective-permute-start | bytes 3145736 | tf_op jit(solution)/shard_map/ppermute | solution.py:43
  362.6 67.4 %collective-permute-start.43 = (bf16[256,2048]{0,1:T(8,128)(2,1)S(1)}, bf16[256,2048]{0,1:T(8,128)(2,1)S(1)}, u32[]{:S(2)}, u32[]{:S(2)}) collective-permute-start(bf16[256,2048]{0,1:T(8,128)(2,1)S(1)} %collective-permute-done.41), channel_id=1, source_target_pairs={{0,4},{8,0},{16,8},{24,16},{28,24},{20,28},{12,20},{4,12},{1,5},{9... | collective-permute-start | bytes 3145736 | tf_op jit(solution)/shard_map/ppermute | solution.py:43
  403.1 83.1 %collective-permute-start.34 = (bf16[256,4096]{1,0:T(8,128)(2,1)S(1)}, bf16[256,4096]{1,0:T(8,128)(2,1)S(1)}, u32[]{:S(2)}, u32[]{:S(2)}) collective-permute-start(bf16[256,4096]{1,0:T(8,128)(2,1)S(1)} %collective-permute-done.32), channel_id=1, source_target_pairs={{0,8},{8,16},{16,24},{24,28},{28,20},{20,12},{12,4},{4,0},{1,9},{9... | collective-permute-start | bytes 6291464 | tf_op jit(solution)/shard_map/ppermute | solution.py:43
  425.7 53.7 %collective-permute-start.44 = (bf16[128,2048]{0,1:T(8,128)(2,1)S(1)}, bf16[128,2048]{0,1:T(8,128)(2,1)S(1)}, u32[]{:S(2)}, u32[]{:S(2)}) collective-permute-start(bf16[128,2048]{0,1:T(8,128)(2,1)S(1)} %slice.1023), channel_id=1, source_target_pairs={{0,8},{8,16},{16,24},{24,28},{28,20},{20,12},{12,4},{4,0},{1,9},{9... | collective-permute-start | bytes 1572872 | tf_op jit(solution)/shard_map/ppermute | solution.py:43
  426.1 62.9 %collective-permute-start.35 = (bf16[256,4096]{1,0:T(8,128)(2,1)S(1)}, bf16[256,4096]{1,0:T(8,128)(2,1)S(1)}, u32[]{:S(2)}, u32[]{:S(2)}) collective-permute-start(bf16[256,4096]{1,0:T(8,128)(2,1)S(1)} %collective-permute-done.33), channel_id=1, source_target_pairs={{0,4},{8,0},{16,8},{24,16},{28,24},{20,28},{12,20},{4,12},{1,5},{9... | collective-permute-start | bytes 6291464 | tf_op jit(solution)/shard_map/ppermute | solution.py:43
  430.1 54.4 %collective-permute-start.45 = (bf16[128,2048]{0,1:T(8,128)(2,1)S(1)}, bf16[128,2048]{0,1:T(8,128)(2,1)S(1)}, u32[]{:S(2)}, u32[]{:S(2)}) collective-permute-start(bf16[128,2048]{0,1:T(8,128)(2,1)S(1)} %slice.1024), channel_id=1, source_target_pairs={{0,4},{8,0},{16,8},{24,16},{28,24},{20,28},{12,20},{4,12},{1,5},{9... | collective-permute-start | bytes 1572872 | tf_op jit(solution)/shard_map/ppermute | solution.py:43
  479.3 36.2 %collective-permute-start.60 = (bf16[256,2048]{1,0:T(8,128)(2,1)S(1)}, bf16[256,2048]{1,0:T(8,128)(2,1)S(1)}, u32[]{:S(2)}, u32[]{:S(2)}) collective-permute-start(bf16[256,2048]{1,0:T(8,128)(2,1)S(1)} %get-tuple-element.261), channel_id=1, source_target_pairs={{0,1},{1,0},{2,3},{3,2},{4,5},{5,4},{6,7},{7,6},{8,9},{9,8},{10,11... | collective-permute-start | bytes 3145736 | tf_op jit(solution)/shard_map/ppermute | solution.py:74
  479.5 26.0 %collective-permute-start.28 = (bf16[256,2048]{1,0:T(8,128)(2,1)}, bf16[256,2048]{1,0:T(8,128)(2,1)}, u32[]{:S(2)}, u32[]{:S(2)}) collective-permute-start(bf16[256,2048]{1,0:T(8,128)(2,1)} %get-tuple-element.260), channel_id=1, source_target_pairs={{0,2},{1,3},{2,0},{3,1},{4,6},{5,7},{6,4},{7,5},{8,10},{9,11},{10,... | collective-permute-start | bytes 3145736 | tf_op jit(solution)/shard_map/ppermute | solution.py:74
  484.5 31.0 %collective-permute-start.62 = (bf16[256,2048]{1,0:T(8,128)(2,1)S(1)}, bf16[256,2048]{1,0:T(8,128)(2,1)S(1)}, u32[]{:S(2)}, u32[]{:S(2)}) collective-permute-start(bf16[256,2048]{1,0:T(8,128)(2,1)S(1)} %collective-permute-done.61), channel_id=1, source_target_pairs={{0,1},{1,0},{2,3},{3,2},{4,5},{5,4},{6,7},{7,6},{8,9},{9,8},{10,11... | collective-permute-start | bytes 3145736 | tf_op jit(solution)/shard_map/ppermute | solution.py:74
  486.3 25.6 %collective-permute-start.36 = (bf16[128,4096]{1,0:T(8,128)(2,1)S(1)}, bf16[128,4096]{1,0:T(8,128)(2,1)S(1)}, u32[]{:S(2)}, u32[]{:S(2)}) collective-permute-start(bf16[128,4096]{1,0:T(8,128)(2,1)S(1)} %slice.1019), channel_id=1, source_target_pairs={{0,8},{8,16},{16,24},{24,28},{28,20},{20,12},{12,4},{4,0},{1,9},{9... | collective-permute-start | bytes 3145736 | tf_op jit(solution)/shard_map/ppermute | solution.py:43
  489.1 25.3 %collective-permute-start.37 = (bf16[128,4096]{1,0:T(8,128)(2,1)S(1)}, bf16[128,4096]{1,0:T(8,128)(2,1)S(1)}, u32[]{:S(2)}, u32[]{:S(2)}) collective-permute-start(bf16[128,4096]{1,0:T(8,128)(2,1)S(1)} %slice.1020), channel_id=1, source_target_pairs={{0,4},{8,0},{16,8},{24,16},{28,24},{20,28},{12,20},{4,12},{1,5},{9... | collective-permute-start | bytes 3145736 | tf_op jit(solution)/shard_map/ppermute | solution.py:43
  505.5 97.4 %collective-permute-start.27 = (bf16[256,2048]{1,0:T(8,128)(2,1)}, bf16[256,2048]{1,0:T(8,128)(2,1)}, u32[]{:S(2)}, u32[]{:S(2)}) collective-permute-start(bf16[256,2048]{1,0:T(8,128)(2,1)} %get-tuple-element.260), channel_id=1, source_target_pairs={{0,1},{1,0},{2,3},{3,2},{4,5},{5,4},{6,7},{7,6},{8,9},{9,8},{10,11... | collective-permute-start | bytes 3145736 | tf_op jit(solution)/shard_map/ppermute | solution.py:74
  511.9 90.9 %collective-permute-start.29 = (bf16[256,2048]{1,0:T(8,128)(2,1)}, bf16[256,2048]{1,0:T(8,128)(2,1)}, u32[]{:S(2)}, u32[]{:S(2)}) collective-permute-start(bf16[256,2048]{1,0:T(8,128)(2,1)} %collective-permute-done.28), channel_id=1, source_target_pairs={{0,1},{1,0},{2,3},{3,2},{4,5},{5,4},{6,7},{7,6},{8,9},{9,8},{10,11... | collective-permute-start | bytes 3145736 | tf_op jit(solution)/shard_map/ppermute | solution.py:74
  554.2 137.6 %collective-permute-start.63 = (bf16[256,2048]{1,0:T(8,128)(2,1)}, bf16[256,2048]{1,0:T(8,128)(2,1)}, u32[]{:S(2)}, u32[]{:S(2)}) collective-permute-start(bf16[256,2048]{1,0:T(8,128)(2,1)} %get-tuple-element.224), channel_id=1, source_target_pairs={{0,1},{1,0},{2,3},{3,2},{4,5},{5,4},{6,7},{7,6},{8,9},{9,8},{10,11... | collective-permute-start | bytes 3145736 | tf_op jit(solution)/shard_map/ppermute | solution.py:74
  602.3 85.8 %collective-permute-start.83 = (bf16[256,2048]{1,0:T(8,128)(2,1)}, bf16[256,2048]{1,0:T(8,128)(2,1)}, u32[]{:S(2)}, u32[]{:S(2)}) collective-permute-start(bf16[256,2048]{1,0:T(8,128)(2,1)} %get-tuple-element.210), channel_id=1, source_target_pairs={{0,1},{1,0},{2,3},{3,2},{4,5},{5,4},{6,7},{7,6},{8,9},{9,8},{10,11... | collective-permute-start | bytes 3145736 | tf_op jit(solution)/shard_map/ppermute | solution.py:74
  602.3 92.6 %collective-permute-start.85 = (bf16[256,2048]{1,0:T(8,128)(2,1)}, bf16[256,2048]{1,0:T(8,128)(2,1)}, u32[]{:S(2)}, u32[]{:S(2)}) collective-permute-start(bf16[256,2048]{1,0:T(8,128)(2,1)} %get-tuple-element.211), channel_id=1, source_target_pairs={{0,1},{1,0},{2,3},{3,2},{4,5},{5,4},{6,7},{7,6},{8,9},{9,8},{10,11... | collective-permute-start | bytes 3145736 | tf_op jit(solution)/shard_map/ppermute | solution.py:74
  690.7 26.1 %collective-permute-start.84 = (bf16[256,2048]{1,0:T(8,128)(2,1)S(1)}, bf16[256,2048]{1,0:T(8,128)(2,1)S(1)}, u32[]{:S(2)}, u32[]{:S(2)}) collective-permute-start(bf16[256,2048]{1,0:T(8,128)(2,1)S(1)} %add_convert_fusion.1), channel_id=1, source_target_pairs={{0,2},{1,3},{2,0},{3,1},{4,6},{5,7},{6,4},{7,5},{8,10},{9,11},{10,... | collective-permute-start | bytes 3145736 | tf_op jit(solution)/shard_map/ppermute | solution.py:74
  691.8 47.5 %collective-permute-start.67 = (bf16[256,2048]{1,0:T(8,128)(2,1)S(1)}, bf16[256,2048]{1,0:T(8,128)(2,1)S(1)}, u32[]{:S(2)}, u32[]{:S(2)}) collective-permute-start(bf16[256,2048]{1,0:T(8,128)(2,1)S(1)} %add_convert_fusion.3), channel_id=1, source_target_pairs={{0,2},{1,3},{2,0},{3,1},{4,6},{5,7},{6,4},{7,5},{8,10},{9,11},{10,... | collective-permute-start | bytes 3145736 | tf_op jit(solution)/shard_map/ppermute | solution.py:74
  695.0 46.9 %collective-permute-start.65 = (bf16[256,2048]{1,0:T(8,128)(2,1)S(1)}, bf16[256,2048]{1,0:T(8,128)(2,1)}, u32[]{:S(2)}, u32[]{:S(2)}) collective-permute-start(bf16[256,2048]{1,0:T(8,128)(2,1)S(1)} %copy-done.84), channel_id=1, source_target_pairs={{0,1},{1,0},{2,3},{3,2},{4,5},{5,4},{6,7},{7,6},{8,9},{9,8},{10,11... | collective-permute-start | bytes 3145736 | tf_op jit(solution)/shard_map/ppermute | solution.py:74
  695.1 66.9 %collective-permute-start.64 = (bf16[256,2048]{1,0:T(8,128)(2,1)S(1)}, bf16[256,2048]{1,0:T(8,128)(2,1)}, u32[]{:S(2)}, u32[]{:S(2)}) collective-permute-start(bf16[256,2048]{1,0:T(8,128)(2,1)S(1)} %add_convert_fusion.5), channel_id=1, source_target_pairs={{0,2},{1,3},{2,0},{3,1},{4,6},{5,7},{6,4},{7,5},{8,10},{9,11},{10,... | collective-permute-start | bytes 3145736 | tf_op jit(solution)/shard_map/ppermute | solution.py:74
  696.5 71.2 %collective-permute-start.48 = (bf16[256,2048]{1,0:T(8,128)(2,1)}, bf16[256,2048]{1,0:T(8,128)(2,1)}, u32[]{:S(2)}, u32[]{:S(2)}) collective-permute-start(bf16[256,2048]{1,0:T(8,128)(2,1)} %get-tuple-element.223), channel_id=1, source_target_pairs={{0,1},{1,0},{2,3},{3,2},{4,5},{5,4},{6,7},{7,6},{8,9},{9,8},{10,11... | collective-permute-start | bytes 3145736 | tf_op jit(solution)/shard_map/ppermute | solution.py:74
  716.9 67.5 %collective-permute-start.47 = (bf16[256,2048]{1,0:T(8,128)(2,1)S(1)}, bf16[256,2048]{1,0:T(8,128)(2,1)}, u32[]{:S(2)}, u32[]{:S(2)}) collective-permute-start(bf16[256,2048]{1,0:T(8,128)(2,1)S(1)} %add_convert_fusion.8), channel_id=1, source_target_pairs={{0,2},{1,3},{2,0},{3,1},{4,6},{5,7},{6,4},{7,5},{8,10},{9,11},{10,... | collective-permute-start | bytes 3145736 | tf_op jit(solution)/shard_map/ppermute | solution.py:74
  767.1 39.8 %collective-permute-start.87 = (bf16[256,2048]{1,0:T(8,128)(2,1)}, bf16[256,2048]{1,0:T(8,128)(2,1)}, u32[]{:S(2)}, u32[]{:S(2)}) collective-permute-start(bf16[256,2048]{1,0:T(8,128)(2,1)} %get-tuple-element.198), channel_id=1, source_target_pairs={{0,2},{1,3},{2,0},{3,1},{4,6},{5,7},{6,4},{7,5},{8,10},{9,11},{10,... | collective-permute-start | bytes 3145736 | tf_op jit(solution)/shard_map/ppermute | solution.py:74
  767.7 90.4 %collective-permute-start.86 = (bf16[256,2048]{1,0:T(8,128)(2,1)}, bf16[256,2048]{1,0:T(8,128)(2,1)}, u32[]{:S(2)}, u32[]{:S(2)}) collective-permute-start(bf16[256,2048]{1,0:T(8,128)(2,1)} %get-tuple-element.198), channel_id=1, source_target_pairs={{0,1},{1,0},{2,3},{3,2},{4,5},{5,4},{6,7},{7,6},{8,9},{9,8},{10,11... | collective-permute-start | bytes 3145736 | tf_op jit(solution)/shard_map/ppermute | solution.py:74
  789.2 68.9 %collective-permute-start.70 = (bf16[256,2048]{1,0:T(8,128)(2,1)}, bf16[256,2048]{1,0:T(8,128)(2,1)}, u32[]{:S(2)}, u32[]{:S(2)}) collective-permute-start(bf16[256,2048]{1,0:T(8,128)(2,1)} %get-tuple-element.196), channel_id=1, source_target_pairs={{0,2},{1,3},{2,0},{3,1},{4,6},{5,7},{6,4},{7,5},{8,10},{9,11},{10,... | collective-permute-start | bytes 3145736 | tf_op jit(solution)/shard_map/ppermute | solution.py:74
  806.9 51.3 %collective-permute-start.88 = (bf16[256,2048]{1,0:T(8,128)(2,1)}, bf16[256,2048]{1,0:T(8,128)(2,1)}, u32[]{:S(2)}, u32[]{:S(2)}) collective-permute-start(bf16[256,2048]{1,0:T(8,128)(2,1)} %collective-permute-done.87), channel_id=1, source_target_pairs={{0,1},{1,0},{2,3},{3,2},{4,5},{5,4},{6,7},{7,6},{8,9},{9,8},{10,11... | collective-permute-start | bytes 3145736 | tf_op jit(solution)/shard_map/ppermute | solution.py:74
  856.1 30.3 %collective-permute-start.69 = (bf16[256,2048]{1,0:T(8,128)(2,1)}, bf16[256,2048]{1,0:T(8,128)(2,1)S(1)}, u32[]{:S(2)}, u32[]{:S(2)}) collective-permute-start(bf16[256,2048]{1,0:T(8,128)(2,1)} %get-tuple-element.196), channel_id=1, source_target_pairs={{0,1},{1,0},{2,3},{3,2},{4,5},{5,4},{6,7},{7,6},{8,9},{9,8},{10,11... | collective-permute-start | bytes 3145736 | tf_op jit(solution)/shard_map/ppermute | solution.py:74
  858.1 29.6 %collective-permute-start.71 = (bf16[256,2048]{1,0:T(8,128)(2,1)}, bf16[256,2048]{1,0:T(8,128)(2,1)S(1)}, u32[]{:S(2)}, u32[]{:S(2)}) collective-permute-start(bf16[256,2048]{1,0:T(8,128)(2,1)} %collective-permute-done.70), channel_id=1, source_target_pairs={{0,1},{1,0},{2,3},{3,2},{4,5},{5,4},{6,7},{7,6},{8,9},{9,8},{10,11... | collective-permute-start | bytes 3145736 | tf_op jit(solution)/shard_map/ppermute | solution.py:74
  882.5 45.0 %collective-permute-start.91 = (bf16[2,80,128]{2,1,0:T(8,128)(2,1)}, bf16[2,80,128]{2,1,0:T(8,128)(2,1)S(1)}, u32[]{:S(2)}, u32[]{:S(2)}) collective-permute-start(bf16[2,80,128]{2,1,0:T(8,128)(2,1)} %slice_bitcast_fusion.2), channel_id=1, source_target_pairs={{8,0},{12,4},{16,8},{20,12},{24,16},{28,20},{9,1},{13,5},{17,9},{2... | collective-permute-start | bytes 122888 | tf_op jit(solution)/shard_map/ppermute | solution.py:101
  883.8 45.0 %collective-permute-start.92 = (bf16[2,80,128]{2,1,0:T(8,128)(2,1)}, bf16[2,80,128]{2,1,0:T(8,128)(2,1)S(1)}, u32[]{:S(2)}, u32[]{:S(2)}) collective-permute-start(bf16[2,80,128]{2,1,0:T(8,128)(2,1)} %slice_bitcast_fusion.2), channel_id=1, source_target_pairs={{12,0},{16,4},{20,8},{24,12},{28,16},{13,1},{17,5},{21,9},{25,13},... | collective-permute-start | bytes 122888 | tf_op jit(solution)/shard_map/ppermute | solution.py:101
  885.1 49.5 %collective-permute-start.93 = (bf16[2,80,128]{2,1,0:T(8,128)(2,1)}, bf16[2,80,128]{2,1,0:T(8,128)(2,1)}, u32[]{:S(2)}, u32[]{:S(2)}) collective-permute-start(bf16[2,80,128]{2,1,0:T(8,128)(2,1)} %slice_bitcast_fusion.2), channel_id=1, source_target_pairs={{16,0},{20,4},{24,8},{28,12},{17,1},{21,5},{25,9},{29,13},{18,2},{... | collective-permute-start | bytes 122888 | tf_op jit(solution)/shard_map/ppermute | solution.py:101
  886.4 49.5 %collective-permute-start.94 = (bf16[2,80,128]{2,1,0:T(8,128)(2,1)}, bf16[2,80,128]{2,1,0:T(8,128)(2,1)}, u32[]{:S(2)}, u32[]{:S(2)}) collective-permute-start(bf16[2,80,128]{2,1,0:T(8,128)(2,1)} %slice_bitcast_fusion.2), channel_id=1, source_target_pairs={{20,0},{24,4},{28,8},{21,1},{25,5},{29,9},{22,2},{26,6},{30,10},{2... | collective-permute-start | bytes 122888 | tf_op jit(solution)/shard_map/ppermute | solution.py:101
  887.7 49.5 %collective-permute-start.95 = (bf16[2,80,128]{2,1,0:T(8,128)(2,1)}, bf16[2,80,128]{2,1,0:T(8,128)(2,1)}, u32[]{:S(2)}, u32[]{:S(2)}) collective-permute-start(bf16[2,80,128]{2,1,0:T(8,128)(2,1)} %slice_bitcast_fusion.2), channel_id=1, source_target_pairs={{24,0},{28,4},{25,1},{29,5},{26,2},{30,6},{27,3},{31,7}} | collective-permute-start | bytes 122888 | tf_op jit(solution)/shard_map/ppermute | solution.py:101
  927.5 12.2 %collective-permute-start.96 = (bf16[2,80,128]{2,1,0:T(8,128)(2,1)}, bf16[2,80,128]{2,1,0:T(8,128)(2,1)S(1)}, u32[]{:S(2)}, u32[]{:S(2)}) collective-permute-start(bf16[2,80,128]{2,1,0:T(8,128)(2,1)} %slice_bitcast_fusion.2), channel_id=1, source_target_pairs={{28,0},{29,1},{30,2},{31,3}} | collective-permute-start | bytes 122888 | tf_op jit(solution)/shard_map/ppermute | solution.py:101
  934.6 23.5 %collective-permute-start.74 = (bf16[2,80,128]{2,1,0:T(8,128)(2,1)}, bf16[2,80,128]{2,1,0:T(8,128)(2,1)S(1)}, u32[]{:S(2)}, u32[]{:S(2)}) collective-permute-start(bf16[2,80,128]{2,1,0:T(8,128)(2,1)} %slice_bitcast_fusion.5), channel_id=1, source_target_pairs={{8,0},{12,4},{16,8},{20,12},{24,16},{28,20},{9,1},{13,5},{17,9},{2... | collective-permute-start | bytes 122888 | tf_op jit(solution)/shard_map/ppermute | solution.py:101
  935.9 23.5 %collective-permute-start.75 = (bf16[2,80,128]{2,1,0:T(8,128)(2,1)}, bf16[2,80,128]{2,1,0:T(8,128)(2,1)S(1)}, u32[]{:S(2)}, u32[]{:S(2)}) collective-permute-start(bf16[2,80,128]{2,1,0:T(8,128)(2,1)} %slice_bitcast_fusion.5), channel_id=1, source_target_pairs={{12,0},{16,4},{20,8},{24,12},{28,16},{13,1},{17,5},{21,9},{25,13},... | collective-permute-start | bytes 122888 | tf_op jit(solution)/shard_map/ppermute | solution.py:101
  937.2 25.3 %collective-permute-start.76 = (bf16[2,80,128]{2,1,0:T(8,128)(2,1)}, bf16[2,80,128]{2,1,0:T(8,128)(2,1)S(1)}, u32[]{:S(2)}, u32[]{:S(2)}) collective-permute-start(bf16[2,80,128]{2,1,0:T(8,128)(2,1)} %slice_bitcast_fusion.5), channel_id=1, source_target_pairs={{16,0},{20,4},{24,8},{28,12},{17,1},{21,5},{25,9},{29,13},{18,2},{... | collective-permute-start | bytes 122888 | tf_op jit(solution)/shard_map/ppermute | solution.py:101
  939.7 24.2 %collective-permute-start.77 = (bf16[2,80,128]{2,1,0:T(8,128)(2,1)}, bf16[2,80,128]{2,1,0:T(8,128)(2,1)S(1)}, u32[]{:S(2)}, u32[]{:S(2)}) collective-permute-start(bf16[2,80,128]{2,1,0:T(8,128)(2,1)} %slice_bitcast_fusion.5), channel_id=1, source_target_pairs={{20,0},{24,4},{28,8},{21,1},{25,5},{29,9},{22,2},{26,6},{30,10},{2... | collective-permute-start | bytes 122888 | tf_op jit(solution)/shard_map/ppermute | solution.py:101
  946.8 17.1 %collective-permute-start.78 = (bf16[2,80,128]{2,1,0:T(8,128)(2,1)}, bf16[2,80,128]{2,1,0:T(8,128)(2,1)S(1)}, u32[]{:S(2)}, u32[]{:S(2)}) collective-permute-start(bf16[2,80,128]{2,1,0:T(8,128)(2,1)} %slice_bitcast_fusion.5), channel_id=1, source_target_pairs={{24,0},{28,4},{25,1},{29,5},{26,2},{30,6},{27,3},{31,7}} | collective-permute-start | bytes 122888 | tf_op jit(solution)/shard_map/ppermute | solution.py:101
  1018.6 25.1 %collective-permute-start.99 = (bf16[256,2048]{1,0:T(8,128)(2,1)}, bf16[256,2048]{1,0:T(8,128)(2,1)}, u32[]{:S(2)}, u32[]{:S(2)}) collective-permute-start(bf16[256,2048]{1,0:T(8,128)(2,1)} %convolution_convert_fusion.8), channel_id=1, source_target_pairs={{0,1},{1,0},{2,3},{3,2},{4,5},{5,4},{6,7},{7,6},{8,9},{9,8},{10,11... | collective-permute-start | bytes 3145736 | tf_op jit(solution)/shard_map/ppermute | solution.py:74
  1019.1 24.6 %collective-permute-start.82 = (bf16[256,2048]{1,0:T(8,128)(2,1)}, bf16[256,2048]{1,0:T(8,128)(2,1)}, u32[]{:S(2)}, u32[]{:S(2)}) collective-permute-start(bf16[256,2048]{1,0:T(8,128)(2,1)} %convolution_convert_fusion.12), channel_id=1, source_target_pairs={{0,1},{1,0},{2,3},{3,2},{4,5},{5,4},{6,7},{7,6},{8,9},{9,8},{10,11... | collective-permute-start | bytes 3145736 | tf_op jit(solution)/shard_map/ppermute | solution.py:74
  1025.6 26.4 %collective-permute-start.98 = (bf16[256,2048]{1,0:T(8,128)(2,1)}, bf16[256,2048]{1,0:T(8,128)(2,1)}, u32[]{:S(2)}, u32[]{:S(2)}) collective-permute-start(bf16[256,2048]{1,0:T(8,128)(2,1)} %add_convert_fusion), channel_id=1, source_target_pairs={{0,2},{1,3},{2,0},{3,1},{4,6},{5,7},{6,4},{7,5},{8,10},{9,11},{10,... | collective-permute-start | bytes 3145736 | tf_op jit(solution)/shard_map/ppermute | solution.py:74
  1031.1 42.3 %collective-permute-start.81 = (bf16[256,2048]{1,0:T(8,128)(2,1)}, bf16[256,2048]{1,0:T(8,128)(2,1)}, u32[]{:S(2)}, u32[]{:S(2)}) collective-permute-start(bf16[256,2048]{1,0:T(8,128)(2,1)} %add_convert_fusion.2), channel_id=1, source_target_pairs={{0,2},{1,3},{2,0},{3,1},{4,6},{5,7},{6,4},{7,5},{8,10},{9,11},{10,... | collective-permute-start | bytes 3145736 | tf_op jit(solution)/shard_map/ppermute | solution.py:74
  (199 other events, 3643.9 us)

commit v2 on v1

v2 whole, which is shorter than its diff:
```python
import functools
import math

import jax
import jax.numpy as jnp
from jax import lax
from jax.experimental import pallas as pl
from jax.experimental.pallas import tpu as pltpu
from jax.sharding import PartitionSpec as P

STRETCH = 64
PAIR = 2 * STRETCH
WIN = 3 * STRETCH
EXT = 80
EPS = 1e-05
ADAPTER_SCALE = 2.0
BF = jnp.bfloat16
F32 = jnp.float32
VMEM_LIMIT = 58 * 1024 * 1024
CHUNK = 256
ROW_TILE = 512


def dotg(left, right, lc, rc):
    return lax.dot_general(left, right, (((lc,), (rc,)), ((), ())), preferred_element_type=F32)


def ring_order(count):
    if count % 8:
        return list(range(count))
    deep, wide = 4, count // 4
    path = [z * wide for z in range(deep)]
    for step, z in enumerate(reversed(range(deep))):
        ys = list(range(1, wide))
        path += [z * wide + y for y in (ys if step % 2 == 0 else ys[::-1])]
    return path


def ring_offsets(count):
    out = [0]
    for distance in range(1, (count + 1) // 2):
        out += [-distance, distance]
    return out + [count // 2]


def ring_sources(count):
    order = ring_order(count)
    return [[order[(order.index(s) + o) % count] for o in ring_offsets(count)] for s in range(count)]


def ring_cut(rows):
    return (rows // 2 + 15) // 16 * 16


def ring_layout(count, rows):
    cut = ring_cut(rows)
    return [(q, 0, rows) for q in range(count - 1)] + [
        (count - 1, 0, cut), (count - 1, cut, rows - cut),
    ]


def pieces_of(width):
    quarter = width // 4
    return [(0, quarter), (quarter, quarter), (2 * quarter, 2 * quarter)]


class Ring:
    def __init__(self, shard):
        self.count = lax.axis_size("seq")
        self.order = ring_order(self.count)
        self.parts = [shard]
        self.ahead = self.back = shard
        self.done = 0

    def move(self, value, step):
        pairs = [(self.order[i], self.order[(i + step) % self.count]) for i in range(self.count)]
        return lax.ppermute(value, "seq", pairs)

    def hop(self, *after):
        self.ahead, self.back, *_ = lax.optimization_barrier((self.ahead, self.back, *after))
        self.done += 1
        if self.done < (self.count + 1) // 2:
            self.ahead, self.back = self.move(self.ahead, 1), self.move(self.back, -1)
            self.parts += [self.ahead, self.back]
        else:
            cut = ring_cut(self.ahead.shape[0])
            self.parts += [self.move(self.ahead[:cut], 1), self.move(self.back[cut:], -1)]

    def hops(self):
        return (self.count + 1) // 2

    def tie(self, *values):
        self.ahead, self.back, *values = lax.optimization_barrier((self.ahead, self.back, *values))
        return values

    def finish(self):
        while self.done < self.hops():
            self.hop()
        return self


def after(value, *others):
    return lax.optimization_barrier((value, *others))[0]


def flip(value, axis, bit):
    count = lax.axis_size(axis)
    return lax.ppermute(value, axis, [(i, i ^ bit) for i in range(count)])


def shifted(value, axis, steps):
    count = lax.axis_size(axis)
    first, last = max(0, -steps), min(count, count - steps)
    return lax.ppermute(value, axis, [(i, i + steps) for i in range(first, last)])


def group_gather(share):
    count = lax.axis_size("grp")
    out = []
    for far in range(0, count, 2):
        mine = share if far == 0 else flip(share, "grp", far)
        out += [mine, flip(mine, "grp", 1)]
    return out


def far_gather(share):
    return [share] + [flip(share, "grp", far) for far in range(2, lax.axis_size("grp"), 2)]


def near_gather(fars):
    out = []
    for far in fars:
        out += [far, flip(far, "grp", 1)]
    return out


def group_exchange(blocks):
    return [blocks[0]] + [flip(blocks[r], "grp", r) for r in range(1, len(blocks))]


def scatter_start(blocks):
    count = len(blocks)
    fars = []
    for far in range(2, count, 2):
        there = flip(blocks[far + 1], "grp", 1)
        fars.append((blocks[far].astype(F32) + there.astype(F32)).astype(BF))
    return fars, [blocks[0], flip(blocks[1], "grp", 1)]


def scatter_end(fars, nears):
    return nears + [flip(far, "grp", 2 * (i + 1)) for i, far in enumerate(fars)]


def exchange(ends, halo, sign):
    count = lax.axis_size("seq")
    wide = max(1, count // 4)
    here = [ends] + [flip(ends, "seq", j) for j in range(1, wide)]
    near = jnp.stack(here)
    out = [near]
    for r in range(1, count // wide):
        out.append(shifted(near if r == 1 else near[:, :, :, 1:], "seq", sign * r * wide))
    return out, shifted(halo, "seq", sign)


class Slots:
    def __init__(self, lens, batch):
        self.starts, self.ends, at = [], [], 0
        for i in range(lens.shape[1]):
            length = lens[batch, i]
            self.starts.append(at)
            self.ends.append(at * STRETCH + length)
            at = at + ((length + STRETCH - 1) >> 6)

    def owner(self, c):
        total = -1
        for start in self.starts:
            total = total + jnp.where(start <= c, 1, 0)
        return total

    def valid(self, c):
        end = 0
        for start, stop in zip(self.starts, self.ends):
            end = jnp.where(start <= c, stop, end)
        return jnp.clip(end - c * STRETCH, 0, STRETCH)

    def same(self, a, b):
        return jnp.where(self.owner(a) == self.owner(b), 1, 0)

    def weight(self, a, b):
        return self.same(a, b).astype(F32)


def entering(slots, info, arrays, blocks, wide, count, sign, place, near_k):
    seq = info[2]
    base = info[0]
    z, y = seq // wide, seq % wide
    edge = base - 1 if sign > 0 else base + blocks
    inner = outer = jnp.zeros((EXT, PAIR), F32)
    for r in range(count // wide):
        for j in range(wide):
            if r == 0 and j == 0:
                continue
            source = (z - sign * r) * wide + (y ^ j)
            ahead = (seq - source) * sign > 0
            end = source * blocks + (blocks - 1 if sign > 0 else 0)
            direct = (seq - source) * sign == 1
            full = arrays[r][j, place, near_k, arrays[r].shape[3] - 1].astype(F32)
            a = jnp.where(ahead & (slots.owner(end) == slots.owner(edge)), 1.0, 0.0)
            outer = outer + a * full
            b = jnp.where(
                ahead & (~direct) & (slots.owner(end) == slots.owner(edge - sign)), 1.0, 0.0
            )
            inner = inner + b * full
            if arrays[r].shape[3] == 2:
                part = arrays[r][j, place, near_k, 0].astype(F32)
                inner = inner + jnp.where(direct, 1.0, 0.0) * part
    return inner, outer


def half_mask(shape):
    return (lax.broadcasted_iota(jnp.int32, shape, 1) & (PAIR - 1)) < STRETCH


def feature_softmax(u):
    top = jnp.exp(u - jnp.max(u, axis=0, keepdims=True))
    bottom = jnp.exp(jnp.min(u, axis=0, keepdims=True) - u)
    top = top * (1.0 / jnp.sum(top, axis=0, keepdims=True))
    bottom = bottom * (1.0 / jnp.sum(bottom, axis=0, keepdims=True))
    return jnp.concatenate([top, bottom], axis=0)


def feature_back(phi, d_phi):
    top, bottom = phi[:STRETCH].astype(F32), phi[STRETCH:].astype(F32)
    a, b = d_phi[:STRETCH], d_phi[STRETCH:]
    return top * (a - jnp.sum(top * a, axis=0, keepdims=True)) - bottom * (
        b - jnp.sum(bottom * b, axis=0, keepdims=True)
    )


def assemble_kernel(parts_of, width, splits, info, *refs):
    ins, outs = refs[: len(parts_of)], refs[len(parts_of) :]
    for (q, first, rows), ref in zip(parts_of, ins):
        column = pl.ds(pl.multiple_of(info[3 + q] * width, width), width)
        at = 0
        for out, size in zip(outs, splits):
            low, high = max(at, first), min(at + size, first + rows)
            if low < high:
                out[low - at : high - at, column] = ref[low - first : high - first, :]
            at += size


def project_kernel(
    batch, q_width, info, lens, normed_ref, w_ref, up_ref, kv_up_ref, wk_ref,
    q_ref, kv_ref, ve_ref, mid_ref, phi_ref, st_ref, ends_ref, halo_ref, carry,
):
    step = pl.program_id(0)
    rows = normed_ref.shape[0]
    width = kv_ref.shape[1]
    heads = width // PAIR

    @pl.when(step == 0)
    def _():
        carry[...] = jnp.zeros_like(carry)

    normed = normed_ref[...]
    mixed = dotg(w_ref[: q_width + 32], normed, 1, 1)
    mids = mixed[q_width:].astype(BF)
    mid_ref[...] = mids
    query = mixed[:q_width] + ADAPTER_SCALE * dotg(up_ref[...], mids, 1, 0)
    q_ref[...] = query.astype(BF)
    kv_all = dotg(normed, w_ref[q_width + 32 :], 1, 1) + ADAPTER_SCALE * dotg(
        mids, kv_up_ref[...], 0, 0
    )
    kv_all = kv_all.astype(BF)
    kv_ref[...] = kv_all
    halo_ref[:, :width] = kv_all[rows - STRETCH :]

    slots = Slots(lens, batch)
    base = info[0]
    lane = lax.broadcasted_iota(jnp.int32, (1, PAIR), 1)
    low = lane < STRETCH
    inside = lane & (STRETCH - 1)
    wide = lax.broadcasted_iota(jnp.int32, (PAIR, PAIR), 1)
    for sub in range(rows // PAIR):
        block = base + 2 * (step * (rows // PAIR) + sub)
        one_a, one_b = slots.weight(block - 1, block), slots.weight(block, block + 1)
        valid = inside < jnp.where(low, slots.valid(block), slots.valid(block + 1))
        valid = jnp.where(valid, 1.0, 0.0)
        valid_low = jnp.where(low, valid, 0.0)
        valid_high = valid - valid_low
        at = sub * PAIR
        for k in range(heads):
            kv = kv_all[at : at + PAIR, k * PAIR : (k + 1) * PAIR]
            moved = pltpu.roll(kv.astype(F32), STRETCH, 1)
            ve = jnp.where(
                wide < STRETCH, moved, jnp.where(wide < STRETCH + 2, 1.0, 0.0)
            ).astype(BF)
            ve_ref[at : at + PAIR, k * PAIR : (k + 1) * PAIR] = ve
            if sub == rows // PAIR - 1:
                halo_ref[:, width + k * PAIR : width + (k + 1) * PAIR] = ve[STRETCH:]
            phi = feature_softmax(dotg(wk_ref[k], kv, 1, 1))
            phi_ref[k * PAIR : (k + 1) * PAIR, at : at + PAIR] = (phi * valid).astype(BF)
            first = dotg(ve, (phi * valid_low).astype(BF), 0, 1)[:EXT]
            second = dotg(ve, (phi * valid_high).astype(BF), 0, 1)[:EXT]
            st_ref[sub, k, :EXT] = first
            st_ref[sub, k, EXT:] = second
            mid = carry[k] * one_a + first
            tail = mid * one_b + second
            carry[k] = tail
            ends_ref[k, 0] = mid.astype(BF)
            ends_ref[k, 1] = tail.astype(BF)


def window_mask(slots, block):
    lane = lax.broadcasted_iota(jnp.int32, (1, PAIR), 1)
    low = lane < STRETCH
    before = slots.valid(block - 1) * slots.same(block - 1, block)
    own = slots.valid(block)
    limits = [
        jnp.where(low, before, 0),
        jnp.where(low, jnp.minimum(lane + 1, own), own * slots.same(block, block + 1)),
        jnp.where(low, 0, jnp.minimum(lane - STRETCH + 1, slots.valid(block + 1))),
    ]
    row = lax.broadcasted_iota(jnp.int32, (STRETCH, PAIR), 0)
    return jnp.concatenate([jnp.where(row < limit, 1.0, 0.0) for limit in limits], axis=0)


def fill_window(batch, kv_ref, ve_ref, halo_ref, kv_all, ve_all):
    width = kv_ref.shape[1]
    kv_all[:STRETCH] = halo_ref[batch, :, :width]
    ve_all[:STRETCH] = halo_ref[batch, :, width:]
    kv_all[STRETCH:] = kv_ref[...]
    ve_all[STRETCH:] = ve_ref[...]


def forward_kernel(
    batch, per, blocks, wide, count, n_far, scale, info, lens, q_ref, kv_ref, ve_ref, halo_ref,
    wq_ref, oin_ref, st_ref, *refs,
):
    fars = refs[:n_far]
    att_ref, w_ref, phi_ref, s_ref, r_ref, carry, kv_all, ve_all = refs[n_far:]
    step = pl.program_id(0)
    heads = kv_ref.shape[1] // PAIR
    slots = Slots(lens, batch)
    block = info[0] + 2 * step

    @pl.when(step == 0)
    def _():
        fill_window(batch, kv_ref, ve_ref, halo_ref, kv_all, ve_all)
        for k in range(heads):
            inner, outer = entering(slots, info, fars, blocks, wide, count, 1, batch, k)
            carry[k, 0] = inner
            carry[k, 1] = outer

    one_a, one_b = slots.weight(block - 1, block), slots.weight(block, block + 1)
    two_a, two_b = slots.weight(block - 2, block), slots.weight(block - 1, block + 1)
    mask = window_mask(slots, block)
    mask = jnp.concatenate([mask] * per, axis=1)
    lanes = per * PAIR
    low = half_mask((EXT, lanes))
    rows = pl.ds(pl.multiple_of(step * PAIR, PAIR), WIN)
    out_mid = jnp.zeros((16, PAIR), F32)
    for k in range(heads):
        kv = kv_all[rows, k * PAIR : (k + 1) * PAIR]
        ve = ve_all[rows, k * PAIR : (k + 1) * PAIR]
        base = k * per * STRETCH
        stacked = q_ref[base : base + per * STRETCH, :]
        q = jnp.concatenate(
            [stacked[g * STRETCH : (g + 1) * STRETCH] for g in range(per)], axis=1
        )
        q = jnp.concatenate([q, jnp.zeros_like(q)], axis=0)
        scores = dotg(kv, q, 1, 0)
        weights = (jnp.exp2(scores * scale) * mask).astype(BF)
        w_ref[0, k] = weights
        mixed = dotg(wq_ref[k], stacked, 1, 0)
        phi = jnp.concatenate(
            [
                feature_softmax(mixed[g * STRETCH : (g + 1) * STRETCH]).astype(BF)
                for g in range(per)
            ],
            axis=1,
        )
        phi_ref[0, k] = phi
        older, old = carry[k, 0], carry[k, 1]
        states = jnp.concatenate([older * two_a, old * two_b], axis=0).astype(BF)
        s_ref[0, k] = states
        linear = dotg(states, phi, 1, 0)
        total = dotg(ve, weights, 0, 0)[:EXT] + jnp.where(low, linear[:EXT], linear[EXT:])
        inverse = 1.0 / total[STRETCH : STRETCH + 1]
        att = (total[:STRETCH] * inverse).astype(BF)
        att = jnp.concatenate([att[:, g * PAIR : (g + 1) * PAIR] for g in range(per)], axis=0)
        att_ref[0, base : base + per * STRETCH, :] = att
        out_mid = out_mid + dotg(oin_ref[base : base + per * STRETCH, :], att, 0, 0)
        for g in range(per):
            r_ref[0, k * per + g : k * per + g + 1, :] = inverse[:, g * PAIR : (g + 1) * PAIR]
        current = old * one_a + st_ref[0, k, :EXT]
        carry[k, 0] = current
        carry[k, 1] = current * one_b + st_ref[0, k, EXT:]
    att_ref[0, heads * per * STRETCH :, :] = (ADAPTER_SCALE * out_mid).astype(BF)


def residual_kernel(n_grp, info, x_ref, gain_ref, *refs):
    atts, weights = refs[:n_grp], refs[n_grp : 2 * n_grp]
    resid_ref, low_ref, mid_ref, buffer, sems = refs[2 * n_grp :]
    copies = [
        pltpu.make_async_copy(weights[r], buffer.at[r], sems.at[r]) for r in range(n_grp)
    ]
    for copy in copies:
        copy.start()
    q_width = buffer.shape[1] - 16
    resid_ref[...] = x_ref[0].astype(F32)
    mid = jnp.zeros(mid_ref.shape, F32)
    for r in range(n_grp):
        copies[r].wait()
        att = atts[r][0] if len(atts[r].shape) == 3 else atts[r][...]
        mid = mid + att[q_width:].astype(F32)
        resid_ref[...] += dotg(att, buffer[r], 0, 0)
    mid_ref[...] = mid.astype(BF)
    resid = resid_ref[...]
    factor = lax.rsqrt(jnp.mean(resid * resid, axis=1, keepdims=True) + EPS)
    low_ref[...] = (resid * factor * gain_ref[...]).astype(BF)


def branch_kernel(n_grp, n_sum, info, dy_ref, resid_ref, gain_ref, mid_ref, *refs):
    summands, refs = refs[:n_sum], refs[n_sum:]
    weights, refs = refs[:n_grp], refs[n_grp:]
    d_resid_ref, wide_ref, refs = refs[0], refs[1], refs[2:]
    outs, (buffer, sems) = refs[:n_grp], refs[n_grp:]
    copies = [
        pltpu.make_async_copy(weights[r], buffer.at[r], sems.at[r]) for r in range(n_grp)
    ]
    for copy in copies:
        copy.start()
    d_in = summands[0][...].astype(F32)
    for summand in summands[1:]:
        d_in = d_in + summand[...].astype(F32)
    resid = resid_ref[...]
    factor = lax.rsqrt(jnp.mean(resid * resid, axis=1, keepdims=True) + EPS)
    e = gain_ref[...] * d_in
    slope = factor * factor * factor * jnp.mean(resid * e, axis=1, keepdims=True)
    d_resid = dy_ref[0].astype(F32) + factor * e - resid * slope
    d_resid_ref[...] = d_resid
    low = d_resid.astype(BF)
    wide_ref[...] = dotg(mid_ref[...], low, 1, 0)
    for r in range(n_grp):
        copies[r].wait()
        outs[r][...] = dotg(buffer[r], low, 1, 1).astype(BF)


def tokens_kernel(n_grp, info, x_ref, gain_ref, d_resid_ref, *refs):
    dqs, rests, weights = refs[:n_grp], refs[n_grp : 2 * n_grp], refs[2 * n_grp : 3 * n_grp]
    out_ref, buffer, total, sems = refs[3 * n_grp :][-4:]
    copies = [
        pltpu.make_async_copy(weights[r], buffer.at[r], sems.at[r]) for r in range(n_grp)
    ]
    for copy in copies:
        copy.start()
    for r in range(n_grp):
        copies[r].wait()
        d_q = dqs[r][0] if len(dqs[r].shape) == 3 else dqs[r][...]
        rest = rests[r][0] if len(rests[r].shape) == 3 else rests[r][...]
        part = dotg(jnp.concatenate([d_q, rest], axis=0), buffer[r], 0, 0)
        if r:
            total[...] += part
        else:
            total[...] = part
    x = x_ref[0].astype(F32)
    factor = lax.rsqrt(jnp.mean(x * x, axis=1, keepdims=True) + EPS)
    e = gain_ref[...] * total[...]
    slope = factor * factor * factor * jnp.mean(x * e, axis=1, keepdims=True)
    out_ref[0] = d_resid_ref[...] + factor * e - x * slope


def mlp_kernel(
    batch, n_grp, layout, sizes, first_half, info, *refs,
):
    n_parts = len(layout)
    xs, refs = refs[:n_grp], refs[n_grp:]
    dy_hbm, refs = refs[0], refs[1:]
    part_sets = []
    for _ in sizes:
        part_sets.append(refs[:n_parts])
        refs = refs[n_parts:]
    n_prev = 0 if first_half else 2
    prevs, refs = refs[:n_prev], refs[n_prev:]
    n_out = 2 if first_half else 2 * n_grp
    outs, refs = refs[:n_out], refs[n_out:]
    x, dy, w, acc_out, acc_in, sem, wsem = refs[:7]
    j, n = pl.program_id(0), pl.num_programs(0)
    slot = j % 2
    share = xs[0].shape[0]
    rows_all = x.shape[0]
    depth = layout[0][2]

    def loads(jj, s, which):
        copies = []
        first_step = sum(sizes[:which]) // CHUNK
        for (q, first, rows), part in zip(layout, part_sets[which]):
            to = pl.ds(pl.multiple_of(info[3 + q] * depth + first, 16), rows)
            for kind in range(3):
                column = pl.multiple_of(kind * sizes[which] + (jj - first_step) * CHUNK, CHUNK)
                copies.append(
                    pltpu.make_async_copy(
                        part.at[:, pl.ds(column, CHUNK)],
                        w.at[s, to, pl.ds(kind * CHUNK, CHUNK)],
                        wsem.at[s],
                    )
                )
        return copies

    def start_loads(jj, s):
        for which in range(len(sizes)):
            low, high = sum(sizes[:which]) // CHUNK, sum(sizes[: which + 1]) // CHUNK

            @pl.when((jj >= low) & (jj < high))
            def _(which=which):
                for copy in loads(jj, s, which):
                    copy.start()

    def inputs():
        copies = []
        for r in range(n_grp):
            rows = pl.ds(r * share, share)
            copies.append(pltpu.make_async_copy(xs[r], x.at[rows], sem.at[0]))
            there = pl.ds(pl.multiple_of((info[1] ^ r) * share, share), share)
            copies.append(pltpu.make_async_copy(dy_hbm.at[batch, there], dy.at[rows], sem.at[0]))
        return copies

    def earlier():
        return [
            pltpu.make_async_copy(prev, refs[7 + i], sem.at[1]) for i, prev in enumerate(prevs)
        ]

    @pl.when(j == 0)
    def _():
        for copy in inputs() + earlier():
            copy.start()
        start_loads(j, 0)
        for copy in inputs():
            copy.wait()

    @pl.when(j + 1 < n)
    def _():
        start_loads(j + 1, 1 - slot)

    for copy in loads(0, slot, 0):
        copy.wait()
    gate_up_w = w.at[slot, :, pl.ds(0, 2 * CHUNK)]
    down_w = w.at[slot, :, pl.ds(2 * CHUNK, CHUNK)]

    def body(i, start):
        rows = pl.ds(pl.multiple_of(i * ROW_TILE, ROW_TILE), ROW_TILE)
        gate_up = dotg(x[rows, :], gate_up_w[...], 1, 0)
        d_hidden = dotg(dy[rows, :], down_w[...], 1, 0)
        gate, up = gate_up[:, :CHUNK], gate_up[:, CHUNK:]
        sig = 1.0 / (1.0 + jnp.exp(-gate))
        act = gate * sig
        hidden = (act * up).astype(BF)
        d_gate = (d_hidden * up * (sig + act * (1.0 - sig))).astype(BF)
        d_up = (d_hidden * act).astype(BF)
        out = dotg(hidden, down_w[...], 1, 1)
        d_in = dotg(jnp.concatenate([d_gate, d_up], axis=1), gate_up_w[...], 1, 1)
        if start:
            acc_out[rows, :] = out
            acc_in[rows, :] = d_in
        else:
            acc_out[rows, :] += out
            acc_in[rows, :] += d_in
        return 0

    tiles = rows_all // ROW_TILE

    @pl.when(j == 0)
    def _():
        lax.fori_loop(0, tiles, lambda i, c: body(i, True), 0)

    @pl.when(j > 0)
    def _():
        lax.fori_loop(0, tiles, lambda i, c: body(i, False), 0)

    @pl.when(j == n - 1)
    def _():
        if first_half:
            x[...] = acc_in[...].astype(BF)
            dy[...] = acc_out[...].astype(BF)
            copies = [
                pltpu.make_async_copy(x, outs[0], sem.at[0]),
                pltpu.make_async_copy(dy, outs[1], sem.at[0]),
            ]
        else:
            for copy in earlier():
                copy.wait()
            x[...] = (acc_in[...] + refs[7][...].astype(F32)).astype(BF)
            dy[...] = (acc_out[...] + refs[8][...].astype(F32)).astype(BF)
            copies = []
            for r in range(n_grp):
                rows = pl.ds(r * share, share)
                copies.append(pltpu.make_async_copy(x.at[rows], outs[r], sem.at[0]))
                copies.append(pltpu.make_async_copy(dy.at[rows], outs[n_grp + r], sem.at[0]))
        for copy in copies:
            copy.start()
        for copy in copies:
            copy.wait()


def backward_kernel(
    batch, per, pairs, n_grp, has_prev, scale, info, lens, q_ref, kv_ref, ve_ref, halo_ref, wq_ref,
    oin_ref, att_ref, w_ref, phi_ref, s_ref, r_ref, *refs,
):
    blocks_in, refs = refs[:n_grp], refs[n_grp:]
    prevs, refs = (refs[:1], refs[1:]) if has_prev else (None, refs)
    (
        dq_ref, dkv_ref, ds_ref, ends_ref, back_ref, map_ref, carry, kv_all, ve_all, d_outs, sem,
    ) = refs
    step = pl.program_id(0)
    pair = pairs - 1 - step
    heads = kv_ref.shape[1] // PAIR
    slots = Slots(lens, batch)
    block = info[0] + 2 * pair
    q_width = q_ref.shape[0]
    per_block = blocks_in[0].shape[1] // PAIR

    @pl.when(step == 0)
    def _():
        copies = []
        for r in range(n_grp):
            for i in range(per_block):
                copies.append(
                    pltpu.make_async_copy(
                        blocks_in[r].at[:, pl.ds(i * PAIR, PAIR)],
                        d_outs.at[(info[1] ^ r) * per_block + i],
                        sem,
                    )
                )
        for copy in copies:
            copy.start()
        fill_window(batch, kv_ref, ve_ref, halo_ref, kv_all, ve_all)
        carry[...] = jnp.zeros_like(carry)
        dkv_ref[...] = jnp.zeros_like(dkv_ref)
        map_ref[...] = prevs[0][...] if has_prev else jnp.zeros_like(map_ref)
        for copy in copies:
            copy.wait()
    one_b = slots.weight(block, block + 1)
    one_c = slots.weight(block + 1, block + 2)
    lanes = per * PAIR
    low = half_mask((EXT, lanes))
    rows = pl.ds(pl.multiple_of(pair * PAIR, PAIR), WIN)
    d_out = d_outs[pair]
    back_out = ADAPTER_SCALE * d_out[q_width:]
    d_att_all = d_out[:q_width].astype(F32) + dotg(oin_ref[...], back_out, 1, 0)
    for k in range(heads):
        kv = kv_all[rows, k * PAIR : (k + 1) * PAIR]
        ve = ve_all[rows, k * PAIR : (k + 1) * PAIR]
        base = k * per * STRETCH

        def side(value):
            return jnp.concatenate(
                [value[g * STRETCH : (g + 1) * STRETCH] for g in range(per)], axis=1
            )

        stacked = q_ref[base : base + per * STRETCH, :]
        q = side(stacked)
        d_att = side(d_att_all[base : base + per * STRETCH])
        att = side(att_ref[0, base : base + per * STRETCH, :]).astype(F32)
        inverse = jnp.concatenate(
            [r_ref[0, k * per + g : k * per + g + 1, :] for g in range(per)], axis=1
        )
        ratio = d_att * inverse
        d_den = -jnp.sum(ratio * att, axis=0, keepdims=True)
        d_high = d_den.astype(BF).astype(F32)
        row = lax.broadcasted_iota(jnp.int32, (EXT - STRETCH, lanes), 0)
        extra = jnp.where(row == 0, d_high, jnp.where(row == 1, d_den - d_high, 0.0))
        ratio_ext = jnp.concatenate([ratio, extra], axis=0)
        ratio_low = ratio_ext.astype(BF)
        weights = w_ref[0, k]
        padded = jnp.concatenate([ratio_low, jnp.zeros((PAIR - EXT, lanes), BF)], axis=0)
        d_weights = dotg(ve, padded, 1, 0)
        d_scores = (d_weights * weights.astype(F32)).astype(BF)
        d_query = dotg(kv, d_scores, 0, 0)[:STRETCH] * scale
        zeros = jnp.zeros((STRETCH, lanes), BF)
        q_scaled = (q.astype(F32) * scale).astype(BF)
        d_kv = dotg(d_scores, jnp.concatenate([q_scaled, zeros], axis=0), 1, 1) + dotg(
            weights, jnp.concatenate([zeros, ratio_low[:STRETCH]], axis=0), 1, 1
        )
        dkv_ref[rows, k * PAIR : (k + 1) * PAIR] += d_kv
        phi = phi_ref[0, k]
        both = jnp.concatenate(
            [jnp.where(low, ratio_ext, 0.0), jnp.where(low, 0.0, ratio_ext)], axis=0
        ).astype(BF)
        d_phi = dotg(s_ref[0, k], both, 0, 0)
        d_state = dotg(both, phi, 1, 1)
        ds_ref[0, k] = d_state
        d_mixed = feature_back(phi, d_phi).astype(BF)
        d_mixed = jnp.concatenate(
            [d_mixed[:, g * PAIR : (g + 1) * PAIR] for g in range(per)], axis=0
        )
        d_stacked = jnp.concatenate(
            [d_query[:, g * PAIR : (g + 1) * PAIR] for g in range(per)], axis=0
        ) + dotg(wq_ref[k], d_mixed, 0, 0)
        dq_ref[0, base : base + per * STRETCH, :] = d_stacked.astype(BF)
        map_ref[k] += dotg(stacked, d_mixed, 1, 1)
        rest = d_state[EXT:] + one_c * carry[k]
        head = d_state[:EXT] + one_b * rest
        carry[k] = head
        ends_ref[k, 0] = rest.astype(BF)
        ends_ref[k, 1] = head.astype(BF)

    @pl.when(step == pairs - 1)
    def _():
        back_ref[...] = dkv_ref[:STRETCH, :].astype(BF)


def keys_kernel(
    batch, pairs, blocks, wide_y, count, n_far, has_prev, info, lens, kv_ref, ve_ref, wk_ref,
    phi_ref, dkv_ref, back_ref, ds_ref, dq_ref, q_up_ref, kv_up_ref, *refs,
):
    fars, refs = refs[:n_far], refs[n_far:]
    prevs, refs = (refs[:1], refs[1:]) if has_prev else (None, refs)
    out_ref, map_ref, carry = refs
    step = pl.program_id(0)
    pair = pairs - 1 - step
    heads = kv_ref.shape[1] // PAIR
    slots = Slots(lens, batch)
    block = info[0] + 2 * pair

    @pl.when(step == 0)
    def _():
        for k in range(heads):
            inner, outer = entering(slots, info, fars, blocks, wide_y, count, -1, 0, k)
            carry[k, 0] = outer
            carry[k, 1] = inner
        map_ref[...] = prevs[0][...] if has_prev else jnp.zeros_like(map_ref)

    one_b = slots.weight(block, block + 1)
    one_c = slots.weight(block + 1, block + 2)
    two_c = slots.weight(block, block + 2)
    two_d = slots.weight(block + 1, block + 3)
    row = lax.broadcasted_iota(jnp.int32, (PAIR, PAIR), 0)
    lane = lax.broadcasted_iota(jnp.int32, (PAIR, PAIR), 1)
    last = jnp.where(step == 0, 1.0, 0.0)
    rows = pl.ds(pl.multiple_of(pair * PAIR + STRETCH, STRETCH), PAIR)
    d_kvs = []
    for k in range(heads):
        kv = kv_ref[:, k * PAIR : (k + 1) * PAIR]
        ve = ve_ref[:, k * PAIR : (k + 1) * PAIR].astype(F32)
        next_one, next_two = carry[k, 0], carry[k, 1]
        pad = jnp.zeros((PAIR - EXT, PAIR), F32)
        grads = jnp.concatenate([next_one * two_c, pad, next_two * two_d, pad], axis=0).astype(BF)
        both = jnp.concatenate(
            [jnp.where(row < STRETCH, ve, 0.0), jnp.where(row < STRETCH, 0.0, ve)], axis=1
        ).astype(BF)
        d_phi = dotg(grads, both, 0, 1)
        phi = phi_ref[k * PAIR : (k + 1) * PAIR, :]
        d_both = dotg(phi, grads, 0, 1)
        d_value = jnp.where(row < STRETCH, d_both[:, :PAIR], d_both[:, PAIR:])
        d_value = jnp.where(lane < STRETCH, 0.0, pltpu.roll(d_value, STRETCH, 1))
        d_mixed = feature_back(phi, d_phi).astype(BF)
        d_key = dotg(d_mixed, wk_ref[k], 0, 0)
        map_ref[k] += dotg(kv, d_mixed, 0, 1)
        total = dkv_ref[rows, k * PAIR : (k + 1) * PAIR] + d_value + d_key
        returned = back_ref[:, k * PAIR : (k + 1) * PAIR].astype(F32) * last
        total = total + jnp.concatenate([jnp.zeros_like(returned), returned], axis=0)
        d_kvs.append(jnp.transpose(total).astype(BF))
        state = ds_ref[0, k]
        rest = state[EXT:] + one_c * next_one
        carry[k, 1] = rest
        carry[k, 0] = state[:EXT] + one_b * rest
    d_kv = jnp.concatenate(d_kvs, axis=0)
    back_in = dotg(q_up_ref[...], dq_ref[0], 1, 0) + dotg(kv_up_ref[...], d_kv, 1, 0)
    out_ref[0, :32, :] = (ADAPTER_SCALE * back_in).astype(BF)
    out_ref[0, 32:, :] = d_kv


def adapter_kernel(
    n_grp, has_prev, info, dq_ref, rest_ref, mid_ref, normed_ref, att_ref, *refs
):
    blocks_in, refs = refs[:n_grp], refs[n_grp:]
    prevs, refs = (refs[:3], refs[3:]) if has_prev else (None, refs)
    up_ref, oin_ref, wide_ref = refs
    share = blocks_in[0].shape[1]
    q_width = dq_ref.shape[1]
    for r in range(n_grp):
        there = pl.ds(pl.multiple_of((info[1] ^ r) * share, share), share)
        mids = mid_ref[:, there]
        rest = rest_ref[r]
        both = jnp.concatenate([dq_ref[r], rest], axis=0)
        up = dotg(mids, both, 1, 1)
        oin = dotg(ADAPTER_SCALE * blocks_in[r][q_width:], att_ref[r, :q_width, :], 1, 1)
        wide = dotg(rest[:32], normed_ref[there, :], 1, 0)
        if r or has_prev:
            up_ref[...] = up + (up_ref[...] if r else prevs[0][...])
            oin_ref[...] = oin + (oin_ref[...] if r else prevs[1][...])
            wide_ref[...] = wide + (wide_ref[...] if r else prevs[2][...])
        else:
            up_ref[...] = up
            oin_ref[...] = oin
            wide_ref[...] = wide


def whole(shape):
    return pl.BlockSpec(shape, lambda i, *_: (0,) * len(shape))


def anywhere():
    return pl.BlockSpec(memory_space=pl.ANY)


def sds(shape, kind):
    return jax.ShapeDtypeStruct(shape, kind)


def call(
    kernel, name, grid, scalars, ins, in_specs, out_specs, out_shape, scratch=(), alias=None
):
    return pl.pallas_call(
        kernel,
        grid_spec=pltpu.PrefetchScalarGridSpec(
            num_scalar_prefetch=len(scalars),
            grid=(grid,),
            in_specs=in_specs,
            out_specs=out_specs,
            scratch_shapes=list(scratch),
        ),
        out_shape=out_shape,
        input_output_aliases=alias or {},
        cost_estimate=pl.CostEstimate(flops=0, transcendentals=0, bytes_accessed=1024),
        compiler_params=pltpu.CompilerParams(
            dimension_semantics=("arbitrary",), vmem_limit_bytes=VMEM_LIMIT
        ),
        name=name,
    )(*scalars, *ins)


def run_assemble(info, ring, splits):
    shape = ring.parts[0].shape
    parts_of = ring_layout(ring.count, shape[0])
    outs = [(size, shape[1] * ring.count) for size in splits]
    return call(
        functools.partial(assemble_kernel, parts_of, shape[1], splits), "assemble", 1, [info],
        ring.parts, [whole(part.shape) for part in ring.parts], [whole(out) for out in outs],
        [sds(out, BF) for out in outs],
    )


def run_project(info, lens, batch, normed, weight, q_up, kv_up, maps):
    rows, model = normed.shape
    heads = maps.shape[0]
    width = heads * PAIR
    q_width = weight.shape[0] - 32 - width
    tile = 2 * PAIR
    pairs = rows // PAIR
    return call(
        functools.partial(project_kernel, batch, q_width),
        "project_states", rows // tile, [info, lens],
        [normed, weight, q_up, kv_up, maps],
        [
            pl.BlockSpec((tile, model), lambda i, *_: (i, 0)),
            whole(weight.shape), whole(q_up.shape), whole(kv_up.shape), whole(maps.shape),
        ],
        [
            pl.BlockSpec((q_width, tile), lambda i, *_: (0, i)),
            pl.BlockSpec((tile, width), lambda i, *_: (i, 0)),
            pl.BlockSpec((tile, width), lambda i, *_: (i, 0)),
            pl.BlockSpec((32, tile), lambda i, *_: (0, i)),
            pl.BlockSpec((width, tile), lambda i, *_: (0, i)),
            pl.BlockSpec((2, heads, 2 * EXT, PAIR), lambda i, *_: (i, 0, 0, 0)),
            whole((heads, 2, EXT, PAIR)),
            whole((STRETCH, 2 * width)),
        ],
        [
            sds((q_width, rows), BF),
            sds((rows, width), BF),
            sds((rows, width), BF),
            sds((32, rows), BF),
            sds((width, rows), BF),
            sds((pairs, heads, 2 * EXT, PAIR), F32),
            sds((heads, 2, EXT, PAIR), BF),
            sds((STRETCH, 2 * width), BF),
        ],
        [pltpu.VMEM((heads, EXT, PAIR), F32)],
    )


def run_forward(info, lens, batch, q, kv, ve, halo, maps, o_in, states, fars):
    q_width, rows = q.shape
    width = kv.shape[1]
    heads, pairs = width // PAIR, rows // PAIR
    per = q_width // STRETCH // heads
    count = lax.axis_size("seq")
    wide = max(1, count // 4)
    scale = STRETCH ** (-0.5) * math.log2(math.e)
    step = lambda *shape: pl.BlockSpec((1,) + shape, lambda i, *_: (i,) + (0,) * len(shape))
    column = lambda n: pl.BlockSpec((n, PAIR), lambda i, *_: (0, i))
    share = rows // lax.axis_size("grp")
    return call(
        functools.partial(
            forward_kernel, batch, per, rows // STRETCH, wide, count, len(fars), scale
        ),
        "attention_forward", pairs, [info, lens],
        [q, kv, ve, halo, maps, o_in, states, *fars],
        [
            column(q_width), whole(kv.shape), whole(ve.shape), whole(halo.shape),
            whole(maps.shape), whole(o_in.shape), step(heads, 2 * EXT, PAIR),
            *[whole(far.shape) for far in fars],
        ],
        [
            block_spec(q_width + 16, share, lambda i: i), step(heads, WIN, per * PAIR),
            step(heads, PAIR, per * PAIR), step(heads, 2 * EXT, PAIR), step(heads * per, PAIR),
        ],
        [
            sds((rows // share, q_width + 16, share), BF),
            sds((pairs, heads, WIN, per * PAIR), BF),
            sds((pairs, heads, PAIR, per * PAIR), BF),
            sds((pairs, heads, 2 * EXT, PAIR), BF),
            sds((pairs, heads * per, PAIR), F32),
        ],
        [
            pltpu.VMEM((heads, 2, EXT, PAIR), F32),
            pltpu.VMEM((rows + STRETCH, width), BF),
            pltpu.VMEM((rows + STRETCH, width), BF),
        ],
    )


def block_spec(height, share, pair_of):
    per_block = share // PAIR
    return pl.BlockSpec(
        (1, height, PAIR),
        lambda i, info, *_: ((pair_of(i) // per_block) ^ info[1], 0, pair_of(i) % per_block),
    )


def own_spec(batch, share, model):
    return pl.BlockSpec((1, share, model), lambda i, info: (batch, info[1], 0))


def front(array):
    if len(array.shape) == 2:
        return whole(array.shape)
    return pl.BlockSpec((1,) + array.shape[1:], lambda i, *_: (0, 0, 0))


def run_residual(info, batch, tokens, gain, atts, weights):
    n_grp = len(atts)
    model = tokens.shape[2]
    share = atts[0].shape[-1]
    return call(
        functools.partial(residual_kernel, n_grp), "residual", 1, [info],
        [tokens, gain, *atts, *weights],
        [own_spec(batch, share, model), whole(gain.shape), *[front(att) for att in atts]]
        + [anywhere()] * n_grp,
        [whole((share, model)), whole((share, model)), whole((16, share))],
        [sds((share, model), F32), sds((share, model), BF), sds((16, share), BF)],
        [
            pltpu.VMEM((n_grp,) + weights[0].shape, BF),
            pltpu.SemaphoreType.DMA((n_grp,)),
        ],
    )


def run_branch(info, batch, cotangent, resid, gain, mid, summands, weights):
    n_grp = len(weights)
    share, model = resid.shape
    out = (weights[0].shape[0], share)
    return call(
        functools.partial(branch_kernel, n_grp, len(summands)), "branch_gradient", 1, [info],
        [cotangent, resid, gain, mid, *summands, *weights],
        [
            own_spec(batch, share, model), whole(resid.shape), whole(gain.shape),
            whole(mid.shape), *[whole(resid.shape) for _ in summands],
        ]
        + [anywhere()] * n_grp,
        [whole((share, model)), whole((16, model))] + [whole(out)] * n_grp,
        [sds((share, model), F32), sds((16, model), F32)] + [sds(out, BF)] * n_grp,
        [
            pltpu.VMEM((n_grp,) + weights[0].shape, BF),
            pltpu.SemaphoreType.DMA((n_grp,)),
        ],
    )


def run_tokens(info, batch, tokens, gain, d_resid, dqs, rests, weights, prev):
    n_grp = len(weights)
    batches, _, model = tokens.shape
    share = d_resid.shape[0]
    ins = [tokens, gain, d_resid, *dqs, *rests, *weights]
    specs = [
        own_spec(batch, share, model), whole(gain.shape), whole(d_resid.shape),
        *[front(a) for a in [*dqs, *rests]],
    ] + [anywhere()] * n_grp
    alias = {}
    if prev is not None:
        alias = {len(ins) + 1: 0}
        ins.append(prev)
        specs.append(anywhere())
    return call(
        functools.partial(tokens_kernel, n_grp), "token_gradient", 1, [info], ins, specs,
        pl.BlockSpec((1, share, model), lambda i, *_: (batch, 0, 0)),
        sds((batches, share, model), F32),
        [
            pltpu.VMEM((n_grp,) + weights[0].shape, BF),
            pltpu.VMEM((share, model), F32),
            pltpu.SemaphoreType.DMA((n_grp,)),
        ],
        alias,
    )


def run_mlp(info, batch, xs, cotangent, rings, prevs, sizes):
    n_grp = len(xs)
    share, model = xs[0].shape
    rows = share * n_grp
    depth = rings[0].parts[0].shape[0]
    layout = ring_layout(rings[0].count, depth)
    first = prevs is None
    prevs = [] if first else list(prevs)
    ins = [*xs, cotangent, *[part for ring in rings for part in ring.parts], *prevs]
    if first:
        out_shape = [sds((rows, model), BF)] * 2
    else:
        out_shape = [sds((share, model), BF)] * (2 * n_grp)
    scratch = [
        pltpu.VMEM((rows, model), BF),
        pltpu.VMEM((rows, model), BF),
        pltpu.VMEM((2, model, 3 * CHUNK), BF),
        pltpu.VMEM((rows, model), F32),
        pltpu.VMEM((rows, model), F32),
        pltpu.SemaphoreType.DMA((2,)),
        pltpu.SemaphoreType.DMA((2,)),
    ] + [pltpu.VMEM((rows, model), BF) for _ in prevs]
    return call(
        functools.partial(mlp_kernel, batch, n_grp, layout, sizes, first),
        "feed_forward", sum(sizes) // CHUNK, [info], ins, [anywhere()] * len(ins),
        [anywhere()] * len(out_shape), out_shape, scratch,
    )


def run_backward(
    info, lens, batch, q, kv, ve, halo, maps, o_in, att, weights, phi, states, inverse, d_outs, prevs,
):
    q_width, rows = q.shape
    width = kv.shape[1]
    heads, pairs = width // PAIR, rows // PAIR
    per = q_width // STRETCH // heads
    share = rows // len(d_outs)
    rev = lambda i: pairs - 1 - i
    step = lambda *shape: pl.BlockSpec((1,) + shape, lambda i, *_: (rev(i),) + (0,) * len(shape))
    column = lambda n: pl.BlockSpec((n, PAIR), lambda i, *_: (0, rev(i)))
    prevs = list(prevs or [])
    sums = [sds(maps.shape, F32)]
    return call(
        functools.partial(
            backward_kernel, batch, per, pairs, len(d_outs), bool(prevs), STRETCH ** (-0.5)
        ),
        "attention_backward", pairs, [info, lens],
        [q, kv, ve, halo, maps, o_in, att, weights, phi, states, inverse, *d_outs, *prevs],
        [
            column(q_width), whole(kv.shape), whole(ve.shape), whole(halo.shape),
            whole(maps.shape), whole(o_in.shape), block_spec(q_width + 16, share, rev),
            step(heads, WIN, per * PAIR), step(heads, PAIR, per * PAIR),
            step(heads, 2 * EXT, PAIR), step(heads * per, PAIR),
            *[anywhere() for _ in d_outs], *[whole(prev.shape) for prev in prevs],
        ],
        [
            block_spec(q_width, share, rev), whole((rows + STRETCH, width)), step(heads, 2 * EXT, PAIR),
            whole((heads, 2, EXT, PAIR)), whole((STRETCH, width)),
            *[whole(item.shape) for item in sums],
        ],
        [
            sds((rows // share, q_width, share), BF),
            sds((rows + STRETCH, width), F32),
            sds((pairs, heads, 2 * EXT, PAIR), F32),
            sds((heads, 2, EXT, PAIR), BF),
            sds((STRETCH, width), BF),
            *sums,
        ],
        [
            pltpu.VMEM((heads, EXT, PAIR), F32),
            pltpu.VMEM((rows + STRETCH, width), BF),
            pltpu.VMEM((rows + STRETCH, width), BF),
            pltpu.VMEM((pairs, q_width + 16, PAIR), BF),
            pltpu.SemaphoreType.DMA,
        ],
    )


def run_keys(
    info, lens, batch, kv, ve, maps, phi, d_kv, returned, d_states, d_q, q_up, kv_up, fars, prevs,
):
    width, rows = phi.shape
    heads, pairs = width // PAIR, rows // PAIR
    n_grp, q_width, share = d_q.shape
    count = lax.axis_size("seq")
    wide = max(1, count // 4)
    rev = lambda i: pairs - 1 - i
    column = lambda n: pl.BlockSpec((n, PAIR), lambda i, *_: (0, rev(i)))
    lines = lambda n: pl.BlockSpec((PAIR, n), lambda i, *_: (rev(i), 0))
    prevs = list(prevs or [])
    sums = [sds((heads, PAIR, STRETCH), F32)]
    return call(
        functools.partial(
            keys_kernel, batch, pairs, rows // STRETCH, wide, count, len(fars), bool(prevs)
        ),
        "attention_keys", pairs, [info, lens],
        [
            kv, ve, maps, phi, d_kv, returned, d_states, d_q, q_up, kv_up, *fars, *prevs,
        ],
        [
            lines(width), lines(width), whole(maps.shape), column(width), whole(d_kv.shape),
            whole(returned.shape),
            pl.BlockSpec((1, heads, 2 * EXT, PAIR), lambda i, *_: (rev(i), 0, 0, 0)),
            block_spec(q_width, share, rev), whole(q_up.shape), whole(kv_up.shape),
            *[whole(far.shape) for far in fars], *[whole(prev.shape) for prev in prevs],
        ],
        [block_spec(32 + width, share, rev), *[whole(item.shape) for item in sums]],
        [sds((n_grp, 32 + width, share), BF), *sums],
        [pltpu.VMEM((heads, 2, EXT, PAIR), F32)],
    )


def run_adapters(info, d_q, rest, mids, normed, att, d_outs, prevs):
    model = normed.shape[1]
    prevs = list(prevs or [])
    ins = [d_q, rest, mids, normed, att, *d_outs, *prevs]
    out_shape = [
        sds((32, d_q.shape[1] + rest.shape[1]), F32), sds((16, d_q.shape[1]), F32),
        sds((32, model), F32),
    ]
    return call(
        functools.partial(adapter_kernel, len(d_outs), bool(prevs)),
        "adapter_gradients", 1, [info], ins, [whole(item.shape) for item in ins],
        [whole(item.shape) for item in out_shape], out_shape,
    )


def summed(value, axis):
    value = value.astype(BF)
    bit = 1
    while bit < lax.axis_size(axis):
        value = (value.astype(F32) + flip(value, axis, bit).astype(F32)).astype(BF)
        bit *= 2
    return value


def local(
    tokens,
    cotangent,
    lengths,
    attention_norm_gain,
    feedforward_norm_gain,
    query_weight,
    keyvalue_weight,
    output_weight,
    gate_up_weight,
    down_weight,
    adapter_width_factor,
    query_up_factor,
    keyvalue_up_factor,
    output_input_factor,
    query_feature_weight,
    key_feature_weight,
):
    batches, rows, model = tokens.shape
    n_seq, n_grp = lax.axis_size("seq"), lax.axis_size("grp")
    group_index, seq_index = lax.axis_index("grp"), lax.axis_index("seq")
    share = rows // n_grp
    rank = adapter_width_factor.shape[2]
    depth, q_width = query_weight.shape
    kv_heads = key_feature_weight.shape[0]
    kv_width = kv_heads * PAIR
    per = query_feature_weight.shape[0] // kv_heads
    hidden_width = down_weight.shape[0]
    gain_attn = attention_norm_gain.astype(F32)[None]
    gain_mlp = feedforward_norm_gain.astype(F32)[None]

    sources = lax.dynamic_index_in_dim(
        jnp.asarray(ring_sources(n_seq), jnp.int32), seq_index, 0, False
    )
    info = jnp.concatenate(
        [jnp.stack([seq_index * (rows // STRETCH), group_index, seq_index]).astype(jnp.int32), sources]
    )

    kv_shard = (
        keyvalue_weight.reshape(depth, 2, kv_heads, STRETCH)
        .transpose(2, 1, 3, 0)
        .reshape(kv_width, depth)
    )
    adapters = adapter_width_factor.transpose(0, 2, 1)
    pad = jnp.zeros((rank, depth), BF)
    in_ring = Ring(
        jnp.concatenate(
            [
                query_weight.T, adapters[:3].reshape(3 * rank, depth), pad, kv_shard,
                output_weight, adapters[3], pad,
            ],
            axis=0,
        )
    )
    down_t = down_weight.T
    half_shards = [
        jnp.concatenate(
            [
                gate_up_weight[:, 0, first : first + size],
                gate_up_weight[:, 1, first : first + size],
                down_t[:, first : first + size],
            ],
            axis=1,
        )
        for first, size in pieces_of(hidden_width)
    ]
    ring_a, ring_b, ring_c = rings = [Ring(shard) for shard in half_shards]
    kv_parts = keyvalue_up_factor.reshape(2, rank, kv_heads, STRETCH)
    kv_up = jnp.zeros((2, rank, kv_heads, 2, STRETCH), BF)
    kv_up = kv_up.at[0, :, :, 0].set(kv_parts[0]).at[1, :, :, 1].set(kv_parts[1])
    kv_up = kv_up.reshape(2 * rank, kv_width)
    kv_up = jnp.concatenate(
        [jnp.zeros((rank, kv_width), BF), kv_up, jnp.zeros((rank, kv_width), BF)]
    )
    q_up = jnp.concatenate([query_up_factor, jnp.zeros((3 * rank, q_width), BF)])
    q_up_t = q_up.T
    o_in = jnp.concatenate([output_input_factor, jnp.zeros((q_width, rank), BF)], axis=1)
    maps_t = query_feature_weight.transpose(0, 2, 1).reshape(kv_heads, per, STRETCH, STRETCH)
    query_maps = jnp.zeros((kv_heads, per, STRETCH, per, STRETCH), BF)
    for g in range(per):
        query_maps = query_maps.at[:, g, :, g, :].set(maps_t[:, g])
    query_maps = query_maps.reshape(kv_heads, per * STRETCH, per * STRETCH)
    key_maps = jnp.concatenate(
        [key_feature_weight.transpose(0, 2, 1), jnp.zeros((kv_heads, STRETCH, STRETCH), BF)], axis=2
    )

    normed_rows = []
    for batch in range(batches):
        x = tokens[batch].astype(F32)
        factor = lax.rsqrt(jnp.mean(x * x, axis=-1, keepdims=True) + EPS)
        normed_rows.append((x * factor * gain_attn).astype(BF))
    in_ring.hop()
    in_ring.hop()
    query_maps, key_maps, kv_up, q_up_t, normed_rows[0] = in_ring.tie(
        query_maps, key_maps, kv_up, q_up_t, normed_rows[0]
    )
    in_ring.hop()
    for ring in rings[:2]:
        ring.ahead, ring.back, *_ = lax.optimization_barrier((ring.ahead, ring.back))
    normed_rows[1] = in_ring.tie(normed_rows[1])[0]
    while in_ring.done < in_ring.hops():
        in_ring.hop()
    ring_a.hop(*in_ring.parts[5:7])
    ring_b.hop(*in_ring.parts[5:7])
    weight_in, weight_out = run_assemble(
        info, in_ring, [q_width + 32 + kv_width, q_width + 2 * rank]
    )
    far_out = far_gather(weight_out)

    saved = []
    for batch in range(batches):
        normed = normed_rows[batch]
        q, kv, ve, mids, phi_key, states, ends, halo = run_project(
            info, lengths, batch, normed, weight_in, q_up_t, kv_up, key_maps
        )
        saved.append([q, kv, ve, mids, normed, phi_key, states, ends, halo])
    ends = jnp.stack([item[7] for item in saved])
    halo = jnp.stack([item[8] for item in saved])
    (ends,) = ring_a.tie(ends)
    (ends,) = ring_b.tie(ends)
    fars, halo = exchange(ends, halo, 1)
    for item in saved:
        item[7:] = [fars, halo]
    ring_a.hop(*fars[1:])
    ring_b.hop(*fars[1:])

    attended = []
    for batch in range(batches):
        q, kv, ve, mids, normed, phi_key, states, fars, halo = saved[batch]
        if batch:
            q = after(q, attended[0][0])
        att, weights, phi, sums, inverse = run_forward(
            info, lengths, batch, q, kv, ve, halo, query_maps, o_in, states, fars
        )
        atts = group_exchange([att[r] for r in range(n_grp)])
        attended.append([att, weights, phi, sums, inverse, atts])
    far_out = [far_out[0]] + [after(far, attended[0][0]) for far in far_out[1:]]
    weights_out = near_gather(far_out)
    mlp_ins = []
    for batch in range(batches):
        att, weights, phi, sums, inverse, atts = attended[batch]
        if batch:
            atts[-1] = after(atts[-1], mlp_ins[0][0])
        resid, mlp_in, mid = run_residual(
            info, batch, tokens, gain_mlp, [att, *atts[1:]], weights_out
        )
        if batch == 0:
            (mlp_in,) = ring_a.tie(mlp_in)
            (mlp_in,) = ring_b.tie(mlp_in)
            ring_a.hop(mlp_in)
            ring_b.hop(mlp_in)
        attended[batch][5:] = [resid, mid]
        mlp_ins.append(group_gather(mlp_in))
    ring_a.hop(mlp_ins[1][0])
    ring_b.hop(mlp_ins[1][0])
    ring_c.hop(mlp_ins[1][0], *ring_a.parts[-2:], *ring_b.parts[-2:])

    sizes = [size for _, size in pieces_of(hidden_width)]
    partial = [None] * batches
    ring_a.finish()
    ring_b.finish()
    partial[0] = list(
        run_mlp(info, 0, mlp_ins[0], cotangent, [ring_a, ring_b], None, sizes[:2])
    )
    partial[0][0], mlp_ins[1][0] = ring_c.tie(partial[0][0], mlp_ins[1][0])
    ring_c.hop()
    far_in = far_gather(after(weight_in, partial[0][0]))
    partial[1] = list(
        run_mlp(info, 1, mlp_ins[1], cotangent, [ring_a, ring_b], None, sizes[:2])
    )
    (partial[1][0],) = ring_c.tie(partial[1][0])
    ring_c.hop()
    ring_c.finish()
    far_in, partial[0][0] = lax.optimization_barrier((far_in, partial[0][0]))
    weights_in = near_gather(far_in)
    partial[0] = list(
        run_mlp(info, 0, mlp_ins[0], cotangent, [ring_c], partial[0], sizes[2:])
    )
    started = [scatter_start(partial[0][:n_grp])]
    started[0][0][0], partial[1][0] = lax.optimization_barrier((started[0][0][0], partial[1][0]))
    partial[1] = list(
        run_mlp(info, 1, mlp_ins[1], cotangent, [ring_c], partial[1], sizes[2:])
    )

    def run_branch_of(batch):
        resid, mid = attended[batch][5:]
        d_resid, wide, *d_out = run_branch(
            info, batch, cotangent, resid, gain_mlp, mid, scatter_end(*started[batch]), weights_out
        )
        return d_resid, wide, group_exchange(d_out)

    def run_backward_of(batch, q, d_outs, sums_back):
        _, kv, ve, mids, normed, phi_key, states, fars, halo = saved[batch]
        att, weights, phi, sums, inverse = attended[batch][:5]
        d_q, d_kv, d_states, ends, back, *sums_back = run_backward(
            info, lengths, batch, q, kv, ve, halo, query_maps, o_in, att, weights, phi, sums,
            inverse, d_outs, sums_back,
        )
        fars, returned = exchange(ends[None], back, -1)
        d_qs = group_exchange([d_q[r] for r in range(n_grp)])
        return [d_q, d_qs, d_kv, d_states, fars, returned], sums_back

    def run_keys_of(batch, kv, gone, sums_keys):
        _, _, ve, mids, normed, phi_key, states, _, _ = saved[batch]
        d_q, d_qs, d_kv, d_states, fars, returned = gone
        rest, *sums_keys = run_keys(
            info, lengths, batch, kv, ve, key_maps, phi_key, d_kv, returned, d_states, d_q, q_up,
            kv_up, fars, sums_keys,
        )
        rests = group_exchange([rest[r] for r in range(n_grp)])
        return [rest, *rests[1:]], sums_keys

    def run_adapters_of(batch, d_q, rest, d_outs, prevs):
        return run_adapters(
            info, d_q, rest, saved[batch][3], saved[batch][4], attended[batch][0], d_outs, prevs
        )

    def run_tokens_of(batch, d_resid, gone, rests, prev):
        d_q, d_qs = gone[:2]
        return run_tokens(
            info, batch, tokens, gain_attn, d_resid, [d_q, *d_qs[1:]], rests, weights_in, prev
        )

    d_resid_a, wide_a, d_outs_a = run_branch_of(0)
    partial[1][0] = after(partial[1][0], d_resid_a)
    started.append(scatter_start(partial[1][:n_grp]))
    started[1][0][0] = after(started[1][0][0], *d_outs_a[1:])
    gone_a, sums_back = run_backward_of(0, saved[0][0], d_outs_a, None)
    attended[1][6] = after(attended[1][6], gone_a[0])
    d_resid_b, wide_b, d_outs_b = run_branch_of(1)
    rests_a, sums_keys = run_keys_of(0, after(saved[0][1], d_resid_b), gone_a, None)
    gone_b, sums_back = run_backward_of(
        1, after(saved[1][0], rests_a[0]), d_outs_b, sums_back
    )
    sums_adapters = run_adapters_of(
        0, after(gone_a[0], gone_b[0]), rests_a[0], d_outs_a, None
    )
    grad_tokens = run_tokens_of(
        0, after(d_resid_a, sums_adapters[0]), gone_a, rests_a, None
    )
    rests_b, sums_keys = run_keys_of(1, after(saved[1][1], grad_tokens), gone_b, sums_keys)
    sums_adapters = run_adapters_of(1, gone_b[0], rests_b[0], d_outs_b, sums_adapters)
    grad_tokens = run_tokens_of(
        1, after(d_resid_b, sums_adapters[0]), gone_b, rests_b, grad_tokens
    )
    wide_out = wide_a + wide_b
    block_rows = []
    for batch, ready in enumerate([rests_a[0], rests_b[0]]):
        blocks = partial[batch][n_grp:]
        blocks[0] = after(blocks[0], ready)
        blocks[1], blocks[-1] = after(blocks[1], ready), after(blocks[-1], ready)
        total = attended[batch][5]
        for summand in scatter_end(*scatter_start(blocks)):
            total = total + summand.astype(F32)
        block_rows.append(total.astype(BF))

    (map_grad,), (key_grad,) = sums_back, sums_keys
    up_grad, oin_grad, wide_in = sums_adapters
    wide = jnp.concatenate([wide_in[: 3 * rank], wide_out[:rank]])
    up_grad = ADAPTER_SCALE * up_grad
    kv_grad = up_grad[rank : 3 * rank, q_width + 32 :].reshape(2, rank, kv_heads, 2, STRETCH)
    kv_grad = jnp.stack([kv_grad[0, :, :, 0], kv_grad[1, :, :, 1]])
    map_blocks = map_grad.reshape(kv_heads, per, STRETCH, per, STRETCH)
    query_grad = jnp.stack([map_blocks[:, g, :, g] for g in range(per)], axis=1)
    pieces = [
        (up_grad[:rank, :q_width], query_up_factor.shape),
        (kv_grad, keyvalue_up_factor.shape),
        (oin_grad[:rank].T, output_input_factor.shape),
        (query_grad, query_feature_weight.shape),
        (key_grad[:, :STRETCH], key_feature_weight.shape),
    ]
    wide = summed(wide, "grp")
    packed = jnp.concatenate(
        [wide.reshape(-1)] + [piece.astype(BF).reshape(-1) for piece, _ in pieces]
    ).reshape(-1, PAIR)
    packed = summed(packed, "seq").reshape(-1).astype(F32)
    wide = packed[: wide.size].reshape(4, rank, n_seq * n_grp, model // (n_seq * n_grp))
    wide = lax.dynamic_index_in_dim(wide, seq_index * n_grp + group_index, 2, False)
    outs, first = [], 4 * rank * model
    for piece, shape in pieces:
        outs.append(packed[first : first + piece.size].reshape(shape))
        first += piece.size
    return (jnp.stack(block_rows), grad_tokens, wide.transpose(0, 2, 1), *outs)


def solution(mesh):
    return jax.shard_map(
        local,
        mesh=mesh,
        in_specs=(
            P(None, "seq", None),
            P(None, "seq", None),
            P(),
            P(),
            P(),
            P("seq", "grp"),
            P("seq", None, "grp"),
            P("grp", "seq"),
            P("seq", None, "grp"),
            P("grp", "seq"),
            P(None, "seq", None),
            P(None, "grp"),
            P(None, None, "grp"),
            P("grp", None),
            P("grp", None, None),
            P("grp", None, None),
        ),
        out_specs=(
            P(None, ("seq", "grp"), None),
            P(None, ("seq", "grp"), None),
            P(None, ("seq", "grp"), None),
            P(None, "grp"),
            P(None, None, "grp"),
            P("grp", None),
            P("grp", None, None),
            P("grp", None, None),
        ),
        check_vma=False,
    )
```

time: 1100 us -> 779 us (0.71)
  Pallas kernels: 68.4 us -> 353 us
  matrix products: 271 us -> 0 us
  waiting for transfers between devices: 366 us -> 224 us
  local copies, waits for them, and re-layouts: 134 us -> 48.6 us
  between operations: 77.5 us -> 2.74 us
  other arithmetic: 55.7 us -> 39.9 us
  starting transfers between devices: 113 us -> 99.9 us
    pallas_call x8 -> x21, Pallas kernels: 68.4 us -> 353 us  [call(): pl.pallas_call(kernel, grid_spec=pltpu.PrefetchScalarGridSpec(num_scalar_...]
    dot_general x52 -> x0, matrix products: 271 us -> none  [dotg(): lax.dot_general(left, right, (((lc,), (rc,)), ((), ())), preferred_elemen...]
    ppermute x32, waiting for transfers between devices: 210 us -> 124 us  [move(): return lax.ppermute(value, 'seq', pairs)]
    ppermute x41 -> x56, waiting for transfers between devices: 146 us -> 96.4 us  [flip(): return lax.ppermute(value, axis, [(i, i ^ bit) for i in range(count)])]
    dynamic_update_slice x36 -> x0, local copies, waits for them, and re-layouts: 26.8 us -> none  [ring_gather(): out = lax.dynamic_update_slice_in_dim(out, part, source * rows + first, 0)]
    ppermute x32 -> x12, starting transfers between devices: 55.3 us -> 31.2 us  [shifted(): lax.ppermute(value, axis, [(i, i + steps) for i in range(first, last)])]
    slice x43 -> x22, local copies, waits for them, and re-layouts: 27.2 us -> 11.3 us  [the longest x2 3.98 us: local(): gate_up_weight[:, 0, first:first + size]]
    dot_general x2 -> x0, local copies, waits for them, and re-layouts: 13.3 us -> none  [dotg(): lax.dot_general(left, right, (((lc,), (rc,)), ((), ())), preferred_elemen...]
  transfers between devices with their start and end apart: 105 -> 100, of which waited for: 36 -> 44; matrix products, arithmetic and copies ran while one was open for 37% -> 9% of each run, Pallas kernels for 5% -> 40%
where the time goes in v2:
time: 779 us; the launch traced here: 768 us
  Pallas kernels  353 us (45%)
  waiting for transfers between devices  224 us (29%)
  starting transfers between devices  99.9 us (13%)
  local copies, waits for them, and re-layouts  48.6 us (6%)
  other arithmetic  39.9 us (5%)
    pallas_call x21, Pallas kernels, call(): pl.pallas_call(kernel, grid_spec=pltpu.PrefetchScalarGridSpec(num_scalar_...  353 us
    ppermute x32, waiting for transfers between devices, move(): return lax.ppermute(value, 'seq', pairs)  124 us
    ppermute x56, waiting for transfers between devices, flip(): return lax.ppermute(value, axis, [(i, i ^ bit) for i in range(count)])  96.4 us
    ppermute x56, starting transfers between devices, flip(): return lax.ppermute(value, axis, [(i, i ^ bit) for i in range(count)])  36.3 us
    ppermute x32, starting transfers between devices, move(): return lax.ppermute(value, 'seq', pairs)  32.4 us
    ppermute x12, starting transfers between devices, shifted(): lax.ppermute(value, axis, [(i, i + steps) for i in range(first, last)])  31.2 us
    unnamed x211, local copies, waits for them, and re-layouts  16.1 us
  transfers between devices with their start and end apart: 100, of which 44 were waited for; matrix products, arithmetic and copies ran while one was open for 9% of the time, Pallas kernels for 40%

profile of v2, /device:TPU:0, one launch (start us, length us, event | category | flops | bytes accessed | tf_op | source)
XLA Modules:
  0.0 768.0 jit_solution(2246892140706293941)
XLA Ops:
  5.4 3.0 collective-permute-start
  13.2 4.4 fusion.3
  17.6 6.0 collective-permute-done.refs_1_
  27.3 6.8 fusion.5
  34.0 7.0 collective-permute-done.2.refs_3_
  46.9 10.3 %collective-permute-done.4.refs_5_ = bf16[1328,256]{1,0:T(8,128)(2,1)S(1)} collective-permute-done((bf16[1328,256]{1,0:T(8,128)(2,1)S(1)}, bf16[1328,256]{1,0:T(8,128)(2,1)S(1)}, u32[]{:S(2)}, u32[]{:S(2)}) %collective-permute-start.4) | collective-permute-done | bytes 679968 | tf_op jit(solution)/shard_map/ppermute | solution.py:77
  57.2 2.3 collective-permute-done.5.refs_6_
  62.2 4.5 collective-permute-done.7.refs_8_
  68.2 6.4 assemble.1
  82.1 17.1 %project_states.3 = (bf16[512,1024]{1,0:T(8,128)(2,1)}, bf16[1024,256]{1,0:T(8,128)(2,1)}, bf16[1024,256]{1,0:T(8,128)(2,1)}, bf16[32,1024]{1,0:T(8,128)(2,1)}, ...) custom-call(s32[11]{0:T(128)} %pad_add_fusion.info, ...), custom_call_target="tpu_custom_call" | custom-call | bytes 1024 | tf_op jit(solution)/shard_map/project_states/pallas_call | solution.py:815
  99.3 17.3 %project_states.2 = (bf16[512,1024]{1,0:T(8,128)(2,1)}, bf16[1024,256]{1,0:T(8,128)(2,1)}, bf16[1024,256]{1,0:T(8,128)(2,1)}, bf16[32,1024]{1,0:T(8,128)(2,1)}, ...) custom-call(s32[11]{0:T(128)} %pad_add_fusion.info, ...), custom_call_target="tpu_custom_call" | custom-call | bytes 1024 | tf_op jit(solution)/shard_map/project_states/pallas_call | solution.py:815
  118.0 4.9 collective-permute-done.13
  122.9 3.5 collective-permute-start.14
  129.9 2.5 collective-permute-start.16
  132.4 13.1 %collective-permute-start.15 = (bf16[2,2,2,1,80,128]{5,4,3,2,1,0:T(8,128)(2,1)}, bf16[2,2,2,1,80,128]{5,4,3,2,1,0:T(8,128)(2,1)S(1)}, u32[]{:S(2)}, u32[]{:S(2)}) collective-permute-start(bf16[2,2,2,1,80,128]{5,4,3,2,1,0:T(8,128)(2,1)} %fusion.8), channel_id=1, source_target_pairs={{0,16},{4,20},{8,24},{12,28},{1,17},{5,21},{9,25},{13,29},{2,18},{... | collective-permute-start | bytes 491528 | tf_op jit(solution)/shard_map/ppermute | solution.py:114
  149.1 11.2 %attention_forward.2 = (bf16[4,528,256]{2,1,0:T(8,128)(2,1)}, bf16[8,2,192,512]{3,2,1,0:T(8,128)(2,1)}, bf16[8,2,128,512]{3,2,1,0:T(8,128)(2,1)}, bf16[8,2,160,128]{3,2,1,0:T(8,128)(2,1)}, f32[8,8,128]{2,1,0:T(8,128)}) custom-call(s32[11]{0:T(128)} %pad_add_fusion.info, s32[2,6]{1,0:T(2,128)} %lens.15, bf16[512,1024]{1,0:T(8,128)(2,1)} %get-tuple-element.276.q_ref, ...), custom_call_target="tpu_custom_call" | custom-call | bytes 1024 | tf_op jit(solution)/shard_map/attention_forward/pallas_call | solution.py:815
  163.8 6.0 collective-permute-done.19.refs_3_
  169.8 6.4 collective-permute-done.18.refs_2_
  178.3 11.3 %attention_forward.3 = (bf16[4,528,256]{2,1,0:T(8,128)(2,1)}, bf16[8,2,192,512]{3,2,1,0:T(8,128)(2,1)}, bf16[8,2,128,512]{3,2,1,0:T(8,128)(2,1)}, bf16[8,2,160,128]{3,2,1,0:T(8,128)(2,1)}, f32[8,8,128]{2,1,0:T(8,128)}) custom-call(s32[11]{0:T(128)} %pad_add_fusion.info, s32[2,6]{1,0:T(2,128)} %lens.15, bf16[512,1024]{1,0:T(8,128)(2,1)} %get-tuple-element.394.q_ref, ...), custom_call_target="tpu_custom_call" | custom-call | bytes 1024 | tf_op jit(solution)/shard_map/attention_forward/pallas_call | solution.py:815
  192.9 9.3 %residual.2 = (f32[256,2048]{1,0:T(8,128)}, bf16[256,2048]{1,0:T(8,128)(2,1)}, bf16[16,256]{1,0:T(8,128)(2,1)}) custom-call(s32[11]{0:T(128)} %pad_add_fusion.info, bf16[2,1024,2048]{2,1,0:T(8,128)(2,1)} %x_ref.7, f32[1,2048]{1,0:T(1,128)} %bitcast.181, bf16[4,528,256]{2,1,0:T(8,128)(2,1)} %get-tuple-element.296.refs_0_.att_ref, ...), custom_call_target="tpu_custom_call" | custom-call | bytes 1024 | tf_op jit(solution)/shard_map/residual/pallas_call | solution.py:815
  202.2 5.0 collective-permute-done.23.refs_17_
  207.3 5.1 collective-permute-done.24.refs_18_
  217.1 6.2 collective-permute-done.31.refs_2_
  223.3 2.5 fusion.21
  226.5 9.2 %residual.3 = (f32[256,2048]{1,0:T(8,128)}, bf16[256,2048]{1,0:T(8,128)(2,1)}, bf16[16,256]{1,0:T(8,128)(2,1)}) custom-call(s32[11]{0:T(128)} %pad_add_fusion.info, bf16[2,1024,2048]{2,1,0:T(8,128)(2,1)} %x_ref.7, f32[1,2048]{1,0:T(1,128)} %bitcast.182, bf16[4,528,256]{2,1,0:T(8,128)(2,1)} %get-tuple-element.316.refs_0_.att_ref, ...), custom_call_target="tpu_custom_call" | custom-call | bytes 1024 | tf_op jit(solution)/shard_map/residual/pallas_call | solution.py:815
  235.8 11.9 %collective-permute-done.33.refs_10_ = bf16[256,1536]{1,0:T(8,128)(2,1)S(1)} collective-permute-done((bf16[256,1536]{1,0:T(8,128)(2,1)}, bf16[256,1536]{1,0:T(8,128)(2,1)S(1)}, u32[]{:S(2)}, u32[]{:S(2)}) %collective-permute-start.33) | collective-permute-done | bytes 786464 | tf_op jit(solution)/shard_map/ppermute | solution.py:77
  254.6 7.4 collective-permute-done.40.refs_22_
  262.3 5.0 collective-permute-done.36.refs_13_
  274.8 36.9 %feed_forward.4 = (bf16[1024,2048]{1,0:T(8,128)(2,1)}, bf16[1024,2048]{1,0:T(8,128)(2,1)}) custom-call(s32[11]{0:T(128)} %pad_add_fusion.info, bf16[256,2048]{1,0:T(8,128)(2,1)} %get-tuple-element.310.refs_0_, bf16[256,2048]{1,0:T(8,128)(2,1)} %collective-permute-done.27.refs_1_, bf16[256,2048]{1,0:T(8,128)(2,1)} %collective-permute-done.28.refs_2_, ...), custom_call_target="tpu_custom_call" | custom-call | bytes 1024 | tf_op jit(solution)/shard_map/feed_forward/pallas_call | solution.py:815
  315.0 3.0 collective-permute-done.45.refs_1_
  319.1 37.0 %feed_forward.5 = (bf16[1024,2048]{1,0:T(8,128)(2,1)}, bf16[1024,2048]{1,0:T(8,128)(2,1)}) custom-call(s32[11]{0:T(128)} %pad_add_fusion.info, bf16[256,2048]{1,0:T(8,128)(2,1)} %get-tuple-element.338.refs_0_, bf16[256,2048]{1,0:T(8,128)(2,1)} %copy-done.19, bf16[256,2048]{1,0:T(8,128)(2,1)} %collective-permute-done.46.refs_2_, ...), custom_call_target="tpu_custom_call" | custom-call | bytes 1024 | tf_op jit(solution)/shard_map/feed_forward/pallas_call | solution.py:815
  359.3 34.6 %collective-permute-done.48.refs_10_ = bf16[256,3072]{1,0:T(8,128)(2,1)S(1)} collective-permute-done((bf16[256,3072]{1,0:T(8,128)(2,1)}, bf16[256,3072]{1,0:T(8,128)(2,1)S(1)}, u32[]{:S(2)}, u32[]{:S(2)}) %collective-permute-start.48) | collective-permute-done | bytes 1572896 | tf_op jit(solution)/shard_map/ppermute | solution.py:77
  397.7 16.2 %collective-permute-done.51.refs_13_ = bf16[128,3072]{1,0:T(8,128)(2,1)S(1)} collective-permute-done((bf16[128,3072]{1,0:T(8,128)(2,1)S(1)}, bf16[128,3072]{1,0:T(8,128)(2,1)S(1)}, u32[]{:S(2)}, u32[]{:S(2)}) %collective-permute-start.51) | collective-permute-done | bytes 786464 | tf_op jit(solution)/shard_map/ppermute | solution.py:77
  414.9 40.0 %feed_forward.6 = (bf16[256,2048]{1,0:T(8,128)(2,1)}, bf16[256,2048]{1,0:T(8,128)(2,1)}, bf16[256,2048]{1,0:T(8,128)(2,1)}, bf16[256,2048]{1,0:T(8,128)(2,1)}, b...) custom-call(s32[11]{0:T(128)} %pad_add_fusion.info, ...), custom_call_target="tpu_custom_call" | custom-call | bytes 1024 | tf_op jit(solution)/shard_map/feed_forward/pallas_call | solution.py:815
  455.4 2.4 collective-permute-done.54
  457.8 2.6 add_convert_fusion.5
  460.9 40.5 %feed_forward.7 = (bf16[256,2048]{1,0:T(8,128)(2,1)}, bf16[256,2048]{1,0:T(8,128)(2,1)}, bf16[256,2048]{1,0:T(8,128)(2,1)}, bf16[256,2048]{1,0:T(8,128)(2,1)}, b...) custom-call(s32[11]{0:T(128)} %pad_add_fusion.info, ...), custom_call_target="tpu_custom_call" | custom-call | bytes 1024 | tf_op jit(solution)/shard_map/feed_forward/pallas_call | solution.py:815
  503.4 11.2 %branch_gradient.2 = (f32[256,2048]{1,0:T(8,128)}, f32[16,2048]{1,0:T(8,128)}, bf16[528,256]{1,0:T(8,128)(2,1)}, bf16[528,256]{1,0:T(8,128)(2,1)}, bf16[528,256]{1,0:T(8,128)(2,1)}, /*index=5*/bf16[528,256]{1,0:T(8,128)(2,1)}) custom-call(s32[11]{0:T(128)} %pad_add_fusion.info, bf16[2,1024,2048]{2,1,0:T(8,128)(2,1)} %dy_ref.3, ...), custom_call_target="tpu_custom_call" | custom-call | bytes 1024 | tf_op jit(solution)/shard_map/branch_gradient/pallas_call | solution.py:815
  516.6 2.6 add_convert_fusion.4
  519.8 4.8 collective-permute-done.57.refs_2_
  524.6 4.0 collective-permute-done.58.refs_3_
  530.2 18.5 %attention_backward.2 = (bf16[4,512,256]{2,1,0:T(8,128)(2,1)}, f32[1088,256]{1,0:T(8,128)}, f32[8,2,160,128]{3,2,1,0:T(8,128)}, bf16[2,2,80,128]{3,2,1,0:T(8,128...) custom-call(s32[11]{0:T(128)} %pad_add_fusion.info, s32[2,6]{1,0:T(2,128)} %lens.15, ...), custom_call_target="tpu_custom_call" | custom-call | bytes 1024 | tf_op jit(solution)/shard_map/attention_backward/pallas_call | solution.py:815
  549.1 4.7 collective-permute-done.63
  564.4 11.2 %branch_gradient.3 = (f32[256,2048]{1,0:T(8,128)}, f32[16,2048]{1,0:T(8,128)}, bf16[528,256]{1,0:T(8,128)(2,1)}, bf16[528,256]{1,0:T(8,128)(2,1)}, bf16[528,256]{1,0:T(8,128)(2,1)}, /*index=5*/bf16[528,256]{1,0:T(8,128)(2,1)}) custom-call(s32[11]{0:T(128)} %pad_add_fusion.info, bf16[2,1024,2048]{2,1,0:T(8,128)(2,1)} %dy_ref.3, ...), custom_call_target="tpu_custom_call" | custom-call | bytes 1024 | tf_op jit(solution)/shard_map/branch_gradient/pallas_call | solution.py:815
  579.1 10.9 %attention_keys.2 = (bf16[4,288,256]{2,1,0:T(8,128)(2,1)}, f32[2,128,64]{2,1,0:T(8,128)}) custom-call(s32[11]{0:T(128)} %pad_add_fusion.info, s32[2,6]{1,0:T(2,128)} %lens.15, bf16[1024,256]{1,0:T(8,128)(2,1)} %get-tuple-element.380.kv_ref, bf16[1024,256]{1,0:T(8,128)(2,1)} %get-tuple-element.278.ve_ref, bf16[2,64,128]{2,1,0:T(8,128)(2,1)} %concatenate.48.wk_ref, ...), custom_call_target="tpu_custom_call" | custom-call | bytes 1024 | tf_op jit(solution)/shard_map/attention_keys/pallas_call | solution.py:815
  594.6 18.5 %attention_backward.3 = (bf16[4,512,256]{2,1,0:T(8,128)(2,1)}, f32[1088,256]{1,0:T(8,128)}, f32[8,2,160,128]{3,2,1,0:T(8,128)}, bf16[2,2,80,128]{3,2,1,0:T(8,128...) custom-call(s32[11]{0:T(128)} %pad_add_fusion.info, s32[2,6]{1,0:T(2,128)} %lens.15, ...), custom_call_target="tpu_custom_call" | custom-call | bytes 1024 | tf_op jit(solution)/shard_map/attention_backward/pallas_call | solution.py:815
  628.3 6.1 adapter_gradients.2
  635.2 11.5 %token_gradient.2.refs_12_ = f32[2,256,2048]{2,1,0:T(8,128)} custom-call(s32[11]{0:T(128)} %pad_add_fusion.info, bf16[2,1024,2048]{2,1,0:T(8,128)(2,1)} %x_ref.7, f32[1,2048]{1,0:T(1,128)} %bitcast.190, f32[256,2048]{1,0:T(8,128)} %get-tuple-element.408.d_resid_ref, bf16[4,512,256]{2,1,0:T(8,128)(2,1)} %get-tuple-element.405.dq_ref.refs_0_, ...), custom_call_target="tpu_custom_call" | custom-call | bytes 1024 | tf_op jit(solution)/shard_map/token_gradient/pallas_call | solution.py:815
  647.4 11.2 %attention_keys.3 = (bf16[4,288,256]{2,1,0:T(8,128)(2,1)}, f32[2,128,64]{2,1,0:T(8,128)}) custom-call(s32[11]{0:T(128)} %pad_add_fusion.info, s32[2,6]{1,0:T(2,128)} %lens.15, bf16[1024,256]{1,0:T(8,128)(2,1)} %get-tuple-element.411.kv_ref, bf16[1024,256]{1,0:T(8,128)(2,1)} %get-tuple-element.314.ve_ref, bf16[2,64,128]{2,1,0:T(8,128)(2,1)} %concatenate.48.wk_ref, ...), custom_call_target="tpu_custom_call" | custom-call | bytes 1024 | tf_op jit(solution)/shard_map/attention_keys/pallas_call | solution.py:815
  658.6 6.3 adapter_gradients.3
  670.7 3.6 collective-permute-done.96
  674.4 2.3 collective-permute-start.97
  678.7 3.3 collective-permute-done.97
  682.8 2.6 collective-permute-start.98
  686.2 4.2 collective-permute-done.90.refs_2_
  691.7 2.2 collective-permute-done.94.refs_7_
  693.9 3.1 collective-permute-done.93.refs_6_
  697.8 11.5 %token_gradient.3 = f32[2,256,2048]{2,1,0:T(8,128)} custom-call(s32[11]{0:T(128)} %pad_add_fusion.info, bf16[2,1024,2048]{2,1,0:T(8,128)(2,1)} %x_ref.7, f32[1,2048]{1,0:T(1,128)} %bitcast.191, f32[256,2048]{1,0:T(8,128)} %get-tuple-element.429.d_resid_ref, bf16[4,512,256]{2,1,0:T(8,128)(2,1)} %get-tuple-element.404.dq_ref.refs_0_, ...), custom_call_target="tpu_custom_call", output_to_operand_aliasing={{}: (16, {})} | custom-call | bytes 1024 | tf_op jit(solution)/shard_map/token_gradient/pallas_call | solution.py:815
  710.3 4.2 collective-permute-start.99
  716.8 9.0 %collective-permute-done.99 = bf16[912,128]{1,0:T(8,128)(2,1)S(1)} collective-permute-done((bf16[912,128]{1,0:T(8,128)(2,1)S(1)}, bf16[912,128]{1,0:T(8,128)(2,1)S(1)}, u32[]{:S(2)}, u32[]{:S(2)}) %collective-permute-start.99) | collective-permute-done | bytes 233504 | tf_op jit(solution)/shard_map/ppermute | solution.py:108
  738.8 3.4 collective-permute-done.69
  742.2 2.5 fusion.6
  744.8 19.2 %collective-permute-done.88 = bf16[256,2048]{1,0:T(8,128)(2,1)} collective-permute-done((bf16[256,2048]{1,0:T(8,128)(2,1)S(1)}, bf16[256,2048]{1,0:T(8,128)(2,1)}, u32[]{:S(2)}, u32[]{:S(2)}) %collective-permute-start.88) | collective-permute-done | bytes 1048608 | tf_op jit(solution)/shard_map/ppermute | solution.py:108
  763.9 2.2 fusion.7
  (473 shorter events, 151.9 us)
Async XLA Ops:
  5.4 18.2 %collective-permute-start = (bf16[1328,256]{1,0:T(8,128)(2,1)S(1)}, bf16[1328,256]{1,0:T(8,128)(2,1)S(1)}, u32[]{:S(2)}, u32[]{:S(2)}) collective-permute-start(bf16[1328,256]{1,0:T(8,128)(2,1)S(1)} %constant_dynamic-update-slice_fusion.refs_0_), channel_id=1, source_target_pairs={{0,8},{8,16},{16,24},{24,28},{28,20},{20,12},{12,4},{4,0},{1,9},{9... | collective-permute-start | bytes 2039816 | tf_op jit(solution)/shard_map/ppermute | solution.py:77
  8.4 16.8 %collective-permute-start.1 = (bf16[1328,256]{1,0:T(8,128)(2,1)S(1)}, bf16[1328,256]{1,0:T(8,128)(2,1)}, u32[]{:S(2)}, u32[]{:S(2)}) collective-permute-start(bf16[1328,256]{1,0:T(8,128)(2,1)S(1)} %constant_dynamic-update-slice_fusion.refs_0_), channel_id=1, source_target_pairs={{0,4},{8,0},{16,8},{24,16},{28,24},{20,28},{12,20},{4,12},{1,5},{9... | collective-permute-start | bytes 2039816 | tf_op jit(solution)/shard_map/ppermute | solution.py:77
  25.2 15.8 %collective-permute-start.2 = (bf16[1328,256]{1,0:T(8,128)(2,1)S(1)}, bf16[1328,256]{1,0:T(8,128)(2,1)S(1)}, u32[]{:S(2)}, u32[]{:S(2)}) collective-permute-start(bf16[1328,256]{1,0:T(8,128)(2,1)S(1)} %collective-permute-done.refs_1_), channel_id=1, source_target_pairs={{0,8},{8,16},{16,24},{24,28},{28,20},{20,12},{12,4},{4,0},{1,9},{9... | collective-permute-start | bytes 2039816 | tf_op jit(solution)/shard_map/ppermute | solution.py:77
  26.8 15.7 %collective-permute-start.3 = (bf16[1328,256]{1,0:T(8,128)(2,1)}, bf16[1328,256]{1,0:T(8,128)(2,1)S(1)}, u32[]{:S(2)}, u32[]{:S(2)}) collective-permute-start(bf16[1328,256]{1,0:T(8,128)(2,1)} %collective-permute-done.1.refs_2_), channel_id=1, source_target_pairs={{0,4},{8,0},{16,8},{24,16},{28,24},{20,28},{12,20},{4,12},{1,5},{9... | collective-permute-start | bytes 2039816 | tf_op jit(solution)/shard_map/ppermute | solution.py:77
  44.1 15.3 %collective-permute-start.5 = (bf16[1328,256]{1,0:T(8,128)(2,1)S(1)}, bf16[1328,256]{1,0:T(8,128)(2,1)S(1)}, u32[]{:S(2)}, u32[]{:S(2)}) collective-permute-start(bf16[1328,256]{1,0:T(8,128)(2,1)S(1)} %collective-permute-done.3.refs_4_), channel_id=1, source_target_pairs={{0,4},{8,0},{16,8},{24,16},{28,24},{20,28},{12,20},{4,12},{1,5},{9... | collective-permute-start | bytes 2039816 | tf_op jit(solution)/shard_map/ppermute | solution.py:77
  74.6 85.7 %collective-permute-start.21 = (bf16[528,2048]{1,0:T(8,128)(2,1)}, bf16[528,2048]{1,0:T(8,128)(2,1)}, u32[]{:S(2)}, u32[]{:S(2)}) collective-permute-start(bf16[528,2048]{1,0:T(8,128)(2,1)} %get-tuple-element.297.refs_4_.refs_3_), channel_id=1, source_target_pairs={{0,2},{1,3},{2,0},{3,1},{4,6},{5,7},{6,4},{7,5},{8,10},{9,11},{10,... | collective-permute-start | bytes 6488072 | tf_op jit(solution)/shard_map/ppermute | solution.py:108
  77.3 40.2 %collective-permute-start.11 = (bf16[256,1536]{1,0:T(8,128)(2,1)S(1)}, bf16[256,1536]{1,0:T(8,128)(2,1)}, u32[]{:S(2)}, u32[]{:S(2)}) collective-permute-start(bf16[256,1536]{1,0:T(8,128)(2,1)S(1)} %pad_maximum_fusion.3.refs_5_), channel_id=1, source_target_pairs={{0,8},{8,16},{16,24},{24,28},{28,20},{20,12},{12,4},{4,0},{1,9},{9... | collective-permute-start | bytes 2359304 | tf_op jit(solution)/shard_map/ppermute | solution.py:77
  78.8 38.7 %collective-permute-start.12 = (bf16[256,1536]{1,0:T(8,128)(2,1)S(1)}, bf16[256,1536]{1,0:T(8,128)(2,1)}, u32[]{:S(2)}, u32[]{:S(2)}) collective-permute-start(bf16[256,1536]{1,0:T(8,128)(2,1)S(1)} %pad_maximum_fusion.3.refs_5_), channel_id=1, source_target_pairs={{0,4},{8,0},{16,8},{24,16},{28,24},{20,28},{12,20},{4,12},{1,5},{9... | collective-permute-start | bytes 2359304 | tf_op jit(solution)/shard_map/ppermute | solution.py:77
  79.3 38.2 %collective-permute-start.9 = (bf16[256,1536]{1,0:T(8,128)(2,1)}, bf16[256,1536]{1,0:T(8,128)(2,1)}, u32[]{:S(2)}, u32[]{:S(2)}) collective-permute-start(bf16[256,1536]{1,0:T(8,128)(2,1)} %pad_maximum_fusion.2.refs_14_), channel_id=1, source_target_pairs={{0,8},{8,16},{16,24},{24,28},{28,20},{20,12},{12,4},{4,0},{1,9},{9... | collective-permute-start | bytes 2359304 | tf_op jit(solution)/shard_map/ppermute | solution.py:77
  80.8 36.7 %collective-permute-start.10 = (bf16[256,1536]{1,0:T(8,128)(2,1)}, bf16[256,1536]{1,0:T(8,128)(2,1)}, u32[]{:S(2)}, u32[]{:S(2)}) collective-permute-start(bf16[256,1536]{1,0:T(8,128)(2,1)} %pad_maximum_fusion.2.refs_14_), channel_id=1, source_target_pairs={{0,4},{8,0},{16,8},{24,16},{28,24},{20,28},{12,20},{4,12},{1,5},{9... | collective-permute-start | bytes 2359304 | tf_op jit(solution)/shard_map/ppermute | solution.py:77
  118.0 60.2 %collective-permute-start.20 = (bf16[528,2048]{1,0:T(8,128)(2,1)S(1)}, bf16[528,2048]{1,0:T(8,128)(2,1)}, u32[]{:S(2)}, u32[]{:S(2)}) collective-permute-start(bf16[528,2048]{1,0:T(8,128)(2,1)S(1)} %copy-done.1), channel_id=1, source_target_pairs={{0,1},{1,0},{2,3},{3,2},{4,5},{5,4},{6,7},{7,6},{8,9},{9,8},{10,11... | collective-permute-start | bytes 6488072 | tf_op jit(solution)/shard_map/ppermute | solution.py:108
  122.9 25.4 %collective-permute-start.14 = (bf16[2,2,2,2,80,128]{5,4,3,2,1,0:T(8,128)(2,1)S(1)}, bf16[2,2,2,2,80,128]{5,4,3,2,1,0:T(8,128)(2,1)S(1)}, u32[]{:S(2)}, u32[]{:S(2)}) collective-permute-start(bf16[2,2,2,2,80,128]{5,4,3,2,1,0:T(8,128)(2,1)S(1)} %pad_maximum_fusion.4.refs_0_), channel_id=1, source_target_pairs={{0,8},{4,12},{8,16},{12,20},{16,24},{20,28},{1,9},{5,13},{9,17},{1... | collective-permute-start | bytes 983048 | tf_op jit(solution)/shard_map/ppermute | solution.py:114
  129.9 16.4 %collective-permute-start.16 = (bf16[2,2,2,1,80,128]{5,4,3,2,1,0:T(8,128)(2,1)}, bf16[2,2,2,1,80,128]{5,4,3,2,1,0:T(8,128)(2,1)S(1)}, u32[]{:S(2)}, u32[]{:S(2)}) collective-permute-start(bf16[2,2,2,1,80,128]{5,4,3,2,1,0:T(8,128)(2,1)} %fusion.8), channel_id=1, source_target_pairs={{0,24},{4,28},{1,25},{5,29},{2,26},{6,30},{3,27},{7,31}} | collective-permute-start | bytes 491528 | tf_op jit(solution)/shard_map/ppermute | solution.py:114
  132.4 16.0 %collective-permute-start.15 = (bf16[2,2,2,1,80,128]{5,4,3,2,1,0:T(8,128)(2,1)}, bf16[2,2,2,1,80,128]{5,4,3,2,1,0:T(8,128)(2,1)S(1)}, u32[]{:S(2)}, u32[]{:S(2)}) collective-permute-start(bf16[2,2,2,1,80,128]{5,4,3,2,1,0:T(8,128)(2,1)} %fusion.8), channel_id=1, source_target_pairs={{0,16},{4,20},{8,24},{12,28},{1,17},{5,21},{9,25},{13,29},{2,18},{... | collective-permute-start | bytes 491528 | tf_op jit(solution)/shard_map/ppermute | solution.py:114
  160.3 31.3 %collective-permute-start.22 = (bf16[528,2048]{1,0:T(8,128)(2,1)}, bf16[528,2048]{1,0:T(8,128)(2,1)S(1)}, u32[]{:S(2)}, u32[]{:S(2)}) collective-permute-start(bf16[528,2048]{1,0:T(8,128)(2,1)} %collective-permute-done.21.refs_6_.refs_5_), channel_id=1, source_target_pairs={{0,1},{1,0},{2,3},{3,2},{4,5},{5,4},{6,7},{7,6},{8,9},{9,8},{10,11... | collective-permute-start | bytes 6488072 | tf_op jit(solution)/shard_map/ppermute | solution.py:108
  169.8 32.4 %collective-permute-start.25 = (bf16[256,1536]{1,0:T(8,128)(2,1)}, bf16[256,1536]{1,0:T(8,128)(2,1)}, u32[]{:S(2)}, u32[]{:S(2)}) collective-permute-start(bf16[256,1536]{1,0:T(8,128)(2,1)} %collective-permute-done.11.refs_6_), channel_id=1, source_target_pairs={{0,8},{8,16},{16,24},{24,28},{28,20},{20,12},{12,4},{4,0},{1,9},{9... | collective-permute-start | bytes 2359304 | tf_op jit(solution)/shard_map/ppermute | solution.py:77
  176.2 26.0 %collective-permute-start.26 = (bf16[256,1536]{1,0:T(8,128)(2,1)}, bf16[256,1536]{1,0:T(8,128)(2,1)}, u32[]{:S(2)}, u32[]{:S(2)}) collective-permute-start(bf16[256,1536]{1,0:T(8,128)(2,1)} %collective-permute-done.12.refs_7_), channel_id=1, source_target_pairs={{0,4},{8,0},{16,8},{24,16},{28,24},{20,28},{12,20},{4,12},{1,5},{9... | collective-permute-start | bytes 2359304 | tf_op jit(solution)/shard_map/ppermute | solution.py:77
  176.2 31.0 %collective-permute-start.23 = (bf16[256,1536]{1,0:T(8,128)(2,1)}, bf16[256,1536]{1,0:T(8,128)(2,1)}, u32[]{:S(2)}, u32[]{:S(2)}) collective-permute-start(bf16[256,1536]{1,0:T(8,128)(2,1)} %collective-permute-done.9.refs_15_), channel_id=1, source_target_pairs={{0,8},{8,16},{16,24},{24,28},{28,20},{20,12},{12,4},{4,0},{1,9},{9... | collective-permute-start | bytes 2359304 | tf_op jit(solution)/shard_map/ppermute | solution.py:77
  178.2 34.2 %collective-permute-start.24 = (bf16[256,1536]{1,0:T(8,128)(2,1)}, bf16[256,1536]{1,0:T(8,128)(2,1)}, u32[]{:S(2)}, u32[]{:S(2)}) collective-permute-start(bf16[256,1536]{1,0:T(8,128)(2,1)} %collective-permute-done.10.refs_16_), channel_id=1, source_target_pairs={{0,4},{8,0},{16,8},{24,16},{28,24},{20,28},{12,20},{4,12},{1,5},{9... | collective-permute-start | bytes 2359304 | tf_op jit(solution)/shard_map/ppermute | solution.py:77
  191.6 24.9 %collective-permute-start.32 = (bf16[528,256]{1,0:T(8,128)(2,1)}, bf16[528,256]{1,0:T(8,128)(2,1)}, u32[]{:S(2)}, u32[]{:S(2)}) collective-permute-start(bf16[528,256]{1,0:T(8,128)(2,1)} %get-tuple-element.465), channel_id=1, source_target_pairs={{0,3},{1,2},{2,1},{3,0},{4,7},{5,6},{6,5},{7,4},{8,11},{9,10},{10,... | collective-permute-start | bytes 811016 | tf_op jit(solution)/shard_map/ppermute | solution.py:108
  212.4 23.3 %collective-permute-start.37 = (bf16[256,1536]{1,0:T(8,128)(2,1)}, bf16[256,1536]{1,0:T(8,128)(2,1)S(1)}, u32[]{:S(2)}, u32[]{:S(2)}) collective-permute-start(bf16[256,1536]{1,0:T(8,128)(2,1)} %collective-permute-done.23.refs_17_), channel_id=1, source_target_pairs={{0,8},{8,16},{16,24},{24,28},{28,20},{20,12},{12,4},{4,0},{1,9},{9... | collective-permute-start | bytes 2359304 | tf_op jit(solution)/shard_map/ppermute | solution.py:77
  214.5 21.2 %collective-permute-start.38 = (bf16[256,1536]{1,0:T(8,128)(2,1)}, bf16[256,1536]{1,0:T(8,128)(2,1)S(1)}, u32[]{:S(2)}, u32[]{:S(2)}) collective-permute-start(bf16[256,1536]{1,0:T(8,128)(2,1)} %collective-permute-done.24.refs_18_), channel_id=1, source_target_pairs={{0,4},{8,0},{16,8},{24,16},{28,24},{20,28},{12,20},{4,12},{1,5},{9... | collective-permute-start | bytes 2359304 | tf_op jit(solution)/shard_map/ppermute | solution.py:77
  214.5 33.1 %collective-permute-start.33 = (bf16[256,1536]{1,0:T(8,128)(2,1)}, bf16[256,1536]{1,0:T(8,128)(2,1)S(1)}, u32[]{:S(2)}, u32[]{:S(2)}) collective-permute-start(bf16[256,1536]{1,0:T(8,128)(2,1)} %collective-permute-done.25.refs_8_), channel_id=1, source_target_pairs={{0,8},{8,16},{16,24},{24,28},{28,20},{20,12},{12,4},{4,0},{1,9},{9... | collective-permute-start | bytes 2359304 | tf_op jit(solution)/shard_map/ppermute | solution.py:77
  216.5 33.2 %collective-permute-start.34 = (bf16[256,1536]{1,0:T(8,128)(2,1)}, bf16[256,1536]{1,0:T(8,128)(2,1)S(1)}, u32[]{:S(2)}, u32[]{:S(2)}) collective-permute-start(bf16[256,1536]{1,0:T(8,128)(2,1)} %collective-permute-done.26.refs_9_), channel_id=1, source_target_pairs={{0,4},{8,0},{16,8},{24,16},{28,24},{20,28},{12,20},{4,12},{1,5},{9... | collective-permute-start | bytes 2359304 | tf_op jit(solution)/shard_map/ppermute | solution.py:77
  225.8 44.5 %collective-permute-start.28 = (bf16[256,2048]{1,0:T(8,128)(2,1)}, bf16[256,2048]{1,0:T(8,128)(2,1)}, u32[]{:S(2)}, u32[]{:S(2)}) collective-permute-start(bf16[256,2048]{1,0:T(8,128)(2,1)} %get-tuple-element.310.refs_0_), channel_id=1, source_target_pairs={{0,2},{1,3},{2,0},{3,1},{4,6},{5,7},{6,4},{7,5},{8,10},{9,11},{10,... | collective-permute-start | bytes 3145736 | tf_op jit(solution)/shard_map/ppermute | solution.py:108
  252.0 15.3 %collective-permute-start.36 = (bf16[128,1536]{1,0:T(8,128)(2,1)S(1)}, bf16[128,1536]{1,0:T(8,128)(2,1)S(1)}, u32[]{:S(2)}, u32[]{:S(2)}) collective-permute-start(bf16[128,1536]{1,0:T(8,128)(2,1)S(1)} %slice.457), channel_id=1, source_target_pairs={{0,4},{8,0},{16,8},{24,16},{28,24},{20,28},{12,20},{4,12},{1,5},{9... | collective-permute-start | bytes 1179656 | tf_op jit(solution)/shard_map/ppermute | solution.py:77
  252.3 15.7 %collective-permute-start.35 = (bf16[128,1536]{1,0:T(8,128)(2,1)S(1)}, bf16[128,1536]{1,0:T(8,128)(2,1)S(1)}, u32[]{:S(2)}, u32[]{:S(2)}) collective-permute-start(bf16[128,1536]{1,0:T(8,128)(2,1)S(1)} %slice.456), channel_id=1, source_target_pairs={{0,8},{8,16},{16,24},{24,28},{28,20},{20,12},{12,4},{4,0},{1,9},{9... | collective-permute-start | bytes 1179656 | tf_op jit(solution)/shard_map/ppermute | solution.py:77
  267.9 43.8 %collective-permute-start.41 = (bf16[256,3072]{1,0:T(8,128)(2,1)S(1)}, bf16[256,3072]{1,0:T(8,128)(2,1)}, u32[]{:S(2)}, u32[]{:S(2)}) collective-permute-start(bf16[256,3072]{1,0:T(8,128)(2,1)S(1)} %pad_maximum_fusion.1.refs_5_), channel_id=1, source_target_pairs={{0,8},{8,16},{16,24},{24,28},{28,20},{20,12},{12,4},{4,0},{1,9},{9... | collective-permute-start | bytes 4718600 | tf_op jit(solution)/shard_map/ppermute | solution.py:77
  269.7 42.1 %collective-permute-start.42 = (bf16[256,3072]{1,0:T(8,128)(2,1)S(1)}, bf16[256,3072]{1,0:T(8,128)(2,1)}, u32[]{:S(2)}, u32[]{:S(2)}) collective-permute-start(bf16[256,3072]{1,0:T(8,128)(2,1)S(1)} %pad_maximum_fusion.1.refs_5_), channel_id=1, source_target_pairs={{0,4},{8,0},{16,8},{24,16},{28,24},{20,28},{12,20},{4,12},{1,5},{9... | collective-permute-start | bytes 4718600 | tf_op jit(solution)/shard_map/ppermute | solution.py:77
  270.9 43.1 %collective-permute-start.46 = (bf16[256,2048]{1,0:T(8,128)(2,1)S(1)}, bf16[256,2048]{1,0:T(8,128)(2,1)}, u32[]{:S(2)}, u32[]{:S(2)}) collective-permute-start(bf16[256,2048]{1,0:T(8,128)(2,1)S(1)} %copy-done.18), channel_id=1, source_target_pairs={{0,2},{1,3},{2,0},{3,1},{4,6},{5,7},{6,4},{7,5},{8,10},{9,11},{10,... | collective-permute-start | bytes 3145736 | tf_op jit(solution)/shard_map/ppermute | solution.py:108
  311.8 44.3 %collective-permute-start.43 = (bf16[256,3072]{1,0:T(8,128)(2,1)}, bf16[256,3072]{1,0:T(8,128)(2,1)S(1)}, u32[]{:S(2)}, u32[]{:S(2)}) collective-permute-start(bf16[256,3072]{1,0:T(8,128)(2,1)} %collective-permute-done.41.refs_6_), channel_id=1, source_target_pairs={{0,8},{8,16},{16,24},{24,28},{28,20},{20,12},{12,4},{4,0},{1,9},{9... | collective-permute-start | bytes 4718600 | tf_op jit(solution)/shard_map/ppermute | solution.py:77
  313.6 42.5 %collective-permute-start.44 = (bf16[256,3072]{1,0:T(8,128)(2,1)}, bf16[256,3072]{1,0:T(8,128)(2,1)}, u32[]{:S(2)}, u32[]{:S(2)}) collective-permute-start(bf16[256,3072]{1,0:T(8,128)(2,1)} %collective-permute-done.42.refs_7_), channel_id=1, source_target_pairs={{0,4},{8,0},{16,8},{24,16},{28,24},{20,28},{12,20},{4,12},{1,5},{9... | collective-permute-start | bytes 4718600 | tf_op jit(solution)/shard_map/ppermute | solution.py:77
  314.5 83.2 %collective-permute-start.52 = (bf16[800,2048]{1,0:T(8,128)(2,1)S(1)}, bf16[800,2048]{1,0:T(8,128)(2,1)}, u32[]{:S(2)}, u32[]{:S(2)}) collective-permute-start(bf16[800,2048]{1,0:T(8,128)(2,1)S(1)} %copy-done), channel_id=1, source_target_pairs={{0,2},{1,3},{2,0},{3,1},{4,6},{5,7},{6,4},{7,5},{8,10},{9,11},{10,... | collective-permute-start | bytes 9830408 | tf_op jit(solution)/shard_map/ppermute | solution.py:108
  357.2 36.6 %collective-permute-start.48 = (bf16[256,3072]{1,0:T(8,128)(2,1)}, bf16[256,3072]{1,0:T(8,128)(2,1)S(1)}, u32[]{:S(2)}, u32[]{:S(2)}) collective-permute-start(bf16[256,3072]{1,0:T(8,128)(2,1)} %copy-done.12), channel_id=1, source_target_pairs={{0,8},{8,16},{16,24},{24,28},{28,20},{20,12},{12,4},{4,0},{1,9},{9... | collective-permute-start | bytes 4718600 | tf_op jit(solution)/shard_map/ppermute | solution.py:77
  359.0 36.4 %collective-permute-start.49 = (bf16[256,3072]{1,0:T(8,128)(2,1)}, bf16[256,3072]{1,0:T(8,128)(2,1)S(1)}, u32[]{:S(2)}, u32[]{:S(2)}) collective-permute-start(bf16[256,3072]{1,0:T(8,128)(2,1)} %collective-permute-done.44.refs_9_), channel_id=1, source_target_pairs={{0,4},{8,0},{16,8},{24,16},{28,24},{20,28},{12,20},{4,12},{1,5},{9... | collective-permute-start | bytes 4718600 | tf_op jit(solution)/shard_map/ppermute | solution.py:77
  395.5 18.5 %collective-permute-start.51 = (bf16[128,3072]{1,0:T(8,128)(2,1)S(1)}, bf16[128,3072]{1,0:T(8,128)(2,1)S(1)}, u32[]{:S(2)}, u32[]{:S(2)}) collective-permute-start(bf16[128,3072]{1,0:T(8,128)(2,1)S(1)} %slice.461), channel_id=1, source_target_pairs={{0,4},{8,0},{16,8},{24,16},{28,24},{20,28},{12,20},{4,12},{1,5},{9... | collective-permute-start | bytes 2359304 | tf_op jit(solution)/shard_map/ppermute | solution.py:77
  395.8 18.5 %collective-permute-start.50 = (bf16[128,3072]{1,0:T(8,128)(2,1)S(1)}, bf16[128,3072]{1,0:T(8,128)(2,1)}, u32[]{:S(2)}, u32[]{:S(2)}) collective-permute-start(bf16[128,3072]{1,0:T(8,128)(2,1)S(1)} %slice.460), channel_id=1, source_target_pairs={{0,8},{8,16},{16,24},{24,28},{28,20},{20,12},{12,4},{4,0},{1,9},{9... | collective-permute-start | bytes 2359304 | tf_op jit(solution)/shard_map/ppermute | solution.py:77
  454.9 47.2 %collective-permute-start.53 = (bf16[256,2048]{1,0:T(8,128)(2,1)}, bf16[256,2048]{1,0:T(8,128)(2,1)S(1)}, u32[]{:S(2)}, u32[]{:S(2)}) collective-permute-start(bf16[256,2048]{1,0:T(8,128)(2,1)} %get-tuple-element.359), channel_id=1, source_target_pairs={{0,1},{1,0},{2,3},{3,2},{4,5},{5,4},{6,7},{7,6},{8,9},{9,8},{10,11... | collective-permute-start | bytes 3145736 | tf_op jit(solution)/shard_map/ppermute | solution.py:108
  460.4 41.7 %collective-permute-start.55 = (bf16[256,2048]{1,0:T(8,128)(2,1)}, bf16[256,2048]{1,0:T(8,128)(2,1)S(1)}, u32[]{:S(2)}, u32[]{:S(2)}) collective-permute-start(bf16[256,2048]{1,0:T(8,128)(2,1)} %add_convert_fusion.5), channel_id=1, source_target_pairs={{0,2},{1,3},{2,0},{3,1},{4,6},{5,7},{6,4},{7,5},{8,10},{9,11},{10,... | collective-permute-start | bytes 3145736 | tf_op jit(solution)/shard_map/ppermute | solution.py:108
  501.5 113.7 %collective-permute-start.79 = (bf16[800,2048]{1,0:T(8,128)(2,1)S(1)}, bf16[800,2048]{1,0:T(8,128)(2,1)}, u32[]{:S(2)}, u32[]{:S(2)}) collective-permute-start(bf16[800,2048]{1,0:T(8,128)(2,1)S(1)} %copy-done), channel_id=1, source_target_pairs={{0,1},{1,0},{2,3},{3,2},{4,5},{5,4},{6,7},{7,6},{8,9},{9,8},{10,11... | collective-permute-start | bytes 9830408 | tf_op jit(solution)/shard_map/ppermute | solution.py:108
  502.0 115.8 %collective-permute-start.80 = (bf16[800,2048]{1,0:T(8,128)(2,1)}, bf16[800,2048]{1,0:T(8,128)(2,1)}, u32[]{:S(2)}, u32[]{:S(2)}) collective-permute-start(bf16[800,2048]{1,0:T(8,128)(2,1)} %collective-permute-done.52.refs_10_), channel_id=1, source_target_pairs={{0,1},{1,0},{2,3},{3,2},{4,5},{5,4},{6,7},{7,6},{8,9},{9,8},{10,11... | collective-permute-start | bytes 9830408 | tf_op jit(solution)/shard_map/ppermute | solution.py:108
  519.2 37.6 %collective-permute-start.59 = (bf16[256,2048]{1,0:T(8,128)(2,1)}, bf16[256,2048]{1,0:T(8,128)(2,1)S(1)}, u32[]{:S(2)}, u32[]{:S(2)}) collective-permute-start(bf16[256,2048]{1,0:T(8,128)(2,1)} %get-tuple-element.375), channel_id=1, source_target_pairs={{0,1},{1,0},{2,3},{3,2},{4,5},{5,4},{6,7},{7,6},{8,9},{9,8},{10,11... | collective-permute-start | bytes 3145736 | tf_op jit(solution)/shard_map/ppermute | solution.py:108
  528.7 32.4 %collective-permute-start.61 = (bf16[256,2048]{1,0:T(8,128)(2,1)}, bf16[256,2048]{1,0:T(8,128)(2,1)}, u32[]{:S(2)}, u32[]{:S(2)}) collective-permute-start(bf16[256,2048]{1,0:T(8,128)(2,1)} %add_convert_fusion.4), channel_id=1, source_target_pairs={{0,2},{1,3},{2,0},{3,1},{4,6},{5,7},{6,4},{7,5},{8,10},{9,11},{10,... | collective-permute-start | bytes 3145736 | tf_op jit(solution)/shard_map/ppermute | solution.py:108
  556.8 18.8 %collective-permute-start.66 = (bf16[2,1,2,1,80,128]{5,4,3,2,1,0:T(8,128)(2,1)S(1)}, bf16[2,1,2,1,80,128]{5,4,3,2,1,0:T(8,128)(2,1)S(1)}, u32[]{:S(2)}, u32[]{:S(2)}) collective-permute-start(bf16[2,1,2,1,80,128]{5,4,3,2,1,0:T(8,128)(2,1)S(1)} %fusion.11), channel_id=1, source_target_pairs={{24,0},{28,4},{25,1},{29,5},{26,2},{30,6},{27,3},{31,7}} | collective-permute-start | bytes 245768 | tf_op jit(solution)/shard_map/ppermute | solution.py:114
  559.8 16.0 %collective-permute-start.65 = (bf16[2,1,2,1,80,128]{5,4,3,2,1,0:T(8,128)(2,1)S(1)}, bf16[2,1,2,1,80,128]{5,4,3,2,1,0:T(8,128)(2,1)S(1)}, u32[]{:S(2)}, u32[]{:S(2)}) collective-permute-start(bf16[2,1,2,1,80,128]{5,4,3,2,1,0:T(8,128)(2,1)S(1)} %fusion.11), channel_id=1, source_target_pairs={{16,0},{20,4},{24,8},{28,12},{17,1},{21,5},{25,9},{29,13},{18,2},{... | collective-permute-start | bytes 245768 | tf_op jit(solution)/shard_map/ppermute | solution.py:114
  561.1 15.7 %collective-permute-start.64 = (bf16[2,1,2,2,80,128]{5,4,3,2,1,0:T(8,128)(2,1)S(1)}, bf16[2,1,2,2,80,128]{5,4,3,2,1,0:T(8,128)(2,1)S(1)}, u32[]{:S(2)}, u32[]{:S(2)}) collective-permute-start(bf16[2,1,2,2,80,128]{5,4,3,2,1,0:T(8,128)(2,1)S(1)} %pad_maximum_fusion.5.refs_0_), channel_id=1, source_target_pairs={{8,0},{12,4},{16,8},{20,12},{24,16},{28,20},{9,1},{13,5},{17,9},{2... | collective-permute-start | bytes 491528 | tf_op jit(solution)/shard_map/ppermute | solution.py:114
  575.7 16.2 %collective-permute-start.70 = (bf16[528,256]{1,0:T(8,128)(2,1)}, bf16[528,256]{1,0:T(8,128)(2,1)S(1)}, u32[]{:S(2)}, u32[]{:S(2)}) collective-permute-start(bf16[528,256]{1,0:T(8,128)(2,1)} %get-tuple-element.400), channel_id=1, source_target_pairs={{0,1},{1,0},{2,3},{3,2},{4,5},{5,4},{6,7},{7,6},{8,9},{9,8},{10,11... | collective-permute-start | bytes 811016 | tf_op jit(solution)/shard_map/ppermute | solution.py:108
  575.8 17.1 %collective-permute-start.71 = (bf16[528,256]{1,0:T(8,128)(2,1)}, bf16[528,256]{1,0:T(8,128)(2,1)S(1)}, u32[]{:S(2)}, u32[]{:S(2)}) collective-permute-start(bf16[528,256]{1,0:T(8,128)(2,1)} %get-tuple-element.401), channel_id=1, source_target_pairs={{0,2},{1,3},{2,0},{3,1},{4,6},{5,7},{6,4},{7,5},{8,10},{9,11},{10,... | collective-permute-start | bytes 811016 | tf_op jit(solution)/shard_map/ppermute | solution.py:108
  576.8 17.1 %collective-permute-start.72 = (bf16[528,256]{1,0:T(8,128)(2,1)}, bf16[528,256]{1,0:T(8,128)(2,1)S(1)}, u32[]{:S(2)}, u32[]{:S(2)}) collective-permute-start(bf16[528,256]{1,0:T(8,128)(2,1)} %get-tuple-element.402), channel_id=1, source_target_pairs={{0,3},{1,2},{2,1},{3,0},{4,7},{5,6},{6,5},{7,4},{8,11},{9,10},{10,... | collective-permute-start | bytes 811016 | tf_op jit(solution)/shard_map/ppermute | solution.py:108
  591.9 29.9 %collective-permute-start.75 = (bf16[512,256]{1,0:T(8,128)(2,1)}, bf16[512,256]{1,0:T(8,128)(2,1)}, u32[]{:S(2)}, u32[]{:S(2)}) collective-permute-start(bf16[512,256]{1,0:T(8,128)(2,1)} %get-tuple-element.471), channel_id=1, source_target_pairs={{0,3},{1,2},{2,1},{3,0},{4,7},{5,6},{6,5},{7,4},{8,11},{9,10},{10,... | collective-permute-start | bytes 786440 | tf_op jit(solution)/shard_map/ppermute | solution.py:108
  592.8 29.0 %collective-permute-start.74 = (bf16[512,256]{1,0:T(8,128)(2,1)}, bf16[512,256]{1,0:T(8,128)(2,1)}, u32[]{:S(2)}, u32[]{:S(2)}) collective-permute-start(bf16[512,256]{1,0:T(8,128)(2,1)} %get-tuple-element.472), channel_id=1, source_target_pairs={{0,2},{1,3},{2,0},{3,1},{4,6},{5,7},{6,4},{7,5},{8,10},{9,11},{10,... | collective-permute-start | bytes 786440 | tf_op jit(solution)/shard_map/ppermute | solution.py:108
  593.9 30.0 %collective-permute-start.73 = (bf16[512,256]{1,0:T(8,128)(2,1)}, bf16[512,256]{1,0:T(8,128)(2,1)}, u32[]{:S(2)}, u32[]{:S(2)}) collective-permute-start(bf16[512,256]{1,0:T(8,128)(2,1)} %get-tuple-element.473), channel_id=1, source_target_pairs={{0,1},{1,0},{2,3},{3,2},{4,5},{5,4},{6,7},{7,6},{8,9},{9,8},{10,11... | collective-permute-start | bytes 786440 | tf_op jit(solution)/shard_map/ppermute | solution.py:108
  621.8 24.9 %collective-permute-start.83 = (bf16[2,1,2,2,80,128]{5,4,3,2,1,0:T(8,128)(2,1)S(1)}, bf16[2,1,2,2,80,128]{5,4,3,2,1,0:T(8,128)(2,1)S(1)}, u32[]{:S(2)}, u32[]{:S(2)}) collective-permute-start(bf16[2,1,2,2,80,128]{5,4,3,2,1,0:T(8,128)(2,1)S(1)} %pad_maximum_fusion.6.refs_0_), channel_id=1, source_target_pairs={{8,0},{12,4},{16,8},{20,12},{24,16},{28,20},{9,1},{13,5},{17,9},{2... | collective-permute-start | bytes 491528 | tf_op jit(solution)/shard_map/ppermute | solution.py:114
  623.9 22.7 %collective-permute-start.81 = (bf16[64,256]{1,0:T(8,128)(2,1)}, bf16[64,256]{1,0:T(8,128)(2,1)S(1)}, u32[]{:S(2)}, u32[]{:S(2)}) collective-permute-start(bf16[64,256]{1,0:T(8,128)(2,1)} %get-tuple-element.414), channel_id=1, source_target_pairs={{4,0},{8,4},{12,8},{16,12},{20,16},{24,20},{28,24},{5,1},{9,5},{13... | collective-permute-start | bytes 98312 | tf_op jit(solution)/shard_map/ppermute | solution.py:114
  625.2 21.4 %collective-permute-start.85 = (bf16[2,1,2,1,80,128]{5,4,3,2,1,0:T(8,128)(2,1)S(1)}, bf16[2,1,2,1,80,128]{5,4,3,2,1,0:T(8,128)(2,1)S(1)}, u32[]{:S(2)}, u32[]{:S(2)}) collective-permute-start(bf16[2,1,2,1,80,128]{5,4,3,2,1,0:T(8,128)(2,1)S(1)} %fusion.10), channel_id=1, source_target_pairs={{24,0},{28,4},{25,1},{29,5},{26,2},{30,6},{27,3},{31,7}} | collective-permute-start | bytes 245768 | tf_op jit(solution)/shard_map/ppermute | solution.py:114
  627.0 19.7 %collective-permute-start.84 = (bf16[2,1,2,1,80,128]{5,4,3,2,1,0:T(8,128)(2,1)S(1)}, bf16[2,1,2,1,80,128]{5,4,3,2,1,0:T(8,128)(2,1)S(1)}, u32[]{:S(2)}, u32[]{:S(2)}) collective-permute-start(bf16[2,1,2,1,80,128]{5,4,3,2,1,0:T(8,128)(2,1)S(1)} %fusion.10), channel_id=1, source_target_pairs={{16,0},{20,4},{24,8},{28,12},{17,1},{21,5},{25,9},{29,13},{18,2},{... | collective-permute-start | bytes 245768 | tf_op jit(solution)/shard_map/ppermute | solution.py:114
  634.5 80.0 %collective-permute-start.68 = (bf16[256,2048]{1,0:T(8,128)(2,1)}, bf16[256,2048]{1,0:T(8,128)(2,1)S(1)}, u32[]{:S(2)}, u32[]{:S(2)}) collective-permute-start(bf16[256,2048]{1,0:T(8,128)(2,1)} %get-tuple-element.392), channel_id=1, source_target_pairs={{0,1},{1,0},{2,3},{3,2},{4,5},{5,4},{6,7},{7,6},{8,9},{9,8},{10,11... | collective-permute-start | bytes 3145736 | tf_op jit(solution)/shard_map/ppermute | solution.py:108
  682.8 26.4 %collective-permute-start.98 = (bf16[912,128]{1,0:T(8,128)(2,1)}, bf16[912,128]{1,0:T(8,128)(2,1)}, u32[]{:S(2)}, u32[]{:S(2)}) collective-permute-start(bf16[912,128]{1,0:T(8,128)(2,1)} %add_convert_fusion.8), channel_id=1, source_target_pairs={{0,8},{4,12},{8,0},{12,4},{16,24},{20,28},{24,16},{28,20},{1,9},{5... | collective-permute-start | bytes 700424 | tf_op jit(solution)/shard_map/ppermute | solution.py:108
  693.9 32.0 %collective-permute-start.87 = (bf16[256,2048]{1,0:T(8,128)(2,1)}, bf16[256,2048]{1,0:T(8,128)(2,1)S(1)}, u32[]{:S(2)}, u32[]{:S(2)}) collective-permute-start(bf16[256,2048]{1,0:T(8,128)(2,1)} %get-tuple-element.424), channel_id=1, source_target_pairs={{0,1},{1,0},{2,3},{3,2},{4,5},{5,4},{6,7},{7,6},{8,9},{9,8},{10,11... | collective-permute-start | bytes 3145736 | tf_op jit(solution)/shard_map/ppermute | solution.py:108
  697.1 41.8 %collective-permute-start.67 = (bf16[256,2048]{1,0:T(8,128)(2,1)}, bf16[256,2048]{1,0:T(8,128)(2,1)}, u32[]{:S(2)}, u32[]{:S(2)}) collective-permute-start(bf16[256,2048]{1,0:T(8,128)(2,1)} %get-tuple-element.389), channel_id=1, source_target_pairs={{0,1},{1,0},{2,3},{3,2},{4,5},{5,4},{6,7},{7,6},{8,9},{9,8},{10,11... | collective-permute-start | bytes 3145736 | tf_op jit(solution)/shard_map/ppermute | solution.py:108
  697.1 47.7 %collective-permute-start.86 = (bf16[256,2048]{1,0:T(8,128)(2,1)}, bf16[256,2048]{1,0:T(8,128)(2,1)}, u32[]{:S(2)}, u32[]{:S(2)}) collective-permute-start(bf16[256,2048]{1,0:T(8,128)(2,1)} %get-tuple-element.421), channel_id=1, source_target_pairs={{0,1},{1,0},{2,3},{3,2},{4,5},{5,4},{6,7},{7,6},{8,9},{9,8},{10,11... | collective-permute-start | bytes 3145736 | tf_op jit(solution)/shard_map/ppermute | solution.py:108
  710.3 15.6 %collective-permute-start.99 = (bf16[912,128]{1,0:T(8,128)(2,1)S(1)}, bf16[912,128]{1,0:T(8,128)(2,1)S(1)}, u32[]{:S(2)}, u32[]{:S(2)}) collective-permute-start(bf16[912,128]{1,0:T(8,128)(2,1)S(1)} %add_convert_fusion.7), channel_id=1, source_target_pairs={{0,16},{4,20},{8,24},{12,28},{16,0},{20,4},{24,8},{28,12},{1,17},{... | collective-permute-start | bytes 700424 | tf_op jit(solution)/shard_map/ppermute | solution.py:108
  715.9 26.3 %collective-permute-start.69 = (bf16[256,2048]{1,0:T(8,128)(2,1)}, bf16[256,2048]{1,0:T(8,128)(2,1)}, u32[]{:S(2)}, u32[]{:S(2)}) collective-permute-start(bf16[256,2048]{1,0:T(8,128)(2,1)} %add_convert_fusion.3), channel_id=1, source_target_pairs={{0,2},{1,3},{2,0},{3,1},{4,6},{5,7},{6,4},{7,5},{8,10},{9,11},{10,... | collective-permute-start | bytes 3145736 | tf_op jit(solution)/shard_map/ppermute | solution.py:108
  726.4 37.6 %collective-permute-start.88 = (bf16[256,2048]{1,0:T(8,128)(2,1)S(1)}, bf16[256,2048]{1,0:T(8,128)(2,1)}, u32[]{:S(2)}, u32[]{:S(2)}) collective-permute-start(bf16[256,2048]{1,0:T(8,128)(2,1)S(1)} %add_convert_fusion.1), channel_id=1, source_target_pairs={{0,2},{1,3},{2,0},{3,1},{4,6},{5,7},{6,4},{7,5},{8,10},{9,11},{10,... | collective-permute-start | bytes 3145736 | tf_op jit(solution)/shard_map/ppermute | solution.py:108
  (128 other events, 1293.6 us)

commit v3 on v2

--- a/solution.py
+++ b/solution.py
@@ -60,8 +60,8 @@
 
 
 def pieces_of(width):
-    quarter = width // 4
-    return [(0, quarter), (quarter, quarter), (2 * quarter, 2 * quarter)]
+    first = width // (2 * CHUNK) * CHUNK
+    return [(0, first), (first, width - first)]
 
 
 class Ring:
@@ -138,12 +138,15 @@
     return [blocks[0]] + [flip(blocks[r], "grp", r) for r in range(1, len(blocks))]
 
 
+def far_pair(here, there):
+    return (here.astype(F32) + flip(there, "grp", 1).astype(F32)).astype(BF)
+
+
 def scatter_start(blocks):
     count = len(blocks)
     fars = []
     for far in range(2, count, 2):
-        there = flip(blocks[far + 1], "grp", 1)
-        fars.append((blocks[far].astype(F32) + there.astype(F32)).astype(BF))
+        fars.append(far_pair(blocks[far], blocks[far + 1]))
     return fars, [blocks[0], flip(blocks[1], "grp", 1)]
 
 
@@ -151,70 +154,147 @@
     return nears + [flip(far, "grp", 2 * (i + 1)) for i, far in enumerate(fars)]
 
 
-def exchange(ends, halo, sign):
+def exchange(table, ends, halo, sign):
     count = lax.axis_size("seq")
     wide = max(1, count // 4)
-    here = [ends] + [flip(ends, "seq", j) for j in range(1, wide)]
-    near = jnp.stack(here)
-    out = [near]
-    for r in range(1, count // wide):
-        out.append(shifted(near if r == 1 else near[:, :, :, 1:], "seq", sign * r * wide))
+    here = [flip(ends, "seq", j) for j in range(1, wide)]
+    full, inner = run_layer(table, [ends, *here], sign)
+    out = here + [shifted(full, "seq", sign * wide), shifted(inner, "seq", sign * wide)]
+    out += [shifted(full, "seq", sign * r * wide) for r in range(2, count // wide)]
     return out, shifted(halo, "seq", sign)
 
 
-class Slots:
-    def __init__(self, lens, batch):
-        self.starts, self.ends, at = [], [], 0
+VALID, ONE, TWO = range(3)
+FULL, INNER, NEXT, LAYER_FULL, LAYER_INNER, LAYER_NEXT = range(6)
+TABLE_ROWS = 15
+
+
+def side_row(sign, row):
+    return 3 + row + (0 if sign > 0 else 6)
+
+
+def table_width(blocks, count):
+    return max(blocks + 4, 2 * count)
+
+
+def layout_kernel(blocks, wide, count, info, lens, out):
+    width = table_width(blocks, count)
+    base, seq = info[0], info[2]
+    z, y = seq // wide, seq % wide
+    for batch in range(lens.shape[0]):
+        starts, ends, at = [], [], 0
         for i in range(lens.shape[1]):
             length = lens[batch, i]
-            self.starts.append(at)
-            self.ends.append(at * STRETCH + length)
+            starts.append(at)
+            ends.append(at * STRETCH + length)
             at = at + ((length + STRETCH - 1) >> 6)
 
-    def owner(self, c):
-        total = -1
-        for start in self.starts:
-            total = total + jnp.where(start <= c, 1, 0)
-        return total
+        def owner(c):
+            total = -1
+            for start in starts:
+                total = total + jnp.where(start <= c, 1, 0)
+            return total
+
+        def put(row, i, value):
+            out[(batch * TABLE_ROWS + row) * width + i] = value
+
+        owned = [owner(base + c) for c in range(-3, blocks + 3)]
+        for i in range(blocks + 4):
+            c = base + i - 1
+            end = 0
+            for start, stop in zip(starts, ends):
+                end = jnp.where(start <= c, stop, end)
+            put(VALID, i, jnp.clip(end - c * STRETCH, 0, STRETCH))
+            put(ONE, i, jnp.where(owned[i + 2] == owned[i + 1], 1, 0))
+            put(TWO, i, jnp.where(owned[i + 2] == owned[i], 1, 0))
+        for sign in (1, -1):
+            edge = base - 1 if sign > 0 else base + blocks
+            outer, inner = owner(edge), owner(edge - sign)
+            end_of = lambda device: device * blocks + (blocks - 1 if sign > 0 else 0)
+            last = wide - 1 if sign > 0 else 0
+            first = wide - 1 - last
+            layer_end = end_of(z * wide + last)
+            layer_outer, layer_inner = owner(layer_end), owner(layer_end - sign)
+            for j in range(wide):
+                source = z * wide + (y ^ j)
+                far = (seq - source) * sign
+                there = owner(end_of(source))
+                put(side_row(sign, FULL), j, jnp.where((far > 0) & (there == outer), 1, 0))
+                put(side_row(sign, INNER), j, jnp.where((far > 1) & (there == inner), 1, 0))
+                put(side_row(sign, NEXT), j, jnp.where(far == 1, 1, 0))
+                put(side_row(sign, LAYER_FULL), j, jnp.where(there == layer_outer, 1, 0))
+                outermost = (y ^ j) == last
+                put(side_row(sign, LAYER_NEXT), j, jnp.where(outermost, 1, 0))
+                put(
+                    side_row(sign, LAYER_INNER), j,
+                    jnp.where((there == layer_inner) & (~outermost), 1, 0),
+                )
+            for r in range(1, count // wide):
+                layer = z - sign * r
+                inside = (layer >= 0) & (layer < count // wide)
+                there = owner(end_of(layer * wide + last))
+                i = wide + r
+                direct = (y == first) if r == 1 else (y != y)
+                put(side_row(sign, FULL), i, jnp.where(inside & (there == outer), 1, 0))
+                put(
+                    side_row(sign, INNER), i,
+                    jnp.where(inside & (there == inner) & (~direct), 1, 0),
+                )
+                put(side_row(sign, NEXT), i, jnp.where(inside & direct, 1, 0))
+
+
+class Slots:
+    def __init__(self, table, batch, blocks, count):
+        self.table, self.batch, self.width = table, batch, table_width(blocks, count)
+
+    def at(self, row, i):
+        return self.table[(self.batch * TABLE_ROWS + row) * self.width + i]
 
     def valid(self, c):
-        end = 0
-        for start, stop in zip(self.starts, self.ends):
-            end = jnp.where(start <= c, stop, end)
-        return jnp.clip(end - c * STRETCH, 0, STRETCH)
-
-    def same(self, a, b):
-        return jnp.where(self.owner(a) == self.owner(b), 1, 0)
-
-    def weight(self, a, b):
-        return self.same(a, b).astype(F32)
-
-
-def entering(slots, info, arrays, blocks, wide, count, sign, place, near_k):
-    seq = info[2]
-    base = info[0]
-    z, y = seq // wide, seq % wide
-    edge = base - 1 if sign > 0 else base + blocks
+        return self.at(VALID, c + 1)
+
+    def one(self, c):
+        return self.at(ONE, c + 1)
+
+    def weight_one(self, c):
+        return self.one(c).astype(F32)
+
+    def weight_two(self, c):
+        return self.at(TWO, c + 1).astype(F32)
+
+
+def entering(slots, arrays, wide, count, sign, place, near_k):
     inner = outer = jnp.zeros((EXT, PAIR), F32)
-    for r in range(count // wide):
-        for j in range(wide):
-            if r == 0 and j == 0:
-                continue
-            source = (z - sign * r) * wide + (y ^ j)
-            ahead = (seq - source) * sign > 0
-            end = source * blocks + (blocks - 1 if sign > 0 else 0)
-            direct = (seq - source) * sign == 1
-            full = arrays[r][j, place, near_k, arrays[r].shape[3] - 1].astype(F32)
-            a = jnp.where(ahead & (slots.owner(end) == slots.owner(edge)), 1.0, 0.0)
-            outer = outer + a * full
-            b = jnp.where(
-                ahead & (~direct) & (slots.owner(end) == slots.owner(edge - sign)), 1.0, 0.0
-            )
-            inner = inner + b * full
-            if arrays[r].shape[3] == 2:
-                part = arrays[r][j, place, near_k, 0].astype(F32)
-                inner = inner + jnp.where(direct, 1.0, 0.0) * part
+    row = lambda name, i: slots.at(side_row(sign, name), i).astype(F32)
+    for j in range(1, wide):
+        array = arrays[j - 1]
+        full = array[place, near_k, 1].astype(F32)
+        outer = outer + row(FULL, j) * full
+        inner = inner + row(INNER, j) * full + row(NEXT, j) * array[place, near_k, 0].astype(F32)
+    layers = arrays[wide - 1 :]
+    for r in range(1, count // wide):
+        full = layers[0 if r == 1 else r][place, near_k].astype(F32)
+        outer = outer + row(FULL, wide + r) * full
+        inner = inner + row(INNER, wide + r) * full
+        if r == 1:
+            inner = inner + row(NEXT, wide + 1) * layers[1][place, near_k].astype(F32)
     return inner, outer
+
+
+def layer_kernel(sign, blocks, count, wide, table, *refs):
+    ends, (full_ref, inner_ref) = refs[:wide], refs[wide:]
+    for batch in range(full_ref.shape[0]):
+        slots = Slots(table, batch, blocks, count)
+        row = lambda name, i: slots.at(side_row(sign, name), i).astype(F32)
+        for k in range(full_ref.shape[1]):
+            full = inner = jnp.zeros((EXT, PAIR), F32)
+            for j in range(wide):
+                value = ends[j][batch, k, 1].astype(F32)
+                full = full + row(LAYER_FULL, j) * value
+                inner = inner + row(LAYER_INNER, j) * value
+                inner = inner + row(LAYER_NEXT, j) * ends[j][batch, k, 0].astype(F32)
+            full_ref[batch, k] = full.astype(BF)
+            inner_ref[batch, k] = inner.astype(BF)
 
 
 def half_mask(shape):
@@ -250,7 +330,7 @@
 
 
 def project_kernel(
-    batch, q_width, info, lens, normed_ref, w_ref, up_ref, kv_up_ref, wk_ref,
+    batch, q_width, blocks, count, table, normed_ref, w_ref, up_ref, kv_up_ref, wk_ref,
     q_ref, kv_ref, ve_ref, mid_ref, phi_ref, st_ref, ends_ref, halo_ref, carry,
 ):
     step = pl.program_id(0)
@@ -275,15 +355,14 @@
     kv_ref[...] = kv_all
     halo_ref[:, :width] = kv_all[rows - STRETCH :]
 
-    slots = Slots(lens, batch)
-    base = info[0]
+    slots = Slots(table, batch, blocks, count)
     lane = lax.broadcasted_iota(jnp.int32, (1, PAIR), 1)
     low = lane < STRETCH
     inside = lane & (STRETCH - 1)
     wide = lax.broadcasted_iota(jnp.int32, (PAIR, PAIR), 1)
     for sub in range(rows // PAIR):
-        block = base + 2 * (step * (rows // PAIR) + sub)
-        one_a, one_b = slots.weight(block - 1, block), slots.weight(block, block + 1)
+        block = 2 * (step * (rows // PAIR) + sub)
+        one_a, one_b = slots.weight_one(block), slots.weight_one(block + 1)
         valid = inside < jnp.where(low, slots.valid(block), slots.valid(block + 1))
         valid = jnp.where(valid, 1.0, 0.0)
         valid_low = jnp.where(low, valid, 0.0)
@@ -314,11 +393,11 @@
 def window_mask(slots, block):
     lane = lax.broadcasted_iota(jnp.int32, (1, PAIR), 1)
     low = lane < STRETCH
-    before = slots.valid(block - 1) * slots.same(block - 1, block)
+    before = slots.valid(block - 1) * slots.one(block)
     own = slots.valid(block)
     limits = [
         jnp.where(low, before, 0),
-        jnp.where(low, jnp.minimum(lane + 1, own), own * slots.same(block, block + 1)),
+        jnp.where(low, jnp.minimum(lane + 1, own), own * slots.one(block + 1)),
         jnp.where(low, 0, jnp.minimum(lane - STRETCH + 1, slots.valid(block + 1))),
     ]
     row = lax.broadcasted_iota(jnp.int32, (STRETCH, PAIR), 0)
@@ -334,26 +413,26 @@
 
 
 def forward_kernel(
-    batch, per, blocks, wide, count, n_far, scale, info, lens, q_ref, kv_ref, ve_ref, halo_ref,
+    batch, per, blocks, wide, count, n_far, scale, info, table, q_ref, kv_ref, ve_ref, halo_ref,
     wq_ref, oin_ref, st_ref, *refs,
 ):
     fars = refs[:n_far]
     att_ref, w_ref, phi_ref, s_ref, r_ref, carry, kv_all, ve_all = refs[n_far:]
     step = pl.program_id(0)
     heads = kv_ref.shape[1] // PAIR
-    slots = Slots(lens, batch)
-    block = info[0] + 2 * step
+    slots = Slots(table, batch, blocks, count)
+    block = 2 * step
 
     @pl.when(step == 0)
     def _():
         fill_window(batch, kv_ref, ve_ref, halo_ref, kv_all, ve_all)
         for k in range(heads):
-            inner, outer = entering(slots, info, fars, blocks, wide, count, 1, batch, k)
+            inner, outer = entering(slots, fars, wide, count, 1, batch, k)
             carry[k, 0] = inner
             carry[k, 1] = outer
 
-    one_a, one_b = slots.weight(block - 1, block), slots.weight(block, block + 1)
-    two_a, two_b = slots.weight(block - 2, block), slots.weight(block - 1, block + 1)
+    one_a, one_b = slots.weight_one(block), slots.weight_one(block + 1)
+    two_a, two_b = slots.weight_two(block), slots.weight_two(block + 1)
     mask = window_mask(slots, block)
     mask = jnp.concatenate([mask] * per, axis=1)
     lanes = per * PAIR
@@ -472,9 +551,10 @@
 
 
 def mlp_kernel(
-    batch, n_grp, layout, sizes, first_half, info, *refs,
+    batch, rels, layout, sizes, first_half, info, *refs,
 ):
     n_parts = len(layout)
+    n_grp = len(rels)
     xs, refs = refs[:n_grp], refs[n_grp:]
     dy_hbm, refs = refs[0], refs[1:]
     part_sets = []
@@ -517,27 +597,49 @@
                 for copy in loads(jj, s, which):
                     copy.start()
 
-    def inputs():
+    per_tile = ROW_TILE // share
+
+    def inputs(tile):
+        copies = []
+        for r in range(tile * per_tile, (tile + 1) * per_tile):
+            rows = pl.ds(r * share, share)
+            copies.append(pltpu.make_async_copy(xs[r], x.at[rows], sem.at[tile]))
+            there = pl.ds(pl.multiple_of((info[1] ^ rels[r]) * share, share), share)
+            copies.append(pltpu.make_async_copy(dy_hbm.at[batch, there], dy.at[rows], sem.at[tile]))
+        return copies
+
+    tiles = rows_all // ROW_TILE
+
+    def earlier():
+        part = pl.ds(rels[0] * share, rows_all)
+        return [
+            pltpu.make_async_copy(prev.at[part], refs[7 + i], sem.at[tiles])
+            for i, prev in enumerate(prevs)
+        ]
+
+    def results():
+        if first_half:
+            return [
+                pltpu.make_async_copy(x, outs[0], sem.at[0]),
+                pltpu.make_async_copy(dy, outs[1], sem.at[1]),
+            ]
         copies = []
         for r in range(n_grp):
             rows = pl.ds(r * share, share)
-            copies.append(pltpu.make_async_copy(xs[r], x.at[rows], sem.at[0]))
-            there = pl.ds(pl.multiple_of((info[1] ^ r) * share, share), share)
-            copies.append(pltpu.make_async_copy(dy_hbm.at[batch, there], dy.at[rows], sem.at[0]))
+            copies.append(pltpu.make_async_copy(x.at[rows], outs[r], sem.at[0]))
+            copies.append(pltpu.make_async_copy(dy.at[rows], outs[n_grp + r], sem.at[0]))
         return copies
-
-    def earlier():
-        return [
-            pltpu.make_async_copy(prev, refs[7 + i], sem.at[1]) for i, prev in enumerate(prevs)
-        ]
 
     @pl.when(j == 0)
     def _():
-        for copy in inputs() + earlier():
+        for copy in inputs(0):
             copy.start()
         start_loads(j, 0)
-        for copy in inputs():
-            copy.wait()
+        for tile in range(1, tiles):
+            for copy in inputs(tile):
+                copy.start()
+        for copy in earlier():
+            copy.start()
 
     @pl.when(j + 1 < n)
     def _():
@@ -548,8 +650,13 @@
     gate_up_w = w.at[slot, :, pl.ds(0, 2 * CHUNK)]
     down_w = w.at[slot, :, pl.ds(2 * CHUNK, CHUNK)]
 
-    def body(i, start):
-        rows = pl.ds(pl.multiple_of(i * ROW_TILE, ROW_TILE), ROW_TILE)
+    def body(tile, start, end):
+        rows = pl.ds(pl.multiple_of(tile * ROW_TILE, ROW_TILE), ROW_TILE)
+        if start:
+            for i in range(per_tile):
+                part = pl.ds(pl.multiple_of(tile * ROW_TILE + i * share, share), share)
+                pltpu.make_async_copy(xs[0], x.at[part], sem.at[tile]).wait()
+                pltpu.make_async_copy(xs[0], dy.at[part], sem.at[tile]).wait()
         gate_up = dotg(x[rows, :], gate_up_w[...], 1, 0)
         d_hidden = dotg(dy[rows, :], down_w[...], 1, 0)
         gate, up = gate_up[:, :CHUNK], gate_up[:, CHUNK:]
@@ -563,48 +670,39 @@
         if start:
             acc_out[rows, :] = out
             acc_in[rows, :] = d_in
-        else:
+        elif not end:
             acc_out[rows, :] += out
             acc_in[rows, :] += d_in
+        else:
+            out, d_in = acc_out[rows, :] + out, acc_in[rows, :] + d_in
+            if not first_half:
+                d_in = d_in + refs[7][rows, :].astype(F32)
+                out = out + refs[8][rows, :].astype(F32)
+            x[rows, :] = d_in.astype(BF)
+            dy[rows, :] = out.astype(BF)
         return 0
-
-    tiles = rows_all // ROW_TILE
 
     @pl.when(j == 0)
     def _():
-        lax.fori_loop(0, tiles, lambda i, c: body(i, True), 0)
-
-    @pl.when(j > 0)
+        lax.fori_loop(0, tiles, lambda i, c: body(i, True, False), 0)
+
+    @pl.when((j > 0) & (j < n - 1))
     def _():
-        lax.fori_loop(0, tiles, lambda i, c: body(i, False), 0)
+        lax.fori_loop(0, tiles, lambda i, c: body(i, False, False), 0)
 
     @pl.when(j == n - 1)
     def _():
-        if first_half:
-            x[...] = acc_in[...].astype(BF)
-            dy[...] = acc_out[...].astype(BF)
-            copies = [
-                pltpu.make_async_copy(x, outs[0], sem.at[0]),
-                pltpu.make_async_copy(dy, outs[1], sem.at[0]),
-            ]
-        else:
-            for copy in earlier():
-                copy.wait()
-            x[...] = (acc_in[...] + refs[7][...].astype(F32)).astype(BF)
-            dy[...] = (acc_out[...] + refs[8][...].astype(F32)).astype(BF)
-            copies = []
-            for r in range(n_grp):
-                rows = pl.ds(r * share, share)
-                copies.append(pltpu.make_async_copy(x.at[rows], outs[r], sem.at[0]))
-                copies.append(pltpu.make_async_copy(dy.at[rows], outs[n_grp + r], sem.at[0]))
-        for copy in copies:
+        for copy in earlier():
+            copy.wait()
+        lax.fori_loop(0, tiles, lambda i, c: body(i, False, True), 0)
+        for copy in results():
             copy.start()
-        for copy in copies:
+        for copy in results():
             copy.wait()
 
 
 def backward_kernel(
-    batch, per, pairs, n_grp, has_prev, scale, info, lens, q_ref, kv_ref, ve_ref, halo_ref, wq_ref,
+    batch, per, pairs, n_grp, has_prev, count, scale, info, table, q_ref, kv_ref, ve_ref, halo_ref, wq_ref,
     oin_ref, att_ref, w_ref, phi_ref, s_ref, r_ref, *refs,
 ):
     blocks_in, refs = refs[:n_grp], refs[n_grp:]
@@ -615,8 +713,8 @@
     step = pl.program_id(0)
     pair = pairs - 1 - step
     heads = kv_ref.shape[1] // PAIR
-    slots = Slots(lens, batch)
-    block = info[0] + 2 * pair
+    slots = Slots(table, batch, 2 * pairs, count)
+    block = 2 * pair
     q_width = q_ref.shape[0]
     per_block = blocks_in[0].shape[1] // PAIR
 
@@ -640,8 +738,8 @@
         map_ref[...] = prevs[0][...] if has_prev else jnp.zeros_like(map_ref)
         for copy in copies:
             copy.wait()
-    one_b = slots.weight(block, block + 1)
-    one_c = slots.weight(block + 1, block + 2)
+    one_b = slots.weight_one(block + 1)
+    one_c = slots.weight_one(block + 2)
     lanes = per * PAIR
     low = half_mask((EXT, lanes))
     rows = pl.ds(pl.multiple_of(pair * PAIR, PAIR), WIN)
@@ -711,7 +809,7 @@
 
 
 def keys_kernel(
-    batch, pairs, blocks, wide_y, count, n_far, has_prev, info, lens, kv_ref, ve_ref, wk_ref,
+    batch, pairs, per_block, wide_y, count, n_far, has_prev, info, table, kv_ref, ve_ref, wk_ref,
     phi_ref, dkv_ref, back_ref, ds_ref, dq_ref, q_up_ref, kv_up_ref, *refs,
 ):
     fars, refs = refs[:n_far], refs[n_far:]
@@ -720,21 +818,21 @@
     step = pl.program_id(0)
     pair = pairs - 1 - step
     heads = kv_ref.shape[1] // PAIR
-    slots = Slots(lens, batch)
-    block = info[0] + 2 * pair
+    slots = Slots(table, batch, 2 * pairs, count)
+    block = 2 * pair
 
     @pl.when(step == 0)
     def _():
         for k in range(heads):
-            inner, outer = entering(slots, info, fars, blocks, wide_y, count, -1, 0, k)
+            inner, outer = entering(slots, fars, wide_y, count, -1, batch, k)
             carry[k, 0] = outer
             carry[k, 1] = inner
         map_ref[...] = prevs[0][...] if has_prev else jnp.zeros_like(map_ref)
 
-    one_b = slots.weight(block, block + 1)
-    one_c = slots.weight(block + 1, block + 2)
-    two_c = slots.weight(block, block + 2)
-    two_d = slots.weight(block + 1, block + 3)
+    one_b = slots.weight_one(block + 1)
+    one_c = slots.weight_one(block + 2)
+    two_c = slots.weight_two(block + 2)
+    two_d = slots.weight_two(block + 3)
     row = lax.broadcasted_iota(jnp.int32, (PAIR, PAIR), 0)
     lane = lax.broadcasted_iota(jnp.int32, (PAIR, PAIR), 1)
     last = jnp.where(step == 0, 1.0, 0.0)
@@ -758,7 +856,7 @@
         d_key = dotg(d_mixed, wk_ref[k], 0, 0)
         map_ref[k] += dotg(kv, d_mixed, 0, 1)
         total = dkv_ref[rows, k * PAIR : (k + 1) * PAIR] + d_value + d_key
-        returned = back_ref[:, k * PAIR : (k + 1) * PAIR].astype(F32) * last
+        returned = back_ref[batch, :, k * PAIR : (k + 1) * PAIR].astype(F32) * last
         total = total + jnp.concatenate([jnp.zeros_like(returned), returned], axis=0)
         d_kvs.append(jnp.transpose(total).astype(BF))
         state = ds_ref[0, k]
@@ -766,17 +864,22 @@
         carry[k, 1] = rest
         carry[k, 0] = state[:EXT] + one_b * rest
     d_kv = jnp.concatenate(d_kvs, axis=0)
-    back_in = dotg(q_up_ref[...], dq_ref[0], 1, 0) + dotg(kv_up_ref[...], d_kv, 1, 0)
-    out_ref[0, :32, :] = (ADAPTER_SCALE * back_in).astype(BF)
-    out_ref[0, 32:, :] = d_kv
+    lanes = pl.ds(pl.multiple_of(pair % per_block * PAIR, PAIR), PAIR)
+    out_ref[(pair // per_block) ^ info[1], 32:, lanes] = d_kv
+
+    @pl.when(step == pairs - 1)
+    def _():
+        for r in range(out_ref.shape[0]):
+            back_in = dotg(q_up_ref[...], dq_ref[r], 1, 0) + dotg(
+                kv_up_ref[...], out_ref[r, 32:, :], 1, 0
+            )
+            out_ref[r, :32, :] = (ADAPTER_SCALE * back_in).astype(BF)
 
 
 def adapter_kernel(
-    n_grp, has_prev, info, dq_ref, rest_ref, mid_ref, normed_ref, att_ref, *refs
+    n_grp, info, dq_ref, rest_ref, mid_ref, normed_ref, att_ref, *refs
 ):
-    blocks_in, refs = refs[:n_grp], refs[n_grp:]
-    prevs, refs = (refs[:3], refs[3:]) if has_prev else (None, refs)
-    up_ref, oin_ref, wide_ref = refs
+    blocks_in, (up_ref, oin_ref, wide_ref) = refs[:n_grp], refs[n_grp:]
     share = blocks_in[0].shape[1]
     q_width = dq_ref.shape[1]
     for r in range(n_grp):
@@ -787,14 +890,85 @@
         up = dotg(mids, both, 1, 1)
         oin = dotg(ADAPTER_SCALE * blocks_in[r][q_width:], att_ref[r, :q_width, :], 1, 1)
         wide = dotg(rest[:32], normed_ref[there, :], 1, 0)
-        if r or has_prev:
-            up_ref[...] = up + (up_ref[...] if r else prevs[0][...])
-            oin_ref[...] = oin + (oin_ref[...] if r else prevs[1][...])
-            wide_ref[...] = wide + (wide_ref[...] if r else prevs[2][...])
-        else:
-            up_ref[...] = up
-            oin_ref[...] = oin
-            wide_ref[...] = wide
+        up_ref[...] = up if r == 0 else up_ref[...] + up
+        oin_ref[...] = oin if r == 0 else oin_ref[...] + oin
+        wide_ref[...] = wide if r == 0 else wide_ref[...] + wide
+
+
+def pack_early_kernel(per, map_ref, oin_a, oin_b, out_ref):
+    heads = map_ref.shape[0]
+    at = 0
+    for k in range(heads):
+        for g in range(0, per, 2):
+            pair = [
+                map_ref[k, h * STRETCH : (h + 1) * STRETCH, h * STRETCH : (h + 1) * STRETCH]
+                for h in (g, g + 1)
+            ]
+            out_ref[at : at + STRETCH, :] = jnp.concatenate(pair, axis=1).astype(BF)
+            at += STRETCH
+    oin = oin_a[...] + oin_b[...]
+    for c in range(oin.shape[1] // PAIR):
+        out_ref[at : at + 16, :] = oin[:, c * PAIR : (c + 1) * PAIR].astype(BF)
+        at += 16
+
+
+def pack_late_kernel(
+    q_width, up_a, up_b, key_ref, wide_in_a, wide_in_b, wide_out_a, wide_out_b, wide_ref, out_ref
+):
+    for c in range(wide_in_a.shape[1] // PAIR):
+        cols = slice(c * PAIR, (c + 1) * PAIR)
+        wide_in = wide_in_a[:24, cols] + wide_in_b[:24, cols]
+        wide_out = wide_out_a[:8, cols] + wide_out_b[:8, cols]
+        wide_ref[c * 32 : (c + 1) * 32, :] = jnp.concatenate([wide_in, wide_out], axis=0).astype(BF)
+    up = ADAPTER_SCALE * (up_a[...] + up_b[...])
+    at = 0
+    for c in range(q_width // PAIR):
+        out_ref[at : at + 16, :] = up[:16, c * PAIR : (c + 1) * PAIR].astype(BF)
+        at += 16
+    for k in range(key_ref.shape[0]):
+        first = q_width + 32 + k * PAIR
+        out_ref[at : at + 16, :] = up[8:24, first : first + PAIR].astype(BF)
+        at += 16
+    for k in range(key_ref.shape[0]):
+        block = key_ref[k, :STRETCH, :]
+        out_ref[at : at + STRETCH, :] = jnp.concatenate([block, block], axis=1).astype(BF)
+        at += STRETCH
+
+
+def unpack_kernel(
+    n_grp, columns, info, early_a, early_b, late_a, late_b,
+    wide_ref, q_ref, kv_ref, oin_ref, map_ref, key_ref, turned,
+):
+    early = early_a[...].astype(F32) + early_b[...].astype(F32)
+    at = 0
+    for h in range(0, map_ref.shape[0], 2):
+        map_ref[h] = early[at : at + STRETCH, :STRETCH]
+        map_ref[h + 1] = early[at : at + STRETCH, STRETCH:]
+        at += STRETCH
+    for c in range(oin_ref.shape[1] // PAIR):
+        oin_ref[:, c * PAIR : (c + 1) * PAIR] = early[at : at + 8, :]
+        at += 16
+    first = (info[2] * n_grp + info[1]) * columns
+    rows = pl.ds(pl.multiple_of((first // PAIR) * 32, 32), 32)
+    sums = late_a[rows, :].astype(F32) + late_b[rows, :].astype(F32)
+    turned[...] = jnp.transpose(sums)
+    wide_ref[...] = turned[pl.ds(pl.multiple_of(first % PAIR, 8), columns), :]
+    at = late_a.shape[0] - sum(
+        [q_ref.shape[1] // PAIR * 16, key_ref.shape[0] * 16, key_ref.shape[0] * STRETCH]
+    )
+    late = late_a[at:, :].astype(F32) + late_b[at:, :].astype(F32)
+    at = 0
+    for c in range(q_ref.shape[1] // PAIR):
+        q_ref[:, c * PAIR : (c + 1) * PAIR] = late[at : at + 8, :]
+        at += 16
+    for k in range(key_ref.shape[0]):
+        cols = slice(k * STRETCH, (k + 1) * STRETCH)
+        kv_ref[0, :, cols] = late[at : at + 8, :STRETCH]
+        kv_ref[1, :, cols] = late[at + 8 : at + 16, STRETCH:]
+        at += 16
+    for k in range(key_ref.shape[0]):
+        key_ref[k] = late[at : at + STRETCH, :STRETCH]
+        at += STRETCH
 
 
 def whole(shape):
@@ -842,7 +1016,28 @@
     )
 
 
-def run_project(info, lens, batch, normed, weight, q_up, kv_up, maps):
+def run_layout(info, lens, blocks):
+    count = lax.axis_size("seq")
+    size = lens.shape[0] * TABLE_ROWS * table_width(blocks, count)
+    return call(
+        functools.partial(layout_kernel, blocks, max(1, count // 4), count), "layout", 1,
+        [info, lens], [], [], pl.BlockSpec(memory_space=pltpu.SMEM), sds((size,), jnp.int32),
+    )
+
+
+def run_layer(table, ends, sign):
+    count = lax.axis_size("seq")
+    batches, heads = ends[0].shape[:2]
+    out = sds((batches, heads, EXT, PAIR), BF)
+    per_batch = table.shape[0] // batches // TABLE_ROWS
+    blocks = max(per_batch - 4, 0)
+    return call(
+        functools.partial(layer_kernel, sign, blocks, count, len(ends)), "layer", 1, [table], ends,
+        [whole(item.shape) for item in ends], [whole(out.shape)] * 2, [out] * 2,
+    )
+
+
+def run_project(table, batch, normed, weight, q_up, kv_up, maps):
     rows, model = normed.shape
     heads = maps.shape[0]
     width = heads * PAIR
@@ -850,8 +1045,10 @@
     tile = 2 * PAIR
     pairs = rows // PAIR
     return call(
-        functools.partial(project_kernel, batch, q_width),
-        "project_states", rows // tile, [info, lens],
+        functools.partial(
+            project_kernel, batch, q_width, rows // STRETCH, lax.axis_size("seq")
+        ),
+        "project_states", rows // tile, [table],
         [normed, weight, q_up, kv_up, maps],
         [
             pl.BlockSpec((tile, model), lambda i, *_: (i, 0)),
@@ -881,7 +1078,7 @@
     )
 
 
-def run_forward(info, lens, batch, q, kv, ve, halo, maps, o_in, states, fars):
+def run_forward(info, table, batch, q, kv, ve, halo, maps, o_in, states, fars):
     q_width, rows = q.shape
     width = kv.shape[1]
     heads, pairs = width // PAIR, rows // PAIR
@@ -896,7 +1093,7 @@
         functools.partial(
             forward_kernel, batch, per, rows // STRETCH, wide, count, len(fars), scale
         ),
-        "attention_forward", pairs, [info, lens],
+        "attention_forward", pairs, [info, table],
         [q, kv, ve, halo, maps, o_in, states, *fars],
         [
             column(q_width), whole(kv.shape), whole(ve.shape), whole(halo.shape),
@@ -1006,7 +1203,7 @@
     )
 
 
-def run_mlp(info, batch, xs, cotangent, rings, prevs, sizes):
+def run_mlp(info, batch, xs, rels, cotangent, rings, prevs, sizes):
     n_grp = len(xs)
     share, model = xs[0].shape
     rows = share * n_grp
@@ -1025,18 +1222,18 @@
         pltpu.VMEM((2, model, 3 * CHUNK), BF),
         pltpu.VMEM((rows, model), F32),
         pltpu.VMEM((rows, model), F32),
-        pltpu.SemaphoreType.DMA((2,)),
+        pltpu.SemaphoreType.DMA((rows // ROW_TILE + 1,)),
         pltpu.SemaphoreType.DMA((2,)),
     ] + [pltpu.VMEM((rows, model), BF) for _ in prevs]
     return call(
-        functools.partial(mlp_kernel, batch, n_grp, layout, sizes, first),
+        functools.partial(mlp_kernel, batch, rels, layout, sizes, first),
         "feed_forward", sum(sizes) // CHUNK, [info], ins, [anywhere()] * len(ins),
         [anywhere()] * len(out_shape), out_shape, scratch,
     )
 
 
 def run_backward(
-    info, lens, batch, q, kv, ve, halo, maps, o_in, att, weights, phi, states, inverse, d_outs, prevs,
+    info, table, batch, q, kv, ve, halo, maps, o_in, att, weights, phi, states, inverse, d_outs, prevs,
 ):
     q_width, rows = q.shape
     width = kv.shape[1]
@@ -1050,9 +1247,10 @@
     sums = [sds(maps.shape, F32)]
     return call(
         functools.partial(
-            backward_kernel, batch, per, pairs, len(d_outs), bool(prevs), STRETCH ** (-0.5)
+            backward_kernel, batch, per, pairs, len(d_outs), bool(prevs), lax.axis_size("seq"),
+            STRETCH ** (-0.5),
         ),
-        "attention_backward", pairs, [info, lens],
+        "attention_backward", pairs, [info, table],
         [q, kv, ve, halo, maps, o_in, att, weights, phi, states, inverse, *d_outs, *prevs],
         [
             column(q_width), whole(kv.shape), whole(ve.shape), whole(halo.shape),
@@ -1085,7 +1283,7 @@
 
 
 def run_keys(
-    info, lens, batch, kv, ve, maps, phi, d_kv, returned, d_states, d_q, q_up, kv_up, fars, prevs,
+    info, table, batch, kv, ve, maps, phi, d_kv, returned, d_states, d_q, q_up, kv_up, fars, prevs,
 ):
     width, rows = phi.shape
     heads, pairs = width // PAIR, rows // PAIR
@@ -1099,9 +1297,9 @@
     sums = [sds((heads, PAIR, STRETCH), F32)]
     return call(
         functools.partial(
-            keys_kernel, batch, pairs, rows // STRETCH, wide, count, len(fars), bool(prevs)
+            keys_kernel, batch, pairs, share // PAIR, wide, count, len(fars), bool(prevs)
         ),
-        "attention_keys", pairs, [info, lens],
+        "attention_keys", pairs, [info, table],
         [
             kv, ve, maps, phi, d_kv, returned, d_states, d_q, q_up, kv_up, *fars, *prevs,
         ],
@@ -1109,37 +1307,41 @@
             lines(width), lines(width), whole(maps.shape), column(width), whole(d_kv.shape),
             whole(returned.shape),
             pl.BlockSpec((1, heads, 2 * EXT, PAIR), lambda i, *_: (rev(i), 0, 0, 0)),
-            block_spec(q_width, share, rev), whole(q_up.shape), whole(kv_up.shape),
+            whole(d_q.shape), whole(q_up.shape), whole(kv_up.shape),
             *[whole(far.shape) for far in fars], *[whole(prev.shape) for prev in prevs],
         ],
-        [block_spec(32 + width, share, rev), *[whole(item.shape) for item in sums]],
+        [whole((n_grp, 32 + width, share)), *[whole(item.shape) for item in sums]],
         [sds((n_grp, 32 + width, share), BF), *sums],
         [pltpu.VMEM((heads, 2, EXT, PAIR), F32)],
     )
 
 
-def run_adapters(info, d_q, rest, mids, normed, att, d_outs, prevs):
+def run_adapters(info, d_q, rest, mids, normed, att, d_outs):
     model = normed.shape[1]
-    prevs = list(prevs or [])
-    ins = [d_q, rest, mids, normed, att, *d_outs, *prevs]
+    ins = [d_q, rest, mids, normed, att, *d_outs]
     out_shape = [
         sds((32, d_q.shape[1] + rest.shape[1]), F32), sds((16, d_q.shape[1]), F32),
         sds((32, model), F32),
     ]
     return call(
-        functools.partial(adapter_kernel, len(d_outs), bool(prevs)),
+        functools.partial(adapter_kernel, len(d_outs)),
         "adapter_gradients", 1, [info], ins, [whole(item.shape) for item in ins],
         [whole(item.shape) for item in out_shape], out_shape,
     )
 
 
-def summed(value, axis):
-    value = value.astype(BF)
-    bit = 1
-    while bit < lax.axis_size(axis):
-        value = (value.astype(F32) + flip(value, axis, bit).astype(F32)).astype(BF)
-        bit *= 2
-    return value
+def run_plain(kernel, name, scalars, ins, out_shape, scratch=()):
+    return call(
+        kernel, name, 1, scalars, ins, [whole(item.shape) for item in ins],
+        [whole(item.shape) for item in out_shape], out_shape, scratch,
+    )
+
+
+def group_sum(value):
+    total = value.astype(F32)
+    for r in range(1, lax.axis_size("grp")):
+        total = total + flip(value, "grp", r).astype(F32)
+    return total.astype(BF)
 
 
 def local(
@@ -1208,7 +1410,7 @@
         )
         for first, size in pieces_of(hidden_width)
     ]
-    ring_a, ring_b, ring_c = rings = [Ring(shard) for shard in half_shards]
+    ring_a, ring_c = [Ring(shard) for shard in half_shards]
     kv_parts = keyvalue_up_factor.reshape(2, rank, kv_heads, STRETCH)
     kv_up = jnp.zeros((2, rank, kv_heads, 2, STRETCH), BF)
     kv_up = kv_up.at[0, :, :, 0].set(kv_parts[0]).at[1, :, :, 1].set(kv_parts[1])
@@ -1235,17 +1437,15 @@
         normed_rows.append((x * factor * gain_attn).astype(BF))
     in_ring.hop()
     in_ring.hop()
-    query_maps, key_maps, kv_up, q_up_t, normed_rows[0] = in_ring.tie(
-        query_maps, key_maps, kv_up, q_up_t, normed_rows[0]
+    table = run_layout(info, lengths, rows // STRETCH)
+    table, query_maps, key_maps, kv_up, q_up_t, normed_rows[0] = in_ring.tie(
+        table, query_maps, key_maps, kv_up, q_up_t, normed_rows[0]
     )
     in_ring.hop()
-    for ring in rings[:2]:
-        ring.ahead, ring.back, *_ = lax.optimization_barrier((ring.ahead, ring.back))
     normed_rows[1] = in_ring.tie(normed_rows[1])[0]
     while in_ring.done < in_ring.hops():
         in_ring.hop()
-    ring_a.hop(*in_ring.parts[5:7])
-    ring_b.hop(*in_ring.parts[5:7])
+    ring_a.hop(*in_ring.parts[-2:])
     weight_in, weight_out = run_assemble(
         info, in_ring, [q_width + 32 + kv_width, q_width + 2 * rank]
     )
@@ -1255,62 +1455,60 @@
     for batch in range(batches):
         normed = normed_rows[batch]
         q, kv, ve, mids, phi_key, states, ends, halo = run_project(
-            info, lengths, batch, normed, weight_in, q_up_t, kv_up, key_maps
+            table, batch, normed, weight_in, q_up_t, kv_up, key_maps
         )
         saved.append([q, kv, ve, mids, normed, phi_key, states, ends, halo])
     ends = jnp.stack([item[7] for item in saved])
     halo = jnp.stack([item[8] for item in saved])
     (ends,) = ring_a.tie(ends)
-    (ends,) = ring_b.tie(ends)
-    fars, halo = exchange(ends, halo, 1)
+    fars, halo = exchange(table, ends, halo, 1)
     for item in saved:
         item[7:] = [fars, halo]
-    ring_a.hop(*fars[1:])
-    ring_b.hop(*fars[1:])
-
-    attended = []
+    ring_a.hop(*fars[1:], halo)
+
+    attended, att_sets, far_mlp, mlp_ins = [], [], [], []
     for batch in range(batches):
         q, kv, ve, mids, normed, phi_key, states, fars, halo = saved[batch]
         if batch:
-            q = after(q, attended[0][0])
+            q = after(q, att)
         att, weights, phi, sums, inverse = run_forward(
-            info, lengths, batch, q, kv, ve, halo, query_maps, o_in, states, fars
+            info, table, batch, q, kv, ve, halo, query_maps, o_in, states, fars
         )
         atts = group_exchange([att[r] for r in range(n_grp)])
-        attended.append([att, weights, phi, sums, inverse, atts])
+        att_sets.append([att, *atts[1:]])
+        attended.append([att, weights, phi, sums, inverse])
     far_out = [far_out[0]] + [after(far, attended[0][0]) for far in far_out[1:]]
     weights_out = near_gather(far_out)
-    mlp_ins = []
+    att_sets[0][0] = after(att_sets[0][0], att_sets[1][0])
     for batch in range(batches):
-        att, weights, phi, sums, inverse, atts = attended[batch]
         if batch:
-            atts[-1] = after(atts[-1], mlp_ins[0][0])
+            att_sets[1][0] = after(att_sets[1][0], mlp_in)
         resid, mlp_in, mid = run_residual(
-            info, batch, tokens, gain_mlp, [att, *atts[1:]], weights_out
+            info, batch, tokens, gain_mlp, att_sets[batch], weights_out
         )
-        if batch == 0:
-            (mlp_in,) = ring_a.tie(mlp_in)
-            (mlp_in,) = ring_b.tie(mlp_in)
-            ring_a.hop(mlp_in)
-            ring_b.hop(mlp_in)
-        attended[batch][5:] = [resid, mid]
-        mlp_ins.append(group_gather(mlp_in))
-    ring_a.hop(mlp_ins[1][0])
-    ring_b.hop(mlp_ins[1][0])
-    ring_c.hop(mlp_ins[1][0], *ring_a.parts[-2:], *ring_b.parts[-2:])
+        attended[batch] += [resid, mid]
+        (mlp_in,) = ring_a.tie(mlp_in)
+        ring_a.hop()
+        far_mlp.append(far_gather(mlp_in))
+    ring_a.finish()
+    held = ring_a.parts[-2:]
+    held = lax.optimization_barrier((*far_mlp[0], *far_mlp[1], *held))
+    far_mlp = [list(held[: len(far_mlp[0])]), list(held[len(far_mlp[0]) : 2 * len(far_mlp[0])])]
+    ring_c.hop(held[0])
+    for batch in range(batches):
+        mlp_ins.append(near_gather(far_mlp[batch]))
 
     sizes = [size for _, size in pieces_of(hidden_width)]
     partial = [None] * batches
-    ring_a.finish()
-    ring_b.finish()
+    every = list(range(n_grp))
     partial[0] = list(
-        run_mlp(info, 0, mlp_ins[0], cotangent, [ring_a, ring_b], None, sizes[:2])
+        run_mlp(info, 0, mlp_ins[0], every, cotangent, [ring_a], None, sizes[:1])
     )
     partial[0][0], mlp_ins[1][0] = ring_c.tie(partial[0][0], mlp_ins[1][0])
     ring_c.hop()
-    far_in = far_gather(after(weight_in, partial[0][0]))
+    far_in = far_gather(after(weight_in, partial[0][0], *mlp_ins[1][2:]))
     partial[1] = list(
-        run_mlp(info, 1, mlp_ins[1], cotangent, [ring_a, ring_b], None, sizes[:2])
+        run_mlp(info, 1, mlp_ins[1], every, cotangent, [ring_a], None, sizes[:1])
     )
     (partial[1][0],) = ring_c.tie(partial[1][0])
     ring_c.hop()
@@ -1318,18 +1516,14 @@
     far_in, partial[0][0] = lax.optimization_barrier((far_in, partial[0][0]))
     weights_in = near_gather(far_in)
     partial[0] = list(
-        run_mlp(info, 0, mlp_ins[0], cotangent, [ring_c], partial[0], sizes[2:])
+        run_mlp(info, 0, mlp_ins[0], every, cotangent, [ring_c], partial[0], sizes[1:])
     )
     started = [scatter_start(partial[0][:n_grp])]
     started[0][0][0], partial[1][0] = lax.optimization_barrier((started[0][0][0], partial[1][0]))
-    partial[1] = list(
-        run_mlp(info, 1, mlp_ins[1], cotangent, [ring_c], partial[1], sizes[2:])
-    )
-
-    def run_branch_of(batch):
+    def run_branch_of(batch, summands):
         resid, mid = attended[batch][5:]
         d_resid, wide, *d_out = run_branch(
-            info, batch, cotangent, resid, gain_mlp, mid, scatter_end(*started[batch]), weights_out
+            info, batch, cotangent, resid, gain_mlp, mid, summands, weights_out
         )
         return d_resid, wide, group_exchange(d_out)
 
@@ -1337,26 +1531,24 @@
         _, kv, ve, mids, normed, phi_key, states, fars, halo = saved[batch]
         att, weights, phi, sums, inverse = attended[batch][:5]
         d_q, d_kv, d_states, ends, back, *sums_back = run_backward(
-            info, lengths, batch, q, kv, ve, halo, query_maps, o_in, att, weights, phi, sums,
+            info, table, batch, q, kv, ve, halo, query_maps, o_in, att, weights, phi, sums,
             inverse, d_outs, sums_back,
         )
-        fars, returned = exchange(ends[None], back, -1)
-        d_qs = group_exchange([d_q[r] for r in range(n_grp)])
-        return [d_q, d_qs, d_kv, d_states, fars, returned], sums_back
+        return [d_q, None, d_kv, d_states], ends, back, sums_back
 
     def run_keys_of(batch, kv, gone, sums_keys):
         _, _, ve, mids, normed, phi_key, states, _, _ = saved[batch]
         d_q, d_qs, d_kv, d_states, fars, returned = gone
         rest, *sums_keys = run_keys(
-            info, lengths, batch, kv, ve, key_maps, phi_key, d_kv, returned, d_states, d_q, q_up,
+            info, table, batch, kv, ve, key_maps, phi_key, d_kv, returned, d_states, d_q, q_up,
             kv_up, fars, sums_keys,
         )
         rests = group_exchange([rest[r] for r in range(n_grp)])
         return [rest, *rests[1:]], sums_keys
 
-    def run_adapters_of(batch, d_q, rest, d_outs, prevs):
+    def run_adapters_of(batch, d_q, rest, d_outs):
         return run_adapters(
-            info, d_q, rest, saved[batch][3], saved[batch][4], attended[batch][0], d_outs, prevs
+            info, d_q, rest, saved[batch][3], saved[batch][4], attended[batch][0], d_outs
         )
 
     def run_tokens_of(batch, d_resid, gone, rests, prev):
@@ -1365,66 +1557,118 @@
             info, batch, tokens, gain_attn, d_resid, [d_q, *d_qs[1:]], rests, weights_in, prev
         )
 
-    d_resid_a, wide_a, d_outs_a = run_branch_of(0)
+    def finish_rows(batch, *ready):
+        blocks = partial[batch][n_grp:]
+        blocks[0] = after(blocks[0], *ready)
+        blocks[1], blocks[-1] = after(blocks[1], *ready), after(blocks[-1], *ready)
+        return scatter_start(blocks)
+
+    def rows_of(batch, summands):
+        total = attended[batch][5]
+        for summand in summands:
+            total = total + summand.astype(F32)
+        return total.astype(BF)
+
+    low = n_grp // 2
+    upper = run_mlp(
+        info, 1, mlp_ins[1][low:], every[low:], cotangent, [ring_c], partial[1], sizes[1:]
+    )
+    summands_a = scatter_end(*started[0])
+    crossed = [flip(upper[far + 1 - low], "grp", 1) for far in range(low, n_grp, 2)]
+    crossed[0], summands_a[-1] = lax.optimization_barrier((crossed[0], summands_a[-1]))
+    far_b = [
+        (upper[far - low].astype(F32) + there.astype(F32)).astype(BF)
+        for far, there in zip(range(low, n_grp, 2), crossed)
+    ]
+    attended[0][6] = after(attended[0][6], far_b[0])
+    d_resid_a, wide_a, d_outs_a = run_branch_of(0, summands_a)
     partial[1][0] = after(partial[1][0], d_resid_a)
-    started.append(scatter_start(partial[1][:n_grp]))
-    started[1][0][0] = after(started[1][0][0], *d_outs_a[1:])
-    gone_a, sums_back = run_backward_of(0, saved[0][0], d_outs_a, None)
-    attended[1][6] = after(attended[1][6], gone_a[0])
-    d_resid_b, wide_b, d_outs_b = run_branch_of(1)
-    rests_a, sums_keys = run_keys_of(0, after(saved[0][1], d_resid_b), gone_a, None)
-    gone_b, sums_back = run_backward_of(
-        1, after(saved[1][0], rests_a[0]), d_outs_b, sums_back
-    )
-    sums_adapters = run_adapters_of(
-        0, after(gone_a[0], gone_b[0]), rests_a[0], d_outs_a, None
-    )
-    grad_tokens = run_tokens_of(
-        0, after(d_resid_a, sums_adapters[0]), gone_a, rests_a, None
-    )
-    rests_b, sums_keys = run_keys_of(1, after(saved[1][1], grad_tokens), gone_b, sums_keys)
-    sums_adapters = run_adapters_of(1, gone_b[0], rests_b[0], d_outs_b, sums_adapters)
-    grad_tokens = run_tokens_of(
-        1, after(d_resid_b, sums_adapters[0]), gone_b, rests_b, grad_tokens
-    )
-    wide_out = wide_a + wide_b
-    block_rows = []
-    for batch, ready in enumerate([rests_a[0], rests_b[0]]):
-        blocks = partial[batch][n_grp:]
-        blocks[0] = after(blocks[0], ready)
-        blocks[1], blocks[-1] = after(blocks[1], ready), after(blocks[-1], ready)
-        total = attended[batch][5]
-        for summand in scatter_end(*scatter_start(blocks)):
-            total = total + summand.astype(F32)
-        block_rows.append(total.astype(BF))
-
-    (map_grad,), (key_grad,) = sums_back, sums_keys
-    up_grad, oin_grad, wide_in = sums_adapters
-    wide = jnp.concatenate([wide_in[: 3 * rank], wide_out[:rank]])
-    up_grad = ADAPTER_SCALE * up_grad
-    kv_grad = up_grad[rank : 3 * rank, q_width + 32 :].reshape(2, rank, kv_heads, 2, STRETCH)
-    kv_grad = jnp.stack([kv_grad[0, :, :, 0], kv_grad[1, :, :, 1]])
-    map_blocks = map_grad.reshape(kv_heads, per, STRETCH, per, STRETCH)
-    query_grad = jnp.stack([map_blocks[:, g, :, g] for g in range(per)], axis=1)
-    pieces = [
-        (up_grad[:rank, :q_width], query_up_factor.shape),
-        (kv_grad, keyvalue_up_factor.shape),
-        (oin_grad[:rank].T, output_input_factor.shape),
-        (query_grad, query_feature_weight.shape),
-        (key_grad[:, :STRETCH], key_feature_weight.shape),
-    ]
-    wide = summed(wide, "grp")
-    packed = jnp.concatenate(
-        [wide.reshape(-1)] + [piece.astype(BF).reshape(-1) for piece, _ in pieces]
-    ).reshape(-1, PAIR)
-    packed = summed(packed, "seq").reshape(-1).astype(F32)
-    wide = packed[: wide.size].reshape(4, rank, n_seq * n_grp, model // (n_seq * n_grp))
-    wide = lax.dynamic_index_in_dim(wide, seq_index * n_grp + group_index, 2, False)
-    outs, first = [], 4 * rank * model
-    for piece, shape in pieces:
-        outs.append(packed[first : first + piece.size].reshape(shape))
-        first += piece.size
-    return (jnp.stack(block_rows), grad_tokens, wide.transpose(0, 2, 1), *outs)
+    lower = list(
+        run_mlp(info, 1, mlp_ins[1][:low], every[:low], cotangent, [ring_c], partial[1], sizes[1:])
+    )
+    late_b = scatter_end(far_b, [])
+    lower[1], late_b[-1] = lax.optimization_barrier((lower[1], late_b[-1]))
+    near_b = [lower[0], flip(lower[1], "grp", 1)]
+    early_b = [far_pair(lower[far], lower[far + 1]) for far in range(2, low, 2)]
+    summands_b = near_b + scatter_end(early_b, []) + late_b
+    partial[1] = [None] * n_grp + list(lower[low:]) + list(upper[low:])
+    d_resid_b, wide_b, d_outs_b = run_branch_of(1, summands_b)
+    gone_a, ends_a, back_a, sums_back = run_backward_of(
+        0, after(saved[0][0], d_resid_b), d_outs_a, None
+    )
+    rows_a = finish_rows(0, *d_outs_a[2:], *d_outs_b[2:])
+    gone_b, ends_b, back_b, sums_back = run_backward_of(
+        1, after(saved[1][0], gone_a[0]), d_outs_b, sums_back
+    )
+    fars, returned = exchange(table, jnp.stack([ends_a, ends_b]), jnp.stack([back_a, back_b]), -1)
+    gone_a += [fars, returned]
+    gone_b += [fars, returned]
+    rows_a = scatter_end(*rows_a)
+    kv_a, rows_a[-1] = lax.optimization_barrier((after(saved[0][1], gone_b[0]), rows_a[-1]))
+    rests_a, sums_keys = run_keys_of(0, kv_a, gone_a, None)
+    kv_b = after(saved[1][1], rests_a[0])
+    d_q = after(gone_a[0], rests_a[0])
+    gone_a[1] = group_exchange([d_q[r] for r in range(n_grp)])
+    rests_b, sums_keys = run_keys_of(1, kv_b, gone_b, sums_keys)
+    d_q = after(gone_b[0], rests_b[0])
+    gone_b[1] = group_exchange([d_q[r] for r in range(n_grp)])
+    sums_a = run_adapters_of(0, after(gone_a[0], rests_b[0]), rests_a[0], d_outs_a)
+    rows_b = finish_rows(1, rests_b[0])
+    sums_b = run_adapters_of(
+        1, after(gone_b[0], sums_a[0], *rests_a[1:], *gone_a[1][1:]), rests_b[0], d_outs_b
+    )
+
+    (early,) = run_plain(
+        functools.partial(pack_early_kernel, per), "pack_early", [],
+        [sums_back[0], sums_a[1], sums_b[1]],
+        [sds((STRETCH * kv_heads * per // 2 + 16 * (q_width // PAIR), PAIR), BF)],
+    )
+    late_rows = 16 * (q_width // PAIR) + (16 + STRETCH) * kv_heads
+    wide, late = run_plain(
+        functools.partial(pack_late_kernel, q_width), "pack_late", [],
+        [sums_a[0], sums_b[0], sums_keys[0], sums_a[2], sums_b[2], wide_a, wide_b],
+        [sds((32 * (model // PAIR), PAIR), BF), sds((late_rows, PAIR), BF)],
+    )
+    wide = group_sum(wide)
+    wide = after(wide, *rests_b[1:], *gone_b[1][1:])
+    first = early.shape[0]
+    columns = model // (n_seq * n_grp)
+    value, bits = jnp.concatenate([early, wide, late]), n_seq.bit_length() - 1
+    grad_tokens, held = None, [d_resid_a, d_resid_b]
+    for step in range(bits):
+        there = flip(value, "seq", 1 << step)
+        batch = step - (bits - 2)
+        if batch >= 0:
+            gone, rests = ((gone_a, rests_a), (gone_b, rests_b))[batch]
+            grad_tokens = run_tokens_of(
+                batch, after(held[batch], value), gone, rests, grad_tokens
+            )
+            there, grad_tokens = lax.optimization_barrier((there, grad_tokens))
+        if step < bits - 1:
+            value = (value.astype(F32) + there.astype(F32)).astype(BF)
+    packed = (value, there)
+    rows_b = scatter_end(*rows_b)
+    block_rows = [rows_of(0, rows_a), rows_of(1, rows_b)]
+    wide, q_grad, kv_grad, oin_grad, query_grad, key_grad = run_plain(
+        functools.partial(unpack_kernel, n_grp, columns), "unpack", [info],
+        [packed[0][:first], packed[1][:first], packed[0][first:], packed[1][first:]],
+        [
+            sds((columns, 32), F32), sds((rank, q_width), F32),
+            sds((2, rank, kv_heads * STRETCH), F32), sds((rank, q_width), F32),
+            sds(query_feature_weight.shape, F32), sds(key_feature_weight.shape, F32),
+        ],
+        [pltpu.VMEM((PAIR, 32), F32)],
+    )
+    return (
+        jnp.stack(block_rows),
+        grad_tokens,
+        wide.reshape(columns, 4, rank).transpose(1, 0, 2),
+        q_grad,
+        kv_grad,
+        oin_grad.T,
+        query_grad,
+        key_grad,
+    )
 
 
 def solution(mesh):

time: 779 us -> 739 us (0.949)
  starting transfers between devices: 99.9 us -> 77.5 us
  other arithmetic: 39.9 us -> 32.1 us
    ppermute x32 -> x24, waiting for transfers between devices: 124 us -> 109 us  [move(): return lax.ppermute(value, 'seq', pairs)]
    ppermute x12 -> x10, starting transfers between devices: 31.2 us -> 19.4 us  [shifted(): lax.ppermute(value, axis, [(i, i + steps) for i in range(first, last)])]
    ppermute x12 -> x10, waiting for transfers between devices: 3.73 us -> 13.4 us  [shifted(): lax.ppermute(value, axis, [(i, i + steps) for i in range(first, last)])]
    ppermute x32 -> x24, starting transfers between devices: 32.4 us -> 27.1 us  [move(): return lax.ppermute(value, 'seq', pairs)]
    pallas_call x21 -> x28, Pallas kernels: 353 us -> 357 us  [call(): pl.pallas_call(kernel, grid_spec=pltpu.PrefetchScalarGridSpec(num_scalar_...]
    unnamed x211 -> x186, local copies, waits for them, and re-layouts: 16.1 us -> 19.9 us
  transfers between devices with their start and end apart: 100 -> 90, of which waited for: 44 -> 45; matrix products, arithmetic and copies ran while one was open for 9% -> 7% of each run, Pallas kernels for 40% -> 43%
where the time goes in v3:
time: 739 us; the launch traced here: 731 us
  Pallas kernels  357 us (48%)
  waiting for transfers between devices  219 us (30%)
  starting transfers between devices  77.5 us (10%)
  local copies, waits for them, and re-layouts  42.9 us (6%)
  other arithmetic  32.1 us (4%)
    pallas_call x28, Pallas kernels, call(): pl.pallas_call(kernel, grid_spec=pltpu.PrefetchScalarGridSpec(num_scalar_...  357 us
    ppermute x24, waiting for transfers between devices, move(): return lax.ppermute(value, 'seq', pairs)  109 us
    ppermute x56, waiting for transfers between devices, flip(): return lax.ppermute(value, axis, [(i, i ^ bit) for i in range(count)])  96.5 us
    ppermute x56, starting transfers between devices, flip(): return lax.ppermute(value, axis, [(i, i ^ bit) for i in range(count)])  31 us
    ppermute x24, starting transfers between devices, move(): return lax.ppermute(value, 'seq', pairs)  27.1 us
    unnamed x186, local copies, waits for them, and re-layouts  19.9 us
    ppermute x10, starting transfers between devices, shifted(): lax.ppermute(value, axis, [(i, i + steps) for i in range(first, last)])  19.4 us
  transfers between devices with their start and end apart: 90, of which 45 were waited for; matrix products, arithmetic and copies ran while one was open for 7% of the time, Pallas kernels for 43%

profile of v3, /device:TPU:0, one launch (start us, length us, event | category | flops | bytes accessed | tf_op | source)
XLA Modules:
  0.0 730.5 jit_solution(17383432082626882869)
XLA Ops:
  5.3 3.0 collective-permute-start
  13.1 2.3 layout.1.table
  16.1 4.6 fusion.3
  20.7 2.9 collective-permute-done.refs_1_
  27.2 4.4 fusion.5
  31.6 9.7 %collective-permute-done.2.refs_3_ = bf16[1328,256]{1,0:T(8,128)(2,1)} collective-permute-done((bf16[1328,256]{1,0:T(8,128)(2,1)}, bf16[1328,256]{1,0:T(8,128)(2,1)}, u32[]{:S(2)}, u32[]{:S(2)}) %collective-permute-start.2) | collective-permute-done | bytes 679968 | tf_op jit(solution)/shard_map/ppermute | solution.py:77
  46.1 3.9 fusion.12
  50.0 7.5 %collective-permute-done.4.refs_5_ = bf16[1328,256]{1,0:T(8,128)(2,1)} collective-permute-done((bf16[1328,256]{1,0:T(8,128)(2,1)}, bf16[1328,256]{1,0:T(8,128)(2,1)}, u32[]{:S(2)}, u32[]{:S(2)}) %collective-permute-start.4) | collective-permute-done | bytes 679968 | tf_op jit(solution)/shard_map/ppermute | solution.py:77
  64.1 3.9 collective-permute-done.7.refs_8_
  69.5 6.4 assemble.1
  81.8 17.1 %project_states.3 = (bf16[512,1024]{1,0:T(8,128)(2,1)}, bf16[1024,256]{1,0:T(8,128)(2,1)}, bf16[1024,256]{1,0:T(8,128)(2,1)}, bf16[32,1024]{1,0:T(8,128)(2,1)}, ...) custom-call(s32[600]{0:T(1024)} %layout.1.table, ...), custom_call_target="tpu_custom_call" | custom-call | bytes 1024 | tf_op jit(solution)/shard_map/project_states/pallas_call | solution.py:989
  99.0 17.3 %project_states.2 = (bf16[512,1024]{1,0:T(8,128)(2,1)}, bf16[1024,256]{1,0:T(8,128)(2,1)}, bf16[1024,256]{1,0:T(8,128)(2,1)}, bf16[32,1024]{1,0:T(8,128)(2,1)}, ...) custom-call(s32[600]{0:T(1024)} %layout.1.table, ...), custom_call_target="tpu_custom_call" | custom-call | bytes 1024 | tf_op jit(solution)/shard_map/project_states/pallas_call | solution.py:989
  118.6 3.5 collective-permute-start.8
  123.3 2.4 layer.2
  125.7 3.4 collective-permute-start.13
  138.2 11.0 %attention_forward.2 = (bf16[4,528,256]{2,1,0:T(8,128)(2,1)}, bf16[8,2,192,512]{3,2,1,0:T(8,128)(2,1)}, bf16[8,2,128,512]{3,2,1,0:T(8,128)(2,1)}, bf16[8,2,160,128]{3,2,1,0:T(8,128)(2,1)}, f32[8,8,128]{2,1,0:T(8,128)}) custom-call(s32[11]{0:T(128)} %pad_add_fusion.info, s32[600]{0:T(1024)} %layout.1.table, bf16[512,1024]{1,0:T(8,128)(2,1)} %get-tuple-element.389.q_ref, ...), custom_call_target="tpu_custom_call" | custom-call | bytes 1024 | tf_op jit(solution)/shard_map/attention_forward/pallas_call | solution.py:989
  153.2 8.2 %collective-permute-done.18.refs_3_ = bf16[528,256]{1,0:T(8,128)(2,1)S(1)} collective-permute-done((bf16[528,256]{1,0:T(8,128)(2,1)S(1)}, bf16[528,256]{1,0:T(8,128)(2,1)S(1)}, u32[]{:S(2)}, u32[]{:S(2)}) %collective-permute-start.18) | collective-permute-done | bytes 270368 | tf_op jit(solution)/shard_map/ppermute | solution.py:108
  161.8 8.4 %collective-permute-done.17.refs_2_ = bf16[528,256]{1,0:T(8,128)(2,1)S(1)} collective-permute-done((bf16[528,256]{1,0:T(8,128)(2,1)S(1)}, bf16[528,256]{1,0:T(8,128)(2,1)S(1)}, u32[]{:S(2)}, u32[]{:S(2)}) %collective-permute-start.17) | collective-permute-done | bytes 270368 | tf_op jit(solution)/shard_map/ppermute | solution.py:108
  171.0 10.9 %attention_forward.3 = (bf16[4,528,256]{2,1,0:T(8,128)(2,1)}, bf16[8,2,192,512]{3,2,1,0:T(8,128)(2,1)}, bf16[8,2,128,512]{3,2,1,0:T(8,128)(2,1)}, bf16[8,2,160,128]{3,2,1,0:T(8,128)(2,1)}, f32[8,8,128]{2,1,0:T(8,128)}) custom-call(s32[11]{0:T(128)} %pad_add_fusion.info, s32[600]{0:T(1024)} %layout.1.table, bf16[512,1024]{1,0:T(8,128)(2,1)} %get-tuple-element.397.q_ref, ...), custom_call_target="tpu_custom_call" | custom-call | bytes 1024 | tf_op jit(solution)/shard_map/attention_forward/pallas_call | solution.py:989
  183.3 9.3 %residual.2 = (f32[256,2048]{1,0:T(8,128)}, bf16[256,2048]{1,0:T(8,128)(2,1)}, bf16[16,256]{1,0:T(8,128)(2,1)}) custom-call(s32[11]{0:T(128)} %pad_add_fusion.info, bf16[2,1024,2048]{2,1,0:T(8,128)(2,1)} %x_ref.7, f32[1,2048]{1,0:T(1,128)} %bitcast.118, bf16[4,528,256]{2,1,0:T(8,128)(2,1)} %get-tuple-element.314.refs_0_.att_ref, ...), custom_call_target="tpu_custom_call" | custom-call | bytes 1024 | tf_op jit(solution)/shard_map/residual/pallas_call | solution.py:989
  196.8 6.7 collective-permute-done.29.refs_3_
  203.9 5.9 collective-permute-done.28.refs_2_
  211.2 9.2 %residual.3 = (f32[256,2048]{1,0:T(8,128)}, bf16[256,2048]{1,0:T(8,128)(2,1)}, bf16[16,256]{1,0:T(8,128)(2,1)}) custom-call(s32[11]{0:T(128)} %pad_add_fusion.info, bf16[2,1024,2048]{2,1,0:T(8,128)(2,1)} %x_ref.7, f32[1,2048]{1,0:T(1,128)} %bitcast.119, bf16[4,528,256]{2,1,0:T(8,128)(2,1)} %get-tuple-element.328.refs_0_.att_ref, ...), custom_call_target="tpu_custom_call" | custom-call | bytes 1024 | tf_op jit(solution)/shard_map/residual/pallas_call | solution.py:989
  220.3 9.2 %collective-permute-done.25.refs_10_ = bf16[256,3072]{1,0:T(8,128)(2,1)S(1)} collective-permute-done((bf16[256,3072]{1,0:T(8,128)(2,1)}, bf16[256,3072]{1,0:T(8,128)(2,1)S(1)}, u32[]{:S(2)}, u32[]{:S(2)}) %collective-permute-start.25) | collective-permute-done | bytes 1572896 | tf_op jit(solution)/shard_map/ppermute | solution.py:77
  234.7 16.0 %collective-permute-done.32.refs_13_ = bf16[128,3072]{1,0:T(8,128)(2,1)S(1)} collective-permute-done((bf16[128,3072]{1,0:T(8,128)(2,1)S(1)}, bf16[128,3072]{1,0:T(8,128)(2,1)S(1)}, u32[]{:S(2)}, u32[]{:S(2)}) %collective-permute-start.32) | collective-permute-done | bytes 786464 | tf_op jit(solution)/shard_map/ppermute | solution.py:77
  251.1 5.2 collective-permute-done.30.refs_2_.refs_0_
  258.9 3.8 collective-permute-done.34.refs_3_
  263.7 35.3 %feed_forward.5 = (bf16[1024,2048]{1,0:T(8,128)(2,1)}, bf16[1024,2048]{1,0:T(8,128)(2,1)}) custom-call(s32[11]{0:T(128)} %pad_add_fusion.info, bf16[256,2048]{1,0:T(8,128)(2,1)} %get-tuple-element.335.refs_0_, bf16[256,2048]{1,0:T(8,128)(2,1)} %collective-permute-done.33.refs_1_, bf16[256,2048]{1,0:T(8,128)(2,1)} %collective-permute-done.24.refs_2_, ...), custom_call_target="tpu_custom_call" | custom-call | bytes 1024 | tf_op jit(solution)/shard_map/feed_forward/pallas_call | solution.py:989
  304.1 35.3 %feed_forward.6 = (bf16[1024,2048]{1,0:T(8,128)(2,1)}, bf16[1024,2048]{1,0:T(8,128)(2,1)}) custom-call(s32[11]{0:T(128)} %pad_add_fusion.info, bf16[256,2048]{1,0:T(8,128)(2,1)} %get-tuple-element.345.refs_0_, bf16[256,2048]{1,0:T(8,128)(2,1)} %collective-permute-done.39.refs_1_, bf16[256,2048]{1,0:T(8,128)(2,1)} %collective-permute-done.30.refs_2_.refs_0_, ...), custom_call_target="tpu_custom_call" | custom-call | bytes 1024 | tf_op jit(solution)/shard_map/feed_forward/pallas_call | solution.py:989
  342.6 34.6 %collective-permute-done.41.refs_10_.refs_8_ = bf16[256,3072]{1,0:T(8,128)(2,1)S(1)} collective-permute-done((bf16[256,3072]{1,0:T(8,128)(2,1)}, bf16[256,3072]{1,0:T(8,128)(2,1)S(1)}, u32[]{:S(2)}, u32[]{:S(2)}) %collective-permute-start.41) | collective-permute-done | bytes 1572896 | tf_op jit(solution)/shard_map/ppermute | solution.py:77
  380.1 16.1 %collective-permute-done.44.refs_13_.refs_11_ = bf16[128,3072]{1,0:T(8,128)(2,1)S(1)} collective-permute-done((bf16[128,3072]{1,0:T(8,128)(2,1)S(1)}, bf16[128,3072]{1,0:T(8,128)(2,1)S(1)}, u32[]{:S(2)}, u32[]{:S(2)}) %collective-permute-start.44) | collective-permute-done | bytes 786464 | tf_op jit(solution)/shard_map/ppermute | solution.py:77
  397.8 35.4 %feed_forward.7 = (bf16[256,2048]{1,0:T(8,128)(2,1)}, bf16[256,2048]{1,0:T(8,128)(2,1)}, bf16[256,2048]{1,0:T(8,128)(2,1)}, bf16[256,2048]{1,0:T(8,128)(2,1)}, b...) custom-call(s32[11]{0:T(128)} %pad_add_fusion.info, ...), custom_call_target="tpu_custom_call" | custom-call | bytes 1024 | tf_op jit(solution)/shard_map/feed_forward/pallas_call | solution.py:989
  433.3 2.9 collective-permute-done.46
  438.3 20.5 %feed_forward.8 = (bf16[256,2048]{1,0:T(8,128)(2,1)}, bf16[256,2048]{1,0:T(8,128)(2,1)}, bf16[256,2048]{1,0:T(8,128)(2,1)}, bf16[256,2048]{1,0:T(8,128)(2,1)}) custom-call(s32[11]{0:T(128)} %pad_add_fusion.info, bf16[256,2048]{1,0:T(8,128)(2,1)} %collective-permute-done.30.refs_2_.refs_0_, bf16[256,2048]{1,0:T(8,128)(2,1)} %collective-permute-done.40.refs_3_.refs_1_, ...), custom_call_target="tpu_custom_call" | custom-call | bytes 1024 | tf_op jit(solution)/shard_map/feed_forward/pallas_call | solution.py:989
  459.4 3.6 collective-permute-done.48.refs_2_
  463.0 3.0 add_convert_fusion.4
  466.6 11.0 %branch_gradient.2 = (f32[256,2048]{1,0:T(8,128)}, f32[16,2048]{1,0:T(8,128)}, bf16[528,256]{1,0:T(8,128)(2,1)}, bf16[528,256]{1,0:T(8,128)(2,1)}, bf16[528,256]{1,0:T(8,128)(2,1)}, /*index=5*/bf16[528,256]{1,0:T(8,128)(2,1)}) custom-call(s32[11]{0:T(128)} %pad_add_fusion.info, bf16[2,1024,2048]{2,1,0:T(8,128)(2,1)} %dy_ref.3, ...), custom_call_target="tpu_custom_call" | custom-call | bytes 1024 | tf_op jit(solution)/shard_map/branch_gradient/pallas_call | solution.py:989
  477.6 20.5 %feed_forward.9 = (bf16[256,2048]{1,0:T(8,128)(2,1)}, bf16[256,2048]{1,0:T(8,128)(2,1)}, bf16[256,2048]{1,0:T(8,128)(2,1)}, bf16[256,2048]{1,0:T(8,128)(2,1)}) custom-call(s32[11]{0:T(128)} %pad_add_fusion.info, bf16[256,2048]{1,0:T(8,128)(2,1)} %get-tuple-element.345.refs_0_, bf16[256,2048]{1,0:T(8,128)(2,1)} %collective-permute-done.39.refs_1_, ...), custom_call_target="tpu_custom_call" | custom-call | bytes 1024 | tf_op jit(solution)/shard_map/feed_forward/pallas_call | solution.py:989
  502.1 11.1 %branch_gradient.3 = (f32[256,2048]{1,0:T(8,128)}, f32[16,2048]{1,0:T(8,128)}, bf16[528,256]{1,0:T(8,128)(2,1)}, bf16[528,256]{1,0:T(8,128)(2,1)}, bf16[528,256]{1,0:T(8,128)(2,1)}, /*index=5*/bf16[528,256]{1,0:T(8,128)(2,1)}) custom-call(s32[11]{0:T(128)} %pad_add_fusion.info, bf16[2,1024,2048]{2,1,0:T(8,128)(2,1)} %dy_ref.3, ...), custom_call_target="tpu_custom_call" | custom-call | bytes 1024 | tf_op jit(solution)/shard_map/branch_gradient/pallas_call | solution.py:989
  514.8 8.0 %collective-permute-done.54.refs_2_ = bf16[528,256]{1,0:T(8,128)(2,1)S(1)} collective-permute-done((bf16[528,256]{1,0:T(8,128)(2,1)}, bf16[528,256]{1,0:T(8,128)(2,1)S(1)}, u32[]{:S(2)}, u32[]{:S(2)}) %collective-permute-start.54) | collective-permute-done | bytes 270368 | tf_op jit(solution)/shard_map/ppermute | solution.py:108
  522.8 4.2 collective-permute-done.55.refs_3_
  527.6 2.5 collective-permute-done.59
  535.3 18.2 %attention_backward.2 = (bf16[4,512,256]{2,1,0:T(8,128)(2,1)}, f32[1088,256]{1,0:T(8,128)}, f32[8,2,160,128]{3,2,1,0:T(8,128)}, bf16[2,2,80,128]{3,2,1,0:T(8,128...) custom-call(s32[11]{0:T(128)} %pad_add_fusion.info, s32[600]{0:T(1024)} %layout.1.table, ...), custom_call_target="tpu_custom_call" | custom-call | bytes 1024 | tf_op jit(solution)/shard_map/attention_backward/pallas_call | solution.py:989
  554.3 18.6 %attention_backward.3 = (bf16[4,512,256]{2,1,0:T(8,128)(2,1)}, f32[1088,256]{1,0:T(8,128)}, f32[8,2,160,128]{3,2,1,0:T(8,128)}, bf16[2,2,80,128]{3,2,1,0:T(8,128...) custom-call(s32[11]{0:T(128)} %pad_add_fusion.info, s32[600]{0:T(1024)} %layout.1.table, ...), custom_call_target="tpu_custom_call" | custom-call | bytes 1024 | tf_op jit(solution)/shard_map/attention_backward/pallas_call | solution.py:989
  574.5 5.5 collective-permute-done.62.refs_1_.refs_0_
  580.7 2.4 layer.3
  586.5 4.9 collective-permute-done.61.back_ref
  595.3 4.4 collective-permute-done.66.refs_4_
  599.7 2.7 collective-permute-done.65.refs_3_
  603.1 10.7 %attention_keys.2 = (bf16[4,288,256]{2,1,0:T(8,128)(2,1)}, f32[2,128,64]{2,1,0:T(8,128)}) custom-call(s32[11]{0:T(128)} %pad_add_fusion.info, s32[600]{0:T(1024)} %layout.1.table, bf16[1024,256]{1,0:T(8,128)(2,1)} %get-tuple-element.412.kv_ref, bf16[1024,256]{1,0:T(8,128)(2,1)} %get-tuple-element.294.ve_ref, bf16[2,64,128]{2,1,0:T(8,128)(2,1)} %concatenate.41.wk_ref, ...), custom_call_target="tpu_custom_call" | custom-call | bytes 1024 | tf_op jit(solution)/shard_map/attention_keys/pallas_call | solution.py:989
  617.5 3.5 collective-permute-done.72.refs_7_
  622.4 2.3 collective-permute-start.74
  625.4 10.8 %attention_keys.3 = (bf16[4,288,256]{2,1,0:T(8,128)(2,1)}, f32[2,128,64]{2,1,0:T(8,128)}) custom-call(s32[11]{0:T(128)} %pad_add_fusion.info, s32[600]{0:T(1024)} %layout.1.table, bf16[1024,256]{1,0:T(8,128)(2,1)} %get-tuple-element.423.kv_ref, bf16[1024,256]{1,0:T(8,128)(2,1)} %get-tuple-element.311.ve_ref, bf16[2,64,128]{2,1,0:T(8,128)(2,1)} %concatenate.41.wk_ref, ...), custom_call_target="tpu_custom_call" | custom-call | bytes 1024 | tf_op jit(solution)/shard_map/attention_keys/pallas_call | solution.py:989
  640.0 6.1 adapter_gradients.2
  646.1 6.2 adapter_gradients.3
  657.1 2.9 collective-permute-done.78
  660.6 2.5 collective-permute-done.77
  669.2 5.2 collective-permute-done.83.refs_2_
  678.7 6.2 collective-permute-done.85
  687.9 11.6 %token_gradient.2.refs_12_ = f32[2,256,2048]{2,1,0:T(8,128)} custom-call(s32[11]{0:T(128)} %pad_add_fusion.info, bf16[2,1024,2048]{2,1,0:T(8,128)(2,1)} %x_ref.7, f32[1,2048]{1,0:T(1,128)} %bitcast.123, f32[256,2048]{1,0:T(8,128)} %get-tuple-element.454.d_resid_ref, bf16[4,512,256]{2,1,0:T(8,128)(2,1)} %get-tuple-element.440.dq_ref.refs_0_, ...), custom_call_target="tpu_custom_call" | custom-call | bytes 1024 | tf_op jit(solution)/shard_map/token_gradient/pallas_call | solution.py:989
  704.9 11.6 %token_gradient.3 = f32[2,256,2048]{2,1,0:T(8,128)} custom-call(s32[11]{0:T(128)} %pad_add_fusion.info, bf16[2,1024,2048]{2,1,0:T(8,128)(2,1)} %x_ref.7, f32[1,2048]{1,0:T(1,128)} %bitcast.124, f32[256,2048]{1,0:T(8,128)} %get-tuple-element.458.d_resid_ref, bf16[4,512,256]{2,1,0:T(8,128)(2,1)} %get-tuple-element.451.dq_ref.refs_0_, ...), custom_call_target="tpu_custom_call", output_to_operand_aliasing={{}: (16, {})} | custom-call | bytes 1024 | tf_op jit(solution)/shard_map/token_gradient/pallas_call | solution.py:989
  717.8 2.6 unpack.1
  721.9 4.4 collective-permute-done.69
  726.3 2.5 fusion.7
  (396 shorter events, 142.5 us)
Async XLA Ops:
  5.3 18.3 %collective-permute-start = (bf16[1328,256]{1,0:T(8,128)(2,1)S(1)}, bf16[1328,256]{1,0:T(8,128)(2,1)}, u32[]{:S(2)}, u32[]{:S(2)}) collective-permute-start(bf16[1328,256]{1,0:T(8,128)(2,1)S(1)} %constant_dynamic-update-slice_fusion.refs_0_), channel_id=1, source_target_pairs={{0,8},{8,16},{16,24},{24,28},{28,20},{20,12},{12,4},{4,0},{1,9},{9... | collective-permute-start | bytes 2039816 | tf_op jit(solution)/shard_map/ppermute | solution.py:77
  8.3 16.8 %collective-permute-start.1 = (bf16[1328,256]{1,0:T(8,128)(2,1)S(1)}, bf16[1328,256]{1,0:T(8,128)(2,1)}, u32[]{:S(2)}, u32[]{:S(2)}) collective-permute-start(bf16[1328,256]{1,0:T(8,128)(2,1)S(1)} %constant_dynamic-update-slice_fusion.refs_0_), channel_id=1, source_target_pairs={{0,4},{8,0},{16,8},{24,16},{28,24},{20,28},{12,20},{4,12},{1,5},{9... | collective-permute-start | bytes 2039816 | tf_op jit(solution)/shard_map/ppermute | solution.py:77
  25.1 16.1 %collective-permute-start.2 = (bf16[1328,256]{1,0:T(8,128)(2,1)}, bf16[1328,256]{1,0:T(8,128)(2,1)}, u32[]{:S(2)}, u32[]{:S(2)}) collective-permute-start(bf16[1328,256]{1,0:T(8,128)(2,1)} %collective-permute-done.refs_1_), channel_id=1, source_target_pairs={{0,8},{8,16},{16,24},{24,28},{28,20},{20,12},{12,4},{4,0},{1,9},{9... | collective-permute-start | bytes 2039816 | tf_op jit(solution)/shard_map/ppermute | solution.py:77
  26.7 15.8 %collective-permute-start.3 = (bf16[1328,256]{1,0:T(8,128)(2,1)}, bf16[1328,256]{1,0:T(8,128)(2,1)}, u32[]{:S(2)}, u32[]{:S(2)}) collective-permute-start(bf16[1328,256]{1,0:T(8,128)(2,1)} %collective-permute-done.1.refs_2_), channel_id=1, source_target_pairs={{0,4},{8,0},{16,8},{24,16},{28,24},{20,28},{12,20},{4,12},{1,5},{9... | collective-permute-start | bytes 2039816 | tf_op jit(solution)/shard_map/ppermute | solution.py:77
  42.5 14.9 %collective-permute-start.4 = (bf16[1328,256]{1,0:T(8,128)(2,1)}, bf16[1328,256]{1,0:T(8,128)(2,1)}, u32[]{:S(2)}, u32[]{:S(2)}) collective-permute-start(bf16[1328,256]{1,0:T(8,128)(2,1)} %collective-permute-done.2.refs_3_), channel_id=1, source_target_pairs={{0,8},{8,16},{16,24},{24,28},{28,20},{20,12},{12,4},{4,0},{1,9},{9... | collective-permute-start | bytes 2039816 | tf_op jit(solution)/shard_map/ppermute | solution.py:77
  44.1 14.6 %collective-permute-start.5 = (bf16[1328,256]{1,0:T(8,128)(2,1)}, bf16[1328,256]{1,0:T(8,128)(2,1)}, u32[]{:S(2)}, u32[]{:S(2)}) collective-permute-start(bf16[1328,256]{1,0:T(8,128)(2,1)} %collective-permute-done.3.refs_4_), channel_id=1, source_target_pairs={{0,4},{8,0},{16,8},{24,16},{28,24},{20,28},{12,20},{4,12},{1,5},{9... | collective-permute-start | bytes 2039816 | tf_op jit(solution)/shard_map/ppermute | solution.py:77
  75.9 73.4 %collective-permute-start.20 = (bf16[528,2048]{1,0:T(8,128)(2,1)}, bf16[528,2048]{1,0:T(8,128)(2,1)}, u32[]{:S(2)}, u32[]{:S(2)}) collective-permute-start(bf16[528,2048]{1,0:T(8,128)(2,1)} %get-tuple-element.315.refs_4_.refs_3_), channel_id=1, source_target_pairs={{0,2},{1,3},{2,0},{3,1},{4,6},{5,7},{6,4},{7,5},{8,10},{9,11},{10,... | collective-permute-start | bytes 6488072 | tf_op jit(solution)/shard_map/ppermute | solution.py:108
  78.6 38.6 %collective-permute-start.9 = (bf16[256,3072]{1,0:T(8,128)(2,1)}, bf16[256,3072]{1,0:T(8,128)(2,1)}, u32[]{:S(2)}, u32[]{:S(2)}) collective-permute-start(bf16[256,3072]{1,0:T(8,128)(2,1)} %pad_maximum_fusion.1.refs_5_), channel_id=1, source_target_pairs={{0,8},{8,16},{16,24},{24,28},{28,20},{20,12},{12,4},{4,0},{1,9},{9... | collective-permute-start | bytes 4718600 | tf_op jit(solution)/shard_map/ppermute | solution.py:77
  80.1 37.1 %collective-permute-start.10 = (bf16[256,3072]{1,0:T(8,128)(2,1)}, bf16[256,3072]{1,0:T(8,128)(2,1)}, u32[]{:S(2)}, u32[]{:S(2)}) collective-permute-start(bf16[256,3072]{1,0:T(8,128)(2,1)} %pad_maximum_fusion.1.refs_5_), channel_id=1, source_target_pairs={{0,4},{8,0},{16,8},{24,16},{28,24},{20,28},{12,20},{4,12},{1,5},{9... | collective-permute-start | bytes 4718600 | tf_op jit(solution)/shard_map/ppermute | solution.py:77
  118.6 14.7 %collective-permute-start.8 = (bf16[2,64,512]{2,1,0:T(8,128)(2,1)S(1)}, bf16[2,64,512]{2,1,0:T(8,128)(2,1)S(1)}, u32[]{:S(2)}, u32[]{:S(2)}) collective-permute-start(bf16[2,64,512]{2,1,0:T(8,128)(2,1)S(1)} %pad_maximum_fusion.6), channel_id=1, source_target_pairs={{0,4},{4,8},{8,12},{12,16},{16,20},{20,24},{24,28},{1,5},{5,9},{9,... | collective-permute-start | bytes 393224 | tf_op jit(solution)/shard_map/ppermute | solution.py:114
  125.7 10.4 %collective-permute-start.13 = (bf16[2,2,80,128]{3,2,1,0:T(8,128)(2,1)}, bf16[2,2,80,128]{3,2,1,0:T(8,128)(2,1)S(1)}, u32[]{:S(2)}, u32[]{:S(2)}) collective-permute-start(bf16[2,2,80,128]{3,2,1,0:T(8,128)(2,1)} %get-tuple-element.306), channel_id=1, source_target_pairs={{0,8},{4,12},{8,16},{12,20},{16,24},{20,28},{1,9},{5,13},{9,17},{1... | collective-permute-start | bytes 245768 | tf_op jit(solution)/shard_map/ppermute | solution.py:114
  136.1 45.8 %collective-permute-start.19 = (bf16[528,2048]{1,0:T(8,128)(2,1)S(1)}, bf16[528,2048]{1,0:T(8,128)(2,1)S(1)}, u32[]{:S(2)}, u32[]{:S(2)}) collective-permute-start(bf16[528,2048]{1,0:T(8,128)(2,1)S(1)} %copy-done.2), channel_id=1, source_target_pairs={{0,1},{1,0},{2,3},{3,2},{4,5},{5,4},{6,7},{7,6},{8,9},{9,8},{10,11... | collective-permute-start | bytes 6488072 | tf_op jit(solution)/shard_map/ppermute | solution.py:108
  149.2 32.7 %collective-permute-start.21 = (bf16[528,2048]{1,0:T(8,128)(2,1)}, bf16[528,2048]{1,0:T(8,128)(2,1)}, u32[]{:S(2)}, u32[]{:S(2)}) collective-permute-start(bf16[528,2048]{1,0:T(8,128)(2,1)} %collective-permute-done.20.refs_6_.refs_5_), channel_id=1, source_target_pairs={{0,1},{1,0},{2,3},{3,2},{4,5},{5,4},{6,7},{7,6},{8,9},{9,8},{10,11... | collective-permute-start | bytes 6488072 | tf_op jit(solution)/shard_map/ppermute | solution.py:108
  149.3 43.2 %collective-permute-start.22 = (bf16[256,3072]{1,0:T(8,128)(2,1)}, bf16[256,3072]{1,0:T(8,128)(2,1)}, u32[]{:S(2)}, u32[]{:S(2)}) collective-permute-start(bf16[256,3072]{1,0:T(8,128)(2,1)} %collective-permute-done.9.refs_6_), channel_id=1, source_target_pairs={{0,8},{8,16},{16,24},{24,28},{28,20},{20,12},{12,4},{4,0},{1,9},{9... | collective-permute-start | bytes 4718600 | tf_op jit(solution)/shard_map/ppermute | solution.py:77
  151.7 40.9 %collective-permute-start.23 = (bf16[256,3072]{1,0:T(8,128)(2,1)}, bf16[256,3072]{1,0:T(8,128)(2,1)}, u32[]{:S(2)}, u32[]{:S(2)}) collective-permute-start(bf16[256,3072]{1,0:T(8,128)(2,1)} %collective-permute-done.10.refs_7_), channel_id=1, source_target_pairs={{0,4},{8,0},{16,8},{24,16},{28,24},{20,28},{12,20},{4,12},{1,5},{9... | collective-permute-start | bytes 4718600 | tf_op jit(solution)/shard_map/ppermute | solution.py:77
  152.8 8.5 %collective-permute-start.18 = (bf16[528,256]{1,0:T(8,128)(2,1)S(1)}, bf16[528,256]{1,0:T(8,128)(2,1)S(1)}, u32[]{:S(2)}, u32[]{:S(2)}) collective-permute-start(bf16[528,256]{1,0:T(8,128)(2,1)S(1)} %get-tuple-element.479), channel_id=1, source_target_pairs={{0,3},{1,2},{2,1},{3,0},{4,7},{5,6},{6,5},{7,4},{8,11},{9,10},{10,... | collective-permute-start | bytes 811016 | tf_op jit(solution)/shard_map/ppermute | solution.py:108
  161.3 9.0 %collective-permute-start.17 = (bf16[528,256]{1,0:T(8,128)(2,1)S(1)}, bf16[528,256]{1,0:T(8,128)(2,1)S(1)}, u32[]{:S(2)}, u32[]{:S(2)}) collective-permute-start(bf16[528,256]{1,0:T(8,128)(2,1)S(1)} %get-tuple-element.480), channel_id=1, source_target_pairs={{0,2},{1,3},{2,0},{3,1},{4,6},{5,7},{6,4},{7,5},{8,10},{9,11},{10,... | collective-permute-start | bytes 811016 | tf_op jit(solution)/shard_map/ppermute | solution.py:108
  170.3 11.6 %collective-permute-start.16 = (bf16[528,256]{1,0:T(8,128)(2,1)S(1)}, bf16[528,256]{1,0:T(8,128)(2,1)S(1)}, u32[]{:S(2)}, u32[]{:S(2)}) collective-permute-start(bf16[528,256]{1,0:T(8,128)(2,1)S(1)} %get-tuple-element.481), channel_id=1, source_target_pairs={{0,1},{1,0},{2,3},{3,2},{4,5},{5,4},{6,7},{7,6},{8,9},{9,8},{10,11... | collective-permute-start | bytes 811016 | tf_op jit(solution)/shard_map/ppermute | solution.py:108
  192.6 37.0 %collective-permute-start.25 = (bf16[256,3072]{1,0:T(8,128)(2,1)}, bf16[256,3072]{1,0:T(8,128)(2,1)S(1)}, u32[]{:S(2)}, u32[]{:S(2)}) collective-permute-start(bf16[256,3072]{1,0:T(8,128)(2,1)} %collective-permute-done.22.refs_8_), channel_id=1, source_target_pairs={{0,8},{8,16},{16,24},{24,28},{28,20},{20,12},{12,4},{4,0},{1,9},{9... | collective-permute-start | bytes 4718600 | tf_op jit(solution)/shard_map/ppermute | solution.py:77
  194.6 36.8 %collective-permute-start.26 = (bf16[256,3072]{1,0:T(8,128)(2,1)}, bf16[256,3072]{1,0:T(8,128)(2,1)S(1)}, u32[]{:S(2)}, u32[]{:S(2)}) collective-permute-start(bf16[256,3072]{1,0:T(8,128)(2,1)} %collective-permute-done.23.refs_9_), channel_id=1, source_target_pairs={{0,4},{8,0},{16,8},{24,16},{28,24},{20,28},{12,20},{4,12},{1,5},{9... | collective-permute-start | bytes 4718600 | tf_op jit(solution)/shard_map/ppermute | solution.py:77
  194.9 8.6 %collective-permute-start.29 = (bf16[528,256]{1,0:T(8,128)(2,1)S(1)}, bf16[528,256]{1,0:T(8,128)(2,1)S(1)}, u32[]{:S(2)}, u32[]{:S(2)}) collective-permute-start(bf16[528,256]{1,0:T(8,128)(2,1)S(1)} %get-tuple-element.476), channel_id=1, source_target_pairs={{0,3},{1,2},{2,1},{3,0},{4,7},{5,6},{6,5},{7,4},{8,11},{9,10},{10,... | collective-permute-start | bytes 811016 | tf_op jit(solution)/shard_map/ppermute | solution.py:108
  195.2 14.6 %collective-permute-start.28 = (bf16[528,256]{1,0:T(8,128)(2,1)S(1)}, bf16[528,256]{1,0:T(8,128)(2,1)S(1)}, u32[]{:S(2)}, u32[]{:S(2)}) collective-permute-start(bf16[528,256]{1,0:T(8,128)(2,1)S(1)} %get-tuple-element.477), channel_id=1, source_target_pairs={{0,2},{1,3},{2,0},{3,1},{4,6},{5,7},{6,4},{7,5},{8,10},{9,11},{10,... | collective-permute-start | bytes 811016 | tf_op jit(solution)/shard_map/ppermute | solution.py:108
  196.7 13.0 %collective-permute-start.27 = (bf16[528,256]{1,0:T(8,128)(2,1)S(1)}, bf16[528,256]{1,0:T(8,128)(2,1)S(1)}, u32[]{:S(2)}, u32[]{:S(2)}) collective-permute-start(bf16[528,256]{1,0:T(8,128)(2,1)S(1)} %get-tuple-element.478), channel_id=1, source_target_pairs={{0,1},{1,0},{2,3},{3,2},{4,5},{5,4},{6,7},{7,6},{8,9},{9,8},{10,11... | collective-permute-start | bytes 811016 | tf_op jit(solution)/shard_map/ppermute | solution.py:108
  203.5 31.3 %collective-permute-start.24 = (bf16[256,2048]{1,0:T(8,128)(2,1)}, bf16[256,2048]{1,0:T(8,128)(2,1)}, u32[]{:S(2)}, u32[]{:S(2)}) collective-permute-start(bf16[256,2048]{1,0:T(8,128)(2,1)} %get-tuple-element.335.refs_0_), channel_id=1, source_target_pairs={{0,2},{1,3},{2,0},{3,1},{4,6},{5,7},{6,4},{7,5},{8,10},{9,11},{10,... | collective-permute-start | bytes 3145736 | tf_op jit(solution)/shard_map/ppermute | solution.py:108
  231.5 24.8 %collective-permute-start.30 = (bf16[256,2048]{1,0:T(8,128)(2,1)}, bf16[256,2048]{1,0:T(8,128)(2,1)}, u32[]{:S(2)}, u32[]{:S(2)}) collective-permute-start(bf16[256,2048]{1,0:T(8,128)(2,1)} %get-tuple-element.345.refs_0_), channel_id=1, source_target_pairs={{0,2},{1,3},{2,0},{3,1},{4,6},{5,7},{6,4},{7,5},{8,10},{9,11},{10,... | collective-permute-start | bytes 3145736 | tf_op jit(solution)/shard_map/ppermute | solution.py:108
  232.1 18.6 %collective-permute-start.32 = (bf16[128,3072]{1,0:T(8,128)(2,1)S(1)}, bf16[128,3072]{1,0:T(8,128)(2,1)S(1)}, u32[]{:S(2)}, u32[]{:S(2)}) collective-permute-start(bf16[128,3072]{1,0:T(8,128)(2,1)S(1)} %slice.346), channel_id=1, source_target_pairs={{0,4},{8,0},{16,8},{24,16},{28,24},{20,28},{12,20},{4,12},{1,5},{9... | collective-permute-start | bytes 2359304 | tf_op jit(solution)/shard_map/ppermute | solution.py:77
  232.4 18.6 %collective-permute-start.31 = (bf16[128,3072]{1,0:T(8,128)(2,1)S(1)}, bf16[128,3072]{1,0:T(8,128)(2,1)S(1)}, u32[]{:S(2)}, u32[]{:S(2)}) collective-permute-start(bf16[128,3072]{1,0:T(8,128)(2,1)S(1)} %slice.345), channel_id=1, source_target_pairs={{0,8},{8,16},{16,24},{24,28},{28,20},{20,12},{12,4},{4,0},{1,9},{9... | collective-permute-start | bytes 2359304 | tf_op jit(solution)/shard_map/ppermute | solution.py:77
  256.3 42.7 %collective-permute-start.35 = (bf16[256,3072]{1,0:T(8,128)(2,1)S(1)}, bf16[256,3072]{1,0:T(8,128)(2,1)}, u32[]{:S(2)}, u32[]{:S(2)}) collective-permute-start(bf16[256,3072]{1,0:T(8,128)(2,1)S(1)} %pad_maximum_fusion.2.refs_5_.refs_3_), channel_id=1, source_target_pairs={{0,8},{8,16},{16,24},{24,28},{28,20},{20,12},{12,4},{4,0},{1,9},{9... | collective-permute-start | bytes 4718600 | tf_op jit(solution)/shard_map/ppermute | solution.py:77
  256.8 42.2 %collective-permute-start.36 = (bf16[256,3072]{1,0:T(8,128)(2,1)S(1)}, bf16[256,3072]{1,0:T(8,128)(2,1)}, u32[]{:S(2)}, u32[]{:S(2)}) collective-permute-start(bf16[256,3072]{1,0:T(8,128)(2,1)S(1)} %pad_maximum_fusion.2.refs_5_.refs_3_), channel_id=1, source_target_pairs={{0,4},{8,0},{16,8},{24,16},{28,24},{20,28},{12,20},{4,12},{1,5},{9... | collective-permute-start | bytes 4718600 | tf_op jit(solution)/shard_map/ppermute | solution.py:77
  258.8 42.5 %collective-permute-start.40 = (bf16[256,2048]{1,0:T(8,128)(2,1)}, bf16[256,2048]{1,0:T(8,128)(2,1)}, u32[]{:S(2)}, u32[]{:S(2)}) collective-permute-start(bf16[256,2048]{1,0:T(8,128)(2,1)} %collective-permute-done.30.refs_2_.refs_0_), channel_id=1, source_target_pairs={{0,1},{1,0},{2,3},{3,2},{4,5},{5,4},{6,7},{7,6},{8,9},{9,8},{10,11... | collective-permute-start | bytes 3145736 | tf_op jit(solution)/shard_map/ppermute | solution.py:108
  299.0 40.4 %collective-permute-start.37 = (bf16[256,3072]{1,0:T(8,128)(2,1)}, bf16[256,3072]{1,0:T(8,128)(2,1)S(1)}, u32[]{:S(2)}, u32[]{:S(2)}) collective-permute-start(bf16[256,3072]{1,0:T(8,128)(2,1)} %collective-permute-done.35.refs_6_.refs_4_), channel_id=1, source_target_pairs={{0,8},{8,16},{16,24},{24,28},{28,20},{20,12},{12,4},{4,0},{1,9},{9... | collective-permute-start | bytes 4718600 | tf_op jit(solution)/shard_map/ppermute | solution.py:77
  299.6 39.9 %collective-permute-start.38 = (bf16[256,3072]{1,0:T(8,128)(2,1)}, bf16[256,3072]{1,0:T(8,128)(2,1)}, u32[]{:S(2)}, u32[]{:S(2)}) collective-permute-start(bf16[256,3072]{1,0:T(8,128)(2,1)} %collective-permute-done.36.refs_7_.refs_5_), channel_id=1, source_target_pairs={{0,4},{8,0},{16,8},{24,16},{28,24},{20,28},{12,20},{4,12},{1,5},{9... | collective-permute-start | bytes 4718600 | tf_op jit(solution)/shard_map/ppermute | solution.py:77
  301.4 78.7 %collective-permute-start.45 = (bf16[800,2048]{1,0:T(8,128)(2,1)S(1)}, bf16[800,2048]{1,0:T(8,128)(2,1)}, u32[]{:S(2)}, u32[]{:S(2)}) collective-permute-start(bf16[800,2048]{1,0:T(8,128)(2,1)S(1)} %copy-done.1), channel_id=1, source_target_pairs={{0,2},{1,3},{2,0},{3,1},{4,6},{5,7},{6,4},{7,5},{8,10},{9,11},{10,... | collective-permute-start | bytes 9830408 | tf_op jit(solution)/shard_map/ppermute | solution.py:108
  340.6 36.6 %collective-permute-start.41 = (bf16[256,3072]{1,0:T(8,128)(2,1)}, bf16[256,3072]{1,0:T(8,128)(2,1)S(1)}, u32[]{:S(2)}, u32[]{:S(2)}) collective-permute-start(bf16[256,3072]{1,0:T(8,128)(2,1)} %copy-done.10), channel_id=1, source_target_pairs={{0,8},{8,16},{16,24},{24,28},{28,20},{20,12},{12,4},{4,0},{1,9},{9... | collective-permute-start | bytes 4718600 | tf_op jit(solution)/shard_map/ppermute | solution.py:77
  341.1 36.4 %collective-permute-start.42 = (bf16[256,3072]{1,0:T(8,128)(2,1)}, bf16[256,3072]{1,0:T(8,128)(2,1)S(1)}, u32[]{:S(2)}, u32[]{:S(2)}) collective-permute-start(bf16[256,3072]{1,0:T(8,128)(2,1)} %collective-permute-done.38.refs_9_.refs_7_), channel_id=1, source_target_pairs={{0,4},{8,0},{16,8},{24,16},{28,24},{20,28},{12,20},{4,12},{1,5},{9... | collective-permute-start | bytes 4718600 | tf_op jit(solution)/shard_map/ppermute | solution.py:77
  377.6 18.6 %collective-permute-start.44 = (bf16[128,3072]{1,0:T(8,128)(2,1)S(1)}, bf16[128,3072]{1,0:T(8,128)(2,1)S(1)}, u32[]{:S(2)}, u32[]{:S(2)}) collective-permute-start(bf16[128,3072]{1,0:T(8,128)(2,1)S(1)} %slice.351), channel_id=1, source_target_pairs={{0,4},{8,0},{16,8},{24,16},{28,24},{20,28},{12,20},{4,12},{1,5},{9... | collective-permute-start | bytes 2359304 | tf_op jit(solution)/shard_map/ppermute | solution.py:77
  379.2 18.6 %collective-permute-start.43 = (bf16[128,3072]{1,0:T(8,128)(2,1)S(1)}, bf16[128,3072]{1,0:T(8,128)(2,1)}, u32[]{:S(2)}, u32[]{:S(2)}) collective-permute-start(bf16[128,3072]{1,0:T(8,128)(2,1)S(1)} %slice.350), channel_id=1, source_target_pairs={{0,8},{8,16},{16,24},{24,28},{28,20},{20,12},{12,4},{4,0},{1,9},{9... | collective-permute-start | bytes 2359304 | tf_op jit(solution)/shard_map/ppermute | solution.py:77
  437.7 25.3 %collective-permute-start.48 = (bf16[256,2048]{1,0:T(8,128)(2,1)S(1)}, bf16[256,2048]{1,0:T(8,128)(2,1)S(1)}, u32[]{:S(2)}, u32[]{:S(2)}) collective-permute-start(bf16[256,2048]{1,0:T(8,128)(2,1)S(1)} %add_convert_fusion.5), channel_id=1, source_target_pairs={{0,2},{1,3},{2,0},{3,1},{4,6},{5,7},{6,4},{7,5},{8,10},{9,11},{10,... | collective-permute-start | bytes 3145736 | tf_op jit(solution)/shard_map/ppermute | solution.py:108
  466.0 32.1 %collective-permute-start.52 = (bf16[256,2048]{1,0:T(8,128)(2,1)}, bf16[256,2048]{1,0:T(8,128)(2,1)S(1)}, u32[]{:S(2)}, u32[]{:S(2)}) collective-permute-start(bf16[256,2048]{1,0:T(8,128)(2,1)} %add_convert_fusion.4), channel_id=1, source_target_pairs={{0,2},{1,3},{2,0},{3,1},{4,6},{5,7},{6,4},{7,5},{8,10},{9,11},{10,... | collective-permute-start | bytes 3145736 | tf_op jit(solution)/shard_map/ppermute | solution.py:108
  498.2 16.6 %collective-permute-start.50 = (bf16[528,256]{1,0:T(8,128)(2,1)}, bf16[528,256]{1,0:T(8,128)(2,1)S(1)}, u32[]{:S(2)}, u32[]{:S(2)}) collective-permute-start(bf16[528,256]{1,0:T(8,128)(2,1)} %get-tuple-element.373), channel_id=1, source_target_pairs={{0,2},{1,3},{2,0},{3,1},{4,6},{5,7},{6,4},{7,5},{8,10},{9,11},{10,... | collective-permute-start | bytes 811016 | tf_op jit(solution)/shard_map/ppermute | solution.py:108
  499.8 15.0 %collective-permute-start.51 = (bf16[528,256]{1,0:T(8,128)(2,1)}, bf16[528,256]{1,0:T(8,128)(2,1)S(1)}, u32[]{:S(2)}, u32[]{:S(2)}) collective-permute-start(bf16[528,256]{1,0:T(8,128)(2,1)} %get-tuple-element.374), channel_id=1, source_target_pairs={{0,3},{1,2},{2,1},{3,0},{4,7},{5,6},{6,5},{7,4},{8,11},{9,10},{10,... | collective-permute-start | bytes 811016 | tf_op jit(solution)/shard_map/ppermute | solution.py:108
  513.2 9.6 %collective-permute-start.54 = (bf16[528,256]{1,0:T(8,128)(2,1)}, bf16[528,256]{1,0:T(8,128)(2,1)S(1)}, u32[]{:S(2)}, u32[]{:S(2)}) collective-permute-start(bf16[528,256]{1,0:T(8,128)(2,1)} %get-tuple-element.383), channel_id=1, source_target_pairs={{0,2},{1,3},{2,0},{3,1},{4,6},{5,7},{6,4},{7,5},{8,10},{9,11},{10,... | collective-permute-start | bytes 811016 | tf_op jit(solution)/shard_map/ppermute | solution.py:108
  514.8 12.2 %collective-permute-start.55 = (bf16[528,256]{1,0:T(8,128)(2,1)}, bf16[528,256]{1,0:T(8,128)(2,1)S(1)}, u32[]{:S(2)}, u32[]{:S(2)}) collective-permute-start(bf16[528,256]{1,0:T(8,128)(2,1)} %get-tuple-element.384), channel_id=1, source_target_pairs={{0,3},{1,2},{2,1},{3,0},{4,7},{5,6},{6,5},{7,4},{8,11},{9,10},{10,... | collective-permute-start | bytes 811016 | tf_op jit(solution)/shard_map/ppermute | solution.py:108
  531.5 62.5 %collective-permute-start.60 = (bf16[256,2048]{1,0:T(8,128)(2,1)}, bf16[256,2048]{1,0:T(8,128)(2,1)S(1)}, u32[]{:S(2)}, u32[]{:S(2)}) collective-permute-start(bf16[256,2048]{1,0:T(8,128)(2,1)} %add_convert_fusion.3), channel_id=1, source_target_pairs={{0,2},{1,3},{2,0},{3,1},{4,6},{5,7},{6,4},{7,5},{8,10},{9,11},{10,... | collective-permute-start | bytes 3145736 | tf_op jit(solution)/shard_map/ppermute | solution.py:108
  533.1 20.4 %collective-permute-start.58 = (bf16[528,256]{1,0:T(8,128)(2,1)S(1)}, bf16[528,256]{1,0:T(8,128)(2,1)S(1)}, u32[]{:S(2)}, u32[]{:S(2)}) collective-permute-start(bf16[528,256]{1,0:T(8,128)(2,1)S(1)} %copy-done.86), channel_id=1, source_target_pairs={{0,1},{1,0},{2,3},{3,2},{4,5},{5,4},{6,7},{7,6},{8,9},{9,8},{10,11... | collective-permute-start | bytes 811016 | tf_op jit(solution)/shard_map/ppermute | solution.py:108
  533.6 153.8 %collective-permute-start.87 = (bf16[800,2048]{1,0:T(8,128)(2,1)S(1)}, bf16[800,2048]{1,0:T(8,128)(2,1)}, u32[]{:S(2)}, u32[]{:S(2)}) collective-permute-start(bf16[800,2048]{1,0:T(8,128)(2,1)S(1)} %copy-done.1), channel_id=1, source_target_pairs={{0,1},{1,0},{2,3},{3,2},{4,5},{5,4},{6,7},{7,6},{8,9},{9,8},{10,11... | collective-permute-start | bytes 9830408 | tf_op jit(solution)/shard_map/ppermute | solution.py:108
  533.6 154.2 %collective-permute-start.88 = (bf16[800,2048]{1,0:T(8,128)(2,1)}, bf16[800,2048]{1,0:T(8,128)(2,1)}, u32[]{:S(2)}, u32[]{:S(2)}) collective-permute-start(bf16[800,2048]{1,0:T(8,128)(2,1)} %collective-permute-done.45.refs_10_), channel_id=1, source_target_pairs={{0,1},{1,0},{2,3},{3,2},{4,5},{5,4},{6,7},{7,6},{8,9},{9,8},{10,11... | collective-permute-start | bytes 9830408 | tf_op jit(solution)/shard_map/ppermute | solution.py:108
  583.2 9.5 %collective-permute-start.64 = (bf16[2,2,80,128]{3,2,1,0:T(8,128)(2,1)}, bf16[2,2,80,128]{3,2,1,0:T(8,128)(2,1)S(1)}, u32[]{:S(2)}, u32[]{:S(2)}) collective-permute-start(bf16[2,2,80,128]{3,2,1,0:T(8,128)(2,1)} %get-tuple-element.421), channel_id=1, source_target_pairs={{8,0},{12,4},{16,8},{20,12},{24,16},{28,20},{9,1},{13,5},{17,9},{2... | collective-permute-start | bytes 245768 | tf_op jit(solution)/shard_map/ppermute | solution.py:114
  592.7 9.7 %collective-permute-start.65 = (bf16[2,2,80,128]{3,2,1,0:T(8,128)(2,1)}, bf16[2,2,80,128]{3,2,1,0:T(8,128)(2,1)S(1)}, u32[]{:S(2)}, u32[]{:S(2)}) collective-permute-start(bf16[2,2,80,128]{3,2,1,0:T(8,128)(2,1)} %get-tuple-element.420), channel_id=1, source_target_pairs={{16,0},{20,4},{24,8},{28,12},{17,1},{21,5},{25,9},{29,13},{18,2},{... | collective-permute-start | bytes 245768 | tf_op jit(solution)/shard_map/ppermute | solution.py:114
  615.5 9.2 %collective-permute-start.70 = (bf16[288,256]{1,0:T(8,128)(2,1)S(1)}, bf16[288,256]{1,0:T(8,128)(2,1)S(1)}, u32[]{:S(2)}, u32[]{:S(2)}) collective-permute-start(bf16[288,256]{1,0:T(8,128)(2,1)S(1)} %get-tuple-element.495), channel_id=1, source_target_pairs={{0,1},{1,0},{2,3},{3,2},{4,5},{5,4},{6,7},{7,6},{8,9},{9,8},{10,11... | collective-permute-start | bytes 442376 | tf_op jit(solution)/shard_map/ppermute | solution.py:108
  621.0 17.0 %collective-permute-start.75 = (bf16[512,256]{1,0:T(8,128)(2,1)}, bf16[512,256]{1,0:T(8,128)(2,1)S(1)}, u32[]{:S(2)}, u32[]{:S(2)}) collective-permute-start(bf16[512,256]{1,0:T(8,128)(2,1)} %get-tuple-element.485), channel_id=1, source_target_pairs={{0,3},{1,2},{2,1},{3,0},{4,7},{5,6},{6,5},{7,4},{8,11},{9,10},{10,... | collective-permute-start | bytes 786440 | tf_op jit(solution)/shard_map/ppermute | solution.py:108
  622.4 15.7 %collective-permute-start.74 = (bf16[512,256]{1,0:T(8,128)(2,1)S(1)}, bf16[512,256]{1,0:T(8,128)(2,1)S(1)}, u32[]{:S(2)}, u32[]{:S(2)}) collective-permute-start(bf16[512,256]{1,0:T(8,128)(2,1)S(1)} %get-tuple-element.486), channel_id=1, source_target_pairs={{0,2},{1,3},{2,0},{3,1},{4,6},{5,7},{6,4},{7,5},{8,10},{9,11},{10,... | collective-permute-start | bytes 786440 | tf_op jit(solution)/shard_map/ppermute | solution.py:108
  624.8 14.8 %collective-permute-start.73 = (bf16[512,256]{1,0:T(8,128)(2,1)S(1)}, bf16[512,256]{1,0:T(8,128)(2,1)S(1)}, u32[]{:S(2)}, u32[]{:S(2)}) collective-permute-start(bf16[512,256]{1,0:T(8,128)(2,1)S(1)} %get-tuple-element.487), channel_id=1, source_target_pairs={{0,1},{1,0},{2,3},{3,2},{4,5},{5,4},{6,7},{7,6},{8,9},{9,8},{10,11... | collective-permute-start | bytes 786440 | tf_op jit(solution)/shard_map/ppermute | solution.py:108
  638.0 16.2 %collective-permute-start.81 = (bf16[288,256]{1,0:T(8,128)(2,1)}, bf16[288,256]{1,0:T(8,128)(2,1)}, u32[]{:S(2)}, u32[]{:S(2)}) collective-permute-start(bf16[288,256]{1,0:T(8,128)(2,1)} %get-tuple-element.490), channel_id=1, source_target_pairs={{0,3},{1,2},{2,1},{3,0},{4,7},{5,6},{6,5},{7,4},{8,11},{9,10},{10,... | collective-permute-start | bytes 442376 | tf_op jit(solution)/shard_map/ppermute | solution.py:108
  638.1 16.6 %collective-permute-start.80 = (bf16[288,256]{1,0:T(8,128)(2,1)}, bf16[288,256]{1,0:T(8,128)(2,1)S(1)}, u32[]{:S(2)}, u32[]{:S(2)}) collective-permute-start(bf16[288,256]{1,0:T(8,128)(2,1)} %get-tuple-element.491), channel_id=1, source_target_pairs={{0,2},{1,3},{2,0},{3,1},{4,6},{5,7},{6,4},{7,5},{8,10},{9,11},{10,... | collective-permute-start | bytes 442376 | tf_op jit(solution)/shard_map/ppermute | solution.py:108
  639.6 16.5 %collective-permute-start.79 = (bf16[288,256]{1,0:T(8,128)(2,1)}, bf16[288,256]{1,0:T(8,128)(2,1)S(1)}, u32[]{:S(2)}, u32[]{:S(2)}) collective-permute-start(bf16[288,256]{1,0:T(8,128)(2,1)} %get-tuple-element.492), channel_id=1, source_target_pairs={{0,1},{1,0},{2,3},{3,2},{4,5},{5,4},{6,7},{7,6},{8,9},{9,8},{10,11... | collective-permute-start | bytes 442376 | tf_op jit(solution)/shard_map/ppermute | solution.py:108
  663.7 10.6 %collective-permute-start.83 = (bf16[512,256]{1,0:T(8,128)(2,1)}, bf16[512,256]{1,0:T(8,128)(2,1)S(1)}, u32[]{:S(2)}, u32[]{:S(2)}) collective-permute-start(bf16[512,256]{1,0:T(8,128)(2,1)} %get-tuple-element.483), channel_id=1, source_target_pairs={{0,2},{1,3},{2,0},{3,1},{4,6},{5,7},{6,4},{7,5},{8,10},{9,11},{10,... | collective-permute-start | bytes 786440 | tf_op jit(solution)/shard_map/ppermute | solution.py:108
  664.8 9.6 %collective-permute-start.82 = (bf16[512,256]{1,0:T(8,128)(2,1)}, bf16[512,256]{1,0:T(8,128)(2,1)S(1)}, u32[]{:S(2)}, u32[]{:S(2)}) collective-permute-start(bf16[512,256]{1,0:T(8,128)(2,1)} %get-tuple-element.484), channel_id=1, source_target_pairs={{0,1},{1,0},{2,3},{3,2},{4,5},{5,4},{6,7},{7,6},{8,9},{9,8},{10,11... | collective-permute-start | bytes 786440 | tf_op jit(solution)/shard_map/ppermute | solution.py:108
  668.2 31.3 %collective-permute-start.68 = (bf16[256,2048]{1,0:T(8,128)(2,1)}, bf16[256,2048]{1,0:T(8,128)(2,1)S(1)}, u32[]{:S(2)}, u32[]{:S(2)}) collective-permute-start(bf16[256,2048]{1,0:T(8,128)(2,1)} %get-tuple-element.434), channel_id=1, source_target_pairs={{0,1},{1,0},{2,3},{3,2},{4,5},{5,4},{6,7},{7,6},{8,9},{9,8},{10,11... | collective-permute-start | bytes 3145736 | tf_op jit(solution)/shard_map/ppermute | solution.py:108
  685.9 13.6 %collective-permute-start.86 = (bf16[1056,128]{1,0:T(8,128)(2,1)S(1)}, bf16[1056,128]{1,0:T(8,128)(2,1)S(1)}, u32[]{:S(2)}, u32[]{:S(2)}) collective-permute-start(bf16[1056,128]{1,0:T(8,128)(2,1)S(1)} %add_convert_fusion.7), channel_id=1, source_target_pairs={{0,8},{4,12},{8,0},{12,4},{16,24},{20,28},{24,16},{28,20},{1,9},{5... | collective-permute-start | bytes 811016 | tf_op jit(solution)/shard_map/ppermute | solution.py:108
  687.3 14.3 %collective-permute-start.56 = (bf16[256,2048]{1,0:T(8,128)(2,1)}, bf16[256,2048]{1,0:T(8,128)(2,1)}, u32[]{:S(2)}, u32[]{:S(2)}) collective-permute-start(bf16[256,2048]{1,0:T(8,128)(2,1)} %get-tuple-element.387), channel_id=1, source_target_pairs={{0,1},{1,0},{2,3},{3,2},{4,5},{5,4},{6,7},{7,6},{8,9},{9,8},{10,11... | collective-permute-start | bytes 3145736 | tf_op jit(solution)/shard_map/ppermute | solution.py:108
  687.4 34.5 %collective-permute-start.67 = (bf16[256,2048]{1,0:T(8,128)(2,1)}, bf16[256,2048]{1,0:T(8,128)(2,1)}, u32[]{:S(2)}, u32[]{:S(2)}) collective-permute-start(bf16[256,2048]{1,0:T(8,128)(2,1)} %get-tuple-element.431), channel_id=1, source_target_pairs={{0,1},{1,0},{2,3},{3,2},{4,5},{5,4},{6,7},{7,6},{8,9},{9,8},{10,11... | collective-permute-start | bytes 3145736 | tf_op jit(solution)/shard_map/ppermute | solution.py:108
  700.9 25.4 %collective-permute-start.69 = (bf16[256,2048]{1,0:T(8,128)(2,1)}, bf16[256,2048]{1,0:T(8,128)(2,1)}, u32[]{:S(2)}, u32[]{:S(2)}) collective-permute-start(bf16[256,2048]{1,0:T(8,128)(2,1)} %add_convert_fusion.1), channel_id=1, source_target_pairs={{0,2},{1,3},{2,0},{3,1},{4,6},{5,7},{6,4},{7,5},{8,10},{9,11},{10,... | collective-permute-start | bytes 3145736 | tf_op jit(solution)/shard_map/ppermute | solution.py:108
  701.0 15.5 %collective-permute-start.89 = (bf16[1056,128]{1,0:T(8,128)(2,1)S(1)}, bf16[1056,128]{1,0:T(8,128)(2,1)S(1)}, u32[]{:S(2)}, u32[]{:S(2)}) collective-permute-start(bf16[1056,128]{1,0:T(8,128)(2,1)S(1)} %add_convert_fusion.6), channel_id=1, source_target_pairs={{0,16},{4,20},{8,24},{12,28},{16,0},{20,4},{24,8},{28,12},{1,17},{... | collective-permute-start | bytes 811016 | tf_op jit(solution)/shard_map/ppermute | solution.py:108
  (113 other events, 1166.8 us)

commit v4 on v3

--- a/solution.py
+++ b/solution.py
@@ -19,6 +19,8 @@
 VMEM_LIMIT = 58 * 1024 * 1024
 CHUNK = 256
 ROW_TILE = 512
+LATE_COST = 2000000
+SMALL_LIMIT = 32 * 1024 * 1024
 
 
 def dotg(left, right, lc, rc):
@@ -154,14 +156,13 @@
     return nears + [flip(far, "grp", 2 * (i + 1)) for i, far in enumerate(fars)]
 
 
-def exchange(table, ends, halo, sign):
+def exchange(table, ends, sign):
     count = lax.axis_size("seq")
     wide = max(1, count // 4)
     here = [flip(ends, "seq", j) for j in range(1, wide)]
-    full, inner = run_layer(table, [ends, *here], sign)
-    out = here + [shifted(full, "seq", sign * wide), shifted(inner, "seq", sign * wide)]
-    out += [shifted(full, "seq", sign * r * wide) for r in range(2, count // wide)]
-    return out, shifted(halo, "seq", sign)
+    near, full = run_layer(table, [ends, *here], sign)
+    out = here + [shifted(near, "seq", sign * wide)]
+    return out + [shifted(full, "seq", sign * r * wide) for r in range(2, count // wide)]
 
 
 VALID, ONE, TWO = range(3)
@@ -265,36 +266,41 @@
 
 def entering(slots, arrays, wide, count, sign, place, near_k):
     inner = outer = jnp.zeros((EXT, PAIR), F32)
+    rows = jnp.zeros((arrays[0].shape[2] - 2 * EXT, PAIR), F32)
     row = lambda name, i: slots.at(side_row(sign, name), i).astype(F32)
-    for j in range(1, wide):
-        array = arrays[j - 1]
-        full = array[place, near_k, 1].astype(F32)
-        outer = outer + row(FULL, j) * full
-        inner = inner + row(INNER, j) * full + row(NEXT, j) * array[place, near_k, 0].astype(F32)
-    layers = arrays[wide - 1 :]
-    for r in range(1, count // wide):
-        full = layers[0 if r == 1 else r][place, near_k].astype(F32)
-        outer = outer + row(FULL, wide + r) * full
-        inner = inner + row(INNER, wide + r) * full
-        if r == 1:
-            inner = inner + row(NEXT, wide + 1) * layers[1][place, near_k].astype(F32)
-    return inner, outer
+    for r in range(1, count // wide + wide - 1):
+        layer = r >= wide
+        i = r + 1 if layer else r
+        array = arrays[r - 1]
+        if r > wide:
+            full = array[place, near_k].astype(F32)
+        else:
+            full = array[place, near_k, EXT : 2 * EXT].astype(F32)
+            inner = inner + row(NEXT, i) * array[place, near_k, :EXT].astype(F32)
+            rows = rows + row(NEXT, i) * array[place, near_k, 2 * EXT :].astype(F32)
+        outer = outer + row(FULL, i) * full
+        inner = inner + row(INNER, i) * full
+    return inner, outer, rows
 
 
 def layer_kernel(sign, blocks, count, wide, table, *refs):
-    ends, (full_ref, inner_ref) = refs[:wide], refs[wide:]
-    for batch in range(full_ref.shape[0]):
+    ends, (near_ref, full_ref) = refs[:wide], refs[wide:]
+    for batch in range(near_ref.shape[0]):
         slots = Slots(table, batch, blocks, count)
         row = lambda name, i: slots.at(side_row(sign, name), i).astype(F32)
-        for k in range(full_ref.shape[1]):
+        for k in range(near_ref.shape[1]):
             full = inner = jnp.zeros((EXT, PAIR), F32)
+            rows = jnp.zeros((near_ref.shape[2] - 2 * EXT, PAIR), F32)
             for j in range(wide):
-                value = ends[j][batch, k, 1].astype(F32)
+                value = ends[j][batch, k, EXT : 2 * EXT].astype(F32)
                 full = full + row(LAYER_FULL, j) * value
                 inner = inner + row(LAYER_INNER, j) * value
-                inner = inner + row(LAYER_NEXT, j) * ends[j][batch, k, 0].astype(F32)
+                inner = inner + row(LAYER_NEXT, j) * ends[j][batch, k, :EXT].astype(F32)
+                rows = rows + row(LAYER_NEXT, j) * ends[j][batch, k, 2 * EXT :].astype(F32)
+            near_ref[batch, k, :EXT] = inner.astype(BF)
+            near_ref[batch, k, EXT : 2 * EXT] = full.astype(BF)
+            near_ref[batch, k, 2 * EXT :] = rows.astype(BF)
             full_ref[batch, k] = full.astype(BF)
-            inner_ref[batch, k] = inner.astype(BF)
 
 
 def half_mask(shape):
@@ -331,7 +337,7 @@
 
 def project_kernel(
     batch, q_width, blocks, count, table, normed_ref, w_ref, up_ref, kv_up_ref, wk_ref,
-    q_ref, kv_ref, ve_ref, mid_ref, phi_ref, st_ref, ends_ref, halo_ref, carry,
+    q_ref, kv_ref, ve_ref, mid_ref, phi_ref, st_ref, ends_ref, carry,
 ):
     step = pl.program_id(0)
     rows = normed_ref.shape[0]
@@ -343,17 +349,17 @@
         carry[...] = jnp.zeros_like(carry)
 
     normed = normed_ref[...]
-    mixed = dotg(w_ref[: q_width + 32], normed, 1, 1)
+    product = dotg(w_ref[...], normed, 1, 1)
+    mixed = product[: q_width + 32]
     mids = mixed[q_width:].astype(BF)
     mid_ref[...] = mids
     query = mixed[:q_width] + ADAPTER_SCALE * dotg(up_ref[...], mids, 1, 0)
     q_ref[...] = query.astype(BF)
-    kv_all = dotg(normed, w_ref[q_width + 32 :], 1, 1) + ADAPTER_SCALE * dotg(
+    kv_all = jnp.transpose(product[q_width + 32 :]) + ADAPTER_SCALE * dotg(
         mids, kv_up_ref[...], 0, 0
     )
     kv_all = kv_all.astype(BF)
     kv_ref[...] = kv_all
-    halo_ref[:, :width] = kv_all[rows - STRETCH :]
 
     slots = Slots(table, batch, blocks, count)
     lane = lax.broadcasted_iota(jnp.int32, (1, PAIR), 1)
@@ -376,7 +382,8 @@
             ).astype(BF)
             ve_ref[at : at + PAIR, k * PAIR : (k + 1) * PAIR] = ve
             if sub == rows // PAIR - 1:
-                halo_ref[:, width + k * PAIR : width + (k + 1) * PAIR] = ve[STRETCH:]
+                ends_ref[k, 2 * EXT : 2 * EXT + STRETCH] = kv[STRETCH:]
+                ends_ref[k, 2 * EXT + STRETCH :] = ve[STRETCH:]
             phi = feature_softmax(dotg(wk_ref[k], kv, 1, 1))
             phi_ref[k * PAIR : (k + 1) * PAIR, at : at + PAIR] = (phi * valid).astype(BF)
             first = dotg(ve, (phi * valid_low).astype(BF), 0, 1)[:EXT]
@@ -386,8 +393,8 @@
             mid = carry[k] * one_a + first
             tail = mid * one_b + second
             carry[k] = tail
-            ends_ref[k, 0] = mid.astype(BF)
-            ends_ref[k, 1] = tail.astype(BF)
+            ends_ref[k, :EXT] = mid.astype(BF)
+            ends_ref[k, EXT : 2 * EXT] = tail.astype(BF)
 
 
 def window_mask(slots, block):
@@ -404,16 +411,16 @@
     return jnp.concatenate([jnp.where(row < limit, 1.0, 0.0) for limit in limits], axis=0)
 
 
-def fill_window(batch, kv_ref, ve_ref, halo_ref, kv_all, ve_all):
-    width = kv_ref.shape[1]
-    kv_all[:STRETCH] = halo_ref[batch, :, :width]
-    ve_all[:STRETCH] = halo_ref[batch, :, width:]
-    kv_all[STRETCH:] = kv_ref[...]
-    ve_all[STRETCH:] = ve_ref[...]
+def fill_window(k, kv_ref, ve_ref, rows, kv_all, ve_all):
+    cols = slice(k * PAIR, (k + 1) * PAIR)
+    kv_all[:STRETCH, cols] = rows[:STRETCH].astype(BF)
+    ve_all[:STRETCH, cols] = rows[STRETCH:].astype(BF)
+    kv_all[STRETCH:, cols] = kv_ref[:, cols]
+    ve_all[STRETCH:, cols] = ve_ref[:, cols]
 
 
 def forward_kernel(
-    batch, per, blocks, wide, count, n_far, scale, info, table, q_ref, kv_ref, ve_ref, halo_ref,
+    batch, per, blocks, wide, count, n_far, scale, info, table, q_ref, kv_ref, ve_ref,
     wq_ref, oin_ref, st_ref, *refs,
 ):
     fars = refs[:n_far]
@@ -425,9 +432,9 @@
 
     @pl.when(step == 0)
     def _():
-        fill_window(batch, kv_ref, ve_ref, halo_ref, kv_all, ve_all)
         for k in range(heads):
-            inner, outer = entering(slots, fars, wide, count, 1, batch, k)
+            inner, outer, rows = entering(slots, fars, wide, count, 1, batch, k)
+            fill_window(k, kv_ref, ve_ref, rows, kv_all, ve_all)
             carry[k, 0] = inner
             carry[k, 1] = outer
 
@@ -702,13 +709,14 @@
 
 
 def backward_kernel(
-    batch, per, pairs, n_grp, has_prev, count, scale, info, table, q_ref, kv_ref, ve_ref, halo_ref, wq_ref,
+    batch, per, pairs, n_grp, has_prev, count, wide, n_far, scale, info, table, q_ref, kv_ref, ve_ref, wq_ref,
     oin_ref, att_ref, w_ref, phi_ref, s_ref, r_ref, *refs,
 ):
+    fars, refs = refs[:n_far], refs[n_far:]
     blocks_in, refs = refs[:n_grp], refs[n_grp:]
     prevs, refs = (refs[:1], refs[1:]) if has_prev else (None, refs)
     (
-        dq_ref, dkv_ref, ds_ref, ends_ref, back_ref, map_ref, carry, kv_all, ve_all, d_outs, sem,
+        dq_ref, dkv_ref, ds_ref, ends_ref, map_ref, carry, kv_all, ve_all, d_outs, sem,
     ) = refs
     step = pl.program_id(0)
     pair = pairs - 1 - step
@@ -732,7 +740,9 @@
                 )
         for copy in copies:
             copy.start()
-        fill_window(batch, kv_ref, ve_ref, halo_ref, kv_all, ve_all)
+        for k in range(heads):
+            rows = entering(slots, fars, wide, count, 1, batch, k)[2]
+            fill_window(k, kv_ref, ve_ref, rows, kv_all, ve_all)
         carry[...] = jnp.zeros_like(carry)
         dkv_ref[...] = jnp.zeros_like(dkv_ref)
         map_ref[...] = prevs[0][...] if has_prev else jnp.zeros_like(map_ref)
@@ -800,21 +810,22 @@
         rest = d_state[EXT:] + one_c * carry[k]
         head = d_state[:EXT] + one_b * rest
         carry[k] = head
-        ends_ref[k, 0] = rest.astype(BF)
-        ends_ref[k, 1] = head.astype(BF)
+        ends_ref[k, :EXT] = rest.astype(BF)
+        ends_ref[k, EXT : 2 * EXT] = head.astype(BF)
 
     @pl.when(step == pairs - 1)
     def _():
-        back_ref[...] = dkv_ref[:STRETCH, :].astype(BF)
+        for k in range(heads):
+            ends_ref[k, 2 * EXT :] = dkv_ref[:STRETCH, k * PAIR : (k + 1) * PAIR].astype(BF)
 
 
 def keys_kernel(
     batch, pairs, per_block, wide_y, count, n_far, has_prev, info, table, kv_ref, ve_ref, wk_ref,
-    phi_ref, dkv_ref, back_ref, ds_ref, dq_ref, q_up_ref, kv_up_ref, *refs,
+    phi_ref, dkv_ref, ds_ref, dq_ref, q_up_ref, kv_up_ref, *refs,
 ):
     fars, refs = refs[:n_far], refs[n_far:]
     prevs, refs = (refs[:1], refs[1:]) if has_prev else (None, refs)
-    out_ref, map_ref, carry = refs
+    out_ref, map_ref, carry, back = refs
     step = pl.program_id(0)
     pair = pairs - 1 - step
     heads = kv_ref.shape[1] // PAIR
@@ -824,7 +835,7 @@
     @pl.when(step == 0)
     def _():
         for k in range(heads):
-            inner, outer = entering(slots, fars, wide_y, count, -1, batch, k)
+            inner, outer, back[k] = entering(slots, fars, wide_y, count, -1, batch, k)
             carry[k, 0] = outer
             carry[k, 1] = inner
         map_ref[...] = prevs[0][...] if has_prev else jnp.zeros_like(map_ref)
@@ -856,7 +867,7 @@
         d_key = dotg(d_mixed, wk_ref[k], 0, 0)
         map_ref[k] += dotg(kv, d_mixed, 0, 1)
         total = dkv_ref[rows, k * PAIR : (k + 1) * PAIR] + d_value + d_key
-        returned = back_ref[batch, :, k * PAIR : (k + 1) * PAIR].astype(F32) * last
+        returned = back[k] * last
         total = total + jnp.concatenate([jnp.zeros_like(returned), returned], axis=0)
         d_kvs.append(jnp.transpose(total).astype(BF))
         state = ds_ref[0, k]
@@ -984,7 +995,8 @@
 
 
 def call(
-    kernel, name, grid, scalars, ins, in_specs, out_specs, out_shape, scratch=(), alias=None
+    kernel, name, grid, scalars, ins, in_specs, out_specs, out_shape, scratch=(), alias=None,
+    cost=1024,
 ):
     return pl.pallas_call(
         kernel,
@@ -997,9 +1009,10 @@
         ),
         out_shape=out_shape,
         input_output_aliases=alias or {},
-        cost_estimate=pl.CostEstimate(flops=0, transcendentals=0, bytes_accessed=1024),
+        cost_estimate=pl.CostEstimate(flops=0, transcendentals=0, bytes_accessed=cost),
         compiler_params=pltpu.CompilerParams(
-            dimension_semantics=("arbitrary",), vmem_limit_bytes=VMEM_LIMIT
+            dimension_semantics=("arbitrary",),
+            vmem_limit_bytes=VMEM_LIMIT if name == "feed_forward" else SMALL_LIMIT,
         ),
         name=name,
     )(*scalars, *ins)
@@ -1028,12 +1041,13 @@
 def run_layer(table, ends, sign):
     count = lax.axis_size("seq")
     batches, heads = ends[0].shape[:2]
-    out = sds((batches, heads, EXT, PAIR), BF)
+    full = sds((batches, heads, EXT, PAIR), BF)
+    out = [sds(ends[0].shape, BF), full]
     per_batch = table.shape[0] // batches // TABLE_ROWS
     blocks = max(per_batch - 4, 0)
     return call(
         functools.partial(layer_kernel, sign, blocks, count, len(ends)), "layer", 1, [table], ends,
-        [whole(item.shape) for item in ends], [whole(out.shape)] * 2, [out] * 2,
+        [whole(item.shape) for item in ends], [whole(item.shape) for item in out], out,
     )
 
 
@@ -1042,7 +1056,7 @@
     heads = maps.shape[0]
     width = heads * PAIR
     q_width = weight.shape[0] - 32 - width
-    tile = 2 * PAIR
+    tile = 4 * PAIR
     pairs = rows // PAIR
     return call(
         functools.partial(
@@ -1060,9 +1074,8 @@
             pl.BlockSpec((tile, width), lambda i, *_: (i, 0)),
             pl.BlockSpec((32, tile), lambda i, *_: (0, i)),
             pl.BlockSpec((width, tile), lambda i, *_: (0, i)),
-            pl.BlockSpec((2, heads, 2 * EXT, PAIR), lambda i, *_: (i, 0, 0, 0)),
-            whole((heads, 2, EXT, PAIR)),
-            whole((STRETCH, 2 * width)),
+            pl.BlockSpec((4, heads, 2 * EXT, PAIR), lambda i, *_: (i, 0, 0, 0)),
+            whole((heads, 2 * PAIR + 32, PAIR)),
         ],
         [
             sds((q_width, rows), BF),
@@ -1071,14 +1084,13 @@
             sds((32, rows), BF),
             sds((width, rows), BF),
             sds((pairs, heads, 2 * EXT, PAIR), F32),
-            sds((heads, 2, EXT, PAIR), BF),
-            sds((STRETCH, 2 * width), BF),
+            sds((heads, 2 * PAIR + 32, PAIR), BF),
         ],
         [pltpu.VMEM((heads, EXT, PAIR), F32)],
     )
 
 
-def run_forward(info, table, batch, q, kv, ve, halo, maps, o_in, states, fars):
+def run_forward(info, table, batch, q, kv, ve, maps, o_in, states, fars):
     q_width, rows = q.shape
     width = kv.shape[1]
     heads, pairs = width // PAIR, rows // PAIR
@@ -1094,9 +1106,9 @@
             forward_kernel, batch, per, rows // STRETCH, wide, count, len(fars), scale
         ),
         "attention_forward", pairs, [info, table],
-        [q, kv, ve, halo, maps, o_in, states, *fars],
+        [q, kv, ve, maps, o_in, states, *fars],
         [
-            column(q_width), whole(kv.shape), whole(ve.shape), whole(halo.shape),
+            column(q_width), whole(kv.shape), whole(ve.shape),
             whole(maps.shape), whole(o_in.shape), step(heads, 2 * EXT, PAIR),
             *[whole(far.shape) for far in fars],
         ],
@@ -1173,6 +1185,7 @@
             pltpu.VMEM((n_grp,) + weights[0].shape, BF),
             pltpu.SemaphoreType.DMA((n_grp,)),
         ],
+        cost=LATE_COST,
     )
 
 
@@ -1200,6 +1213,7 @@
             pltpu.SemaphoreType.DMA((n_grp,)),
         ],
         alias,
+        LATE_COST,
     )
 
 
@@ -1233,13 +1247,14 @@
 
 
 def run_backward(
-    info, table, batch, q, kv, ve, halo, maps, o_in, att, weights, phi, states, inverse, d_outs, prevs,
+    info, table, batch, q, kv, ve, maps, o_in, att, weights, phi, states, inverse, fars, d_outs, prevs,
 ):
     q_width, rows = q.shape
     width = kv.shape[1]
     heads, pairs = width // PAIR, rows // PAIR
     per = q_width // STRETCH // heads
     share = rows // len(d_outs)
+    count = lax.axis_size("seq")
     rev = lambda i: pairs - 1 - i
     step = lambda *shape: pl.BlockSpec((1,) + shape, lambda i, *_: (rev(i),) + (0,) * len(shape))
     column = lambda n: pl.BlockSpec((n, PAIR), lambda i, *_: (0, rev(i)))
@@ -1247,29 +1262,28 @@
     sums = [sds(maps.shape, F32)]
     return call(
         functools.partial(
-            backward_kernel, batch, per, pairs, len(d_outs), bool(prevs), lax.axis_size("seq"),
-            STRETCH ** (-0.5),
+            backward_kernel, batch, per, pairs, len(d_outs), bool(prevs), count, max(1, count // 4),
+            len(fars), STRETCH ** (-0.5),
         ),
         "attention_backward", pairs, [info, table],
-        [q, kv, ve, halo, maps, o_in, att, weights, phi, states, inverse, *d_outs, *prevs],
+        [q, kv, ve, maps, o_in, att, weights, phi, states, inverse, *fars, *d_outs, *prevs],
         [
-            column(q_width), whole(kv.shape), whole(ve.shape), whole(halo.shape),
+            column(q_width), whole(kv.shape), whole(ve.shape),
             whole(maps.shape), whole(o_in.shape), block_spec(q_width + 16, share, rev),
             step(heads, WIN, per * PAIR), step(heads, PAIR, per * PAIR),
             step(heads, 2 * EXT, PAIR), step(heads * per, PAIR),
-            *[anywhere() for _ in d_outs], *[whole(prev.shape) for prev in prevs],
+            *[whole(far.shape) for far in fars], *[anywhere() for _ in d_outs],
+            *[whole(prev.shape) for prev in prevs],
         ],
         [
             block_spec(q_width, share, rev), whole((rows + STRETCH, width)), step(heads, 2 * EXT, PAIR),
-            whole((heads, 2, EXT, PAIR)), whole((STRETCH, width)),
-            *[whole(item.shape) for item in sums],
+            whole((heads, 2 * EXT + STRETCH, PAIR)), *[whole(item.shape) for item in sums],
         ],
         [
             sds((rows // share, q_width, share), BF),
             sds((rows + STRETCH, width), F32),
             sds((pairs, heads, 2 * EXT, PAIR), F32),
-            sds((heads, 2, EXT, PAIR), BF),
-            sds((STRETCH, width), BF),
+            sds((heads, 2 * EXT + STRETCH, PAIR), BF),
             *sums,
         ],
         [
@@ -1279,11 +1293,12 @@
             pltpu.VMEM((pairs, q_width + 16, PAIR), BF),
             pltpu.SemaphoreType.DMA,
         ],
+        cost=LATE_COST,
     )
 
 
 def run_keys(
-    info, table, batch, kv, ve, maps, phi, d_kv, returned, d_states, d_q, q_up, kv_up, fars, prevs,
+    info, table, batch, kv, ve, maps, phi, d_kv, d_states, d_q, q_up, kv_up, fars, prevs,
 ):
     width, rows = phi.shape
     heads, pairs = width // PAIR, rows // PAIR
@@ -1301,18 +1316,18 @@
         ),
         "attention_keys", pairs, [info, table],
         [
-            kv, ve, maps, phi, d_kv, returned, d_states, d_q, q_up, kv_up, *fars, *prevs,
+            kv, ve, maps, phi, d_kv, d_states, d_q, q_up, kv_up, *fars, *prevs,
         ],
         [
             lines(width), lines(width), whole(maps.shape), column(width), whole(d_kv.shape),
-            whole(returned.shape),
             pl.BlockSpec((1, heads, 2 * EXT, PAIR), lambda i, *_: (rev(i), 0, 0, 0)),
             whole(d_q.shape), whole(q_up.shape), whole(kv_up.shape),
             *[whole(far.shape) for far in fars], *[whole(prev.shape) for prev in prevs],
         ],
         [whole((n_grp, 32 + width, share)), *[whole(item.shape) for item in sums]],
         [sds((n_grp, 32 + width, share), BF), *sums],
-        [pltpu.VMEM((heads, 2, EXT, PAIR), F32)],
+        [pltpu.VMEM((heads, 2, EXT, PAIR), F32), pltpu.VMEM((heads, STRETCH, PAIR), F32)],
+        cost=LATE_COST,
     )
 
 
@@ -1327,6 +1342,7 @@
         functools.partial(adapter_kernel, len(d_outs)),
         "adapter_gradients", 1, [info], ins, [whole(item.shape) for item in ins],
         [whole(item.shape) for item in out_shape], out_shape,
+        cost=LATE_COST,
     )
 
 
@@ -1454,32 +1470,32 @@
     saved = []
     for batch in range(batches):
         normed = normed_rows[batch]
-        q, kv, ve, mids, phi_key, states, ends, halo = run_project(
+        q, kv, ve, mids, phi_key, states, ends = run_project(
             table, batch, normed, weight_in, q_up_t, kv_up, key_maps
         )
-        saved.append([q, kv, ve, mids, normed, phi_key, states, ends, halo])
+        saved.append([q, kv, ve, mids, normed, phi_key, states, ends])
     ends = jnp.stack([item[7] for item in saved])
-    halo = jnp.stack([item[8] for item in saved])
     (ends,) = ring_a.tie(ends)
-    fars, halo = exchange(table, ends, halo, 1)
+    fars = exchange(table, ends, 1)
     for item in saved:
-        item[7:] = [fars, halo]
-    ring_a.hop(*fars[1:], halo)
+        item[7] = fars
+    far_out = [far_out[0]] + [after(far, *fars[1:]) for far in far_out[1:]]
+    weights_out = near_gather(far_out)
+    ring_a.hop(*fars[1:])
 
     attended, att_sets, far_mlp, mlp_ins = [], [], [], []
     for batch in range(batches):
-        q, kv, ve, mids, normed, phi_key, states, fars, halo = saved[batch]
+        q, kv, ve, mids, normed, phi_key, states, fars = saved[batch]
         if batch:
             q = after(q, att)
         att, weights, phi, sums, inverse = run_forward(
-            info, table, batch, q, kv, ve, halo, query_maps, o_in, states, fars
+            info, table, batch, q, kv, ve, query_maps, o_in, states, fars
         )
         atts = group_exchange([att[r] for r in range(n_grp)])
         att_sets.append([att, *atts[1:]])
         attended.append([att, weights, phi, sums, inverse])
-    far_out = [far_out[0]] + [after(far, attended[0][0]) for far in far_out[1:]]
-    weights_out = near_gather(far_out)
-    att_sets[0][0] = after(att_sets[0][0], att_sets[1][0])
+    att_sets[0][0], att_sets[1][0] = ring_a.tie(att_sets[0][0], att_sets[1][0])
+    ring_a.hop()
     for batch in range(batches):
         if batch:
             att_sets[1][0] = after(att_sets[1][0], mlp_in)
@@ -1487,14 +1503,16 @@
             info, batch, tokens, gain_mlp, att_sets[batch], weights_out
         )
         attended[batch] += [resid, mid]
-        (mlp_in,) = ring_a.tie(mlp_in)
-        ring_a.hop()
+        if batch:
+            mlp_in, *far_mlp[0][1:] = ring_a.tie(mlp_in, *far_mlp[0][1:])
+            ring_a.hop()
+        else:
+            mlp_in, *att_sets[1][2:] = lax.optimization_barrier((mlp_in, *att_sets[1][2:]))
         far_mlp.append(far_gather(mlp_in))
     ring_a.finish()
-    held = ring_a.parts[-2:]
-    held = lax.optimization_barrier((*far_mlp[0], *far_mlp[1], *held))
-    far_mlp = [list(held[: len(far_mlp[0])]), list(held[len(far_mlp[0]) : 2 * len(far_mlp[0])])]
-    ring_c.hop(held[0])
+    ring_c.hop(*ring_a.parts[-2:])
+    far_mlp[1] = list(lax.optimization_barrier((*far_mlp[1], *ring_a.parts[-2:])))[: len(far_mlp[1])]
+    far_mlp[0][0] = after(far_mlp[0][0], *far_mlp[1][1:])
     for batch in range(batches):
         mlp_ins.append(near_gather(far_mlp[batch]))
 
@@ -1528,20 +1546,20 @@
         return d_resid, wide, group_exchange(d_out)
 
     def run_backward_of(batch, q, d_outs, sums_back):
-        _, kv, ve, mids, normed, phi_key, states, fars, halo = saved[batch]
+        _, kv, ve, mids, normed, phi_key, states, fars = saved[batch]
         att, weights, phi, sums, inverse = attended[batch][:5]
-        d_q, d_kv, d_states, ends, back, *sums_back = run_backward(
-            info, table, batch, q, kv, ve, halo, query_maps, o_in, att, weights, phi, sums,
-            inverse, d_outs, sums_back,
+        d_q, d_kv, d_states, ends, *sums_back = run_backward(
+            info, table, batch, q, kv, ve, query_maps, o_in, att, weights, phi, sums, inverse, fars,
+            d_outs, sums_back,
         )
-        return [d_q, None, d_kv, d_states], ends, back, sums_back
+        return [d_q, None, d_kv, d_states], ends, sums_back
 
     def run_keys_of(batch, kv, gone, sums_keys):
-        _, _, ve, mids, normed, phi_key, states, _, _ = saved[batch]
-        d_q, d_qs, d_kv, d_states, fars, returned = gone
+        _, _, ve, mids, normed, phi_key, states, _ = saved[batch]
+        d_q, d_qs, d_kv, d_states, fars = gone
         rest, *sums_keys = run_keys(
-            info, table, batch, kv, ve, key_maps, phi_key, d_kv, returned, d_states, d_q, q_up,
-            kv_up, fars, sums_keys,
+            info, table, batch, kv, ve, key_maps, phi_key, d_kv, d_states, d_q, q_up, kv_up, fars,
+            sums_keys,
         )
         rests = group_exchange([rest[r] for r in range(n_grp)])
         return [rest, *rests[1:]], sums_keys
@@ -1592,30 +1610,39 @@
     early_b = [far_pair(lower[far], lower[far + 1]) for far in range(2, low, 2)]
     summands_b = near_b + scatter_end(early_b, []) + late_b
     partial[1] = [None] * n_grp + list(lower[low:]) + list(upper[low:])
+    attended[1][6] = after(attended[1][6], *d_outs_a[2:])
     d_resid_b, wide_b, d_outs_b = run_branch_of(1, summands_b)
-    gone_a, ends_a, back_a, sums_back = run_backward_of(
+    gone_a, ends_a, sums_back = run_backward_of(
         0, after(saved[0][0], d_resid_b), d_outs_a, None
     )
-    rows_a = finish_rows(0, *d_outs_a[2:], *d_outs_b[2:])
-    gone_b, ends_b, back_b, sums_back = run_backward_of(
-        1, after(saved[1][0], gone_a[0]), d_outs_b, sums_back
-    )
-    fars, returned = exchange(table, jnp.stack([ends_a, ends_b]), jnp.stack([back_a, back_b]), -1)
-    gone_a += [fars, returned]
-    gone_b += [fars, returned]
-    rows_a = scatter_end(*rows_a)
+    blocks = partial[0][n_grp:]
+    crossed = [flip(after(blocks[r + 1], d_resid_b), "grp", 1) for r in range(0, n_grp, 2)]
+    crossed[-1] = after(crossed[-1], gone_a[0], *d_outs_b[2:])
+    fars_a = [
+        (blocks[r].astype(F32) + crossed[r // 2].astype(F32)).astype(BF)
+        for r in range(2, n_grp, 2)
+    ]
+    rows_a = scatter_end(fars_a, [blocks[0], crossed[0]])
+    gone_b, ends_b, sums_back = run_backward_of(
+        1, after(saved[1][0], gone_a[0], *fars_a), d_outs_b, sums_back
+    )
+    fars = exchange(table, jnp.stack([ends_a, ends_b]), -1)
+    gone_a.append(fars)
+    gone_b.append(fars)
+    for gone in (gone_a, gone_b):
+        held = after(gone[0], gone_b[0])
+        gone[1] = group_exchange([held[r] for r in range(n_grp)])
     kv_a, rows_a[-1] = lax.optimization_barrier((after(saved[0][1], gone_b[0]), rows_a[-1]))
     rests_a, sums_keys = run_keys_of(0, kv_a, gone_a, None)
     kv_b = after(saved[1][1], rests_a[0])
-    d_q = after(gone_a[0], rests_a[0])
-    gone_a[1] = group_exchange([d_q[r] for r in range(n_grp)])
+    kv_b = after(kv_b, *gone_a[1][1:], *gone_b[1][1:])
     rests_b, sums_keys = run_keys_of(1, kv_b, gone_b, sums_keys)
-    d_q = after(gone_b[0], rests_b[0])
-    gone_b[1] = group_exchange([d_q[r] for r in range(n_grp)])
-    sums_a = run_adapters_of(0, after(gone_a[0], rests_b[0]), rests_a[0], d_outs_a)
-    rows_b = finish_rows(1, rests_b[0])
+    sums_a = run_adapters_of(
+        0, after(gone_a[0], rests_b[0]), rests_a[0], d_outs_a
+    )
+    fars_b, nears_b = finish_rows(1, rests_b[0])
     sums_b = run_adapters_of(
-        1, after(gone_b[0], sums_a[0], *rests_a[1:], *gone_a[1][1:]), rests_b[0], d_outs_b
+        1, after(gone_b[0], sums_a[0], *rests_a[1:]), rests_b[0], d_outs_b
     )
 
     (early,) = run_plain(
@@ -1624,13 +1651,15 @@
         [sds((STRETCH * kv_heads * per // 2 + 16 * (q_width // PAIR), PAIR), BF)],
     )
     late_rows = 16 * (q_width // PAIR) + (16 + STRETCH) * kv_heads
+    wide_a = after(wide_a, fars_b[0])
+    rows_b = scatter_end(fars_b, nears_b)
     wide, late = run_plain(
         functools.partial(pack_late_kernel, q_width), "pack_late", [],
         [sums_a[0], sums_b[0], sums_keys[0], sums_a[2], sums_b[2], wide_a, wide_b],
         [sds((32 * (model // PAIR), PAIR), BF), sds((late_rows, PAIR), BF)],
     )
     wide = group_sum(wide)
-    wide = after(wide, *rests_b[1:], *gone_b[1][1:])
+    wide = after(wide, *rests_b[1:])
     first = early.shape[0]
     columns = model // (n_seq * n_grp)
     value, bits = jnp.concatenate([early, wide, late]), n_seq.bit_length() - 1
@@ -1644,10 +1673,11 @@
                 batch, after(held[batch], value), gone, rests, grad_tokens
             )
             there, grad_tokens = lax.optimization_barrier((there, grad_tokens))
+            if batch == 0:
+                held[1], rows_b[-1] = lax.optimization_barrier((held[1], rows_b[-1]))
         if step < bits - 1:
             value = (value.astype(F32) + there.astype(F32)).astype(BF)
     packed = (value, there)
-    rows_b = scatter_end(*rows_b)
     block_rows = [rows_of(0, rows_a), rows_of(1, rows_b)]
     wide, q_grad, kv_grad, oin_grad, query_grad, key_grad = run_plain(
         functools.partial(unpack_kernel, n_grp, columns), "unpack", [info],

time: 739 us -> 693 us (0.938)
  Pallas kernels: 357 us -> 289 us
  local copies, waits for them, and re-layouts: 42.9 us -> 73 us
  other arithmetic: 32.1 us -> 24.3 us
    pallas_call x28, Pallas kernels: 357 us -> 289 us  [call(): pl.pallas_call(kernel, grid_spec=pltpu.PrefetchScalarGridSpec(num_scalar_...]
    unnamed x186 -> x316, local copies, waits for them, and re-layouts: 19.9 us -> 56.7 us
    ppermute x24, waiting for transfers between devices: 109 us -> 127 us  [move(): return lax.ppermute(value, 'seq', pairs)]
    ppermute x56, waiting for transfers between devices: 96.5 us -> 87 us  [flip(): return lax.ppermute(value, axis, [(i, i ^ bit) for i in range(count)])]
    ppermute x10 -> x6, starting transfers between devices: 19.4 us -> 12 us  [shifted(): lax.ppermute(value, axis, [(i, i + steps) for i in range(first, last)])]
  transfers between devices with their start and end apart: 90 -> 86, of which waited for: 45 -> 47; matrix products, arithmetic and copies ran while one was open for 7% -> 5% of each run, Pallas kernels for 43% -> 35%
where the time goes in v4:
time: 693 us; the launch traced here: 686 us
  Pallas kernels  289 us (42%)
  waiting for transfers between devices  224 us (32%)
  local copies, waits for them, and re-layouts  73 us (11%)
  starting transfers between devices  72 us (10%)
  other arithmetic  24.3 us (4%)
    pallas_call x28, Pallas kernels, call(): pl.pallas_call(kernel, grid_spec=pltpu.PrefetchScalarGridSpec(num_scalar_...  289 us
    ppermute x24, waiting for transfers between devices, move(): return lax.ppermute(value, 'seq', pairs)  127 us
    ppermute x56, waiting for transfers between devices, flip(): return lax.ppermute(value, axis, [(i, i ^ bit) for i in range(count)])  87 us
    unnamed x316, local copies, waits for them, and re-layouts  56.7 us
    ppermute x56, starting transfers between devices, flip(): return lax.ppermute(value, axis, [(i, i ^ bit) for i in range(count)])  31.9 us
    ppermute x24, starting transfers between devices, move(): return lax.ppermute(value, 'seq', pairs)  28.1 us
  transfers between devices with their start and end apart: 86, of which 47 were waited for; matrix products, arithmetic and copies ran while one was open for 5% of the time, Pallas kernels for 35%

profile of v4, /device:TPU:0, one launch (start us, length us, event | category | flops | bytes accessed | tf_op | source)
XLA Modules:
  0.0 685.6 jit_solution(889830329204030743)
XLA Ops:
  5.3 3.0 collective-permute-start
  11.9 2.2 layout.1.table
  14.8 4.6 fusion.3
  19.4 4.1 collective-permute-done.refs_1_
  27.1 4.4 fusion.5
  31.5 9.3 %collective-permute-done.2.refs_3_ = bf16[1328,256]{1,0:T(8,128)(2,1)S(1)} collective-permute-done((bf16[1328,256]{1,0:T(8,128)(2,1)S(1)}, bf16[1328,256]{1,0:T(8,128)(2,1)S(1)}, u32[]{:S(2)}, u32[]{:S(2)}) %collective-permute-start.2) | collective-permute-done | bytes 679968 | tf_op jit(solution)/shard_map/ppermute | solution.py:79
  44.3 4.5 fusion.12
  48.8 2.3 copy.62
  51.1 2.2 fusion.13
  53.7 3.1 collective-permute-done.4.refs_5_
  56.9 2.5 collective-permute-done.5.refs_6_
  62.7 4.1 collective-permute-done.7.refs_8_
  66.8 2.9 collective-permute-done.6.refs_7_
  74.5 3.7 assemble.1
  85.8 9.1 %project_states.3 = (bf16[512,1024]{1,0:T(8,128)(2,1)S(1)}, bf16[1024,256]{1,0:T(8,128)(2,1)S(1)}, bf16[1024,256]{1,0:T(8,128)(2,1)S(1)}, bf16[32,1024]{1,0:T(8,...) custom-call(s32[600]{0:T(1024)S(1)} %layout.1.table, ...), custom_call_target="tpu_custom_call" | custom-call | bytes 1024 | tf_op jit(solution)/shard_map/project_states/pallas_call | solution.py:1001
  99.9 9.1 %project_states.2 = (bf16[512,1024]{1,0:T(8,128)(2,1)S(1)}, bf16[1024,256]{1,0:T(8,128)(2,1)S(1)}, bf16[1024,256]{1,0:T(8,128)(2,1)S(1)}, bf16[32,1024]{1,0:T(8,...) custom-call(s32[600]{0:T(1024)S(1)} %layout.1.table, ...), custom_call_target="tpu_custom_call" | custom-call | bytes 1024 | tf_op jit(solution)/shard_map/project_states/pallas_call | solution.py:1001
  112.5 6.3 collective-permute-done.10.refs_1_.refs_0_
  119.4 3.9 collective-permute-start.11
  123.3 2.4 collective-permute-start.13
  129.7 2.6 collective-permute-start.14
  137.2 8.8 %attention_forward.2 = (bf16[4,528,256]{2,1,0:T(8,128)(2,1)S(1)}, bf16[8,2,192,512]{3,2,1,0:T(8,128)(2,1)S(1)}, bf16[8,2,128,512]{3,2,1,0:T(8,128)(2,1)S(1)}, bf...) custom-call(s32[11]{0:T(128)S(1)} %pad_add_fusion.info, s32[600]{0:T(1024)S(1)} %layout.1.table, ...), custom_call_target="tpu_custom_call" | custom-call | bytes 1024 | tf_op jit(solution)/shard_map/attention_forward/pallas_call | solution.py:1001
  150.3 16.6 %collective-permute-done.14.refs_8_ = bf16[256,3072]{1,0:T(8,128)(2,1)} collective-permute-done((bf16[256,3072]{1,0:T(8,128)(2,1)}, bf16[256,3072]{1,0:T(8,128)(2,1)}, u32[]{:S(2)}, u32[]{:S(2)}) %collective-permute-start.14) | collective-permute-done | bytes 1572896 | tf_op jit(solution)/shard_map/ppermute | solution.py:79
  169.2 8.8 %attention_forward.3 = (bf16[4,528,256]{2,1,0:T(8,128)(2,1)S(1)}, bf16[8,2,192,512]{3,2,1,0:T(8,128)(2,1)S(1)}, bf16[8,2,128,512]{3,2,1,0:T(8,128)(2,1)S(1)}, bf...) custom-call(s32[11]{0:T(128)S(1)} %pad_add_fusion.info, s32[600]{0:T(1024)S(1)} %layout.1.table, ...), custom_call_target="tpu_custom_call" | custom-call | bytes 1024 | tf_op jit(solution)/shard_map/attention_forward/pallas_call | solution.py:1001
  181.8 2.2 collective-permute-start.24
  186.3 3.4 copy-done.1
  189.6 7.4 %residual.2 = (f32[256,2048]{1,0:T(8,128)S(1)}, bf16[256,2048]{1,0:T(8,128)(2,1)}, bf16[16,256]{1,0:T(8,128)(2,1)S(1)}) custom-call(s32[11]{0:T(128)S(1)} %pad_add_fusion.info, bf16[2,1024,2048]{2,1,0:T(8,128)(2,1)S(1)} %copy-done.1, f32[1,2048]{1,0:T(1,128)S(1)} %bitcast.109, bf16[4,528,256]{2,1,0:T(8,128)(2,1)S(1)} %get-tuple-element.320.refs_0_.att_ref, ...), custom_call_target="tpu_custom_call" | custom-call | bytes 1024 | tf_op jit(solution)/shard_map/residual/pallas_call | solution.py:1001
  202.3 6.1 residual.3
  208.5 10.5 %collective-permute-done.24.refs_10_ = bf16[256,3072]{1,0:T(8,128)(2,1)} collective-permute-done((bf16[256,3072]{1,0:T(8,128)(2,1)}, bf16[256,3072]{1,0:T(8,128)(2,1)}, u32[]{:S(2)}, u32[]{:S(2)}) %collective-permute-start.24) | collective-permute-done | bytes 1572896 | tf_op jit(solution)/shard_map/ppermute | solution.py:79
  221.0 3.1 collective-permute-done.27.refs_2_
  231.5 14.6 %collective-permute-done.30.refs_13_ = bf16[128,3072]{1,0:T(8,128)(2,1)S(1)} collective-permute-done((bf16[128,3072]{1,0:T(8,128)(2,1)S(1)}, bf16[128,3072]{1,0:T(8,128)(2,1)S(1)}, u32[]{:S(2)}, u32[]{:S(2)}) %collective-permute-start.30) | collective-permute-done | bytes 786464 | tf_op jit(solution)/shard_map/ppermute | solution.py:79
  248.4 5.0 collective-permute-done.28.refs_2_.refs_0_
  256.4 35.2 %feed_forward.5 = (bf16[1024,2048]{1,0:T(8,128)(2,1)}, bf16[1024,2048]{1,0:T(8,128)(2,1)}) custom-call(s32[11]{0:T(128)} %copy-done.94, bf16[256,2048]{1,0:T(8,128)(2,1)} %get-tuple-element.341.refs_0_, bf16[256,2048]{1,0:T(8,128)(2,1)} %collective-permute-done.31.refs_1_, bf16[256,2048]{1,0:T(8,128)(2,1)} %copy-done.125, bf16[256,2048]{1,0:T(8,128)(2,1)} %copy-done.126, ...), custom_call_target="tpu_custom_call" | custom-call | bytes 1024 | tf_op jit(solution)/shard_map/feed_forward/pallas_call | solution.py:1001
  294.6 2.4 collective-permute-done.37.refs_1_
  297.0 35.3 %feed_forward.6 = (bf16[1024,2048]{1,0:T(8,128)(2,1)}, bf16[1024,2048]{1,0:T(8,128)(2,1)}) custom-call(s32[11]{0:T(128)} %copy-done.94, bf16[256,2048]{1,0:T(8,128)(2,1)} %copy-done.33, bf16[256,2048]{1,0:T(8,128)(2,1)} %collective-permute-done.37.refs_1_, bf16[256,2048]{1,0:T(8,128)(2,1)} %collective-permute-done.28.refs_2_.refs_0_, ...), custom_call_target="tpu_custom_call" | custom-call | bytes 1024 | tf_op jit(solution)/shard_map/feed_forward/pallas_call | solution.py:1001
  334.4 34.6 %collective-permute-done.39.refs_10_.refs_8_ = bf16[256,3072]{1,0:T(8,128)(2,1)S(1)} collective-permute-done((bf16[256,3072]{1,0:T(8,128)(2,1)}, bf16[256,3072]{1,0:T(8,128)(2,1)S(1)}, u32[]{:S(2)}, u32[]{:S(2)}) %collective-permute-start.39) | collective-permute-done | bytes 1572896 | tf_op jit(solution)/shard_map/ppermute | solution.py:79
  373.1 16.0 %collective-permute-done.42.refs_13_.refs_11_ = bf16[128,3072]{1,0:T(8,128)(2,1)S(1)} collective-permute-done((bf16[128,3072]{1,0:T(8,128)(2,1)S(1)}, bf16[128,3072]{1,0:T(8,128)(2,1)S(1)}, u32[]{:S(2)}, u32[]{:S(2)}) %collective-permute-start.42) | collective-permute-done | bytes 786464 | tf_op jit(solution)/shard_map/ppermute | solution.py:79
  390.9 35.4 %feed_forward.7 = (bf16[256,2048]{1,0:T(8,128)(2,1)}, bf16[256,2048]{1,0:T(8,128)(2,1)}, bf16[256,2048]{1,0:T(8,128)(2,1)}, bf16[256,2048]{1,0:T(8,128)(2,1)}, b...) custom-call(s32[11]{0:T(128)} %copy-done.94, ...), custom_call_target="tpu_custom_call" | custom-call | bytes 1024 | tf_op jit(solution)/shard_map/feed_forward/pallas_call | solution.py:1001
  426.4 2.9 collective-permute-done.44
  429.2 2.6 add_convert_fusion.5
  432.5 20.2 %feed_forward.8 = (bf16[256,2048]{1,0:T(8,128)(2,1)}, bf16[256,2048]{1,0:T(8,128)(2,1)}, bf16[256,2048]{1,0:T(8,128)(2,1)}, bf16[256,2048]{1,0:T(8,128)(2,1)}) custom-call(s32[11]{0:T(128)} %copy-done.94, bf16[256,2048]{1,0:T(8,128)(2,1)} %collective-permute-done.28.refs_2_.refs_0_, bf16[256,2048]{1,0:T(8,128)(2,1)} %collective-permute-done.38.refs_3_.refs_1_, ...), custom_call_target="tpu_custom_call" | custom-call | bytes 1024 | tf_op jit(solution)/shard_map/feed_forward/pallas_call | solution.py:1001
  453.3 4.1 collective-permute-done.46.refs_2_
  457.4 2.6 add_convert_fusion.4
  460.6 9.1 %branch_gradient.2 = (f32[256,2048]{1,0:T(8,128)S(1)}, f32[16,2048]{1,0:T(8,128)S(1)}, bf16[528,256]{1,0:T(8,128)(2,1)S(1)}, bf16[528,256]{1,0:T(8,128)(2,1)S(1)...) custom-call(s32[11]{0:T(128)S(1)} %copy-done.95, bf16[2,1024,2048]{2,1,0:T(8,128)(2,1)} %dy_ref.3, ...), custom_call_target="tpu_custom_call" | custom-call | bytes 2000000 | tf_op jit(solution)/shard_map/branch_gradient/pallas_call | solution.py:1001
  474.6 20.1 %feed_forward.9 = (bf16[256,2048]{1,0:T(8,128)(2,1)}, bf16[256,2048]{1,0:T(8,128)(2,1)}, bf16[256,2048]{1,0:T(8,128)(2,1)}, bf16[256,2048]{1,0:T(8,128)(2,1)}) custom-call(s32[11]{0:T(128)} %copy-done.94, bf16[256,2048]{1,0:T(8,128)(2,1)} %copy-done.33, bf16[256,2048]{1,0:T(8,128)(2,1)} %collective-permute-done.37.refs_1_, bf16[2,1024,2048]{2,1,0:T(8,128)(2,1)} %dy_ref.3, ...), custom_call_target="tpu_custom_call" | custom-call | bytes 1024 | tf_op jit(solution)/shard_map/feed_forward/pallas_call | solution.py:1001
  496.7 7.7 %collective-permute-done.48.refs_6_.refs_2_ = bf16[528,256]{1,0:T(8,128)(2,1)S(1)} collective-permute-done((bf16[528,256]{1,0:T(8,128)(2,1)}, bf16[528,256]{1,0:T(8,128)(2,1)S(1)}, u32[]{:S(2)}, u32[]{:S(2)}) %collective-permute-start.48) | collective-permute-done | bytes 270368 | tf_op jit(solution)/shard_map/ppermute | solution.py:110
  504.4 4.9 collective-permute-done.49.refs_7_.refs_3_
  513.0 10.3 %branch_gradient.3 = (f32[256,2048]{1,0:T(8,128)S(1)}, f32[16,2048]{1,0:T(8,128)S(1)}, bf16[528,256]{1,0:T(8,128)(2,1)S(1)}, bf16[528,256]{1,0:T(8,128)(2,1)S(1)...) custom-call(s32[11]{0:T(128)S(1)} %copy-done.96, bf16[2,1024,2048]{2,1,0:T(8,128)(2,1)} %dy_ref.3, ...), custom_call_target="tpu_custom_call" | custom-call | bytes 2000000 | tf_op jit(solution)/shard_map/branch_gradient/pallas_call | solution.py:1001
  531.4 14.5 %attention_backward.2 = (bf16[4,512,256]{2,1,0:T(8,128)(2,1)S(1)}, f32[1088,256]{1,0:T(8,128)S(1)}, f32[8,2,160,128]{3,2,1,0:T(8,128)S(1)}, bf16[2,224,128]{2,1,0:T(8,128)(2,1)S(1)}, f32[2,256,256]{2,1,0:T(8,128)S(1)}) custom-call(s32[11]{0:T(128)S(1)} %copy-done.96, s32[600]{0:T(1024)S(1)} %layout.1.table, bf16[512,1024]{1,0:T(8,128)(2,1)S(1)} %copy-done.39, ...), custom_call_target="tpu_custom_call" | custom-call | bytes 2000000 | tf_op jit(solution)/shard_map/attention_backward/pallas_call | solution.py:1001
  549.5 14.5 %attention_backward.3 = (bf16[4,512,256]{2,1,0:T(8,128)(2,1)S(1)}, f32[1088,256]{1,0:T(8,128)S(1)}, f32[8,2,160,128]{3,2,1,0:T(8,128)S(1)}, bf16[2,224,128]{2,1,0:T(8,128)(2,1)S(1)}, f32[2,256,256]{2,1,0:T(8,128)S(1)}) custom-call(s32[11]{0:T(128)S(1)} %copy-done.96, s32[600]{0:T(1024)S(1)} %layout.1.table, bf16[512,1024]{1,0:T(8,128)(2,1)S(1)} %copy-done.36, ...), custom_call_target="tpu_custom_call" | custom-call | bytes 2000000 | tf_op jit(solution)/shard_map/attention_backward/pallas_call | solution.py:1001
  565.0 6.9 %collective-permute-done.59.refs_1_.refs_0_ = bf16[2,2,224,128]{3,2,1,0:T(8,128)(2,1)S(1)} collective-permute-done((bf16[2,2,224,128]{3,2,1,0:T(8,128)(2,1)S(1)}, bf16[2,2,224,128]{3,2,1,0:T(8,128)(2,1)S(1)}, u32[]{:S(2)}, u32[]{:S(2)}) %collective-permute-start.59) | collective-permute-done | bytes 229408 | tf_op jit(solution)/shard_map/ppermute | solution.py:110
  578.3 3.0 collective-permute-done.62.refs_3_
  581.2 2.7 collective-permute-done.61.refs_2_
  583.9 2.7 collective-permute-done.60.refs_1_
  587.2 6.8 attention_keys.2
  594.0 2.7 collective-permute-done.67.refs_2_
  596.8 6.7 attention_keys.3
  606.4 4.2 collective-permute-done.74.refs_7_
  621.1 3.4 collective-permute-done.77
  630.6 3.4 collective-permute-done.79.refs_6_
  634.5 7.5 %collective-permute-done.81 = bf16[1056,128]{1,0:T(8,128)(2,1)S(1)} collective-permute-done((bf16[1056,128]{1,0:T(8,128)(2,1)S(1)}, bf16[1056,128]{1,0:T(8,128)(2,1)S(1)}, u32[]{:S(2)}, u32[]{:S(2)}) %collective-permute-start.81) | collective-permute-done | bytes 270368 | tf_op jit(solution)/shard_map/ppermute | solution.py:110
  645.2 9.4 %token_gradient.2.refs_12_ = f32[2,256,2048]{2,1,0:T(8,128)} custom-call(s32[11]{0:T(128)S(1)} %copy-done.96, bf16[2,1024,2048]{2,1,0:T(8,128)(2,1)} %x_ref.7, f32[1,2048]{1,0:T(1,128)S(1)} %bitcast.115, f32[256,2048]{1,0:T(8,128)S(1)} %copy-done.45, bf16[4,512,256]{2,1,0:T(8,128)(2,1)S(1)} %get-tuple-element.444.dq_ref.refs_0_, ...), custom_call_target="tpu_custom_call" | custom-call | bytes 2000000 | tf_op jit(solution)/shard_map/token_gradient/pallas_call | solution.py:1001
  658.2 11.0 %collective-permute-done.71 = bf16[256,2048]{1,0:T(8,128)(2,1)S(1)} collective-permute-done((bf16[256,2048]{1,0:T(8,128)(2,1)S(1)}, bf16[256,2048]{1,0:T(8,128)(2,1)S(1)}, u32[]{:S(2)}, u32[]{:S(2)}) %collective-permute-start.71) | collective-permute-done | bytes 1048608 | tf_op jit(solution)/shard_map/ppermute | solution.py:110
  669.3 9.8 %token_gradient.3 = f32[2,256,2048]{2,1,0:T(8,128)} custom-call(s32[11]{0:T(128)S(1)} %copy-done.96, bf16[2,1024,2048]{2,1,0:T(8,128)(2,1)} %x_ref.7, f32[1,2048]{1,0:T(1,128)S(1)} %bitcast.116, f32[256,2048]{1,0:T(8,128)S(1)} %copy-done.47, bf16[4,512,256]{2,1,0:T(8,128)(2,1)S(1)} %get-tuple-element.448.dq_ref.refs_0_, ...), custom_call_target="tpu_custom_call", output_to_operand_aliasing={{}: (16, {})} | custom-call | bytes 2000000 | tf_op jit(solution)/shard_map/token_gradient/pallas_call | solution.py:1001
  681.2 2.6 fusion.7
  (517 shorter events, 155.1 us)
Async XLA Ops:
  5.3 18.2 %collective-permute-start = (bf16[1328,256]{1,0:T(8,128)(2,1)S(1)}, bf16[1328,256]{1,0:T(8,128)(2,1)S(1)}, u32[]{:S(2)}, u32[]{:S(2)}) collective-permute-start(bf16[1328,256]{1,0:T(8,128)(2,1)S(1)} %constant_dynamic-update-slice_fusion.refs_0_), channel_id=1, source_target_pairs={{0,8},{8,16},{16,24},{24,28},{28,20},{20,12},{12,4},{4,0},{1,9},{9... | collective-permute-start | bytes 2039816 | tf_op jit(solution)/shard_map/ppermute | solution.py:79
  8.3 16.7 %collective-permute-start.1 = (bf16[1328,256]{1,0:T(8,128)(2,1)S(1)}, bf16[1328,256]{1,0:T(8,128)(2,1)S(1)}, u32[]{:S(2)}, u32[]{:S(2)}) collective-permute-start(bf16[1328,256]{1,0:T(8,128)(2,1)S(1)} %constant_dynamic-update-slice_fusion.refs_0_), channel_id=1, source_target_pairs={{0,4},{8,0},{16,8},{24,16},{28,24},{20,28},{12,20},{4,12},{1,5},{9... | collective-permute-start | bytes 2039816 | tf_op jit(solution)/shard_map/ppermute | solution.py:79
  25.0 15.8 %collective-permute-start.2 = (bf16[1328,256]{1,0:T(8,128)(2,1)S(1)}, bf16[1328,256]{1,0:T(8,128)(2,1)S(1)}, u32[]{:S(2)}, u32[]{:S(2)}) collective-permute-start(bf16[1328,256]{1,0:T(8,128)(2,1)S(1)} %collective-permute-done.refs_1_), channel_id=1, source_target_pairs={{0,8},{8,16},{16,24},{24,28},{28,20},{20,12},{12,4},{4,0},{1,9},{9... | collective-permute-start | bytes 2039816 | tf_op jit(solution)/shard_map/ppermute | solution.py:79
  26.6 15.6 %collective-permute-start.3 = (bf16[1328,256]{1,0:T(8,128)(2,1)S(1)}, bf16[1328,256]{1,0:T(8,128)(2,1)}, u32[]{:S(2)}, u32[]{:S(2)}) collective-permute-start(bf16[1328,256]{1,0:T(8,128)(2,1)S(1)} %collective-permute-done.1.refs_2_), channel_id=1, source_target_pairs={{0,4},{8,0},{16,8},{24,16},{28,24},{20,28},{12,20},{4,12},{1,5},{9... | collective-permute-start | bytes 2039816 | tf_op jit(solution)/shard_map/ppermute | solution.py:79
  42.2 14.6 %collective-permute-start.4 = (bf16[1328,256]{1,0:T(8,128)(2,1)S(1)}, bf16[1328,256]{1,0:T(8,128)(2,1)S(1)}, u32[]{:S(2)}, u32[]{:S(2)}) collective-permute-start(bf16[1328,256]{1,0:T(8,128)(2,1)S(1)} %collective-permute-done.2.refs_3_), channel_id=1, source_target_pairs={{0,8},{8,16},{16,24},{24,28},{28,20},{20,12},{12,4},{4,0},{1,9},{9... | collective-permute-start | bytes 2039816 | tf_op jit(solution)/shard_map/ppermute | solution.py:79
  43.8 15.5 %collective-permute-start.5 = (bf16[1328,256]{1,0:T(8,128)(2,1)}, bf16[1328,256]{1,0:T(8,128)(2,1)S(1)}, u32[]{:S(2)}, u32[]{:S(2)}) collective-permute-start(bf16[1328,256]{1,0:T(8,128)(2,1)} %collective-permute-done.3.refs_4_), channel_id=1, source_target_pairs={{0,4},{8,0},{16,8},{24,16},{28,24},{20,28},{12,20},{4,12},{1,5},{9... | collective-permute-start | bytes 2039816 | tf_op jit(solution)/shard_map/ppermute | solution.py:79
  59.9 9.8 %collective-permute-start.6 = (bf16[672,256]{1,0:T(8,128)(2,1)S(1)}, bf16[672,256]{1,0:T(8,128)(2,1)S(1)}, u32[]{:S(2)}, u32[]{:S(2)}) collective-permute-start(bf16[672,256]{1,0:T(8,128)(2,1)S(1)} %slice.337), channel_id=1, source_target_pairs={{0,8},{8,16},{16,24},{24,28},{28,20},{20,12},{12,4},{4,0},{1,9},{9... | collective-permute-start | bytes 1032200 | tf_op jit(solution)/shard_map/ppermute | solution.py:79
  69.7 42.2 %collective-permute-start.8 = (bf16[256,3072]{1,0:T(8,128)(2,1)}, bf16[256,3072]{1,0:T(8,128)(2,1)}, u32[]{:S(2)}, u32[]{:S(2)}) collective-permute-start(bf16[256,3072]{1,0:T(8,128)(2,1)} %pad_maximum_fusion.1.refs_5_), channel_id=1, source_target_pairs={{0,8},{8,16},{16,24},{24,28},{28,20},{20,12},{12,4},{4,0},{1,9},{9... | collective-permute-start | bytes 4718600 | tf_op jit(solution)/shard_map/ppermute | solution.py:79
  71.4 40.6 %collective-permute-start.9 = (bf16[256,3072]{1,0:T(8,128)(2,1)}, bf16[256,3072]{1,0:T(8,128)(2,1)}, u32[]{:S(2)}, u32[]{:S(2)}) collective-permute-start(bf16[256,3072]{1,0:T(8,128)(2,1)} %pad_maximum_fusion.1.refs_5_), channel_id=1, source_target_pairs={{0,4},{8,0},{16,8},{24,16},{28,24},{20,28},{12,20},{4,12},{1,5},{9... | collective-permute-start | bytes 4718600 | tf_op jit(solution)/shard_map/ppermute | solution.py:79
  78.2 51.4 %collective-permute-start.20 = (bf16[528,2048]{1,0:T(8,128)(2,1)}, bf16[528,2048]{1,0:T(8,128)(2,1)}, u32[]{:S(2)}, u32[]{:S(2)}) collective-permute-start(bf16[528,2048]{1,0:T(8,128)(2,1)} %get-tuple-element.321.refs_4_.refs_3_), channel_id=1, source_target_pairs={{0,2},{1,3},{2,0},{3,1},{4,6},{5,7},{6,4},{7,5},{8,10},{9,11},{10,... | collective-permute-start | bytes 6488072 | tf_op jit(solution)/shard_map/ppermute | solution.py:110
  112.5 69.4 %collective-permute-start.19 = (bf16[528,2048]{1,0:T(8,128)(2,1)}, bf16[528,2048]{1,0:T(8,128)(2,1)S(1)}, u32[]{:S(2)}, u32[]{:S(2)}) collective-permute-start(bf16[528,2048]{1,0:T(8,128)(2,1)} %get-tuple-element.321.refs_4_.refs_3_), channel_id=1, source_target_pairs={{0,1},{1,0},{2,3},{3,2},{4,5},{5,4},{6,7},{7,6},{8,9},{9,8},{10,11... | collective-permute-start | bytes 6488072 | tf_op jit(solution)/shard_map/ppermute | solution.py:110
  119.4 10.2 %collective-permute-start.11 = (bf16[2,2,288,128]{3,2,1,0:T(8,128)(2,1)S(1)}, bf16[2,2,288,128]{3,2,1,0:T(8,128)(2,1)S(1)}, u32[]{:S(2)}, u32[]{:S(2)}) collective-permute-start(bf16[2,2,288,128]{3,2,1,0:T(8,128)(2,1)S(1)} %get-tuple-element.304), channel_id=1, source_target_pairs={{0,8},{4,12},{8,16},{12,20},{16,24},{20,28},{1,9},{5,13},{9,17},{1... | collective-permute-start | bytes 884744 | tf_op jit(solution)/shard_map/ppermute | solution.py:116
  129.6 56.6 %collective-permute-start.21 = (bf16[528,2048]{1,0:T(8,128)(2,1)}, bf16[528,2048]{1,0:T(8,128)(2,1)}, u32[]{:S(2)}, u32[]{:S(2)}) collective-permute-start(bf16[528,2048]{1,0:T(8,128)(2,1)} %collective-permute-done.20.refs_6_.refs_5_), channel_id=1, source_target_pairs={{0,1},{1,0},{2,3},{3,2},{4,5},{5,4},{6,7},{7,6},{8,9},{9,8},{10,11... | collective-permute-start | bytes 6488072 | tf_op jit(solution)/shard_map/ppermute | solution.py:110
  129.7 37.2 %collective-permute-start.14 = (bf16[256,3072]{1,0:T(8,128)(2,1)}, bf16[256,3072]{1,0:T(8,128)(2,1)}, u32[]{:S(2)}, u32[]{:S(2)}) collective-permute-start(bf16[256,3072]{1,0:T(8,128)(2,1)} %collective-permute-done.8.refs_6_), channel_id=1, source_target_pairs={{0,8},{8,16},{16,24},{24,28},{28,20},{20,12},{12,4},{4,0},{1,9},{9... | collective-permute-start | bytes 4718600 | tf_op jit(solution)/shard_map/ppermute | solution.py:79
  132.3 36.8 %collective-permute-start.15 = (bf16[256,3072]{1,0:T(8,128)(2,1)}, bf16[256,3072]{1,0:T(8,128)(2,1)}, u32[]{:S(2)}, u32[]{:S(2)}) collective-permute-start(bf16[256,3072]{1,0:T(8,128)(2,1)} %collective-permute-done.9.refs_7_), channel_id=1, source_target_pairs={{0,4},{8,0},{16,8},{24,16},{28,24},{20,28},{12,20},{4,12},{1,5},{9... | collective-permute-start | bytes 4718600 | tf_op jit(solution)/shard_map/ppermute | solution.py:79
  149.9 34.1 %collective-permute-start.18 = (bf16[528,256]{1,0:T(8,128)(2,1)S(1)}, bf16[528,256]{1,0:T(8,128)(2,1)S(1)}, u32[]{:S(2)}, u32[]{:S(2)}) collective-permute-start(bf16[528,256]{1,0:T(8,128)(2,1)S(1)} %get-tuple-element.487), channel_id=1, source_target_pairs={{0,3},{1,2},{2,1},{3,0},{4,7},{5,6},{6,5},{7,4},{8,11},{9,10},{10,... | collective-permute-start | bytes 811016 | tf_op jit(solution)/shard_map/ppermute | solution.py:110
  166.9 17.4 %collective-permute-start.17 = (bf16[528,256]{1,0:T(8,128)(2,1)S(1)}, bf16[528,256]{1,0:T(8,128)(2,1)S(1)}, u32[]{:S(2)}, u32[]{:S(2)}) collective-permute-start(bf16[528,256]{1,0:T(8,128)(2,1)S(1)} %get-tuple-element.488), channel_id=1, source_target_pairs={{0,2},{1,3},{2,0},{3,1},{4,6},{5,7},{6,4},{7,5},{8,10},{9,11},{10,... | collective-permute-start | bytes 811016 | tf_op jit(solution)/shard_map/ppermute | solution.py:110
  169.1 15.7 %collective-permute-start.16 = (bf16[528,256]{1,0:T(8,128)(2,1)S(1)}, bf16[528,256]{1,0:T(8,128)(2,1)S(1)}, u32[]{:S(2)}, u32[]{:S(2)}) collective-permute-start(bf16[528,256]{1,0:T(8,128)(2,1)S(1)} %get-tuple-element.489), channel_id=1, source_target_pairs={{0,1},{1,0},{2,3},{3,2},{4,5},{5,4},{6,7},{7,6},{8,9},{9,8},{10,11... | collective-permute-start | bytes 811016 | tf_op jit(solution)/shard_map/ppermute | solution.py:110
  181.8 37.1 %collective-permute-start.24 = (bf16[256,3072]{1,0:T(8,128)(2,1)}, bf16[256,3072]{1,0:T(8,128)(2,1)}, u32[]{:S(2)}, u32[]{:S(2)}) collective-permute-start(bf16[256,3072]{1,0:T(8,128)(2,1)} %collective-permute-done.14.refs_8_), channel_id=1, source_target_pairs={{0,8},{8,16},{16,24},{24,28},{28,20},{20,12},{12,4},{4,0},{1,9},{9... | collective-permute-start | bytes 4718600 | tf_op jit(solution)/shard_map/ppermute | solution.py:79
  184.1 37.0 %collective-permute-start.25 = (bf16[256,3072]{1,0:T(8,128)(2,1)}, bf16[256,3072]{1,0:T(8,128)(2,1)}, u32[]{:S(2)}, u32[]{:S(2)}) collective-permute-start(bf16[256,3072]{1,0:T(8,128)(2,1)} %collective-permute-done.15.refs_9_), channel_id=1, source_target_pairs={{0,4},{8,0},{16,8},{24,16},{28,24},{20,28},{12,20},{4,12},{1,5},{9... | collective-permute-start | bytes 4718600 | tf_op jit(solution)/shard_map/ppermute | solution.py:79
  184.3 14.1 %collective-permute-start.23 = (bf16[528,256]{1,0:T(8,128)(2,1)S(1)}, bf16[528,256]{1,0:T(8,128)(2,1)S(1)}, u32[]{:S(2)}, u32[]{:S(2)}) collective-permute-start(bf16[528,256]{1,0:T(8,128)(2,1)S(1)} %get-tuple-element.485), channel_id=1, source_target_pairs={{0,3},{1,2},{2,1},{3,0},{4,7},{5,6},{6,5},{7,4},{8,11},{9,10},{10,... | collective-permute-start | bytes 811016 | tf_op jit(solution)/shard_map/ppermute | solution.py:110
  184.8 14.2 %collective-permute-start.22 = (bf16[528,256]{1,0:T(8,128)(2,1)S(1)}, bf16[528,256]{1,0:T(8,128)(2,1)S(1)}, u32[]{:S(2)}, u32[]{:S(2)}) collective-permute-start(bf16[528,256]{1,0:T(8,128)(2,1)S(1)} %get-tuple-element.486), channel_id=1, source_target_pairs={{0,2},{1,3},{2,0},{3,1},{4,6},{5,7},{6,4},{7,5},{8,10},{9,11},{10,... | collective-permute-start | bytes 811016 | tf_op jit(solution)/shard_map/ppermute | solution.py:110
  198.9 25.2 %collective-permute-start.27 = (bf16[256,2048]{1,0:T(8,128)(2,1)}, bf16[256,2048]{1,0:T(8,128)(2,1)S(1)}, u32[]{:S(2)}, u32[]{:S(2)}) collective-permute-start(bf16[256,2048]{1,0:T(8,128)(2,1)} %get-tuple-element.341.refs_0_), channel_id=1, source_target_pairs={{0,2},{1,3},{2,0},{3,1},{4,6},{5,7},{6,4},{7,5},{8,10},{9,11},{10,... | collective-permute-start | bytes 3145736 | tf_op jit(solution)/shard_map/ppermute | solution.py:110
  227.0 19.2 %collective-permute-start.30 = (bf16[128,3072]{1,0:T(8,128)(2,1)S(1)}, bf16[128,3072]{1,0:T(8,128)(2,1)S(1)}, u32[]{:S(2)}, u32[]{:S(2)}) collective-permute-start(bf16[128,3072]{1,0:T(8,128)(2,1)S(1)} %slice.346), channel_id=1, source_target_pairs={{0,4},{8,0},{16,8},{24,16},{28,24},{20,28},{12,20},{4,12},{1,5},{9... | collective-permute-start | bytes 2359304 | tf_op jit(solution)/shard_map/ppermute | solution.py:79
  227.3 18.9 %collective-permute-start.29 = (bf16[128,3072]{1,0:T(8,128)(2,1)S(1)}, bf16[128,3072]{1,0:T(8,128)(2,1)S(1)}, u32[]{:S(2)}, u32[]{:S(2)}) collective-permute-start(bf16[128,3072]{1,0:T(8,128)(2,1)S(1)} %slice.345), channel_id=1, source_target_pairs={{0,8},{8,16},{16,24},{24,28},{28,20},{20,12},{12,4},{4,0},{1,9},{9... | collective-permute-start | bytes 2359304 | tf_op jit(solution)/shard_map/ppermute | solution.py:79
  229.3 24.1 %collective-permute-start.28 = (bf16[256,2048]{1,0:T(8,128)(2,1)S(1)}, bf16[256,2048]{1,0:T(8,128)(2,1)}, u32[]{:S(2)}, u32[]{:S(2)}) collective-permute-start(bf16[256,2048]{1,0:T(8,128)(2,1)S(1)} %get-tuple-element.351.refs_0_), channel_id=1, source_target_pairs={{0,2},{1,3},{2,0},{3,1},{4,6},{5,7},{6,4},{7,5},{8,10},{9,11},{10,... | collective-permute-start | bytes 3145736 | tf_op jit(solution)/shard_map/ppermute | solution.py:110
  246.2 45.5 %collective-permute-start.33 = (bf16[256,3072]{1,0:T(8,128)(2,1)}, bf16[256,3072]{1,0:T(8,128)(2,1)}, u32[]{:S(2)}, u32[]{:S(2)}) collective-permute-start(bf16[256,3072]{1,0:T(8,128)(2,1)} %pad_maximum_fusion.2.refs_5_.refs_3_), channel_id=1, source_target_pairs={{0,8},{8,16},{16,24},{24,28},{28,20},{20,12},{12,4},{4,0},{1,9},{9... | collective-permute-start | bytes 4718600 | tf_op jit(solution)/shard_map/ppermute | solution.py:79
  248.0 43.7 %collective-permute-start.34 = (bf16[256,3072]{1,0:T(8,128)(2,1)}, bf16[256,3072]{1,0:T(8,128)(2,1)}, u32[]{:S(2)}, u32[]{:S(2)}) collective-permute-start(bf16[256,3072]{1,0:T(8,128)(2,1)} %pad_maximum_fusion.2.refs_5_.refs_3_), channel_id=1, source_target_pairs={{0,4},{8,0},{16,8},{24,16},{28,24},{20,28},{12,20},{4,12},{1,5},{9... | collective-permute-start | bytes 4718600 | tf_op jit(solution)/shard_map/ppermute | solution.py:79
  253.4 40.6 %collective-permute-start.38 = (bf16[256,2048]{1,0:T(8,128)(2,1)}, bf16[256,2048]{1,0:T(8,128)(2,1)}, u32[]{:S(2)}, u32[]{:S(2)}) collective-permute-start(bf16[256,2048]{1,0:T(8,128)(2,1)} %collective-permute-done.28.refs_2_.refs_0_), channel_id=1, source_target_pairs={{0,1},{1,0},{2,3},{3,2},{4,5},{5,4},{6,7},{7,6},{8,9},{9,8},{10,11... | collective-permute-start | bytes 3145736 | tf_op jit(solution)/shard_map/ppermute | solution.py:110
  291.7 40.6 %collective-permute-start.35 = (bf16[256,3072]{1,0:T(8,128)(2,1)}, bf16[256,3072]{1,0:T(8,128)(2,1)}, u32[]{:S(2)}, u32[]{:S(2)}) collective-permute-start(bf16[256,3072]{1,0:T(8,128)(2,1)} %collective-permute-done.33.refs_6_.refs_4_), channel_id=1, source_target_pairs={{0,8},{8,16},{16,24},{24,28},{28,20},{20,12},{12,4},{4,0},{1,9},{9... | collective-permute-start | bytes 4718600 | tf_op jit(solution)/shard_map/ppermute | solution.py:79
  293.5 38.8 %collective-permute-start.36 = (bf16[256,3072]{1,0:T(8,128)(2,1)}, bf16[256,3072]{1,0:T(8,128)(2,1)}, u32[]{:S(2)}, u32[]{:S(2)}) collective-permute-start(bf16[256,3072]{1,0:T(8,128)(2,1)} %collective-permute-done.34.refs_7_.refs_5_), channel_id=1, source_target_pairs={{0,4},{8,0},{16,8},{24,16},{28,24},{20,28},{12,20},{4,12},{1,5},{9... | collective-permute-start | bytes 4718600 | tf_op jit(solution)/shard_map/ppermute | solution.py:79
  294.0 79.1 %collective-permute-start.43 = (bf16[800,2048]{1,0:T(8,128)(2,1)S(1)}, bf16[800,2048]{1,0:T(8,128)(2,1)}, u32[]{:S(2)}, u32[]{:S(2)}) collective-permute-start(bf16[800,2048]{1,0:T(8,128)(2,1)S(1)} %copy-done.3), channel_id=1, source_target_pairs={{0,2},{1,3},{2,0},{3,1},{4,6},{5,7},{6,4},{7,5},{8,10},{9,11},{10,... | collective-permute-start | bytes 9830408 | tf_op jit(solution)/shard_map/ppermute | solution.py:110
  332.3 36.7 %collective-permute-start.39 = (bf16[256,3072]{1,0:T(8,128)(2,1)}, bf16[256,3072]{1,0:T(8,128)(2,1)S(1)}, u32[]{:S(2)}, u32[]{:S(2)}) collective-permute-start(bf16[256,3072]{1,0:T(8,128)(2,1)} %collective-permute-done.35.refs_8_.refs_6_), channel_id=1, source_target_pairs={{0,8},{8,16},{16,24},{24,28},{28,20},{20,12},{12,4},{4,0},{1,9},{9... | collective-permute-start | bytes 4718600 | tf_op jit(solution)/shard_map/ppermute | solution.py:79
  334.1 36.4 %collective-permute-start.40 = (bf16[256,3072]{1,0:T(8,128)(2,1)}, bf16[256,3072]{1,0:T(8,128)(2,1)S(1)}, u32[]{:S(2)}, u32[]{:S(2)}) collective-permute-start(bf16[256,3072]{1,0:T(8,128)(2,1)} %collective-permute-done.36.refs_9_.refs_7_), channel_id=1, source_target_pairs={{0,4},{8,0},{16,8},{24,16},{28,24},{20,28},{12,20},{4,12},{1,5},{9... | collective-permute-start | bytes 4718600 | tf_op jit(solution)/shard_map/ppermute | solution.py:79
  370.6 18.5 %collective-permute-start.42 = (bf16[128,3072]{1,0:T(8,128)(2,1)S(1)}, bf16[128,3072]{1,0:T(8,128)(2,1)S(1)}, u32[]{:S(2)}, u32[]{:S(2)}) collective-permute-start(bf16[128,3072]{1,0:T(8,128)(2,1)S(1)} %slice.351), channel_id=1, source_target_pairs={{0,4},{8,0},{16,8},{24,16},{28,24},{20,28},{12,20},{4,12},{1,5},{9... | collective-permute-start | bytes 2359304 | tf_op jit(solution)/shard_map/ppermute | solution.py:79
  370.9 18.7 %collective-permute-start.41 = (bf16[128,3072]{1,0:T(8,128)(2,1)S(1)}, bf16[128,3072]{1,0:T(8,128)(2,1)S(1)}, u32[]{:S(2)}, u32[]{:S(2)}) collective-permute-start(bf16[128,3072]{1,0:T(8,128)(2,1)S(1)} %slice.350), channel_id=1, source_target_pairs={{0,8},{8,16},{16,24},{24,28},{28,20},{20,12},{12,4},{4,0},{1,9},{9... | collective-permute-start | bytes 2359304 | tf_op jit(solution)/shard_map/ppermute | solution.py:79
  431.8 25.5 %collective-permute-start.46 = (bf16[256,2048]{1,0:T(8,128)(2,1)}, bf16[256,2048]{1,0:T(8,128)(2,1)}, u32[]{:S(2)}, u32[]{:S(2)}) collective-permute-start(bf16[256,2048]{1,0:T(8,128)(2,1)} %add_convert_fusion.5), channel_id=1, source_target_pairs={{0,2},{1,3},{2,0},{3,1},{4,6},{5,7},{6,4},{7,5},{8,10},{9,11},{10,... | collective-permute-start | bytes 3145736 | tf_op jit(solution)/shard_map/ppermute | solution.py:110
  460.0 34.8 %collective-permute-start.50 = (bf16[256,2048]{1,0:T(8,128)(2,1)}, bf16[256,2048]{1,0:T(8,128)(2,1)}, u32[]{:S(2)}, u32[]{:S(2)}) collective-permute-start(bf16[256,2048]{1,0:T(8,128)(2,1)} %add_convert_fusion.4), channel_id=1, source_target_pairs={{0,2},{1,3},{2,0},{3,1},{4,6},{5,7},{6,4},{7,5},{8,10},{9,11},{10,... | collective-permute-start | bytes 3145736 | tf_op jit(solution)/shard_map/ppermute | solution.py:110
  494.7 14.5 %collective-permute-start.51 = (bf16[256,2048]{1,0:T(8,128)(2,1)}, bf16[256,2048]{1,0:T(8,128)(2,1)S(1)}, u32[]{:S(2)}, u32[]{:S(2)}) collective-permute-start(bf16[256,2048]{1,0:T(8,128)(2,1)} %get-tuple-element.388), channel_id=1, source_target_pairs={{0,1},{1,0},{2,3},{3,2},{4,5},{5,4},{6,7},{7,6},{8,9},{9,8},{10,11... | collective-permute-start | bytes 3145736 | tf_op jit(solution)/shard_map/ppermute | solution.py:110
  494.8 9.6 %collective-permute-start.48 = (bf16[528,256]{1,0:T(8,128)(2,1)}, bf16[528,256]{1,0:T(8,128)(2,1)S(1)}, u32[]{:S(2)}, u32[]{:S(2)}) collective-permute-start(bf16[528,256]{1,0:T(8,128)(2,1)} %copy-done.119), channel_id=1, source_target_pairs={{0,2},{1,3},{2,0},{3,1},{4,6},{5,7},{6,4},{7,5},{8,10},{9,11},{10,... | collective-permute-start | bytes 811016 | tf_op jit(solution)/shard_map/ppermute | solution.py:110
  496.3 12.9 %collective-permute-start.49 = (bf16[528,256]{1,0:T(8,128)(2,1)}, bf16[528,256]{1,0:T(8,128)(2,1)S(1)}, u32[]{:S(2)}, u32[]{:S(2)}) collective-permute-start(bf16[528,256]{1,0:T(8,128)(2,1)} %copy-done.118), channel_id=1, source_target_pairs={{0,3},{1,2},{2,1},{3,0},{4,7},{5,6},{6,5},{7,4},{8,11},{9,10},{10,... | collective-permute-start | bytes 811016 | tf_op jit(solution)/shard_map/ppermute | solution.py:110
  524.7 21.3 %collective-permute-start.54 = (bf16[256,2048]{1,0:T(8,128)(2,1)}, bf16[256,2048]{1,0:T(8,128)(2,1)S(1)}, u32[]{:S(2)}, u32[]{:S(2)}) collective-permute-start(bf16[256,2048]{1,0:T(8,128)(2,1)} %get-tuple-element.402), channel_id=1, source_target_pairs={{0,1},{1,0},{2,3},{3,2},{4,5},{5,4},{6,7},{7,6},{8,9},{9,8},{10,11... | collective-permute-start | bytes 3145736 | tf_op jit(solution)/shard_map/ppermute | solution.py:110
  525.2 20.7 %collective-permute-start.55 = (bf16[528,256]{1,0:T(8,128)(2,1)}, bf16[528,256]{1,0:T(8,128)(2,1)S(1)}, u32[]{:S(2)}, u32[]{:S(2)}) collective-permute-start(bf16[528,256]{1,0:T(8,128)(2,1)} %get-tuple-element.403), channel_id=1, source_target_pairs={{0,2},{1,3},{2,0},{3,1},{4,6},{5,7},{6,4},{7,5},{8,10},{9,11},{10,... | collective-permute-start | bytes 811016 | tf_op jit(solution)/shard_map/ppermute | solution.py:110
  526.7 19.3 %collective-permute-start.56 = (bf16[528,256]{1,0:T(8,128)(2,1)}, bf16[528,256]{1,0:T(8,128)(2,1)S(1)}, u32[]{:S(2)}, u32[]{:S(2)}) collective-permute-start(bf16[528,256]{1,0:T(8,128)(2,1)} %get-tuple-element.404), channel_id=1, source_target_pairs={{0,3},{1,2},{2,1},{3,0},{4,7},{5,6},{6,5},{7,4},{8,11},{9,10},{10,... | collective-permute-start | bytes 811016 | tf_op jit(solution)/shard_map/ppermute | solution.py:110
  546.4 40.7 %collective-permute-start.58 = (bf16[256,2048]{1,0:T(8,128)(2,1)S(1)}, bf16[256,2048]{1,0:T(8,128)(2,1)S(1)}, u32[]{:S(2)}, u32[]{:S(2)}) collective-permute-start(bf16[256,2048]{1,0:T(8,128)(2,1)S(1)} %add_convert_fusion.3), channel_id=1, source_target_pairs={{0,2},{1,3},{2,0},{3,1},{4,6},{5,7},{6,4},{7,5},{8,10},{9,11},{10,... | collective-permute-start | bytes 3145736 | tf_op jit(solution)/shard_map/ppermute | solution.py:110
  564.6 12.2 %collective-permute-start.65 = (bf16[512,256]{1,0:T(8,128)(2,1)S(1)}, bf16[512,256]{1,0:T(8,128)(2,1)S(1)}, u32[]{:S(2)}, u32[]{:S(2)}) collective-permute-start(bf16[512,256]{1,0:T(8,128)(2,1)S(1)} %get-tuple-element.493), channel_id=1, source_target_pairs={{0,3},{1,2},{2,1},{3,0},{4,7},{5,6},{6,5},{7,4},{8,11},{9,10},{10,... | collective-permute-start | bytes 786440 | tf_op jit(solution)/shard_map/ppermute | solution.py:110
  572.5 8.7 %collective-permute-start.62 = (bf16[2,2,80,128]{3,2,1,0:T(8,128)(2,1)S(1)}, bf16[2,2,80,128]{3,2,1,0:T(8,128)(2,1)S(1)}, u32[]{:S(2)}, u32[]{:S(2)}) collective-permute-start(bf16[2,2,80,128]{3,2,1,0:T(8,128)(2,1)S(1)} %get-tuple-element.425), channel_id=1, source_target_pairs={{24,0},{28,4},{25,1},{29,5},{26,2},{30,6},{27,3},{31,7}} | collective-permute-start | bytes 245768 | tf_op jit(solution)/shard_map/ppermute | solution.py:116
  573.8 10.0 %collective-permute-start.61 = (bf16[2,2,80,128]{3,2,1,0:T(8,128)(2,1)S(1)}, bf16[2,2,80,128]{3,2,1,0:T(8,128)(2,1)S(1)}, u32[]{:S(2)}, u32[]{:S(2)}) collective-permute-start(bf16[2,2,80,128]{3,2,1,0:T(8,128)(2,1)S(1)} %get-tuple-element.425), channel_id=1, source_target_pairs={{16,0},{20,4},{24,8},{28,12},{17,1},{21,5},{25,9},{29,13},{18,2},{... | collective-permute-start | bytes 245768 | tf_op jit(solution)/shard_map/ppermute | solution.py:116
  575.1 11.4 %collective-permute-start.60 = (bf16[2,2,224,128]{3,2,1,0:T(8,128)(2,1)S(1)}, bf16[2,2,224,128]{3,2,1,0:T(8,128)(2,1)S(1)}, u32[]{:S(2)}, u32[]{:S(2)}) collective-permute-start(bf16[2,2,224,128]{3,2,1,0:T(8,128)(2,1)S(1)} %get-tuple-element.424), channel_id=1, source_target_pairs={{8,0},{12,4},{16,8},{20,12},{24,16},{28,20},{9,1},{13,5},{17,9},{2... | collective-permute-start | bytes 688136 | tf_op jit(solution)/shard_map/ppermute | solution.py:116
  576.8 17.2 %collective-permute-start.64 = (bf16[512,256]{1,0:T(8,128)(2,1)S(1)}, bf16[512,256]{1,0:T(8,128)(2,1)S(1)}, u32[]{:S(2)}, u32[]{:S(2)}) collective-permute-start(bf16[512,256]{1,0:T(8,128)(2,1)S(1)} %get-tuple-element.494), channel_id=1, source_target_pairs={{0,2},{1,3},{2,0},{3,1},{4,6},{5,7},{6,4},{7,5},{8,10},{9,11},{10,... | collective-permute-start | bytes 786440 | tf_op jit(solution)/shard_map/ppermute | solution.py:110
  581.2 12.8 %collective-permute-start.63 = (bf16[512,256]{1,0:T(8,128)(2,1)S(1)}, bf16[512,256]{1,0:T(8,128)(2,1)S(1)}, u32[]{:S(2)}, u32[]{:S(2)}) collective-permute-start(bf16[512,256]{1,0:T(8,128)(2,1)S(1)} %get-tuple-element.495), channel_id=1, source_target_pairs={{0,1},{1,0},{2,3},{3,2},{4,5},{5,4},{6,7},{7,6},{8,9},{9,8},{10,11... | collective-permute-start | bytes 786440 | tf_op jit(solution)/shard_map/ppermute | solution.py:110
  583.9 10.1 %collective-permute-start.68 = (bf16[512,256]{1,0:T(8,128)(2,1)S(1)}, bf16[512,256]{1,0:T(8,128)(2,1)S(1)}, u32[]{:S(2)}, u32[]{:S(2)}) collective-permute-start(bf16[512,256]{1,0:T(8,128)(2,1)S(1)} %get-tuple-element.490), channel_id=1, source_target_pairs={{0,3},{1,2},{2,1},{3,0},{4,7},{5,6},{6,5},{7,4},{8,11},{9,10},{10,... | collective-permute-start | bytes 786440 | tf_op jit(solution)/shard_map/ppermute | solution.py:110
  586.5 10.2 %collective-permute-start.67 = (bf16[512,256]{1,0:T(8,128)(2,1)S(1)}, bf16[512,256]{1,0:T(8,128)(2,1)S(1)}, u32[]{:S(2)}, u32[]{:S(2)}) collective-permute-start(bf16[512,256]{1,0:T(8,128)(2,1)S(1)} %get-tuple-element.491), channel_id=1, source_target_pairs={{0,2},{1,3},{2,0},{3,1},{4,6},{5,7},{6,4},{7,5},{8,10},{9,11},{10,... | collective-permute-start | bytes 786440 | tf_op jit(solution)/shard_map/ppermute | solution.py:110
  587.1 9.7 %collective-permute-start.66 = (bf16[512,256]{1,0:T(8,128)(2,1)S(1)}, bf16[512,256]{1,0:T(8,128)(2,1)S(1)}, u32[]{:S(2)}, u32[]{:S(2)}) collective-permute-start(bf16[512,256]{1,0:T(8,128)(2,1)S(1)} %get-tuple-element.492), channel_id=1, source_target_pairs={{0,1},{1,0},{2,3},{3,2},{4,5},{5,4},{6,7},{7,6},{8,9},{9,8},{10,11... | collective-permute-start | bytes 786440 | tf_op jit(solution)/shard_map/ppermute | solution.py:110
  603.5 14.4 %collective-permute-start.70 = (bf16[256,2048]{1,0:T(8,128)(2,1)S(1)}, bf16[256,2048]{1,0:T(8,128)(2,1)S(1)}, u32[]{:S(2)}, u32[]{:S(2)}) collective-permute-start(bf16[256,2048]{1,0:T(8,128)(2,1)S(1)} %copy-done.149), channel_id=1, source_target_pairs={{0,1},{1,0},{2,3},{3,2},{4,5},{5,4},{6,7},{7,6},{8,9},{9,8},{10,11... | collective-permute-start | bytes 3145736 | tf_op jit(solution)/shard_map/ppermute | solution.py:110
  604.0 39.6 %collective-permute-start.83 = (bf16[800,2048]{1,0:T(8,128)(2,1)S(1)}, bf16[800,2048]{1,0:T(8,128)(2,1)S(1)}, u32[]{:S(2)}, u32[]{:S(2)}) collective-permute-start(bf16[800,2048]{1,0:T(8,128)(2,1)S(1)} %copy-done.3), channel_id=1, source_target_pairs={{0,1},{1,0},{2,3},{3,2},{4,5},{5,4},{6,7},{7,6},{8,9},{9,8},{10,11... | collective-permute-start | bytes 9830408 | tf_op jit(solution)/shard_map/ppermute | solution.py:110
  604.1 41.1 %collective-permute-start.84 = (bf16[800,2048]{1,0:T(8,128)(2,1)}, bf16[800,2048]{1,0:T(8,128)(2,1)}, u32[]{:S(2)}, u32[]{:S(2)}) collective-permute-start(bf16[800,2048]{1,0:T(8,128)(2,1)} %collective-permute-done.43.refs_10_), channel_id=1, source_target_pairs={{0,1},{1,0},{2,3},{3,2},{4,5},{5,4},{6,7},{7,6},{8,9},{9,8},{10,11... | collective-permute-start | bytes 9830408 | tf_op jit(solution)/shard_map/ppermute | solution.py:110
  621.1 8.5 %collective-permute-start.75 = (bf16[512,128]{1,0:T(8,128)(2,1)S(1)}, bf16[512,128]{1,0:T(8,128)(2,1)S(1)}, u32[]{:S(2)}, u32[]{:S(2)}) collective-permute-start(bf16[512,128]{1,0:T(8,128)(2,1)S(1)} %get-tuple-element.458), channel_id=1, source_target_pairs={{0,1},{1,0},{2,3},{3,2},{4,5},{5,4},{6,7},{7,6},{8,9},{9,8},{10,11... | collective-permute-start | bytes 393224 | tf_op jit(solution)/shard_map/ppermute | solution.py:110
  634.0 8.0 %collective-permute-start.81 = (bf16[1056,128]{1,0:T(8,128)(2,1)S(1)}, bf16[1056,128]{1,0:T(8,128)(2,1)S(1)}, u32[]{:S(2)}, u32[]{:S(2)}) collective-permute-start(bf16[1056,128]{1,0:T(8,128)(2,1)S(1)} %pad_maximum_fusion.4), channel_id=1, source_target_pairs={{0,4},{4,0},{8,12},{12,8},{16,20},{20,16},{24,28},{28,24},{1,5},{5... | collective-permute-start | bytes 811016 | tf_op jit(solution)/shard_map/ppermute | solution.py:110
  634.5 22.0 %collective-permute-start.52 = (bf16[256,2048]{1,0:T(8,128)(2,1)S(1)}, bf16[256,2048]{1,0:T(8,128)(2,1)S(1)}, u32[]{:S(2)}, u32[]{:S(2)}) collective-permute-start(bf16[256,2048]{1,0:T(8,128)(2,1)S(1)} %copy-done.148), channel_id=1, source_target_pairs={{0,1},{1,0},{2,3},{3,2},{4,5},{5,4},{6,7},{7,6},{8,9},{9,8},{10,11... | collective-permute-start | bytes 3145736 | tf_op jit(solution)/shard_map/ppermute | solution.py:110
  642.0 12.6 %collective-permute-start.82 = (bf16[1056,128]{1,0:T(8,128)(2,1)S(1)}, bf16[1056,128]{1,0:T(8,128)(2,1)S(1)}, u32[]{:S(2)}, u32[]{:S(2)}) collective-permute-start(bf16[1056,128]{1,0:T(8,128)(2,1)S(1)} %add_convert_fusion.7), channel_id=1, source_target_pairs={{0,8},{4,12},{8,0},{12,4},{16,24},{20,28},{24,16},{28,20},{1,9},{5... | collective-permute-start | bytes 811016 | tf_op jit(solution)/shard_map/ppermute | solution.py:110
  643.7 37.5 %collective-permute-start.69 = (bf16[256,2048]{1,0:T(8,128)(2,1)}, bf16[256,2048]{1,0:T(8,128)(2,1)}, u32[]{:S(2)}, u32[]{:S(2)}) collective-permute-start(bf16[256,2048]{1,0:T(8,128)(2,1)} %get-tuple-element.438), channel_id=1, source_target_pairs={{0,1},{1,0},{2,3},{3,2},{4,5},{5,4},{6,7},{7,6},{8,9},{9,8},{10,11... | collective-permute-start | bytes 3145736 | tf_op jit(solution)/shard_map/ppermute | solution.py:110
  643.7 25.6 %collective-permute-start.71 = (bf16[256,2048]{1,0:T(8,128)(2,1)S(1)}, bf16[256,2048]{1,0:T(8,128)(2,1)S(1)}, u32[]{:S(2)}, u32[]{:S(2)}) collective-permute-start(bf16[256,2048]{1,0:T(8,128)(2,1)S(1)} %add_convert_fusion.1), channel_id=1, source_target_pairs={{0,2},{1,3},{2,0},{3,1},{4,6},{5,7},{6,4},{7,5},{8,10},{9,11},{10,... | collective-permute-start | bytes 3145736 | tf_op jit(solution)/shard_map/ppermute | solution.py:110
  654.8 24.4 %collective-permute-start.85 = (bf16[1056,128]{1,0:T(8,128)(2,1)S(1)}, bf16[1056,128]{1,0:T(8,128)(2,1)S(1)}, u32[]{:S(2)}, u32[]{:S(2)}) collective-permute-start(bf16[1056,128]{1,0:T(8,128)(2,1)S(1)} %add_convert_fusion.6), channel_id=1, source_target_pairs={{0,16},{4,20},{8,24},{12,28},{16,0},{20,4},{24,8},{28,12},{1,17},{... | collective-permute-start | bytes 811016 | tf_op jit(solution)/shard_map/ppermute | solution.py:110
  (174 other events, 1975.2 us)

commit v5 on v4

--- a/solution.py
+++ b/solution.py
@@ -21,6 +21,7 @@
 ROW_TILE = 512
 LATE_COST = 2000000
 SMALL_LIMIT = 32 * 1024 * 1024
+LARGE = ("feed_forward", "project_states", "attention_forward", "residual", "branch_gradient")
 
 
 def dotg(left, right, lc, rc):
@@ -1012,7 +1013,7 @@
         cost_estimate=pl.CostEstimate(flops=0, transcendentals=0, bytes_accessed=cost),
         compiler_params=pltpu.CompilerParams(
             dimension_semantics=("arbitrary",),
-            vmem_limit_bytes=VMEM_LIMIT if name == "feed_forward" else SMALL_LIMIT,
+            vmem_limit_bytes=VMEM_LIMIT if name in LARGE else SMALL_LIMIT,
         ),
         name=name,
     )(*scalars, *ins)
@@ -1128,6 +1129,7 @@
             pltpu.VMEM((rows + STRETCH, width), BF),
             pltpu.VMEM((rows + STRETCH, width), BF),
         ],
+        cost=LATE_COST,
     )
 
 
@@ -1494,7 +1496,7 @@
         atts = group_exchange([att[r] for r in range(n_grp)])
         att_sets.append([att, *atts[1:]])
         attended.append([att, weights, phi, sums, inverse])
-    att_sets[0][0], att_sets[1][0] = ring_a.tie(att_sets[0][0], att_sets[1][0])
+    att_sets[0][1], att_sets[1][1] = ring_a.tie(att_sets[0][1], att_sets[1][1])
     ring_a.hop()
     for batch in range(batches):
         if batch:
@@ -1605,12 +1607,11 @@
         run_mlp(info, 1, mlp_ins[1][:low], every[:low], cotangent, [ring_c], partial[1], sizes[1:])
     )
     late_b = scatter_end(far_b, [])
-    lower[1], late_b[-1] = lax.optimization_barrier((lower[1], late_b[-1]))
+    lower[1], late_b[-1] = lax.optimization_barrier((after(lower[1], *d_outs_a[2:]), late_b[-1]))
     near_b = [lower[0], flip(lower[1], "grp", 1)]
     early_b = [far_pair(lower[far], lower[far + 1]) for far in range(2, low, 2)]
     summands_b = near_b + scatter_end(early_b, []) + late_b
     partial[1] = [None] * n_grp + list(lower[low:]) + list(upper[low:])
-    attended[1][6] = after(attended[1][6], *d_outs_a[2:])
     d_resid_b, wide_b, d_outs_b = run_branch_of(1, summands_b)
     gone_a, ends_a, sums_back = run_backward_of(
         0, after(saved[0][0], d_resid_b), d_outs_a, None

time: 693 us -> 665 us (0.960)
  local copies, waits for them, and re-layouts: 73 us -> 43.7 us
  Pallas kernels: 289 us -> 309 us
  waiting for transfers between devices: 224 us -> 207 us
    unnamed x316 -> x266, local copies, waits for them, and re-layouts: 56.7 us -> 27.9 us
    pallas_call x28, Pallas kernels: 289 us -> 309 us  [call(): pl.pallas_call(kernel, grid_spec=pltpu.PrefetchScalarGridSpec(num_scalar_...]
    ppermute x24, waiting for transfers between devices: 127 us -> 114 us  [move(): return lax.ppermute(value, 'seq', pairs)]
  transfers between devices with their start and end apart: 86 -> 86, of which waited for: 47 -> 48; matrix products, arithmetic and copies ran while one was open for 5% -> 5% of each run, Pallas kernels for 35% -> 39%
where the time goes in v5:
time: 665 us; the launch traced here: 657 us
  Pallas kernels  309 us (46%)
  waiting for transfers between devices  207 us (31%)
  starting transfers between devices  71.6 us (11%)
  local copies, waits for them, and re-layouts  43.7 us (7%)
  other arithmetic  23.3 us (4%)
    pallas_call x28, Pallas kernels, call(): pl.pallas_call(kernel, grid_spec=pltpu.PrefetchScalarGridSpec(num_scalar_...  309 us
    ppermute x24, waiting for transfers between devices, move(): return lax.ppermute(value, 'seq', pairs)  114 us
    ppermute x56, waiting for transfers between devices, flip(): return lax.ppermute(value, axis, [(i, i ^ bit) for i in range(count)])  82.4 us
    ppermute x56, starting transfers between devices, flip(): return lax.ppermute(value, axis, [(i, i ^ bit) for i in range(count)])  31.2 us
    ppermute x24, starting transfers between devices, move(): return lax.ppermute(value, 'seq', pairs)  28.4 us
    unnamed x266, local copies, waits for them, and re-layouts  27.9 us
  transfers between devices with their start and end apart: 86, of which 48 were waited for; matrix products, arithmetic and copies ran while one was open for 5% of the time, Pallas kernels for 39%

profile of v5, /device:TPU:0, one launch (start us, length us, event | category | flops | bytes accessed | tf_op | source)
XLA Modules:
  0.0 656.5 jit_solution(6686883057182684677)
XLA Ops:
  5.3 3.0 collective-permute-start
  12.6 2.2 layout.1.table
  15.5 4.6 fusion.3
  20.1 3.5 collective-permute-done.refs_1_
  27.1 4.4 fusion.5
  31.5 9.4 %collective-permute-done.2.refs_3_ = bf16[1328,256]{1,0:T(8,128)(2,1)S(1)} collective-permute-done((bf16[1328,256]{1,0:T(8,128)(2,1)S(1)}, bf16[1328,256]{1,0:T(8,128)(2,1)S(1)}, u32[]{:S(2)}, u32[]{:S(2)}) %collective-permute-start.2) | collective-permute-done | bytes 679968 | tf_op jit(solution)/shard_map/ppermute | solution.py:80
  44.3 4.5 fusion.12
  52.4 4.4 collective-permute-done.4.refs_5_
  56.9 2.5 collective-permute-done.5.refs_6_
  62.8 4.1 collective-permute-done.7.refs_8_
  66.8 2.9 collective-permute-done.6.refs_7_
  73.4 2.4 assemble.1
  79.8 12.6 %project_states.3 = (bf16[512,1024]{1,0:T(8,128)(2,1)}, bf16[1024,256]{1,0:T(8,128)(2,1)}, bf16[1024,256]{1,0:T(8,128)(2,1)}, bf16[32,1024]{1,0:T(8,128)(2,1)}, ...) custom-call(s32[600]{0:T(1024)} %copy-done.66, ...), custom_call_target="tpu_custom_call" | custom-call | bytes 1024 | tf_op jit(solution)/shard_map/project_states/pallas_call | solution.py:1002
  92.5 12.8 %project_states.2 = (bf16[512,1024]{1,0:T(8,128)(2,1)}, bf16[1024,256]{1,0:T(8,128)(2,1)}, bf16[1024,256]{1,0:T(8,128)(2,1)}, bf16[32,1024]{1,0:T(8,128)(2,1)}, ...) custom-call(s32[600]{0:T(1024)} %copy-done.66, ...), custom_call_target="tpu_custom_call" | custom-call | bytes 1024 | tf_op jit(solution)/shard_map/project_states/pallas_call | solution.py:1002
  106.8 6.3 collective-permute-done.10.refs_1_.refs_0_
  113.8 3.9 collective-permute-start.11
  117.7 2.4 collective-permute-start.13
  124.1 2.6 collective-permute-start.14
  127.5 11.0 %attention_forward.2 = (bf16[4,528,256]{2,1,0:T(8,128)(2,1)}, bf16[8,2,192,512]{3,2,1,0:T(8,128)(2,1)}, bf16[8,2,128,512]{3,2,1,0:T(8,128)(2,1)}, bf16[8,2,160,128]{3,2,1,0:T(8,128)(2,1)}, f32[8,8,128]{2,1,0:T(8,128)}) custom-call(s32[11]{0:T(128)} %copy-done.71, s32[600]{0:T(1024)} %copy-done.66, bf16[512,1024]{1,0:T(8,128)(2,1)} %get-tuple-element.392.q_ref, ...), custom_call_target="tpu_custom_call" | custom-call | bytes 2000000 | tf_op jit(solution)/shard_map/attention_forward/pallas_call | solution.py:1002
  140.7 11.1 %attention_forward.3 = (bf16[4,528,256]{2,1,0:T(8,128)(2,1)}, bf16[8,2,192,512]{3,2,1,0:T(8,128)(2,1)}, bf16[8,2,128,512]{3,2,1,0:T(8,128)(2,1)}, bf16[8,2,160,128]{3,2,1,0:T(8,128)(2,1)}, f32[8,8,128]{2,1,0:T(8,128)}) custom-call(s32[11]{0:T(128)} %copy-done.71, s32[600]{0:T(1024)} %copy-done.66, bf16[512,1024]{1,0:T(8,128)(2,1)} %get-tuple-element.406.q_ref, ...), custom_call_target="tpu_custom_call" | custom-call | bytes 2000000 | tf_op jit(solution)/shard_map/attention_forward/pallas_call | solution.py:1002
  155.2 6.0 collective-permute-done.14.refs_8_
  163.4 2.2 collective-permute-start.25
  165.9 4.1 collective-permute-done.18.refs_2_
  172.0 9.2 %residual.2 = (f32[256,2048]{1,0:T(8,128)}, bf16[256,2048]{1,0:T(8,128)(2,1)}, bf16[16,256]{1,0:T(8,128)(2,1)}) custom-call(s32[11]{0:T(128)} %copy-done.71, bf16[2,1024,2048]{2,1,0:T(8,128)(2,1)} %x_ref.7, f32[1,2048]{1,0:T(1,128)} %bitcast.118, bf16[4,528,256]{2,1,0:T(8,128)(2,1)} %get-tuple-element.309.refs_0_.att_ref, bf16[528,256]{1,0:T(8,128)(2,1)} %copy-done.112, ...), custom_call_target="tpu_custom_call" | custom-call | bytes 1024 | tf_op jit(solution)/shard_map/residual/pallas_call | solution.py:1002
  182.7 9.2 %residual.3 = (f32[256,2048]{1,0:T(8,128)}, bf16[256,2048]{1,0:T(8,128)(2,1)}, bf16[16,256]{1,0:T(8,128)(2,1)}) custom-call(s32[11]{0:T(128)} %copy-done.71, bf16[2,1024,2048]{2,1,0:T(8,128)(2,1)} %x_ref.7, f32[1,2048]{1,0:T(1,128)} %bitcast.119, bf16[4,528,256]{2,1,0:T(8,128)(2,1)} %get-tuple-element.330.refs_0_.att_ref, bf16[528,256]{1,0:T(8,128)(2,1)} %copy-done.113, ...), custom_call_target="tpu_custom_call" | custom-call | bytes 1024 | tf_op jit(solution)/shard_map/residual/pallas_call | solution.py:1002
  191.9 7.5 %collective-permute-done.25.refs_10_ = bf16[256,3072]{1,0:T(8,128)(2,1)S(1)} collective-permute-done((bf16[256,3072]{1,0:T(8,128)(2,1)}, bf16[256,3072]{1,0:T(8,128)(2,1)S(1)}, u32[]{:S(2)}, u32[]{:S(2)}) %collective-permute-start.25) | collective-permute-done | bytes 1572896 | tf_op jit(solution)/shard_map/ppermute | solution.py:80
  199.4 2.2 collective-permute-done.26.refs_11_
  201.7 4.2 collective-permute-done.27.refs_2_
  209.3 14.6 %collective-permute-done.30.refs_13_ = bf16[128,3072]{1,0:T(8,128)(2,1)S(1)} collective-permute-done((bf16[128,3072]{1,0:T(8,128)(2,1)S(1)}, bf16[128,3072]{1,0:T(8,128)(2,1)S(1)}, u32[]{:S(2)}, u32[]{:S(2)}) %collective-permute-start.30) | collective-permute-done | bytes 786464 | tf_op jit(solution)/shard_map/ppermute | solution.py:80
  226.8 4.3 collective-permute-done.28.refs_2_.refs_0_
  232.7 2.7 collective-permute-done.31.refs_1_
  235.4 35.2 %feed_forward.5 = (bf16[1024,2048]{1,0:T(8,128)(2,1)}, bf16[1024,2048]{1,0:T(8,128)(2,1)}) custom-call(s32[11]{0:T(128)} %copy-done.71, bf16[256,2048]{1,0:T(8,128)(2,1)} %get-tuple-element.341.refs_0_, bf16[256,2048]{1,0:T(8,128)(2,1)} %collective-permute-done.31.refs_1_, bf16[256,2048]{1,0:T(8,128)(2,1)} %copy-done.91, bf16[256,2048]{1,0:T(8,128)(2,1)} %copy-done.94, ...), custom_call_target="tpu_custom_call" | custom-call | bytes 1024 | tf_op jit(solution)/shard_map/feed_forward/pallas_call | solution.py:1002
  273.4 2.5 collective-permute-done.37.refs_1_
  276.8 35.3 %feed_forward.6 = (bf16[1024,2048]{1,0:T(8,128)(2,1)}, bf16[1024,2048]{1,0:T(8,128)(2,1)}) custom-call(s32[11]{0:T(128)} %copy-done.71, bf16[256,2048]{1,0:T(8,128)(2,1)} %get-tuple-element.351.refs_0_, bf16[256,2048]{1,0:T(8,128)(2,1)} %copy-done.93, bf16[256,2048]{1,0:T(8,128)(2,1)} %collective-permute-done.28.refs_2_.refs_0_, ...), custom_call_target="tpu_custom_call" | custom-call | bytes 1024 | tf_op jit(solution)/shard_map/feed_forward/pallas_call | solution.py:1002
  314.3 34.6 %collective-permute-done.39.refs_10_.refs_8_ = bf16[256,3072]{1,0:T(8,128)(2,1)S(1)} collective-permute-done((bf16[256,3072]{1,0:T(8,128)(2,1)}, bf16[256,3072]{1,0:T(8,128)(2,1)S(1)}, u32[]{:S(2)}, u32[]{:S(2)}) %collective-permute-start.39) | collective-permute-done | bytes 1572896 | tf_op jit(solution)/shard_map/ppermute | solution.py:80
  352.5 16.0 %collective-permute-done.42.refs_13_.refs_11_ = bf16[128,3072]{1,0:T(8,128)(2,1)S(1)} collective-permute-done((bf16[128,3072]{1,0:T(8,128)(2,1)S(1)}, bf16[128,3072]{1,0:T(8,128)(2,1)S(1)}, u32[]{:S(2)}, u32[]{:S(2)}) %collective-permute-start.42) | collective-permute-done | bytes 786464 | tf_op jit(solution)/shard_map/ppermute | solution.py:80
  369.5 35.3 %feed_forward.7 = (bf16[256,2048]{1,0:T(8,128)(2,1)}, bf16[256,2048]{1,0:T(8,128)(2,1)}, bf16[256,2048]{1,0:T(8,128)(2,1)}, bf16[256,2048]{1,0:T(8,128)(2,1)}, b...) custom-call(s32[11]{0:T(128)} %copy-done.71, ...), custom_call_target="tpu_custom_call" | custom-call | bytes 1024 | tf_op jit(solution)/shard_map/feed_forward/pallas_call | solution.py:1002
  404.9 2.9 collective-permute-done.44
  409.8 20.5 %feed_forward.8 = (bf16[256,2048]{1,0:T(8,128)(2,1)}, bf16[256,2048]{1,0:T(8,128)(2,1)}, bf16[256,2048]{1,0:T(8,128)(2,1)}, bf16[256,2048]{1,0:T(8,128)(2,1)}) custom-call(s32[11]{0:T(128)} %copy-done.71, bf16[256,2048]{1,0:T(8,128)(2,1)} %collective-permute-done.28.refs_2_.refs_0_, bf16[256,2048]{1,0:T(8,128)(2,1)} %collective-permute-done.38.refs_3_.refs_1_, ...), custom_call_target="tpu_custom_call" | custom-call | bytes 1024 | tf_op jit(solution)/shard_map/feed_forward/pallas_call | solution.py:1002
  430.9 3.8 collective-permute-done.46.refs_2_
  437.7 11.0 %branch_gradient.2 = (f32[256,2048]{1,0:T(8,128)}, f32[16,2048]{1,0:T(8,128)}, bf16[528,256]{1,0:T(8,128)(2,1)}, bf16[528,256]{1,0:T(8,128)(2,1)}, bf16[528,256]{1,0:T(8,128)(2,1)}, /*index=5*/bf16[528,256]{1,0:T(8,128)(2,1)}) custom-call(s32[11]{0:T(128)} %copy-done.71, bf16[2,1024,2048]{2,1,0:T(8,128)(2,1)} %dy_ref.3, ...), custom_call_target="tpu_custom_call" | custom-call | bytes 2000000 | tf_op jit(solution)/shard_map/branch_gradient/pallas_call | solution.py:1002
  450.5 20.4 %feed_forward.9 = (bf16[256,2048]{1,0:T(8,128)(2,1)}, bf16[256,2048]{1,0:T(8,128)(2,1)}, bf16[256,2048]{1,0:T(8,128)(2,1)}, bf16[256,2048]{1,0:T(8,128)(2,1)}) custom-call(s32[11]{0:T(128)} %copy-done.71, bf16[256,2048]{1,0:T(8,128)(2,1)} %get-tuple-element.351.refs_0_, bf16[256,2048]{1,0:T(8,128)(2,1)} %copy-done.93, bf16[2,1024,2048]{2,1,0:T(8,128)(2,1)} %dy_ref.3, ...), custom_call_target="tpu_custom_call" | custom-call | bytes 1024 | tf_op jit(solution)/shard_map/feed_forward/pallas_call | solution.py:1002
  473.8 2.5 collective-permute-done.51.refs_1_
  477.4 11.2 %branch_gradient.3 = (f32[256,2048]{1,0:T(8,128)}, f32[16,2048]{1,0:T(8,128)}, bf16[528,256]{1,0:T(8,128)(2,1)}, bf16[528,256]{1,0:T(8,128)(2,1)}, bf16[528,256]{1,0:T(8,128)(2,1)}, /*index=5*/bf16[528,256]{1,0:T(8,128)(2,1)}) custom-call(s32[11]{0:T(128)} %copy-done.71, bf16[2,1024,2048]{2,1,0:T(8,128)(2,1)} %dy_ref.3, ...), custom_call_target="tpu_custom_call" | custom-call | bytes 2000000 | tf_op jit(solution)/shard_map/branch_gradient/pallas_call | solution.py:1002
  501.7 14.5 %attention_backward.2 = (bf16[4,512,256]{2,1,0:T(8,128)(2,1)S(1)}, f32[1088,256]{1,0:T(8,128)S(1)}, f32[8,2,160,128]{3,2,1,0:T(8,128)S(1)}, bf16[2,224,128]{2,1,0:T(8,128)(2,1)S(1)}, f32[2,256,256]{2,1,0:T(8,128)S(1)}) custom-call(s32[11]{0:T(128)S(1)} %copy-done.72, s32[600]{0:T(1024)S(1)} %copy-done.68, bf16[512,1024]{1,0:T(8,128)(2,1)S(1)} %copy-done.20, ...), custom_call_target="tpu_custom_call" | custom-call | bytes 2000000 | tf_op jit(solution)/shard_map/attention_backward/pallas_call | solution.py:1002
  520.3 14.5 %attention_backward.3 = (bf16[4,512,256]{2,1,0:T(8,128)(2,1)S(1)}, f32[1088,256]{1,0:T(8,128)S(1)}, f32[8,2,160,128]{3,2,1,0:T(8,128)S(1)}, bf16[2,224,128]{2,1,0:T(8,128)(2,1)S(1)}, f32[2,256,256]{2,1,0:T(8,128)S(1)}) custom-call(s32[11]{0:T(128)S(1)} %copy-done.72, s32[600]{0:T(1024)S(1)} %copy-done.68, bf16[512,1024]{1,0:T(8,128)(2,1)S(1)} %copy-done.19, ...), custom_call_target="tpu_custom_call" | custom-call | bytes 2000000 | tf_op jit(solution)/shard_map/attention_backward/pallas_call | solution.py:1002
  536.4 6.2 collective-permute-done.59.refs_1_.refs_0_
  549.2 2.8 collective-permute-done.62.refs_3_
  552.0 2.7 collective-permute-done.61.refs_2_
  554.6 2.7 collective-permute-done.60.refs_1_
  558.6 6.9 %attention_keys.2 = (bf16[4,288,256]{2,1,0:T(8,128)(2,1)S(1)}, f32[2,128,64]{2,1,0:T(8,128)S(1)}) custom-call(s32[11]{0:T(128)S(1)} %copy-done.72, s32[600]{0:T(1024)S(1)} %copy-done.68, bf16[1024,256]{1,0:T(8,128)(2,1)S(1)} %copy-done.14, bf16[1024,256]{1,0:T(8,128)(2,1)S(1)} %copy-done.16, bf16[2,64,128]{2,1,0:T(8,128)(2,1)S(1)} %copy-done.53, ...), custom_call_target="tpu_custom_call" | custom-call | bytes 2000000 | tf_op jit(solution)/shard_map/attention_keys/pallas_call | solution.py:1002
  565.5 2.8 collective-permute-done.67.refs_2_
  568.4 6.7 %attention_keys.3 = (bf16[4,288,256]{2,1,0:T(8,128)(2,1)S(1)}, f32[2,128,64]{2,1,0:T(8,128)S(1)}) custom-call(s32[11]{0:T(128)S(1)} %copy-done.72, s32[600]{0:T(1024)S(1)} %copy-done.68, bf16[1024,256]{1,0:T(8,128)(2,1)S(1)} %copy-done.12, bf16[1024,256]{1,0:T(8,128)(2,1)S(1)} %copy-done.13, bf16[2,64,128]{2,1,0:T(8,128)(2,1)S(1)} %copy-done.53, ...), custom_call_target="tpu_custom_call" | custom-call | bytes 2000000 | tf_op jit(solution)/shard_map/attention_keys/pallas_call | solution.py:1002
  577.9 3.7 collective-permute-done.74.refs_7_
  585.2 2.1 collective-permute-done.72.refs_5_
  592.4 3.5 collective-permute-done.77
  596.7 2.4 collective-permute-done.76
  601.7 3.6 collective-permute-done.79.refs_6_
  606.1 7.3 %collective-permute-done.81 = bf16[1056,128]{1,0:T(8,128)(2,1)S(1)} collective-permute-done((bf16[1056,128]{1,0:T(8,128)(2,1)S(1)}, bf16[1056,128]{1,0:T(8,128)(2,1)S(1)}, u32[]{:S(2)}, u32[]{:S(2)}) %collective-permute-start.81) | collective-permute-done | bytes 270368 | tf_op jit(solution)/shard_map/ppermute | solution.py:111
  615.3 9.8 %token_gradient.2.refs_12_ = f32[2,256,2048]{2,1,0:T(8,128)} custom-call(s32[11]{0:T(128)S(1)} %copy-done.72, bf16[2,1024,2048]{2,1,0:T(8,128)(2,1)} %x_ref.7, f32[1,2048]{1,0:T(1,128)S(1)} %bitcast.107, f32[256,2048]{1,0:T(8,128)S(1)} %copy-done.24, bf16[4,512,256]{2,1,0:T(8,128)(2,1)S(1)} %get-tuple-element.444.dq_ref.refs_0_, ...), custom_call_target="tpu_custom_call" | custom-call | bytes 2000000 | tf_op jit(solution)/shard_map/token_gradient/pallas_call | solution.py:1002
  625.3 2.6 collective-permute-start.85
  629.9 10.1 %collective-permute-done.71 = bf16[256,2048]{1,0:T(8,128)(2,1)S(1)} collective-permute-done((bf16[256,2048]{1,0:T(8,128)(2,1)S(1)}, bf16[256,2048]{1,0:T(8,128)(2,1)S(1)}, u32[]{:S(2)}, u32[]{:S(2)}) %collective-permute-start.71) | collective-permute-done | bytes 1048608 | tf_op jit(solution)/shard_map/ppermute | solution.py:111
  640.0 9.7 %token_gradient.3 = f32[2,256,2048]{2,1,0:T(8,128)} custom-call(s32[11]{0:T(128)S(1)} %copy-done.72, bf16[2,1024,2048]{2,1,0:T(8,128)(2,1)} %x_ref.7, f32[1,2048]{1,0:T(1,128)S(1)} %bitcast.108, f32[256,2048]{1,0:T(8,128)S(1)} %copy-done.25, bf16[4,512,256]{2,1,0:T(8,128)(2,1)S(1)} %get-tuple-element.448.dq_ref.refs_0_, ...), custom_call_target="tpu_custom_call", output_to_operand_aliasing={{}: (16, {})} | custom-call | bytes 2000000 | tf_op jit(solution)/shard_map/token_gradient/pallas_call | solution.py:1002
  651.9 2.9 fusion.7
  (466 shorter events, 128.5 us)
Async XLA Ops:
  5.3 18.2 %collective-permute-start = (bf16[1328,256]{1,0:T(8,128)(2,1)S(1)}, bf16[1328,256]{1,0:T(8,128)(2,1)S(1)}, u32[]{:S(2)}, u32[]{:S(2)}) collective-permute-start(bf16[1328,256]{1,0:T(8,128)(2,1)S(1)} %constant_dynamic-update-slice_fusion.refs_0_), channel_id=1, source_target_pairs={{0,8},{8,16},{16,24},{24,28},{28,20},{20,12},{12,4},{4,0},{1,9},{9... | collective-permute-start | bytes 2039816 | tf_op jit(solution)/shard_map/ppermute | solution.py:80
  8.3 16.7 %collective-permute-start.1 = (bf16[1328,256]{1,0:T(8,128)(2,1)S(1)}, bf16[1328,256]{1,0:T(8,128)(2,1)S(1)}, u32[]{:S(2)}, u32[]{:S(2)}) collective-permute-start(bf16[1328,256]{1,0:T(8,128)(2,1)S(1)} %constant_dynamic-update-slice_fusion.refs_0_), channel_id=1, source_target_pairs={{0,4},{8,0},{16,8},{24,16},{28,24},{20,28},{12,20},{4,12},{1,5},{9... | collective-permute-start | bytes 2039816 | tf_op jit(solution)/shard_map/ppermute | solution.py:80
  25.0 15.8 %collective-permute-start.2 = (bf16[1328,256]{1,0:T(8,128)(2,1)S(1)}, bf16[1328,256]{1,0:T(8,128)(2,1)S(1)}, u32[]{:S(2)}, u32[]{:S(2)}) collective-permute-start(bf16[1328,256]{1,0:T(8,128)(2,1)S(1)} %collective-permute-done.refs_1_), channel_id=1, source_target_pairs={{0,8},{8,16},{16,24},{24,28},{28,20},{20,12},{12,4},{4,0},{1,9},{9... | collective-permute-start | bytes 2039816 | tf_op jit(solution)/shard_map/ppermute | solution.py:80
  26.6 15.6 %collective-permute-start.3 = (bf16[1328,256]{1,0:T(8,128)(2,1)S(1)}, bf16[1328,256]{1,0:T(8,128)(2,1)}, u32[]{:S(2)}, u32[]{:S(2)}) collective-permute-start(bf16[1328,256]{1,0:T(8,128)(2,1)S(1)} %collective-permute-done.1.refs_2_), channel_id=1, source_target_pairs={{0,4},{8,0},{16,8},{24,16},{28,24},{20,28},{12,20},{4,12},{1,5},{9... | collective-permute-start | bytes 2039816 | tf_op jit(solution)/shard_map/ppermute | solution.py:80
  42.2 14.6 %collective-permute-start.4 = (bf16[1328,256]{1,0:T(8,128)(2,1)S(1)}, bf16[1328,256]{1,0:T(8,128)(2,1)S(1)}, u32[]{:S(2)}, u32[]{:S(2)}) collective-permute-start(bf16[1328,256]{1,0:T(8,128)(2,1)S(1)} %collective-permute-done.2.refs_3_), channel_id=1, source_target_pairs={{0,8},{8,16},{16,24},{24,28},{28,20},{20,12},{12,4},{4,0},{1,9},{9... | collective-permute-start | bytes 2039816 | tf_op jit(solution)/shard_map/ppermute | solution.py:80
  43.8 15.5 %collective-permute-start.5 = (bf16[1328,256]{1,0:T(8,128)(2,1)}, bf16[1328,256]{1,0:T(8,128)(2,1)S(1)}, u32[]{:S(2)}, u32[]{:S(2)}) collective-permute-start(bf16[1328,256]{1,0:T(8,128)(2,1)} %collective-permute-done.3.refs_4_), channel_id=1, source_target_pairs={{0,4},{8,0},{16,8},{24,16},{28,24},{20,28},{12,20},{4,12},{1,5},{9... | collective-permute-start | bytes 2039816 | tf_op jit(solution)/shard_map/ppermute | solution.py:80
  59.9 9.8 %collective-permute-start.6 = (bf16[672,256]{1,0:T(8,128)(2,1)S(1)}, bf16[672,256]{1,0:T(8,128)(2,1)S(1)}, u32[]{:S(2)}, u32[]{:S(2)}) collective-permute-start(bf16[672,256]{1,0:T(8,128)(2,1)S(1)} %slice.334), channel_id=1, source_target_pairs={{0,8},{8,16},{16,24},{24,28},{28,20},{20,12},{12,4},{4,0},{1,9},{9... | collective-permute-start | bytes 1032200 | tf_op jit(solution)/shard_map/ppermute | solution.py:80
  69.7 36.6 %collective-permute-start.8 = (bf16[256,3072]{1,0:T(8,128)(2,1)}, bf16[256,3072]{1,0:T(8,128)(2,1)}, u32[]{:S(2)}, u32[]{:S(2)}) collective-permute-start(bf16[256,3072]{1,0:T(8,128)(2,1)} %pad_maximum_fusion.1.refs_5_), channel_id=1, source_target_pairs={{0,8},{8,16},{16,24},{24,28},{28,20},{20,12},{12,4},{4,0},{1,9},{9... | collective-permute-start | bytes 4718600 | tf_op jit(solution)/shard_map/ppermute | solution.py:80
  71.4 34.9 %collective-permute-start.9 = (bf16[256,3072]{1,0:T(8,128)(2,1)}, bf16[256,3072]{1,0:T(8,128)(2,1)}, u32[]{:S(2)}, u32[]{:S(2)}) collective-permute-start(bf16[256,3072]{1,0:T(8,128)(2,1)} %pad_maximum_fusion.1.refs_5_), channel_id=1, source_target_pairs={{0,4},{8,0},{16,8},{24,16},{28,24},{20,28},{12,20},{4,12},{1,5},{9... | collective-permute-start | bytes 4718600 | tf_op jit(solution)/shard_map/ppermute | solution.py:80
  77.6 46.4 %collective-permute-start.21 = (bf16[528,2048]{1,0:T(8,128)(2,1)S(1)}, bf16[528,2048]{1,0:T(8,128)(2,1)}, u32[]{:S(2)}, u32[]{:S(2)}) collective-permute-start(bf16[528,2048]{1,0:T(8,128)(2,1)S(1)} %get-tuple-element.321.refs_4_.refs_3_), channel_id=1, source_target_pairs={{0,2},{1,3},{2,0},{3,1},{4,6},{5,7},{6,4},{7,5},{8,10},{9,11},{10,... | collective-permute-start | bytes 6488072 | tf_op jit(solution)/shard_map/ppermute | solution.py:111
  106.8 58.8 %collective-permute-start.20 = (bf16[528,2048]{1,0:T(8,128)(2,1)S(1)}, bf16[528,2048]{1,0:T(8,128)(2,1)}, u32[]{:S(2)}, u32[]{:S(2)}) collective-permute-start(bf16[528,2048]{1,0:T(8,128)(2,1)S(1)} %get-tuple-element.321.refs_4_.refs_3_), channel_id=1, source_target_pairs={{0,1},{1,0},{2,3},{3,2},{4,5},{5,4},{6,7},{7,6},{8,9},{9,8},{10,11... | collective-permute-start | bytes 6488072 | tf_op jit(solution)/shard_map/ppermute | solution.py:111
  113.8 10.2 %collective-permute-start.11 = (bf16[2,2,288,128]{3,2,1,0:T(8,128)(2,1)S(1)}, bf16[2,2,288,128]{3,2,1,0:T(8,128)(2,1)S(1)}, u32[]{:S(2)}, u32[]{:S(2)}) collective-permute-start(bf16[2,2,288,128]{3,2,1,0:T(8,128)(2,1)S(1)} %get-tuple-element.307), channel_id=1, source_target_pairs={{0,8},{4,12},{8,16},{12,20},{16,24},{20,28},{1,9},{5,13},{9,17},{1... | collective-permute-start | bytes 884744 | tf_op jit(solution)/shard_map/ppermute | solution.py:117
  124.0 48.0 %collective-permute-start.22 = (bf16[528,2048]{1,0:T(8,128)(2,1)}, bf16[528,2048]{1,0:T(8,128)(2,1)}, u32[]{:S(2)}, u32[]{:S(2)}) collective-permute-start(bf16[528,2048]{1,0:T(8,128)(2,1)} %collective-permute-done.21.refs_6_.refs_5_), channel_id=1, source_target_pairs={{0,1},{1,0},{2,3},{3,2},{4,5},{5,4},{6,7},{7,6},{8,9},{9,8},{10,11... | collective-permute-start | bytes 6488072 | tf_op jit(solution)/shard_map/ppermute | solution.py:111
  124.1 37.2 %collective-permute-start.14 = (bf16[256,3072]{1,0:T(8,128)(2,1)}, bf16[256,3072]{1,0:T(8,128)(2,1)}, u32[]{:S(2)}, u32[]{:S(2)}) collective-permute-start(bf16[256,3072]{1,0:T(8,128)(2,1)} %collective-permute-done.8.refs_6_), channel_id=1, source_target_pairs={{0,8},{8,16},{16,24},{24,28},{28,20},{20,12},{12,4},{4,0},{1,9},{9... | collective-permute-start | bytes 4718600 | tf_op jit(solution)/shard_map/ppermute | solution.py:80
  126.6 36.8 %collective-permute-start.15 = (bf16[256,3072]{1,0:T(8,128)(2,1)}, bf16[256,3072]{1,0:T(8,128)(2,1)}, u32[]{:S(2)}, u32[]{:S(2)}) collective-permute-start(bf16[256,3072]{1,0:T(8,128)(2,1)} %collective-permute-done.9.refs_7_), channel_id=1, source_target_pairs={{0,4},{8,0},{16,8},{24,16},{28,24},{20,28},{12,20},{4,12},{1,5},{9... | collective-permute-start | bytes 4718600 | tf_op jit(solution)/shard_map/ppermute | solution.py:80
  140.5 12.5 %collective-permute-start.16 = (bf16[528,256]{1,0:T(8,128)(2,1)S(1)}, bf16[528,256]{1,0:T(8,128)(2,1)S(1)}, u32[]{:S(2)}, u32[]{:S(2)}) collective-permute-start(bf16[528,256]{1,0:T(8,128)(2,1)S(1)} %get-tuple-element.489), channel_id=1, source_target_pairs={{0,1},{1,0},{2,3},{3,2},{4,5},{5,4},{6,7},{7,6},{8,9},{9,8},{10,11... | collective-permute-start | bytes 811016 | tf_op jit(solution)/shard_map/ppermute | solution.py:111
  154.7 11.1 %collective-permute-start.19 = (bf16[528,256]{1,0:T(8,128)(2,1)}, bf16[528,256]{1,0:T(8,128)(2,1)S(1)}, u32[]{:S(2)}, u32[]{:S(2)}) collective-permute-start(bf16[528,256]{1,0:T(8,128)(2,1)} %get-tuple-element.487), channel_id=1, source_target_pairs={{0,3},{1,2},{2,1},{3,0},{4,7},{5,6},{6,5},{7,4},{8,11},{9,10},{10,... | collective-permute-start | bytes 811016 | tf_op jit(solution)/shard_map/ppermute | solution.py:111
  161.2 8.8 %collective-permute-start.18 = (bf16[528,256]{1,0:T(8,128)(2,1)}, bf16[528,256]{1,0:T(8,128)(2,1)S(1)}, u32[]{:S(2)}, u32[]{:S(2)}) collective-permute-start(bf16[528,256]{1,0:T(8,128)(2,1)} %get-tuple-element.488), channel_id=1, source_target_pairs={{0,2},{1,3},{2,0},{3,1},{4,6},{5,7},{6,4},{7,5},{8,10},{9,11},{10,... | collective-permute-start | bytes 811016 | tf_op jit(solution)/shard_map/ppermute | solution.py:111
  163.4 36.0 %collective-permute-start.25 = (bf16[256,3072]{1,0:T(8,128)(2,1)}, bf16[256,3072]{1,0:T(8,128)(2,1)S(1)}, u32[]{:S(2)}, u32[]{:S(2)}) collective-permute-start(bf16[256,3072]{1,0:T(8,128)(2,1)} %collective-permute-done.14.refs_8_), channel_id=1, source_target_pairs={{0,8},{8,16},{16,24},{24,28},{28,20},{20,12},{12,4},{4,0},{1,9},{9... | collective-permute-start | bytes 4718600 | tf_op jit(solution)/shard_map/ppermute | solution.py:80
  165.6 36.0 %collective-permute-start.26 = (bf16[256,3072]{1,0:T(8,128)(2,1)}, bf16[256,3072]{1,0:T(8,128)(2,1)S(1)}, u32[]{:S(2)}, u32[]{:S(2)}) collective-permute-start(bf16[256,3072]{1,0:T(8,128)(2,1)} %collective-permute-done.15.refs_9_), channel_id=1, source_target_pairs={{0,4},{8,0},{16,8},{24,16},{28,24},{20,28},{12,20},{4,12},{1,5},{9... | collective-permute-start | bytes 4718600 | tf_op jit(solution)/shard_map/ppermute | solution.py:80
  165.8 15.4 %collective-permute-start.24 = (bf16[528,256]{1,0:T(8,128)(2,1)S(1)}, bf16[528,256]{1,0:T(8,128)(2,1)S(1)}, u32[]{:S(2)}, u32[]{:S(2)}) collective-permute-start(bf16[528,256]{1,0:T(8,128)(2,1)S(1)} %get-tuple-element.484), channel_id=1, source_target_pairs={{0,3},{1,2},{2,1},{3,0},{4,7},{5,6},{6,5},{7,4},{8,11},{9,10},{10,... | collective-permute-start | bytes 811016 | tf_op jit(solution)/shard_map/ppermute | solution.py:111
  170.7 10.5 %collective-permute-start.23 = (bf16[528,256]{1,0:T(8,128)(2,1)S(1)}, bf16[528,256]{1,0:T(8,128)(2,1)S(1)}, u32[]{:S(2)}, u32[]{:S(2)}) collective-permute-start(bf16[528,256]{1,0:T(8,128)(2,1)S(1)} %get-tuple-element.485), channel_id=1, source_target_pairs={{0,2},{1,3},{2,0},{3,1},{4,6},{5,7},{6,4},{7,5},{8,10},{9,11},{10,... | collective-permute-start | bytes 811016 | tf_op jit(solution)/shard_map/ppermute | solution.py:111
  181.2 24.7 %collective-permute-start.27 = (bf16[256,2048]{1,0:T(8,128)(2,1)}, bf16[256,2048]{1,0:T(8,128)(2,1)S(1)}, u32[]{:S(2)}, u32[]{:S(2)}) collective-permute-start(bf16[256,2048]{1,0:T(8,128)(2,1)} %get-tuple-element.341.refs_0_), channel_id=1, source_target_pairs={{0,2},{1,3},{2,0},{3,1},{4,6},{5,7},{6,4},{7,5},{8,10},{9,11},{10,... | collective-permute-start | bytes 3145736 | tf_op jit(solution)/shard_map/ppermute | solution.py:111
  206.0 17.9 %collective-permute-start.30 = (bf16[128,3072]{1,0:T(8,128)(2,1)S(1)}, bf16[128,3072]{1,0:T(8,128)(2,1)S(1)}, u32[]{:S(2)}, u32[]{:S(2)}) collective-permute-start(bf16[128,3072]{1,0:T(8,128)(2,1)S(1)} %slice.346), channel_id=1, source_target_pairs={{0,4},{8,0},{16,8},{24,16},{28,24},{20,28},{12,20},{4,12},{1,5},{9... | collective-permute-start | bytes 2359304 | tf_op jit(solution)/shard_map/ppermute | solution.py:80
  207.1 16.9 %collective-permute-start.29 = (bf16[128,3072]{1,0:T(8,128)(2,1)S(1)}, bf16[128,3072]{1,0:T(8,128)(2,1)S(1)}, u32[]{:S(2)}, u32[]{:S(2)}) collective-permute-start(bf16[128,3072]{1,0:T(8,128)(2,1)S(1)} %slice.345), channel_id=1, source_target_pairs={{0,8},{8,16},{16,24},{24,28},{28,20},{20,12},{12,4},{4,0},{1,9},{9... | collective-permute-start | bytes 2359304 | tf_op jit(solution)/shard_map/ppermute | solution.py:80
  208.1 23.0 %collective-permute-start.28 = (bf16[256,2048]{1,0:T(8,128)(2,1)S(1)}, bf16[256,2048]{1,0:T(8,128)(2,1)}, u32[]{:S(2)}, u32[]{:S(2)}) collective-permute-start(bf16[256,2048]{1,0:T(8,128)(2,1)S(1)} %copy-done.89), channel_id=1, source_target_pairs={{0,2},{1,3},{2,0},{3,1},{4,6},{5,7},{6,4},{7,5},{8,10},{9,11},{10,... | collective-permute-start | bytes 3145736 | tf_op jit(solution)/shard_map/ppermute | solution.py:111
  224.0 46.6 %collective-permute-start.33 = (bf16[256,3072]{1,0:T(8,128)(2,1)S(1)}, bf16[256,3072]{1,0:T(8,128)(2,1)}, u32[]{:S(2)}, u32[]{:S(2)}) collective-permute-start(bf16[256,3072]{1,0:T(8,128)(2,1)S(1)} %pad_maximum_fusion.2.refs_5_.refs_3_), channel_id=1, source_target_pairs={{0,8},{8,16},{16,24},{24,28},{28,20},{20,12},{12,4},{4,0},{1,9},{9... | collective-permute-start | bytes 4718600 | tf_op jit(solution)/shard_map/ppermute | solution.py:80
  225.7 45.0 %collective-permute-start.34 = (bf16[256,3072]{1,0:T(8,128)(2,1)S(1)}, bf16[256,3072]{1,0:T(8,128)(2,1)}, u32[]{:S(2)}, u32[]{:S(2)}) collective-permute-start(bf16[256,3072]{1,0:T(8,128)(2,1)S(1)} %pad_maximum_fusion.2.refs_5_.refs_3_), channel_id=1, source_target_pairs={{0,4},{8,0},{16,8},{24,16},{28,24},{20,28},{12,20},{4,12},{1,5},{9... | collective-permute-start | bytes 4718600 | tf_op jit(solution)/shard_map/ppermute | solution.py:80
  231.2 41.8 %collective-permute-start.38 = (bf16[256,2048]{1,0:T(8,128)(2,1)}, bf16[256,2048]{1,0:T(8,128)(2,1)}, u32[]{:S(2)}, u32[]{:S(2)}) collective-permute-start(bf16[256,2048]{1,0:T(8,128)(2,1)} %collective-permute-done.28.refs_2_.refs_0_), channel_id=1, source_target_pairs={{0,1},{1,0},{2,3},{3,2},{4,5},{5,4},{6,7},{7,6},{8,9},{9,8},{10,11... | collective-permute-start | bytes 3145736 | tf_op jit(solution)/shard_map/ppermute | solution.py:111
  270.7 41.5 %collective-permute-start.35 = (bf16[256,3072]{1,0:T(8,128)(2,1)}, bf16[256,3072]{1,0:T(8,128)(2,1)}, u32[]{:S(2)}, u32[]{:S(2)}) collective-permute-start(bf16[256,3072]{1,0:T(8,128)(2,1)} %collective-permute-done.33.refs_6_.refs_4_), channel_id=1, source_target_pairs={{0,8},{8,16},{16,24},{24,28},{28,20},{20,12},{12,4},{4,0},{1,9},{9... | collective-permute-start | bytes 4718600 | tf_op jit(solution)/shard_map/ppermute | solution.py:80
  271.9 40.3 %collective-permute-start.36 = (bf16[256,3072]{1,0:T(8,128)(2,1)}, bf16[256,3072]{1,0:T(8,128)(2,1)}, u32[]{:S(2)}, u32[]{:S(2)}) collective-permute-start(bf16[256,3072]{1,0:T(8,128)(2,1)} %collective-permute-done.34.refs_7_.refs_5_), channel_id=1, source_target_pairs={{0,4},{8,0},{16,8},{24,16},{28,24},{20,28},{12,20},{4,12},{1,5},{9... | collective-permute-start | bytes 4718600 | tf_op jit(solution)/shard_map/ppermute | solution.py:80
  273.0 79.5 %collective-permute-start.43 = (bf16[800,2048]{1,0:T(8,128)(2,1)S(1)}, bf16[800,2048]{1,0:T(8,128)(2,1)}, u32[]{:S(2)}, u32[]{:S(2)}) collective-permute-start(bf16[800,2048]{1,0:T(8,128)(2,1)S(1)} %copy-done.1), channel_id=1, source_target_pairs={{0,2},{1,3},{2,0},{3,1},{4,6},{5,7},{6,4},{7,5},{8,10},{9,11},{10,... | collective-permute-start | bytes 9830408 | tf_op jit(solution)/shard_map/ppermute | solution.py:111
  312.2 36.7 %collective-permute-start.39 = (bf16[256,3072]{1,0:T(8,128)(2,1)}, bf16[256,3072]{1,0:T(8,128)(2,1)S(1)}, u32[]{:S(2)}, u32[]{:S(2)}) collective-permute-start(bf16[256,3072]{1,0:T(8,128)(2,1)} %collective-permute-done.35.refs_8_.refs_6_), channel_id=1, source_target_pairs={{0,8},{8,16},{16,24},{24,28},{28,20},{20,12},{12,4},{4,0},{1,9},{9... | collective-permute-start | bytes 4718600 | tf_op jit(solution)/shard_map/ppermute | solution.py:80
  313.5 36.4 %collective-permute-start.40 = (bf16[256,3072]{1,0:T(8,128)(2,1)}, bf16[256,3072]{1,0:T(8,128)(2,1)S(1)}, u32[]{:S(2)}, u32[]{:S(2)}) collective-permute-start(bf16[256,3072]{1,0:T(8,128)(2,1)} %collective-permute-done.36.refs_9_.refs_7_), channel_id=1, source_target_pairs={{0,4},{8,0},{16,8},{24,16},{28,24},{20,28},{12,20},{4,12},{1,5},{9... | collective-permute-start | bytes 4718600 | tf_op jit(solution)/shard_map/ppermute | solution.py:80
  350.0 18.5 %collective-permute-start.42 = (bf16[128,3072]{1,0:T(8,128)(2,1)S(1)}, bf16[128,3072]{1,0:T(8,128)(2,1)S(1)}, u32[]{:S(2)}, u32[]{:S(2)}) collective-permute-start(bf16[128,3072]{1,0:T(8,128)(2,1)S(1)} %slice.351), channel_id=1, source_target_pairs={{0,4},{8,0},{16,8},{24,16},{28,24},{20,28},{12,20},{4,12},{1,5},{9... | collective-permute-start | bytes 2359304 | tf_op jit(solution)/shard_map/ppermute | solution.py:80
  350.8 18.7 %collective-permute-start.41 = (bf16[128,3072]{1,0:T(8,128)(2,1)S(1)}, bf16[128,3072]{1,0:T(8,128)(2,1)}, u32[]{:S(2)}, u32[]{:S(2)}) collective-permute-start(bf16[128,3072]{1,0:T(8,128)(2,1)S(1)} %slice.350), channel_id=1, source_target_pairs={{0,8},{8,16},{16,24},{24,28},{28,20},{20,12},{12,4},{4,0},{1,9},{9... | collective-permute-start | bytes 2359304 | tf_op jit(solution)/shard_map/ppermute | solution.py:80
  409.4 25.3 %collective-permute-start.46 = (bf16[256,2048]{1,0:T(8,128)(2,1)S(1)}, bf16[256,2048]{1,0:T(8,128)(2,1)S(1)}, u32[]{:S(2)}, u32[]{:S(2)}) collective-permute-start(bf16[256,2048]{1,0:T(8,128)(2,1)S(1)} %add_convert_fusion.5), channel_id=1, source_target_pairs={{0,2},{1,3},{2,0},{3,1},{4,6},{5,7},{6,4},{7,5},{8,10},{9,11},{10,... | collective-permute-start | bytes 3145736 | tf_op jit(solution)/shard_map/ppermute | solution.py:111
  437.3 35.2 %collective-permute-start.50 = (bf16[256,2048]{1,0:T(8,128)(2,1)S(1)}, bf16[256,2048]{1,0:T(8,128)(2,1)S(1)}, u32[]{:S(2)}, u32[]{:S(2)}) collective-permute-start(bf16[256,2048]{1,0:T(8,128)(2,1)S(1)} %add_convert_fusion.4), channel_id=1, source_target_pairs={{0,2},{1,3},{2,0},{3,1},{4,6},{5,7},{6,4},{7,5},{8,10},{9,11},{10,... | collective-permute-start | bytes 3145736 | tf_op jit(solution)/shard_map/ppermute | solution.py:111
  448.7 22.1 %collective-permute-start.48 = (bf16[528,256]{1,0:T(8,128)(2,1)}, bf16[528,256]{1,0:T(8,128)(2,1)S(1)}, u32[]{:S(2)}, u32[]{:S(2)}) collective-permute-start(bf16[528,256]{1,0:T(8,128)(2,1)} %get-tuple-element.385), channel_id=1, source_target_pairs={{0,2},{1,3},{2,0},{3,1},{4,6},{5,7},{6,4},{7,5},{8,10},{9,11},{10,... | collective-permute-start | bytes 811016 | tf_op jit(solution)/shard_map/ppermute | solution.py:111
  450.5 21.3 %collective-permute-start.49 = (bf16[528,256]{1,0:T(8,128)(2,1)}, bf16[528,256]{1,0:T(8,128)(2,1)S(1)}, u32[]{:S(2)}, u32[]{:S(2)}) collective-permute-start(bf16[528,256]{1,0:T(8,128)(2,1)} %get-tuple-element.386), channel_id=1, source_target_pairs={{0,3},{1,2},{2,1},{3,0},{4,7},{5,6},{6,5},{7,4},{8,11},{9,10},{10,... | collective-permute-start | bytes 811016 | tf_op jit(solution)/shard_map/ppermute | solution.py:111
  488.6 28.8 %collective-permute-start.54 = (bf16[256,2048]{1,0:T(8,128)(2,1)}, bf16[256,2048]{1,0:T(8,128)(2,1)S(1)}, u32[]{:S(2)}, u32[]{:S(2)}) collective-permute-start(bf16[256,2048]{1,0:T(8,128)(2,1)} %get-tuple-element.402), channel_id=1, source_target_pairs={{0,1},{1,0},{2,3},{3,2},{4,5},{5,4},{6,7},{7,6},{8,9},{9,8},{10,11... | collective-permute-start | bytes 3145736 | tf_op jit(solution)/shard_map/ppermute | solution.py:111
  489.1 28.1 %collective-permute-start.55 = (bf16[528,256]{1,0:T(8,128)(2,1)}, bf16[528,256]{1,0:T(8,128)(2,1)S(1)}, u32[]{:S(2)}, u32[]{:S(2)}) collective-permute-start(bf16[528,256]{1,0:T(8,128)(2,1)} %get-tuple-element.403), channel_id=1, source_target_pairs={{0,2},{1,3},{2,0},{3,1},{4,6},{5,7},{6,4},{7,5},{8,10},{9,11},{10,... | collective-permute-start | bytes 811016 | tf_op jit(solution)/shard_map/ppermute | solution.py:111
  490.0 27.3 %collective-permute-start.56 = (bf16[528,256]{1,0:T(8,128)(2,1)}, bf16[528,256]{1,0:T(8,128)(2,1)S(1)}, u32[]{:S(2)}, u32[]{:S(2)}) collective-permute-start(bf16[528,256]{1,0:T(8,128)(2,1)} %get-tuple-element.404), channel_id=1, source_target_pairs={{0,3},{1,2},{2,1},{3,0},{4,7},{5,6},{6,5},{7,4},{8,11},{9,10},{10,... | collective-permute-start | bytes 811016 | tf_op jit(solution)/shard_map/ppermute | solution.py:111
  517.7 40.8 %collective-permute-start.58 = (bf16[256,2048]{1,0:T(8,128)(2,1)S(1)}, bf16[256,2048]{1,0:T(8,128)(2,1)S(1)}, u32[]{:S(2)}, u32[]{:S(2)}) collective-permute-start(bf16[256,2048]{1,0:T(8,128)(2,1)S(1)} %add_convert_fusion.3), channel_id=1, source_target_pairs={{0,2},{1,3},{2,0},{3,1},{4,6},{5,7},{6,4},{7,5},{8,10},{9,11},{10,... | collective-permute-start | bytes 3145736 | tf_op jit(solution)/shard_map/ppermute | solution.py:111
  535.7 12.6 %collective-permute-start.65 = (bf16[512,256]{1,0:T(8,128)(2,1)S(1)}, bf16[512,256]{1,0:T(8,128)(2,1)S(1)}, u32[]{:S(2)}, u32[]{:S(2)}) collective-permute-start(bf16[512,256]{1,0:T(8,128)(2,1)S(1)} %get-tuple-element.493), channel_id=1, source_target_pairs={{0,3},{1,2},{2,1},{3,0},{4,7},{5,6},{6,5},{7,4},{8,11},{9,10},{10,... | collective-permute-start | bytes 786440 | tf_op jit(solution)/shard_map/ppermute | solution.py:111
  543.3 8.7 %collective-permute-start.62 = (bf16[2,2,80,128]{3,2,1,0:T(8,128)(2,1)S(1)}, bf16[2,2,80,128]{3,2,1,0:T(8,128)(2,1)S(1)}, u32[]{:S(2)}, u32[]{:S(2)}) collective-permute-start(bf16[2,2,80,128]{3,2,1,0:T(8,128)(2,1)S(1)} %get-tuple-element.425), channel_id=1, source_target_pairs={{24,0},{28,4},{25,1},{29,5},{26,2},{30,6},{27,3},{31,7}} | collective-permute-start | bytes 245768 | tf_op jit(solution)/shard_map/ppermute | solution.py:117
  544.6 10.0 %collective-permute-start.61 = (bf16[2,2,80,128]{3,2,1,0:T(8,128)(2,1)S(1)}, bf16[2,2,80,128]{3,2,1,0:T(8,128)(2,1)S(1)}, u32[]{:S(2)}, u32[]{:S(2)}) collective-permute-start(bf16[2,2,80,128]{3,2,1,0:T(8,128)(2,1)S(1)} %get-tuple-element.425), channel_id=1, source_target_pairs={{16,0},{20,4},{24,8},{28,12},{17,1},{21,5},{25,9},{29,13},{18,2},{... | collective-permute-start | bytes 245768 | tf_op jit(solution)/shard_map/ppermute | solution.py:117
  545.9 11.4 %collective-permute-start.60 = (bf16[2,2,224,128]{3,2,1,0:T(8,128)(2,1)S(1)}, bf16[2,2,224,128]{3,2,1,0:T(8,128)(2,1)S(1)}, u32[]{:S(2)}, u32[]{:S(2)}) collective-permute-start(bf16[2,2,224,128]{3,2,1,0:T(8,128)(2,1)S(1)} %get-tuple-element.424), channel_id=1, source_target_pairs={{8,0},{12,4},{16,8},{20,12},{24,16},{28,20},{9,1},{13,5},{17,9},{2... | collective-permute-start | bytes 688136 | tf_op jit(solution)/shard_map/ppermute | solution.py:117
  548.3 17.2 %collective-permute-start.64 = (bf16[512,256]{1,0:T(8,128)(2,1)S(1)}, bf16[512,256]{1,0:T(8,128)(2,1)S(1)}, u32[]{:S(2)}, u32[]{:S(2)}) collective-permute-start(bf16[512,256]{1,0:T(8,128)(2,1)S(1)} %get-tuple-element.494), channel_id=1, source_target_pairs={{0,2},{1,3},{2,0},{3,1},{4,6},{5,7},{6,4},{7,5},{8,10},{9,11},{10,... | collective-permute-start | bytes 786440 | tf_op jit(solution)/shard_map/ppermute | solution.py:111
  552.0 13.5 %collective-permute-start.63 = (bf16[512,256]{1,0:T(8,128)(2,1)S(1)}, bf16[512,256]{1,0:T(8,128)(2,1)S(1)}, u32[]{:S(2)}, u32[]{:S(2)}) collective-permute-start(bf16[512,256]{1,0:T(8,128)(2,1)S(1)} %get-tuple-element.495), channel_id=1, source_target_pairs={{0,1},{1,0},{2,3},{3,2},{4,5},{5,4},{6,7},{7,6},{8,9},{9,8},{10,11... | collective-permute-start | bytes 786440 | tf_op jit(solution)/shard_map/ppermute | solution.py:111
  554.6 10.9 %collective-permute-start.68 = (bf16[512,256]{1,0:T(8,128)(2,1)S(1)}, bf16[512,256]{1,0:T(8,128)(2,1)S(1)}, u32[]{:S(2)}, u32[]{:S(2)}) collective-permute-start(bf16[512,256]{1,0:T(8,128)(2,1)S(1)} %get-tuple-element.490), channel_id=1, source_target_pairs={{0,3},{1,2},{2,1},{3,0},{4,7},{5,6},{6,5},{7,4},{8,11},{9,10},{10,... | collective-permute-start | bytes 786440 | tf_op jit(solution)/shard_map/ppermute | solution.py:111
  557.3 11.0 %collective-permute-start.67 = (bf16[512,256]{1,0:T(8,128)(2,1)S(1)}, bf16[512,256]{1,0:T(8,128)(2,1)S(1)}, u32[]{:S(2)}, u32[]{:S(2)}) collective-permute-start(bf16[512,256]{1,0:T(8,128)(2,1)S(1)} %get-tuple-element.491), channel_id=1, source_target_pairs={{0,2},{1,3},{2,0},{3,1},{4,6},{5,7},{6,4},{7,5},{8,10},{9,11},{10,... | collective-permute-start | bytes 786440 | tf_op jit(solution)/shard_map/ppermute | solution.py:111
  558.5 9.8 %collective-permute-start.66 = (bf16[512,256]{1,0:T(8,128)(2,1)S(1)}, bf16[512,256]{1,0:T(8,128)(2,1)S(1)}, u32[]{:S(2)}, u32[]{:S(2)}) collective-permute-start(bf16[512,256]{1,0:T(8,128)(2,1)S(1)} %get-tuple-element.492), channel_id=1, source_target_pairs={{0,1},{1,0},{2,3},{3,2},{4,5},{5,4},{6,7},{7,6},{8,9},{9,8},{10,11... | collective-permute-start | bytes 786440 | tf_op jit(solution)/shard_map/ppermute | solution.py:111
  575.1 14.2 %collective-permute-start.70 = (bf16[256,2048]{1,0:T(8,128)(2,1)}, bf16[256,2048]{1,0:T(8,128)(2,1)S(1)}, u32[]{:S(2)}, u32[]{:S(2)}) collective-permute-start(bf16[256,2048]{1,0:T(8,128)(2,1)} %get-tuple-element.441), channel_id=1, source_target_pairs={{0,1},{1,0},{2,3},{3,2},{4,5},{5,4},{6,7},{7,6},{8,9},{9,8},{10,11... | collective-permute-start | bytes 3145736 | tf_op jit(solution)/shard_map/ppermute | solution.py:111
  575.3 39.2 %collective-permute-start.83 = (bf16[800,2048]{1,0:T(8,128)(2,1)S(1)}, bf16[800,2048]{1,0:T(8,128)(2,1)S(1)}, u32[]{:S(2)}, u32[]{:S(2)}) collective-permute-start(bf16[800,2048]{1,0:T(8,128)(2,1)S(1)} %copy-done.1), channel_id=1, source_target_pairs={{0,1},{1,0},{2,3},{3,2},{4,5},{5,4},{6,7},{7,6},{8,9},{9,8},{10,11... | collective-permute-start | bytes 9830408 | tf_op jit(solution)/shard_map/ppermute | solution.py:111
  575.7 39.6 %collective-permute-start.84 = (bf16[800,2048]{1,0:T(8,128)(2,1)}, bf16[800,2048]{1,0:T(8,128)(2,1)S(1)}, u32[]{:S(2)}, u32[]{:S(2)}) collective-permute-start(bf16[800,2048]{1,0:T(8,128)(2,1)} %collective-permute-done.43.refs_10_), channel_id=1, source_target_pairs={{0,1},{1,0},{2,3},{3,2},{4,5},{5,4},{6,7},{7,6},{8,9},{9,8},{10,11... | collective-permute-start | bytes 9830408 | tf_op jit(solution)/shard_map/ppermute | solution.py:111
  576.4 8.8 %collective-permute-start.73 = (bf16[288,256]{1,0:T(8,128)(2,1)S(1)}, bf16[288,256]{1,0:T(8,128)(2,1)S(1)}, u32[]{:S(2)}, u32[]{:S(2)}) collective-permute-start(bf16[288,256]{1,0:T(8,128)(2,1)S(1)} %get-tuple-element.502), channel_id=1, source_target_pairs={{0,2},{1,3},{2,0},{3,1},{4,6},{5,7},{6,4},{7,5},{8,10},{9,11},{10,... | collective-permute-start | bytes 442376 | tf_op jit(solution)/shard_map/ppermute | solution.py:111
  591.0 8.1 %collective-permute-start.76 = (bf16[512,128]{1,0:T(8,128)(2,1)S(1)}, bf16[512,128]{1,0:T(8,128)(2,1)S(1)}, u32[]{:S(2)}, u32[]{:S(2)}) collective-permute-start(bf16[512,128]{1,0:T(8,128)(2,1)S(1)} %get-tuple-element.458), channel_id=1, source_target_pairs={{0,2},{1,3},{2,0},{3,1},{4,6},{5,7},{6,4},{7,5},{8,10},{9,11},{10,... | collective-permute-start | bytes 393224 | tf_op jit(solution)/shard_map/ppermute | solution.py:111
  605.4 8.0 %collective-permute-start.81 = (bf16[1056,128]{1,0:T(8,128)(2,1)S(1)}, bf16[1056,128]{1,0:T(8,128)(2,1)S(1)}, u32[]{:S(2)}, u32[]{:S(2)}) collective-permute-start(bf16[1056,128]{1,0:T(8,128)(2,1)S(1)} %pad_maximum_fusion.4), channel_id=1, source_target_pairs={{0,4},{4,0},{8,12},{12,8},{16,20},{20,16},{24,28},{28,24},{1,5},{5... | collective-permute-start | bytes 811016 | tf_op jit(solution)/shard_map/ppermute | solution.py:111
  606.1 21.7 %collective-permute-start.52 = (bf16[256,2048]{1,0:T(8,128)(2,1)}, bf16[256,2048]{1,0:T(8,128)(2,1)}, u32[]{:S(2)}, u32[]{:S(2)}) collective-permute-start(bf16[256,2048]{1,0:T(8,128)(2,1)} %get-tuple-element.391), channel_id=1, source_target_pairs={{0,1},{1,0},{2,3},{3,2},{4,5},{5,4},{6,7},{7,6},{8,9},{9,8},{10,11... | collective-permute-start | bytes 3145736 | tf_op jit(solution)/shard_map/ppermute | solution.py:111
  613.5 11.7 %collective-permute-start.82 = (bf16[1056,128]{1,0:T(8,128)(2,1)S(1)}, bf16[1056,128]{1,0:T(8,128)(2,1)S(1)}, u32[]{:S(2)}, u32[]{:S(2)}) collective-permute-start(bf16[1056,128]{1,0:T(8,128)(2,1)S(1)} %add_convert_fusion.7), channel_id=1, source_target_pairs={{0,8},{4,12},{8,0},{12,4},{16,24},{20,28},{24,16},{28,20},{1,9},{5... | collective-permute-start | bytes 811016 | tf_op jit(solution)/shard_map/ppermute | solution.py:111
  614.4 37.4 %collective-permute-start.69 = (bf16[256,2048]{1,0:T(8,128)(2,1)}, bf16[256,2048]{1,0:T(8,128)(2,1)}, u32[]{:S(2)}, u32[]{:S(2)}) collective-permute-start(bf16[256,2048]{1,0:T(8,128)(2,1)} %get-tuple-element.438), channel_id=1, source_target_pairs={{0,1},{1,0},{2,3},{3,2},{4,5},{5,4},{6,7},{7,6},{8,9},{9,8},{10,11... | collective-permute-start | bytes 3145736 | tf_op jit(solution)/shard_map/ppermute | solution.py:111
  614.5 25.6 %collective-permute-start.71 = (bf16[256,2048]{1,0:T(8,128)(2,1)S(1)}, bf16[256,2048]{1,0:T(8,128)(2,1)S(1)}, u32[]{:S(2)}, u32[]{:S(2)}) collective-permute-start(bf16[256,2048]{1,0:T(8,128)(2,1)S(1)} %add_convert_fusion.1), channel_id=1, source_target_pairs={{0,2},{1,3},{2,0},{3,1},{4,6},{5,7},{6,4},{7,5},{8,10},{9,11},{10,... | collective-permute-start | bytes 3145736 | tf_op jit(solution)/shard_map/ppermute | solution.py:111
  625.3 24.5 %collective-permute-start.85 = (bf16[1056,128]{1,0:T(8,128)(2,1)S(1)}, bf16[1056,128]{1,0:T(8,128)(2,1)S(1)}, u32[]{:S(2)}, u32[]{:S(2)}) collective-permute-start(bf16[1056,128]{1,0:T(8,128)(2,1)S(1)} %add_convert_fusion.6), channel_id=1, source_target_pairs={{0,16},{4,20},{8,24},{12,28},{16,0},{20,4},{24,8},{28,12},{1,17},{... | collective-permute-start | bytes 811016 | tf_op jit(solution)/shard_map/ppermute | solution.py:111
  (149 other events, 1606.4 us)
